TPU v7x, 32 devices: a whole 2x2x4 slice. The times are simulated.
32 devices in a mesh: lat: 4 (over x, core), lon: 8 (over z, y).
Axes of the slice: x: 2, y: 2, z: 4, core: 2. Of those that a mesh axis runs over, the one named last changes fastest.
Arguments:
- queries: bfloat16 [32, 128, 512], P('lat', 'lon'), may hold values from -180 to 180
- key_cells: bfloat16 [32, 128, 512], P('lat', 'lon'), may hold values from -15 to 15
- value_cells: bfloat16 [32, 128, 512], P('lat', 'lon'), may hold values from -5 to 5
- grad_output: bfloat16 [32, 128, 512], P('lat', 'lon'), may hold values from -5 to 5
- rel_bias: float32 [8, 169], replicated, may hold values from -4 to 4
Outputs:
- output: bfloat16 [32, 128, 512], P('lat', 'lon')
- grad_query: bfloat16 [32, 128, 512], P('lat', 'lon')
- grad_key: bfloat16 [32, 128, 512], P('lat', 'lon')
- grad_value: bfloat16 [32, 128, 512], P('lat', 'lon')
All inputs are finite; a program needn't handle non-finite values.
Results may differ from a plain program's by a relative error of at most 0.009.
Values may be sent and summed in bfloat16 or wider, within the bound.
No kernel may reach another device: no remote copies, remote signals or barrier semaphores. Data moves between devices by JAX's collectives and lax.ppermute only.
A program may use at most 64 MiB of HBM per device.

v0:
```python
import jax
import jax.numpy as jnp
from jax import lax
from jax.sharding import PartitionSpec as P

HEAD_DIM = 64
TILE = 8
RADIUS = 6


HIGH = lax.Precision.HIGHEST


def padded_2(block, sides, width):
    for axis, dim in sides:
        count = lax.axis_size(axis)
        forward = [(i, i + 1) for i in range(count - 1)]
        forward.append((count - 1, 0))
        backward = [(target, source) for source, target in forward]
        low = lax.ppermute(
            lax.slice_in_dim(block, block.shape[dim] - width, None, axis=dim), axis, forward
        )
        high = lax.ppermute(lax.slice_in_dim(block, 0, width, axis=dim), axis, backward)
        block = jnp.concatenate([low, block, high], axis=dim)
    return block


def shifted(shard, axis, by):
    count = lax.axis_size(axis)
    return lax.ppermute(shard, axis, [(i, (i + by) % count) for i in range(count)])


def from_behind(value, axis, steps):
    count = lax.axis_size(axis)
    leading, last = (max(0, -steps), min(count, count - steps))
    return lax.ppermute(value, axis, [(source, source + steps) for source in range(leading, last)])


def offset_onehot(inner_len, outer_len, span_len, direction, offset):
    shape_all = (inner_len, outer_len, span_len)
    offset_index = lax.broadcasted_iota(jnp.int32, shape_all, 2)
    inner_index = lax.broadcasted_iota(jnp.int32, shape_all, 0)
    outer_index = lax.broadcasted_iota(jnp.int32, shape_all, 1)
    return (offset_index == direction * (outer_index - inner_index) + offset).astype(jnp.float32)


def expand_bias(rel_bias, direction, offset):
    span_len = 2 * RADIUS + 1
    extent = TILE + 2 * RADIUS
    head_count = rel_bias.shape[0]
    offsets_table = rel_bias.reshape(head_count, span_len, span_len)
    onehot = offset_onehot(TILE, extent, span_len, direction, offset)
    partial_sum = jnp.einsum("hab,jcb->hajc", offsets_table, onehot, precision=HIGH)
    expanded = jnp.einsum("ira,hajc->hijrc", onehot, partial_sum, precision=HIGH)
    inside = jnp.einsum("ira,jcb->ijrc", onehot, onehot, precision=HIGH) > 0.5
    return (
        expanded.reshape(head_count, TILE * TILE, extent * extent),
        inside.reshape(TILE * TILE, extent * extent),
    )


def to_tiles(values):
    height, breadth, channels = values.shape
    arranged = values.reshape(height // TILE, TILE, breadth // TILE, TILE, channels).transpose(
        0, 2, 1, 3, 4
    )
    return arranged.reshape(-1, TILE * TILE, channels)


def from_tiles(tiled, height, breadth):
    channels = tiled.shape[-1]
    arranged = tiled.reshape(height // TILE, breadth // TILE, TILE, TILE, channels).transpose(
        0, 2, 1, 3, 4
    )
    return arranged.reshape(height, breadth, channels)


def neighbourhoods(padded, breadth):
    extent = TILE + 2 * RADIUS
    pieces = []
    for col_tile in range(breadth // TILE):
        pieces.append(padded[0:extent, col_tile * TILE : col_tile * TILE + extent])
    stacked = jnp.stack(pieces)
    return stacked.reshape(len(pieces), extent * extent, padded.shape[-1])


def query_group(
    query_tiles, key_blocks, value_blocks, grad_tiles, bias_part, allowed, factor, group_size
):
    tile_count, query_len, span_cols = query_tiles.shape
    key_len = key_blocks.shape[1]
    head_size = span_cols // group_size
    query_heads = query_tiles.reshape(tile_count, query_len, group_size, head_size)
    grad_heads = grad_tiles.reshape(tile_count, query_len, group_size, head_size)
    key_heads = key_blocks.reshape(tile_count, key_len, group_size, head_size)
    value_heads = value_blocks.reshape(tile_count, key_len, group_size, head_size)
    scores = (
        jnp.einsum("tqhd,tkhd->thqk", query_heads, key_heads, preferred_element_type=jnp.float32)
        * factor
        + bias_part[None]
    )
    scores = jnp.where(allowed[:, None], scores, -jnp.inf)
    row_max = jnp.max(scores, axis=-1, keepdims=True)
    log_total = row_max + jnp.log(jnp.sum(jnp.exp(scores - row_max), axis=-1, keepdims=True))
    probability = jnp.exp(scores - log_total)
    weights = probability.astype(jnp.bfloat16)
    attended = jnp.einsum(
        "thqk,tkhd->tqhd", weights, value_heads, preferred_element_type=jnp.float32
    )
    row_dot = jnp.sum(grad_heads.astype(jnp.float32) * attended, axis=-1)
    grad_prob = jnp.einsum(
        "tqhd,tkhd->thqk", grad_heads, value_heads, preferred_element_type=jnp.float32
    )
    dscore = (probability * (grad_prob - jnp.transpose(row_dot, (0, 2, 1))[..., None])).astype(
        jnp.bfloat16
    )
    grad_q = (
        jnp.einsum("thqk,tkhd->tqhd", dscore, key_heads, preferred_element_type=jnp.float32)
        * factor
    )
    return (
        attended.reshape(tile_count, query_len, span_cols),
        grad_q.reshape(tile_count, query_len, span_cols),
        jnp.transpose(log_total[..., 0], (0, 2, 1)),
        row_dot,
        dscore,
        weights,
        query_heads,
        grad_heads,
    )


def shards(queries, key_cells, value_cells, grad_output, rel_bias):
    height, breadth, channels = queries.shape
    head_count = rel_bias.shape[0]
    group_size = 4
    group_cols = group_size * HEAD_DIM
    extent = TILE + 2 * RADIUS
    factor = HEAD_DIM ** (-0.5)
    lat_total = height * lax.axis_size("lat")
    lat_first = lax.axis_index("lat") * height
    grid_shape = (height // TILE, breadth // TILE, extent)
    tile_row = lax.broadcasted_iota(jnp.int32, grid_shape, 0)
    position = lax.broadcasted_iota(jnp.int32, grid_shape, 2)
    global_row = lat_first + tile_row * TILE - RADIUS + position
    row_inside = ((global_row >= 0) & (global_row < lat_total)).reshape(-1, extent, 1)
    cell_inside = jnp.broadcast_to(row_inside, (row_inside.shape[0], extent, extent)).reshape(
        -1, extent * extent
    )
    paired = jnp.stack([key_cells, value_cells])
    padded = padded_2(paired, (("lat", 1), ("lon", 2)), RADIUS)
    query_tiles = to_tiles(queries)
    grad_tiles = to_tiles(grad_output)
    bias_query, inside_query = expand_bias(rel_bias, 1, 0)
    allowed = inside_query[None] & cell_inside[:, None, :]
    collected = jnp.zeros((2, height + 2 * RADIUS, breadth + 2 * RADIUS, channels), jnp.float32)
    outputs, grads_q, totals, dots = ([], [], [], [])
    for group in range(head_count // group_size):
        start_col = group * group_cols
        key_blocks = neighbourhoods(padded[0, :, :, start_col : start_col + group_cols], breadth)
        value_blocks = neighbourhoods(padded[1, :, :, start_col : start_col + group_cols], breadth)
        results = query_group(
            query_tiles[:, :, start_col : start_col + group_cols],
            key_blocks,
            value_blocks,
            grad_tiles[:, :, start_col : start_col + group_cols],
            bias_query[group * group_size : (group + 1) * group_size],
            allowed,
            factor,
            group_size,
        )
        attended, grad_q, log_total, row_dot, dscore, weights, query_heads, grad_heads = results
        outputs.append(attended.astype(jnp.bfloat16))
        grads_q.append(grad_q.astype(jnp.bfloat16))
        totals.append(log_total)
        dots.append(row_dot)
        grad_k = (
            jnp.einsum("thqk,tqhd->tkhd", dscore, query_heads, preferred_element_type=jnp.float32)
            * factor
        )
        grad_v = jnp.einsum(
            "thqk,tqhd->tkhd", weights, grad_heads, preferred_element_type=jnp.float32
        )
        both_terms = jnp.stack([grad_k, grad_v]).reshape(
            2, grad_k.shape[0], extent, extent, group_cols
        )
        index = 0
        for col_tile in range(breadth // TILE):
            row_start = 0
            col_start = col_tile * TILE
            collected = collected.at[
                :,
                row_start : row_start + extent,
                col_start : col_start + extent,
                start_col : start_col + group_cols,
            ].add(both_terms[:, index])
            index = index + 1
    output = from_tiles(jnp.concatenate(outputs, axis=-1), height, breadth)
    grad_query = from_tiles(jnp.concatenate(grads_q, axis=-1), height, breadth)
    westward = shifted(collected[:, :, :RADIUS], "lon", -1)
    eastward = shifted(collected[:, :, breadth + RADIUS :], "lon", 1)
    collected = collected[:, :, RADIUS : breadth + RADIUS]
    collected = collected.at[:, :, breadth - RADIUS :].add(westward)
    collected = collected.at[:, :, :RADIUS].add(eastward)
    northward = from_behind(collected[:, :RADIUS], "lat", -1)
    southward = from_behind(collected[:, height + RADIUS :], "lat", 1)
    collected = collected[:, RADIUS : height + RADIUS]
    collected = collected.at[:, height - RADIUS :].add(northward)
    collected = collected.at[:, :RADIUS].add(southward)
    grad_key = collected[0].astype(jnp.bfloat16)
    grad_value = collected[1].astype(jnp.bfloat16)
    return (output, grad_query, grad_key, grad_value)


def solution(mesh):
    in_specs = (
        P("lat", "lon", None),
        P("lat", "lon", None),
        P("lat", "lon", None),
        P("lat", "lon", None),
        P(),
    )
    out_specs = (
        P("lat", "lon", None),
        P("lat", "lon", None),
        P("lat", "lon", None),
        P("lat", "lon", None),
    )
    return jax.shard_map(shards, mesh=mesh, in_specs=in_specs, out_specs=out_specs, check_vma=False)
```

profile of v0, /device:TPU:30, one launch (start us, length us, event | category | flops | bytes accessed | tf_op | source)
XLA Modules:
  0.0 147.5 jit_solution(1028451981249594400)
XLA Ops:
  0.6 1.1 fusion.31
  4.2 2.8 %convolution_bitcast_fusion = f32[8,8,8,20,20]{3,4,1,2,0:T(8,128)S(1)} fusion(f32[8,13,8,20,1]{3,1,4,2,0:T(8,128)S(1)} %convolution_bitcast_fusion.3), kind=kOutput, calls=%fused_computation | convolution fusion | flops 31952960 | bytes 885760 | tf_op jit(solution)/shard_map/ira,hajc->hijrc/dot_general | solution.py:54
  7.0 3.0 %fusion.49 = (f32[4,8,8,20,20]{3,4,1,2,0:T(8,128)}, f32[4,8,8,20,20]{3,4,1,2,0:T(8,128)}) fusion(f32[8,8,8,20,20]{3,4,1,2,0:T(8,128)S(1)} %convolution_bitcast_fusion), kind=kLoop, calls=%fused_computation.105 | loop fusion | bytes 1638400 | tf_op jit(solution)/shard_map/slice | solution.py:167
  14.4 4.2 %collective-permute-start.2 = (bf16[2,20,6,512]{3,2,1,0:T(8,128)(2,1)}, bf16[2,20,6,512]{3,2,1,0:T(8,128)(2,1)}, u32[]{:S(2)}, u32[]{:S(2)}) collective-permute-start(bf16[2,20,6,512]{3,2,1,0:T(8,128)(2,1)} %get-tuple-element.112), channel_id=1, source_target_pairs={{0,1},{1,2},{2,3},{3,4},{4,5},{5,6},{6,7},{7,0},{8,9},{9,10},{10,1... | collective-permute-start | bytes 737288 | tf_op jit(solution)/shard_map/ppermute | solution.py:20
  19.4 3.2 %copy.138 = f32[4,8,8,20,20]{4,3,2,1,0:T(8,128)S(1)} copy(f32[4,8,8,20,20]{3,4,1,2,0:T(8,128)} %get-tuple-element.101) | data formatting | bytes 819200 | tf_op jit(solution)/shard_map/slice | solution.py:167
  22.6 1.5 %add.109 = f32[4,64,400]{2,1,0:T(8,128)} reshape(f32[4,8,8,20,20]{4,3,2,1,0:T(8,128)S(1)} %copy.138) | data formatting | bytes 819200 | tf_op jit(solution)/shard_map/add | solution.py:98
  25.0 1.8 %and.54 = pred[64,400]{1,0:T(8,128)(4,1)} reshape(pred[8,8,20,20]{3,2,1,0:T(8,128)(4,1)} %fusion.26) | data formatting | bytes 51200 | tf_op jit(solution)/shard_map/and | solution.py:155
  26.9 1.0 copy.142
  27.8 3.2 %copy.131 = f32[4,8,8,20,20]{4,3,2,1,0:T(8,128)S(1)} copy(f32[4,8,8,20,20]{3,4,1,2,0:T(8,128)} %get-tuple-element.100) | data formatting | bytes 819200 | tf_op jit(solution)/shard_map/slice | solution.py:167
  31.0 1.5 %add.105 = f32[4,64,400]{2,1,0:T(8,128)} reshape(f32[4,8,8,20,20]{4,3,2,1,0:T(8,128)S(1)} %copy.131) | data formatting | bytes 819200 | tf_op jit(solution)/shard_map/add | solution.py:98
  32.5 1.0 copy.170
  34.3 1.9 %pad_maximum_fusion = bf16[2,20,28,512]{3,2,1,0:T(8,128)(2,1)S(1)} fusion(bf16[2,20,6,512]{3,2,1,0:T(8,128)(2,1)} %collective-permute-done.3, bf16[2,6,16,512]{3,2,1,0:T(8,128)(2,1)} %copy-done.27, bf16[1,8,16,512]{3,2,1,0:T(8,128)(2,1)S(1)} %bitcast.157, bf16[1,8,16,512]{3,2,1,0:T(8,128)(2,1)S(1)} %bitcast.154, bf16[2,6,16,512]{3,2,1,0:T(8,128)(2,1)} %copy-done.28, ...), kind=kLoop, calls=%fused_computation.23 | loop fusion | flops 6881280 | bytes 2293760 | tf_op jit(solution)/shard_map/concatenate | solution.py:24
  40.2 1.3 stack.67
  41.5 1.0 copy.126
  42.7 1.0 copy.125
  44.5 1.4 convolution_bitcast_fusion.1
  45.9 1.1 multiply_reduce_fusion
  47.0 1.2 fusion.13
  49.4 1.1 multiply_reduce_fusion.1
  51.7 1.3 fusion.1
  53.0 2.1 %copy.150 = f32[2,400,4,64]{3,2,0,1:T(4,128)S(1)} copy(f32[2,400,4,64]{1,3,2,0:T(8,128)} %fusion.1) | data formatting | bytes 1638400 | tf_op jit(solution)/shard_map/mul | solution.py:178
  55.1 2.1 %stack.78 = f32[1,2,20,20,256]{4,1,3,2,0:T(2,128)} reshape(f32[2,400,4,64]{3,2,0,1:T(4,128)S(1)} %copy.150) | data formatting | bytes 1638400 | tf_op jit(solution)/shard_map/stack | solution.py:184
  57.2 2.3 %constant_dynamic-update-slice_fusion.1 = f32[2,2,20,20,256]{4,1,3,2,0:T(2,128)} fusion(f32[1,2,20,20,256]{4,1,3,2,0:T(2,128)} %stack.78), kind=kLoop, calls=%fused_computation.91 | loop fusion | bytes 1638400
  60.5 2.1 %stack.79 = f32[1,2,20,20,256]{4,1,3,2,0:T(2,128)} reshape(f32[2,400,4,64]{3,2,0,1:T(4,128)S(1)} %copy.151) | data formatting | bytes 1638400 | tf_op jit(solution)/shard_map/stack | solution.py:184
  62.6 1.5 %constant_dynamic-update-slice_fusion = f32[2,2,20,20,256]{4,1,3,2,0:T(2,128)S(1)} fusion(f32[2,2,20,20,256]{4,1,3,2,0:T(2,128)S(1)} %copy-done.4, f32[1,2,20,20,256]{4,1,3,2,0:T(2,128)} %stack.79), kind=kLoop, calls=%fused_computation.90 | loop fusion | bytes 1638400 | tf_op jit(solution)/shard_map/stack | solution.py:184
  64.1 2.2 %fusion.51 = (f32[2,1,20,20,256]{4,1,3,2,0:T(1,128)}, f32[2,1,20,20,256]{4,1,3,2,0:T(1,128)S(1)}) fusion(f32[2,2,20,20,256]{4,1,3,2,0:T(2,128)S(1)} %constant_dynamic-update-slice_fusion), kind=kLoop, calls=%fused_computation.107 | loop fusion | bytes 3276800 | tf_op jit(solution)/shard_map/slice | solution.py:196
  66.3 1.5 %copy.180 = f32[2,1,20,20,256]{4,0,3,2,1:T(2,128)} copy(f32[2,1,20,20,256]{4,1,3,2,0:T(1,128)S(1)} %get-tuple-element.105) | data formatting | bytes 1638400 | tf_op jit(solution)/shard_map/slice | solution.py:196
  69.0 1.5 %reshape.499 = f32[1,2,20,20,256]{4,0,3,2,1:T(1,128)S(1)} reshape(f32[2,400,4,64]{3,2,1,0:T(4,128)S(1)} %copy.164) | data formatting | bytes 1638400 | tf_op jit(solution)/shard_map/stack | solution.py:184
  70.5 2.0 %copy.165 = f32[2,400,4,64]{3,2,1,0:T(4,128)S(1)} copy(f32[2,400,4,64]{1,3,2,0:T(8,128)} %convolution_bitcast_fusion.1) | data formatting | bytes 1638400 | tf_op jit(solution)/shard_map/stack | solution.py:184
  72.5 2.4 %reshape.500 = f32[1,2,20,20,256]{4,0,3,2,1:T(1,128)} reshape(f32[2,400,4,64]{3,2,1,0:T(4,128)S(1)} %copy.165) | data formatting | bytes 1638400 | tf_op jit(solution)/shard_map/stack | solution.py:184
  74.9 2.3 %scatter-add.26 = f32[2,20,28,512]{3,0,2,1:T(2,128)S(1)} pad(f32[2,20,20,256]{3,0,2,1:T(2,128)} %bitcast.151, f32[]{:T(128)} %constant.234.clone.1), padding=0_0x0_0x0_8x0_256 | pad | bytes 3112964 | tf_op jit(solution)/shard_map/scatter-add | solution.py:196
  77.3 1.0 fusion.25
  78.3 3.7 %add_select_fusion = f32[2,20,20,256]{3,0,2,1:T(2,128)} fusion(f32[1,2,20,20,256]{4,0,3,2,1:T(1,128)S(1)} %reshape.499, f32[1,2,20,20,256]{4,0,3,2,1:T(1,128)S(1)} %copy-done.3, f32[2,20,28,512]{3,0,2,1:T(2,128)S(1)} %fusion.25, s32[]{:T(128)} %bitcast.41, s32[]{:T(128)} %bitcast.42, pred[]{:T(512)} %and_reduce_fusion), kind=kLoop, calls=%fused_computation.27 | loop fusion | flops 614400 | bytes 3276809 | tf_op jit(solution)/shard_map/select.10
  82.0 17.5 %scatter-add.30 = f32[2,20,28,512]{3,0,2,1:T(2,128)S(1)} dynamic-update-slice(f32[2,20,28,512]{3,0,2,1:T(2,128)S(1)} %fusion.25, f32[2,20,20,256]{3,0,2,1:T(2,128)} %add_select_fusion, s32[]{:T(128)} %constant.239.clone.1, s32[]{:T(128)} %constant.239.clone.1, s32[]{:T(128)} %bitcast.41, s32[]{:T(128)} %bitcast.42) | dynamic-update-slice | bytes 1638404 | tf_op jit(solution)/shard_map/scatter-add | solution.py:196
  99.5 2.0 %fusion.24 = f32[2,20,28,512]{3,0,2,1:T(2,128)S(1)} fusion(f32[2,20,28,512]{3,0,2,1:T(2,128)S(1)} %scatter-add.30, f32[1,2,20,20,256]{4,0,3,2,1:T(1,128)} %reshape.500, f32[1,2,20,20,256]{4,0,3,2,1:T(1,128)S(1)} %reshape.499), kind=kLoop, calls=%fused_computation.47 | loop fusion | flops 409600 | bytes 3276800 | tf_op jit(solution)/shard_map/scatter-add | solution.py:196
  101.6 1.3 fusion.50
  102.9 1.5 %slice.429 = f32[2,20,16,512]{3,0,2,1:T(2,128)} slice(f32[2,20,28,512]{3,0,2,1:T(2,128)S(1)} %fusion.24), slice={[0:2], [0:20], [6:22], [0:512]} | slice | bytes 2621440 | tf_op jit(solution)/shard_map/slice | solution.py:202
  104.4 1.0 copy.139
  105.6 1.0 copy.132
  107.4 4.7 %collective-permute-start.5 = (f32[2,20,6,512]{3,0,2,1:T(2,128)}, f32[2,20,6,512]{3,0,2,1:T(2,128)S(1)}, u32[]{:S(2)}, u32[]{:S(2)}) collective-permute-start(f32[2,20,6,512]{3,0,2,1:T(2,128)} %get-tuple-element.102), channel_id=1, source_target_pairs={{0,1},{1,2},{2,3},{3,4},{4,5},{5,6},{6,7},{7,0},{8,9},{9,10},{10,1... | collective-permute-start | bytes 1474568 | tf_op jit(solution)/shard_map/ppermute | solution.py:30
  113.1 12.1 %collective-permute-done.4 = f32[2,20,6,512]{3,0,2,1:T(2,128)} collective-permute-done((f32[2,20,6,512]{3,0,2,1:T(2,128)}, f32[2,20,6,512]{3,0,2,1:T(2,128)}, u32[]{:S(2)}, u32[]{:S(2)}) %collective-permute-start.4) | collective-permute-done | bytes 491552 | tf_op jit(solution)/shard_map/ppermute | solution.py:30
  125.2 2.1 %fusion.28 = f32[2,20,16,512]{3,0,2,1:T(2,128)} fusion(f32[2,20,16,512]{3,0,2,1:T(2,128)} %slice.429, f32[2,20,6,512]{3,0,2,1:T(2,128)} %collective-permute-done.4, f32[2,20,28,512]{3,0,2,1:T(2,128)S(1)} %fusion.24), kind=kLoop, calls=%fused_computation.61 | loop fusion | flops 122880 | bytes 1474560 | tf_op jit(solution)/shard_map/scatter-add | solution.py:203
  127.3 2.7 %collective-permute-done.5 = f32[2,20,6,512]{3,0,2,1:T(2,128)S(1)} collective-permute-done((f32[2,20,6,512]{3,0,2,1:T(2,128)}, f32[2,20,6,512]{3,0,2,1:T(2,128)S(1)}, u32[]{:S(2)}, u32[]{:S(2)}) %collective-permute-start.5) | collective-permute-done | bytes 491552 | tf_op jit(solution)/shard_map/ppermute | solution.py:30
  130.0 2.1 %fusion.27 = f32[2,20,16,512]{3,0,2,1:T(2,128)} fusion(f32[2,20,16,512]{3,0,2,1:T(2,128)} %fusion.28, f32[2,20,6,512]{3,0,2,1:T(2,128)S(1)} %collective-permute-done.5), kind=kLoop, calls=%fused_computation.59 | loop fusion | flops 122880 | bytes 1474560 | tf_op jit(solution)/shard_map/scatter-add | solution.py:204
  132.1 1.5 %fusion.52 = (f32[2,6,16,512]{3,0,2,1:T(2,128)S(1)}, f32[2,6,16,512]{3,0,2,1:T(2,128)S(1)}) fusion(f32[2,20,16,512]{3,0,2,1:T(2,128)} %fusion.27), kind=kLoop, calls=%fused_computation.108 | loop fusion | bytes 1572864 | tf_op jit(solution)/shard_map/slice | solution.py:206
  133.6 2.2 %collective-permute-start.6 = (f32[2,6,16,512]{3,0,2,1:T(2,128)S(1)}, f32[2,6,16,512]{3,0,2,1:T(2,128)S(1)}, u32[]{:S(2)}, u32[]{:S(2)}) collective-permute-start(f32[2,6,16,512]{3,0,2,1:T(2,128)S(1)} %get-tuple-element.107), channel_id=1, source_target_pairs={{8,0},{16,8},{24,16},{9,1},{17,9},{25,17},{10,2},{18,10},{26,18},{... | collective-permute-start | bytes 1179656 | tf_op jit(solution)/shard_map/ppermute | solution.py:36
  136.1 2.2 %collective-permute-start.7 = (f32[2,6,16,512]{3,0,2,1:T(2,128)S(1)}, f32[2,6,16,512]{3,0,2,1:T(2,128)S(1)}, u32[]{:S(2)}, u32[]{:S(2)}) collective-permute-start(f32[2,6,16,512]{3,0,2,1:T(2,128)S(1)} %get-tuple-element.106), channel_id=1, source_target_pairs={{0,8},{8,16},{16,24},{1,9},{9,17},{17,25},{2,10},{10,18},{18,26},{... | collective-permute-start | bytes 1179656 | tf_op jit(solution)/shard_map/ppermute | solution.py:36
  141.3 3.9 %collective-permute-done.7 = f32[2,6,16,512]{3,0,2,1:T(2,128)S(1)} collective-permute-done((f32[2,6,16,512]{3,0,2,1:T(2,128)S(1)}, f32[2,6,16,512]{3,0,2,1:T(2,128)S(1)}, u32[]{:S(2)}, u32[]{:S(2)}) %collective-permute-start.7) | collective-permute-done | bytes 393248 | tf_op jit(solution)/shard_map/ppermute | solution.py:36
  (138 shorter events, 26.0 us)
Async XLA Ops:
  0.6 1.7 %copy-start = (bf16[8,16,512]{2,1,0:T(8,128)(2,1)S(1)}, bf16[8,16,512]{2,1,0:T(8,128)(2,1)}, u32[]{:S(2)}) copy-start(bf16[8,16,512]{2,1,0:T(8,128)(2,1)} %param.24) | copy-start | bytes 393220
  1.8 11.1 %collective-permute-start.1 = (bf16[2,6,16,512]{3,2,1,0:T(8,128)(2,1)S(1)}, bf16[2,6,16,512]{3,2,1,0:T(8,128)(2,1)S(1)}, u32[]{:S(2)}, u32[]{:S(2)}) collective-permute-start(bf16[2,6,16,512]{3,2,1,0:T(8,128)(2,1)S(1)} %get-tuple-element.129), channel_id=1, source_target_pairs={{8,0},{16,8},{24,16},{0,24},{9,1},{17,9},{25,17},{1,25},{10,2},{18... | collective-permute-start | bytes 589832 | tf_op jit(solution)/shard_map/ppermute | solution.py:23
  1.8 11.0 %collective-permute-start = (bf16[2,6,16,512]{3,2,1,0:T(8,128)(2,1)S(1)}, bf16[2,6,16,512]{3,2,1,0:T(8,128)(2,1)S(1)}, u32[]{:S(2)}, u32[]{:S(2)}) collective-permute-start(bf16[2,6,16,512]{3,2,1,0:T(8,128)(2,1)S(1)} %get-tuple-element.128), channel_id=1, source_target_pairs={{0,8},{8,16},{16,24},{24,0},{1,9},{9,17},{17,25},{25,1},{2,10},{10... | collective-permute-start | bytes 589832 | tf_op jit(solution)/shard_map/ppermute | solution.py:20
  6.9 3.1 %copy-start.30 = (bf16[8,16,512]{2,1,0:T(8,128)(2,1)S(1)}, bf16[8,16,512]{2,1,0:T(8,128)(2,1)}, u32[]{:S(2)}) copy-start(bf16[8,16,512]{2,1,0:T(8,128)(2,1)} %param.21) | copy-start | bytes 393220
  6.9 4.6 %copy-start.32 = (s32[4]{0:T(128)S(1)}, s32[4]{0:T(128)}, u32[]{:S(2)}) copy-start(s32[4]{0:T(128)} %constant.245.clone.1) | copy-start | bytes 52
  7.0 5.9 %copy-start.12 = (bf16[8,16,512]{2,1,0:T(8,128)(2,1)S(1)}, bf16[8,16,512]{2,1,0:T(8,128)(2,1)}, u32[]{:S(2)}) copy-start(bf16[8,16,512]{2,1,0:T(8,128)(2,1)} %param.22) | copy-start | bytes 393220
  7.0 5.9 %copy-start.13 = (bf16[8,16,512]{2,1,0:T(8,128)(2,1)S(1)}, bf16[8,16,512]{2,1,0:T(8,128)(2,1)}, u32[]{:S(2)}) copy-start(bf16[8,16,512]{2,1,0:T(8,128)(2,1)} %param.23) | copy-start | bytes 393220
  12.9 6.5 %copy-start.27 = (bf16[2,6,16,512]{3,2,1,0:T(8,128)(2,1)}, bf16[2,6,16,512]{3,2,1,0:T(8,128)(2,1)S(1)}, u32[]{:S(2)}) copy-start(bf16[2,6,16,512]{3,2,1,0:T(8,128)(2,1)S(1)} %collective-permute-done.1) | copy-start | bytes 589828
  12.9 6.5 %copy-start.28 = (bf16[2,6,16,512]{3,2,1,0:T(8,128)(2,1)}, bf16[2,6,16,512]{3,2,1,0:T(8,128)(2,1)S(1)}, u32[]{:S(2)}) copy-start(bf16[2,6,16,512]{3,2,1,0:T(8,128)(2,1)S(1)} %collective-permute-done) | copy-start | bytes 589828
  13.9 20.4 %collective-permute-start.3 = (bf16[2,20,6,512]{3,2,1,0:T(8,128)(2,1)}, bf16[2,20,6,512]{3,2,1,0:T(8,128)(2,1)}, u32[]{:S(2)}, u32[]{:S(2)}) collective-permute-start(bf16[2,20,6,512]{3,2,1,0:T(8,128)(2,1)} %get-tuple-element.113), channel_id=1, source_target_pairs={{1,0},{2,1},{3,2},{4,3},{5,4},{6,5},{7,6},{0,7},{9,8},{10,9},{11,1... | collective-permute-start | bytes 737288 | tf_op jit(solution)/shard_map/ppermute | solution.py:23
  14.4 19.9 %collective-permute-start.2 = (bf16[2,20,6,512]{3,2,1,0:T(8,128)(2,1)}, bf16[2,20,6,512]{3,2,1,0:T(8,128)(2,1)}, u32[]{:S(2)}, u32[]{:S(2)}) collective-permute-start(bf16[2,20,6,512]{3,2,1,0:T(8,128)(2,1)} %get-tuple-element.112), channel_id=1, source_target_pairs={{0,1},{1,2},{2,3},{3,4},{4,5},{5,6},{6,7},{7,0},{8,9},{9,10},{10,1... | collective-permute-start | bytes 737288 | tf_op jit(solution)/shard_map/ppermute | solution.py:20
  36.9 6.8 %copy-start.19 = (bf16[1,400,4,64]{1,3,2,0:T(8,128)(2,1)}, bf16[1,400,4,64]{1,3,2,0:T(8,128)(2,1)S(1)}, u32[]{:S(2)}) copy-start(bf16[1,400,4,64]{1,3,2,0:T(8,128)(2,1)S(1)} %copy.136) | copy-start | bytes 614404
  37.4 6.3 %copy-start.23 = (bf16[1,400,4,64]{1,3,2,0:T(8,128)(2,1)}, bf16[1,400,4,64]{1,3,2,0:T(8,128)(2,1)S(1)}, u32[]{:S(2)}) copy-start(bf16[1,400,4,64]{1,3,2,0:T(8,128)(2,1)S(1)} %copy.135) | copy-start | bytes 614404
  39.4 4.3 %copy-start.11 = (f32[4,64,400]{2,1,0:T(8,128)S(1)}, f32[4,64,400]{2,1,0:T(8,128)}, u32[]{:S(2)}) copy-start(f32[4,64,400]{2,1,0:T(8,128)} %add.109) | copy-start | bytes 1228804
  39.4 4.3 %copy-start.15 = (bf16[2,64,256]{1,2,0:T(8,128)(2,1)S(1)}, bf16[2,64,256]{1,2,0:T(8,128)(2,1)}, u32[]{:S(2)}) copy-start(bf16[2,64,256]{1,2,0:T(8,128)(2,1)} %copy.171) | copy-start | bytes 196612
  39.7 8.5 %copy-start.17 = (bf16[1,400,4,64]{1,3,2,0:T(8,128)(2,1)}, bf16[1,400,4,64]{1,3,2,0:T(8,128)(2,1)S(1)}, u32[]{:S(2)}) copy-start(bf16[1,400,4,64]{1,3,2,0:T(8,128)(2,1)S(1)} %copy.128) | copy-start | bytes 614404
  40.2 8.0 %copy-start.21 = (bf16[1,400,4,64]{1,3,2,0:T(8,128)(2,1)}, bf16[1,400,4,64]{1,3,2,0:T(8,128)(2,1)S(1)}, u32[]{:S(2)}) copy-start(bf16[1,400,4,64]{1,3,2,0:T(8,128)(2,1)S(1)} %copy.127) | copy-start | bytes 614404
  42.5 2.0 %copy-start.14 = (bf16[2,64,256]{1,2,0:T(8,128)(2,1)S(1)}, bf16[2,64,256]{1,2,0:T(8,128)(2,1)}, u32[]{:S(2)}) copy-start(bf16[2,64,256]{1,2,0:T(8,128)(2,1)} %copy.145) | copy-start | bytes 196612
  45.9 2.3 %copy-start.10 = (f32[4,64,400]{2,1,0:T(8,128)S(1)}, f32[4,64,400]{2,1,0:T(8,128)}, u32[]{:S(2)}) copy-start(f32[4,64,400]{2,1,0:T(8,128)} %add.105) | copy-start | bytes 1228804
  48.2 1.2 copy-start.25
  48.2 1.2 copy-start.26
  50.9 0.8 copy-start.6
  60.5 2.2 %copy-start.4 = (f32[2,2,20,20,256]{4,1,3,2,0:T(2,128)S(1)}, f32[2,2,20,20,256]{4,1,3,2,0:T(2,128)}, u32[]{:S(2)}) copy-start(f32[2,2,20,20,256]{4,1,3,2,0:T(2,128)} %constant_dynamic-update-slice_fusion.1) | copy-start | bytes 4915204
  64.1 3.8 %copy-start.8 = (bf16[2,4,64,400]{3,2,1,0:T(8,128)(2,1)S(1)}, bf16[2,4,64,400]{3,2,1,0:T(8,128)(2,1)}, u32[]{:S(2)}) copy-start(bf16[2,4,64,400]{3,2,1,0:T(8,128)(2,1)} %fusion.13) | copy-start | bytes 1228804
  64.1 3.7 %copy-start.16 = (bf16[2,64,256]{1,2,0:T(8,128)(2,1)S(1)}, bf16[2,64,256]{1,2,0:T(8,128)(2,1)}, u32[]{:S(2)}) copy-start(bf16[2,64,256]{1,2,0:T(8,128)(2,1)} %copy.171) | copy-start | bytes 196612
  74.9 2.3 %copy-start.5 = (f32[2,1,20,20,256]{4,1,3,2,0:T(1,128)S(1)}, f32[2,1,20,20,256]{4,1,3,2,0:T(1,128)}, u32[]{:S(2)}) copy-start(f32[2,1,20,20,256]{4,1,3,2,0:T(1,128)} %get-tuple-element.104) | copy-start | bytes 2457604
  74.9 3.4 %copy-start.3 = (f32[1,2,20,20,256]{4,0,3,2,1:T(1,128)S(1)}, f32[1,2,20,20,256]{4,0,3,2,1:T(1,128)}, u32[]{:S(2)}) copy-start(f32[1,2,20,20,256]{4,0,3,2,1:T(1,128)} %reshape.500) | copy-start | bytes 2457604
  101.6 10.6 %copy-start.9 = (bf16[2,4,64,400]{3,2,1,0:T(8,128)(2,1)S(1)}, bf16[2,4,64,400]{3,2,1,0:T(8,128)(2,1)}, u32[]{:S(2)}) copy-start(bf16[2,4,64,400]{3,2,1,0:T(8,128)(2,1)} %fusion.13) | copy-start | bytes 1228804
  101.6 10.6 %copy-start.20 = (bf16[1,400,4,64]{1,3,2,0:T(8,128)(2,1)S(1)}, bf16[1,400,4,64]{1,3,2,0:T(8,128)(2,1)}, u32[]{:S(2)}) copy-start(bf16[1,400,4,64]{1,3,2,0:T(8,128)(2,1)} %copy-done.19) | copy-start | bytes 614404
  101.6 10.6 %copy-start.24 = (bf16[1,400,4,64]{1,3,2,0:T(8,128)(2,1)S(1)}, bf16[1,400,4,64]{1,3,2,0:T(8,128)(2,1)}, u32[]{:S(2)}) copy-start(bf16[1,400,4,64]{1,3,2,0:T(8,128)(2,1)} %copy-done.23) | copy-start | bytes 614404
  102.9 22.3 %collective-permute-start.4 = (f32[2,20,6,512]{3,0,2,1:T(2,128)}, f32[2,20,6,512]{3,0,2,1:T(2,128)}, u32[]{:S(2)}, u32[]{:S(2)}) collective-permute-start(f32[2,20,6,512]{3,0,2,1:T(2,128)} %get-tuple-element.103), channel_id=1, source_target_pairs={{0,7},{1,0},{2,1},{3,2},{4,3},{5,4},{6,5},{7,6},{8,15},{9,8},{10,9... | collective-permute-start | bytes 1474568 | tf_op jit(solution)/shard_map/ppermute | solution.py:30
  107.4 22.5 %collective-permute-start.5 = (f32[2,20,6,512]{3,0,2,1:T(2,128)}, f32[2,20,6,512]{3,0,2,1:T(2,128)S(1)}, u32[]{:S(2)}, u32[]{:S(2)}) collective-permute-start(f32[2,20,6,512]{3,0,2,1:T(2,128)} %get-tuple-element.102), channel_id=1, source_target_pairs={{0,1},{1,2},{2,3},{3,4},{4,5},{5,6},{6,7},{7,0},{8,9},{9,10},{10,1... | collective-permute-start | bytes 1474568 | tf_op jit(solution)/shard_map/ppermute | solution.py:30
  113.1 22.7 %copy-start.7 = (bf16[2,4,64,400]{3,2,1,0:T(8,128)(2,1)S(1)}, bf16[2,4,64,400]{3,2,1,0:T(8,128)(2,1)}, u32[]{:S(2)}) copy-start(bf16[2,4,64,400]{3,2,1,0:T(8,128)(2,1)} %copy-done.6) | copy-start | bytes 1228804
  113.1 22.7 %copy-start.18 = (bf16[1,400,4,64]{1,3,2,0:T(8,128)(2,1)S(1)}, bf16[1,400,4,64]{1,3,2,0:T(8,128)(2,1)}, u32[]{:S(2)}) copy-start(bf16[1,400,4,64]{1,3,2,0:T(8,128)(2,1)} %copy-done.17) | copy-start | bytes 614404
  113.1 22.7 %copy-start.22 = (bf16[1,400,4,64]{1,3,2,0:T(8,128)(2,1)S(1)}, bf16[1,400,4,64]{1,3,2,0:T(8,128)(2,1)}, u32[]{:S(2)}) copy-start(bf16[1,400,4,64]{1,3,2,0:T(8,128)(2,1)} %copy-done.21) | copy-start | bytes 614404
  127.3 11.0 %copy-start.29 = (bf16[1,2,8,8,256]{4,3,2,1,0:T(8,128)(2,1)S(1)}, bf16[1,2,8,8,256]{4,3,2,1,0:T(8,128)(2,1)}, u32[]{:S(2)}) copy-start(bf16[1,2,8,8,256]{4,3,2,1,0:T(8,128)(2,1)} %convert_element_type.90) | copy-start | bytes 196612
  127.3 11.6 %copy-start.31 = (bf16[2,64,4,64]{1,3,2,0:T(8,128)(2,1)S(1)}, bf16[2,64,4,64]{1,3,2,0:T(8,128)(2,1)}, u32[]{:S(2)}) copy-start(bf16[2,64,4,64]{1,3,2,0:T(8,128)(2,1)} %fusion.16) | copy-start | bytes 196612
  132.1 8.1 %copy-start.2 = (f32[2,20,16,512]{3,0,2,1:T(2,128)S(1)}, f32[2,20,16,512]{3,0,2,1:T(2,128)}, u32[]{:S(2)}) copy-start(f32[2,20,16,512]{3,0,2,1:T(2,128)} %fusion.27) | copy-start | bytes 3932164
  133.6 7.5 %collective-permute-start.6 = (f32[2,6,16,512]{3,0,2,1:T(2,128)S(1)}, f32[2,6,16,512]{3,0,2,1:T(2,128)S(1)}, u32[]{:S(2)}, u32[]{:S(2)}) collective-permute-start(f32[2,6,16,512]{3,0,2,1:T(2,128)S(1)} %get-tuple-element.107), channel_id=1, source_target_pairs={{8,0},{16,8},{24,16},{9,1},{17,9},{25,17},{10,2},{18,10},{26,18},{... | collective-permute-start | bytes 1179656 | tf_op jit(solution)/shard_map/ppermute | solution.py:36
  136.1 9.1 %collective-permute-start.7 = (f32[2,6,16,512]{3,0,2,1:T(2,128)S(1)}, f32[2,6,16,512]{3,0,2,1:T(2,128)S(1)}, u32[]{:S(2)}, u32[]{:S(2)}) collective-permute-start(f32[2,6,16,512]{3,0,2,1:T(2,128)S(1)} %get-tuple-element.106), channel_id=1, source_target_pairs={{0,8},{8,16},{16,24},{1,9},{9,17},{17,25},{2,10},{10,18},{18,26},{... | collective-permute-start | bytes 1179656 | tf_op jit(solution)/shard_map/ppermute | solution.py:36
  140.2 7.2 %copy-start.1 = (bf16[8,16,512]{2,1,0:T(8,128)(2,1)S(1)}, bf16[8,16,512]{2,1,0:T(8,128)(2,1)}, u32[]{:S(2)}) copy-start(bf16[8,16,512]{2,1,0:T(8,128)(2,1)} %param.24) | copy-start | bytes 393220
where the time goes:
time: 149 us; the launch traced here: 147 us
  local copies, waits for them, and re-layouts  80.9 us (54%)
  waiting for transfers between devices  19.5 us (13%)
  other arithmetic  19.1 us (13%)
  starting transfers between devices  14.3 us (10%)
  matrix products  12.3 us (8%)
    scatter-add x2, local copies, waits for them, and re-layouts, shards(): collected = collected.at[:, row_start:row_start + extent, col_start:col_s...  19.9 us
    ppermute x2, waiting for transfers between devices, shifted(): lax.ppermute(shard, axis, [(i, (i + by) % count) for i in range(count)])  14.7 us
    another operation x7, local copies, waits for them, and re-layouts, shards(): jnp.stack([grad_k, grad_v])  12.5 us
    slice x3, local copies, waits for them, and re-layouts, shards(): bias_query[group * group_size:(group + 1) * group_size]  9.39 us
    another operation x16, local copies, waits for them, and re-layouts, neighbourhoods(): stacked = jnp.stack(pieces)  6.33 us
    ppermute x2, starting transfers between devices, shifted(): lax.ppermute(shard, axis, [(i, (i + by) % count) for i in range(count)])  4.72 us
    ppermute x2, waiting for transfers between devices, from_behind(): lax.ppermute(value, axis, [(source, source + steps) for source in range(l...  4.72 us
    ppermute x2, starting transfers between devices, padded_2(): lax.ppermute(lax.slice_in_dim(block, block.shape[dim] - width, None, axis...  4.71 us
  transfers between devices with their start and end apart: 8, of which 4 were waited for; matrix products, arithmetic and copies ran while one was open for 24% of the time, Pallas kernels for 0%

commit v1 on v0

v1 whole, which is shorter than its diff:
```python
import functools

import jax
import jax.numpy as jnp
from jax import lax
from jax.experimental import pallas as pl
from jax.experimental.pallas import tpu as pltpu
from jax.sharding import PartitionSpec as P

HEAD_DIM = 64
RADIUS = 6
SPAN = 2 * RADIUS + 1
ROWS = 8
COLS = 16
CELLS = ROWS * COLS
SIDE = ROWS * RADIUS
BAND = RADIUS * COLS
BACK = BAND + 2 * SIDE
PAIR = 2 * HEAD_DIM
BASE = 336
TABLE = 512
MASKED = -1e30

OWN_AT = 0
LON_AT = CELLS
LAT_AT = LON_AT + 2 * SIDE
CORNER_AT = LAT_AT + 2 * BAND
KEYS = CORNER_AT + 4 * SIDE

F32 = jnp.float32
BF16 = jnp.bfloat16


def pair_exchange(value, axis, odd, wrap):
    count = lax.axis_size(axis)
    pairs = []
    for first in range(odd, count, 2):
        second = first + 1
        if second >= count and not wrap:
            continue
        second %= count
        pairs += [(first, second), (second, first)]
    return lax.ppermute(value, axis, pairs)


def is_odd(axis):
    return lax.axis_index(axis) % 2 == 1


def pick_matrix(first_col):
    shape = (SIDE, CELLS)
    place = lax.broadcasted_iota(jnp.int32, shape, 0)
    cell = lax.broadcasted_iota(jnp.int32, shape, 1)
    source = (place % ROWS) * COLS + first_col + place // ROWS
    return (cell == source).astype(BF16)


def pack_kernel(k_ref, v_ref, bias_ref, lon_odd_ref, lon_even_ref, lat_even_ref, lat_odd_ref, line_ref):
    lon_odd = is_odd("lon")
    lat_odd = is_odd("lat")
    pick_odd = pick_matrix(jnp.where(lon_odd, COLS - RADIUS, 0))
    pick_even = pick_matrix(jnp.where(lon_odd, 0, COLS - RADIUS))
    low, high = 0, CELLS - BAND
    start_even = pl.multiple_of(jnp.where(lat_odd, low, high), 32)
    start_odd = pl.multiple_of(jnp.where(lat_odd, high, low), 32)
    for slot, source in ((0, k_ref), (1, v_ref)):
        whole = source[...]
        lon_odd_ref[slot] = jnp.dot(pick_odd, whole, preferred_element_type=F32).astype(BF16)
        lon_even_ref[slot] = jnp.dot(pick_even, whole, preferred_element_type=F32).astype(BF16)
        lat_even_ref[slot] = source[pl.ds(start_even, BAND), :]
        lat_odd_ref[slot] = source[pl.ds(start_odd, BAND), :]
    shape = (SPAN * SPAN, TABLE)
    entry = lax.broadcasted_iota(jnp.int32, shape, 0)
    offset = BASE - lax.broadcasted_iota(jnp.int32, shape, 1)
    chosen = (offset == (entry // SPAN) * COLS + entry % SPAN).astype(F32)
    line = jnp.dot(bias_ref[...], chosen, preferred_element_type=F32, precision=lax.Precision.HIGHEST)
    offset = BASE - lax.broadcasted_iota(jnp.int32, (1, TABLE), 1)
    valid = (offset >= 0) & (offset < SPAN * COLS) & (offset % COLS < SPAN)
    line_ref[...] = jnp.where(valid, line, MASKED)


def bias_kernel(line_ref, table_ref):
    lon_odd = is_odd("lon")
    lat_odd = is_odd("lat")
    has_north = lax.axis_index("lat") > 0
    has_south = lax.axis_index("lat") < lax.axis_size("lat") - 1
    head = pl.program_id(0)
    line = jnp.broadcast_to(line_ref[pl.ds(head, 1), :], (8, TABLE))
    by_one = pltpu.roll(line, 0, 1, stride=1, stride_axis=0)
    by_row = pltpu.roll(line, 0, 1, stride=COLS, stride_axis=0)
    query_col = lax.broadcasted_iota(jnp.int32, (8, CELLS), 1) % COLS
    sub = lax.broadcasted_iota(jnp.int32, (8, CELLS), 0)

    def window(source, row, col):
        first = BASE - (COLS * row + col)
        return source[:, first : first + CELLS]

    def near(delta):
        return (delta >= 0) & (delta < SPAN)

    def put(at, values):
        table_ref[0, pl.ds(pl.multiple_of(at, 8), 8), :] = values

    def cells(at, row, row_count, there):
        for half in range(COLS // 8):
            allowed = near(RADIUS + 8 * half + sub - query_col)
            if there is not None:
                allowed = allowed & there
            for step in range(row_count):
                values = window(by_one, row + step, RADIUS + 8 * half)
                put(at + step * COLS + 8 * half, jnp.where(allowed, values, MASKED))

    def sides(at, row, first_col, there):
        for step in range(RADIUS):
            allowed = near(first_col + step - query_col)
            if there is not None:
                allowed = allowed & there
            values = window(by_row, row, first_col + step)
            put(at + step * ROWS, jnp.where(allowed, values, MASKED))

    west, east = 0, COLS + RADIUS
    west_slot = jnp.where(lon_odd, SIDE, 0)
    east_slot = SIDE - west_slot
    cells(OWN_AT, RADIUS, ROWS, None)
    sides(LON_AT + west_slot, RADIUS, west, None)
    sides(LON_AT + east_slot, RADIUS, east, None)
    north_slot = jnp.where(lat_odd, 0, 1)
    south_slot = 1 - north_slot
    for slot, row, there in ((north_slot, 0, has_north), (south_slot, ROWS + RADIUS, has_south)):
        cells(LAT_AT + slot * BAND, row, RADIUS, there)
        first = row if row else row - (ROWS - RADIUS)
        sides(CORNER_AT + slot * 2 * SIDE + west_slot, first, west, there)
        sides(CORNER_AT + slot * 2 * SIDE + east_slot, first, east, there)


def main_kernel(
    q_ref, do_ref, k_ref, v_ref, lon_odd_ref, lon_even_ref, lat_even_ref, lat_odd_ref,
    c0_ref, c1_ref, c2_ref, c3_ref, table_ref,
    out_ref, dq_ref, own_ref, dlon_odd_ref, dlon_even_ref, back_even_ref, back_odd_ref,
):
    parts = (lon_odd_ref, lon_even_ref, lat_even_ref, lat_odd_ref, c0_ref, c1_ref, c2_ref, c3_ref)
    keys = jnp.concatenate([k_ref[...]] + [part[0] for part in parts], axis=0)
    values = jnp.concatenate([v_ref[...]] + [part[1] for part in parts], axis=0)
    first_head = lax.broadcasted_iota(jnp.int32, (CELLS, PAIR), 1) < HEAD_DIM
    factor = HEAD_DIM ** (-0.5)

    def both_heads(block):
        zero = jnp.zeros_like(block)
        return jnp.concatenate([jnp.where(first_head, block, zero), jnp.where(first_head, zero, block)], axis=0)

    queries = both_heads(q_ref[...] * jnp.asarray(factor, BF16))
    grads = both_heads(do_ref[...])
    last = (((1,), (1,)), ((), ()))
    scores = lax.dot_general(keys, queries, last, preferred_element_type=F32)
    scores = scores + jnp.concatenate([table_ref[0], table_ref[1]], axis=1)
    grad_prob = lax.dot_general(values, grads, last, preferred_element_type=F32)
    largest = jnp.max(scores, axis=0, keepdims=True)
    raised = jnp.exp(scores - largest)
    total = jnp.sum(raised, axis=0, keepdims=True)
    inverse = 1.0 / total
    row_dot = jnp.sum(raised * grad_prob, axis=0, keepdims=True) * inverse
    probability = raised * inverse
    weights = probability.astype(BF16)
    dscore = (probability * (grad_prob - row_dot)).astype(BF16)

    def per_query(cells, coefficients):
        turned = jnp.dot(cells.T, coefficients, preferred_element_type=F32)
        mine = jnp.concatenate([turned[:HEAD_DIM, :CELLS], turned[HEAD_DIM:, CELLS:]], axis=0)
        return mine.T

    out_ref[...] = per_query(values, weights).astype(BF16)
    dq_ref[...] = (per_query(keys, dscore) * factor).astype(BF16)
    for slot, coefficients, other in ((0, dscore, queries), (1, weights, grads)):
        grad = jnp.dot(coefficients, other, preferred_element_type=F32)
        own_ref[slot] = grad[:CELLS]
        dlon_odd_ref[slot] = grad[LON_AT : LON_AT + SIDE]
        dlon_even_ref[slot] = grad[LON_AT + SIDE : LAT_AT]
        for index, back in ((0, back_even_ref), (1, back_odd_ref)):
            at = LAT_AT + index * BAND
            back[slot, :BAND] = grad[at : at + BAND].astype(BF16)
            at = CORNER_AT + index * 2 * SIDE
            back[slot, BAND:] = grad[at : at + 2 * SIDE].astype(BF16)


def middle_kernel(dlon_odd_ref, dlon_even_ref, back_even_ref, back_odd_ref, send_odd_ref, send_even_ref):
    for index, (mine, send) in enumerate(((dlon_odd_ref, send_odd_ref), (dlon_even_ref, send_even_ref))):
        at = BAND + index * SIDE
        from_even = back_even_ref[:, at : at + SIDE].astype(F32)
        from_odd = back_odd_ref[:, at : at + SIDE].astype(F32)
        send[...] = (mine[...] + from_even + from_odd).astype(BF16)


def final_kernel(own_ref, back_even_ref, back_odd_ref, side_odd_ref, side_even_ref, dk_ref, dv_ref, sum_ref):
    lon_odd = is_odd("lon")
    lat_odd = is_odd("lat")
    start_even = pl.multiple_of(jnp.where(lat_odd, 0, CELLS - BAND), 32)
    start_odd = pl.multiple_of(jnp.where(lat_odd, CELLS - BAND, 0), 32)
    shape = (CELLS, SIDE)
    cell = lax.broadcasted_iota(jnp.int32, shape, 0)
    place = lax.broadcasted_iota(jnp.int32, shape, 1)

    def spread(first_col):
        return (cell == (place % ROWS) * COLS + first_col + place // ROWS).astype(BF16)

    spread_odd = spread(jnp.where(lon_odd, COLS - RADIUS, 0))
    spread_even = spread(jnp.where(lon_odd, 0, COLS - RADIUS))
    for slot, out in ((0, dk_ref), (1, dv_ref)):
        sum_ref[...] = (
            own_ref[slot]
            + jnp.dot(spread_odd, side_odd_ref[slot], preferred_element_type=F32)
            + jnp.dot(spread_even, side_even_ref[slot], preferred_element_type=F32)
        )
        sum_ref[pl.ds(start_even, BAND), :] += back_even_ref[slot, :BAND].astype(F32)
        sum_ref[pl.ds(start_odd, BAND), :] += back_odd_ref[slot, :BAND].astype(F32)
        out[...] = sum_ref[...].astype(BF16)


def arr(shape, dtype):
    return jax.ShapeDtypeStruct(shape, dtype)


PARAMS = pltpu.CompilerParams(vmem_limit_bytes=48 * 1024 * 1024)


def shards(queries, key_cells, value_cells, grad_output, rel_bias):
    block = queries.shape
    heads = rel_bias.shape[0]
    feat = block[-1]
    q, k, v, g = (x.reshape(CELLS, feat) for x in (queries, key_cells, value_cells, grad_output))
    side, band, back = (2, SIDE, feat), (2, BAND, feat), (2, BACK, feat)

    lon_odd, lon_even, lat_even, lat_odd, line = pl.pallas_call(
        pack_kernel,
        out_shape=[arr(side, BF16), arr(side, BF16), arr(band, BF16), arr(band, BF16), arr((heads, TABLE), F32)],
        compiler_params=PARAMS,
        name="pack",
    )(k, v, rel_bias)

    lon_odd = pair_exchange(lon_odd, "lon", 1, True)
    lon_even = pair_exchange(lon_even, "lon", 0, True)
    lat_even = pair_exchange(lat_even, "lat", 0, False)
    lat_odd = pair_exchange(lat_odd, "lat", 1, False)

    table = pl.pallas_call(
        bias_kernel,
        out_shape=arr((heads, KEYS, CELLS), F32),
        grid=(heads,),
        in_specs=[pl.BlockSpec((heads, TABLE), lambda i: (0, 0))],
        out_specs=pl.BlockSpec((1, KEYS, CELLS), lambda i: (i, 0, 0)),
        compiler_params=PARAMS,
        cost_estimate=pl.CostEstimate(flops=4 * heads * KEYS * CELLS, bytes_accessed=4 * heads * KEYS * CELLS, transcendentals=0),
        name="bias_table",
    )(line)

    corners = [
        pair_exchange(piece, "lat", odd, False) for odd in (0, 1) for piece in (lon_odd, lon_even)
    ]

    def cut(shape):
        if len(shape) == 2:
            return pl.BlockSpec((shape[0], PAIR), lambda i: (0, i))
        return pl.BlockSpec((shape[0], shape[1], PAIR), lambda i: (0, 0, i))

    inputs = (q, g, k, v, lon_odd, lon_even, lat_even, lat_odd, *corners)
    outs = [
        arr((CELLS, feat), BF16), arr((CELLS, feat), BF16), arr((2, CELLS, feat), F32),
        arr(side, F32), arr(side, F32), arr(back, BF16), arr(back, BF16),
    ]
    out, dq, own, dlon_odd, dlon_even, back_even, back_odd = pl.pallas_call(
        main_kernel,
        out_shape=outs,
        grid=(feat // PAIR,),
        in_specs=[cut(x.shape) for x in inputs] + [pl.BlockSpec((2, KEYS, CELLS), lambda i: (i, 0, 0))],
        out_specs=[cut(x.shape) for x in outs],
        compiler_params=PARAMS,
        name="attention",
    )(*inputs, table)

    back_even = pair_exchange(back_even, "lat", 0, False)
    back_odd = pair_exchange(back_odd, "lat", 1, False)
    send_odd, send_even = pl.pallas_call(
        middle_kernel,
        out_shape=[arr(side, BF16), arr(side, BF16)],
        compiler_params=PARAMS,
        name="middle",
    )(dlon_odd, dlon_even, back_even, back_odd)
    side_odd = pair_exchange(send_odd, "lon", 1, True)
    side_even = pair_exchange(send_even, "lon", 0, True)
    dk, dv = pl.pallas_call(
        final_kernel,
        out_shape=[arr((CELLS, feat), BF16), arr((CELLS, feat), BF16)],
        scratch_shapes=[pltpu.VMEM((CELLS, feat), F32)],
        compiler_params=PARAMS,
        name="final",
    )(own, back_even, back_odd, side_odd, side_even)
    return tuple(x.reshape(block) for x in (out, dq, dk, dv))


def solution(mesh):
    spec = P("lat", "lon", None)
    return jax.shard_map(
        shards, mesh=mesh, in_specs=(spec, spec, spec, spec, P()), out_specs=(spec,) * 4, check_vma=False
    )
```

time: 149 us -> 47.7 us (0.32)
  the two profiles are of different devices: /device:TPU:30 before, /device:TPU:2 now
where the time goes in v1:
time: 47.7 us; the launch traced here: 47.5 us
  starting transfers between devices  19.2 us (40%)
  waiting for transfers between devices  16.1 us (34%)
  Pallas kernels  8.93 us (19%)
  local copies, waits for them, and re-layouts  2.51 us (5%)
  between operations  0.78 us (2%)
    ppermute x12, starting transfers between devices, pair_exchange(): return lax.ppermute(value, axis, pairs)  19.2 us
    ppermute x12, waiting for transfers between devices, pair_exchange(): return lax.ppermute(value, axis, pairs)  16.1 us
    pallas_call x1, Pallas kernels, shards(): pl.pallas_call(main_kernel, out_shape=outs, grid=(feat // PAIR,), in_spec...  5.47 us
    unnamed x12, local copies, waits for them, and re-layouts  2.51 us
    pallas_call x1, Pallas kernels, shards(): pl.pallas_call(bias_kernel, out_shape=arr((heads, KEYS, CELLS), F32), gri...  2.05 us
    pallas_call x1, Pallas kernels, shards(): pl.pallas_call(final_kernel, out_shape=[arr((CELLS, feat), BF16), arr((CE...  1.04 us
  transfers between devices with their start and end apart: 12, of which 5 were waited for; matrix products, arithmetic and copies ran while one was open for 0% of the time, Pallas kernels for 4%

profile of v1, /device:TPU:2, one launch (start us, length us, event | category | flops | bytes accessed | tf_op | source)
XLA Modules:
  0.0 47.5 jit_solution(5560370870349492945)
XLA Ops:
  0.6 0.0 copy-start
  0.6 0.9 %copy-done = bf16[8,16,512]{2,1,0:T(8,128)(2,1)S(1)} copy-done((bf16[8,16,512]{2,1,0:T(8,128)(2,1)S(1)}, bf16[8,16,512]{2,1,0:T(8,128)(2,1)}, u32[]{:S(2)}) %copy-start) | copy-done | bytes 131096
  1.5 0.0 copy-start.2
  1.5 0.9 %copy-done.2 = bf16[8,16,512]{2,1,0:T(8,128)(2,1)S(1)} copy-done((bf16[8,16,512]{2,1,0:T(8,128)(2,1)S(1)}, bf16[8,16,512]{2,1,0:T(8,128)(2,1)}, u32[]{:S(2)}) %copy-start.2) | copy-done | bytes 131096
  2.4 0.0 copy-start.5
  2.4 0.7 %copy-done.5 = f32[8,169]{1,0:T(8,128)S(1)} copy-done((f32[8,169]{1,0:T(8,128)S(1)}, f32[8,169]{1,0:T(8,128)}, u32[]{:S(2)}) %copy-start.5) | copy-done | bytes 5432
  3.1 0.0 copy-start.1
  3.1 0.0 copy-start.3
  3.1 0.0 copy-start.4
  3.1 0.3 pack.1
  3.5 4.7 %collective-permute-start = (bf16[2,48,512]{2,1,0:T(8,128)(2,1)S(1)}, bf16[2,48,512]{2,1,0:T(8,128)(2,1)S(1)}, u32[]{:S(2)}, u32[]{:S(2)}) collective-permute-start(bf16[2,48,512]{2,1,0:T(8,128)(2,1)S(1)} %get-tuple-element.20), channel_id=1, source_target_pairs={{1,2},{2,1},{3,4},{4,3},{5,6},{6,5},{7,0},{0,7},{9,10},{10,9},{11,... | collective-permute-start | bytes 294920 | tf_op jit(solution)/shard_map/ppermute | solution.py:43
  8.1 0.0 collective-permute-start.1
  8.1 2.9 %collective-permute-done.lon_odd_ref = bf16[2,48,512]{2,1,0:T(8,128)(2,1)S(1)} collective-permute-done((bf16[2,48,512]{2,1,0:T(8,128)(2,1)S(1)}, bf16[2,48,512]{2,1,0:T(8,128)(2,1)S(1)}, u32[]{:S(2)}, u32[]{:S(2)}) %collective-permute-start) | collective-permute-done | bytes 98336 | tf_op jit(solution)/shard_map/ppermute | solution.py:43
  11.0 1.9 %collective-permute-start.6 = (bf16[2,48,512]{2,1,0:T(8,128)(2,1)S(1)}, bf16[2,48,512]{2,1,0:T(8,128)(2,1)S(1)}, u32[]{:S(2)}, u32[]{:S(2)}) collective-permute-start(bf16[2,48,512]{2,1,0:T(8,128)(2,1)S(1)} %collective-permute-done.lon_odd_ref), channel_id=1, source_target_pairs={{8,16},{16,8},{9,17},{17,9},{10,18},{18,10},{11,19},{19,11},{12,20... | collective-permute-start | bytes 294920 | tf_op jit(solution)/shard_map/ppermute | solution.py:43
  12.9 0.1 collective-permute-start.2
  13.0 3.6 %collective-permute-start.3 = (bf16[2,96,512]{2,1,0:T(8,128)(2,1)S(1)}, bf16[2,96,512]{2,1,0:T(8,128)(2,1)S(1)}, u32[]{:S(2)}, u32[]{:S(2)}) collective-permute-start(bf16[2,96,512]{2,1,0:T(8,128)(2,1)S(1)} %get-tuple-element.23), channel_id=1, source_target_pairs={{8,16},{16,8},{9,17},{17,9},{10,18},{18,10},{11,19},{19,11},{12,20... | collective-permute-start | bytes 589832 | tf_op jit(solution)/shard_map/ppermute | solution.py:43
  16.6 0.1 collective-permute-start.4
  16.7 0.0 collective-permute-done.1.lon_even_ref
  16.7 1.9 %collective-permute-start.7 = (bf16[2,48,512]{2,1,0:T(8,128)(2,1)S(1)}, bf16[2,48,512]{2,1,0:T(8,128)(2,1)S(1)}, u32[]{:S(2)}, u32[]{:S(2)}) collective-permute-start(bf16[2,48,512]{2,1,0:T(8,128)(2,1)S(1)} %collective-permute-done.1.lon_even_ref), channel_id=1, source_target_pairs={{8,16},{16,8},{9,17},{17,9},{10,18},{18,10},{11,19},{19,11},{12,20... | collective-permute-start | bytes 294920 | tf_op jit(solution)/shard_map/ppermute | solution.py:43
  18.6 0.0 collective-permute-done.6.c2_ref
  18.6 0.1 collective-permute-start.5
  18.7 2.1 %bias_table.1.table_ref = f32[8,608,128]{2,1,0:T(8,128)S(1)} custom-call(f32[8,512]{1,0:T(8,128)S(1)} %get-tuple-element.24.line_ref), custom_call_target="tpu_custom_call" | custom-call | flops 2490368 | bytes 2490368 | tf_op jit(solution)/shard_map/bias_table/pallas_call | solution.py:244
  20.8 0.0 collective-permute-done.4.c0_ref
  20.8 1.8 %collective-permute-done.7.c3_ref = bf16[2,48,512]{2,1,0:T(8,128)(2,1)S(1)} collective-permute-done((bf16[2,48,512]{2,1,0:T(8,128)(2,1)S(1)}, bf16[2,48,512]{2,1,0:T(8,128)(2,1)S(1)}, u32[]{:S(2)}, u32[]{:S(2)}) %collective-permute-start.7) | collective-permute-done | bytes 98336 | tf_op jit(solution)/shard_map/ppermute | solution.py:43
  22.6 0.0 collective-permute-done.5.c1_ref
  22.6 0.0 collective-permute-done.2.lat_even_ref
  22.6 0.0 collective-permute-done.3.lat_odd_ref
  22.7 0.0 copy-done.1
  22.7 0.0 copy-done.3
  22.7 0.0 copy-done.4
  22.7 5.5 %attention.1 = (bf16[128,512]{1,0:T(8,128)(2,1)}, bf16[128,512]{1,0:T(8,128)(2,1)}, f32[2,128,512]{2,1,0:T(8,128)S(1)}, f32[2,48,512]{2,1,0:T(8,128)S(1)}, f32[2...) custom-call(bf16[128,512]{1,0:T(8,128)(2,1)S(1)} %bitcast.12, ...), custom_call_target="tpu_custom_call" | custom-call | tf_op jit(solution)/shard_map/attention/pallas_call | solution.py:269
  28.2 0.0 collective-permute-start.8
  28.2 2.3 %collective-permute-start.9 = (bf16[2,192,512]{2,1,0:T(8,128)(2,1)S(1)}, bf16[2,192,512]{2,1,0:T(8,128)(2,1)S(1)}, u32[]{:S(2)}, u32[]{:S(2)}) collective-permute-start(bf16[2,192,512]{2,1,0:T(8,128)(2,1)S(1)} %get-tuple-element.29), channel_id=1, source_target_pairs={{8,16},{16,8},{9,17},{17,9},{10,18},{18,10},{11,19},{19,11},{12,20... | collective-permute-start | bytes 1179656 | tf_op jit(solution)/shard_map/ppermute | solution.py:43
  30.5 0.0 collective-permute-done.8.back_even_ref
  30.5 6.8 %collective-permute-done.9.back_odd_ref = bf16[2,192,512]{2,1,0:T(8,128)(2,1)S(1)} collective-permute-done((bf16[2,192,512]{2,1,0:T(8,128)(2,1)S(1)}, bf16[2,192,512]{2,1,0:T(8,128)(2,1)S(1)}, u32[]{:S(2)}, u32[]{:S(2)}) %collective-permute-start.9) | collective-permute-done | bytes 393248 | tf_op jit(solution)/shard_map/ppermute | solution.py:43
  37.2 0.1 middle.1
  37.3 4.5 %collective-permute-start.10 = (bf16[2,48,512]{2,1,0:T(8,128)(2,1)S(1)}, bf16[2,48,512]{2,1,0:T(8,128)(2,1)S(1)}, u32[]{:S(2)}, u32[]{:S(2)}) collective-permute-start(bf16[2,48,512]{2,1,0:T(8,128)(2,1)S(1)} %get-tuple-element.32), channel_id=1, source_target_pairs={{1,2},{2,1},{3,4},{4,3},{5,6},{6,5},{7,0},{0,7},{9,10},{10,9},{11,... | collective-permute-start | bytes 294920 | tf_op jit(solution)/shard_map/ppermute | solution.py:43
  41.8 0.0 collective-permute-start.11
  41.8 2.9 %collective-permute-done.10.side_odd_ref = bf16[2,48,512]{2,1,0:T(8,128)(2,1)S(1)} collective-permute-done((bf16[2,48,512]{2,1,0:T(8,128)(2,1)S(1)}, bf16[2,48,512]{2,1,0:T(8,128)(2,1)S(1)}, u32[]{:S(2)}, u32[]{:S(2)}) %collective-permute-start.10) | collective-permute-done | bytes 98336 | tf_op jit(solution)/shard_map/ppermute | solution.py:43
  44.7 1.8 %collective-permute-done.11.side_even_ref = bf16[2,48,512]{2,1,0:T(8,128)(2,1)S(1)} collective-permute-done((bf16[2,48,512]{2,1,0:T(8,128)(2,1)S(1)}, bf16[2,48,512]{2,1,0:T(8,128)(2,1)S(1)}, u32[]{:S(2)}, u32[]{:S(2)}) %collective-permute-start.11) | collective-permute-done | bytes 98336 | tf_op jit(solution)/shard_map/ppermute | solution.py:43
  46.4 1.0 %final.1 = (bf16[128,512]{1,0:T(8,128)(2,1)}, bf16[128,512]{1,0:T(8,128)(2,1)}) custom-call(f32[2,128,512]{2,1,0:T(8,128)S(1)} %get-tuple-element.27.own_ref, bf16[2,192,512]{2,1,0:T(8,128)(2,1)S(1)} %collective-permute-done.8.back_even_ref, bf16[2,192,512]{2,1,0:T(8,128)(2,1)S(1)} %collective-permute-done.9.back_odd_ref, ...), custom_call_target="tpu_custom_call" | custom-call | tf_op jit(solution)/shard_map/final/pallas_call | solution.py:289
Async XLA Ops:
  0.6 0.9 %copy-start = (bf16[8,16,512]{2,1,0:T(8,128)(2,1)S(1)}, bf16[8,16,512]{2,1,0:T(8,128)(2,1)}, u32[]{:S(2)}) copy-start(bf16[8,16,512]{2,1,0:T(8,128)(2,1)} %param.6) | copy-start | bytes 393220
  1.5 0.9 %copy-start.2 = (bf16[8,16,512]{2,1,0:T(8,128)(2,1)S(1)}, bf16[8,16,512]{2,1,0:T(8,128)(2,1)}, u32[]{:S(2)}) copy-start(bf16[8,16,512]{2,1,0:T(8,128)(2,1)} %param.7) | copy-start | bytes 393220
  2.4 0.7 %copy-start.5 = (f32[8,169]{1,0:T(8,128)S(1)}, f32[8,169]{1,0:T(8,128)}, u32[]{:S(2)}) copy-start(f32[8,169]{1,0:T(8,128)} %bias_ref.1) | copy-start | bytes 16228
  3.1 19.5 %copy-start.1 = (bf16[8,16,512]{2,1,0:T(8,128)(2,1)S(1)}, bf16[8,16,512]{2,1,0:T(8,128)(2,1)}, u32[]{:S(2)}) copy-start(bf16[8,16,512]{2,1,0:T(8,128)(2,1)} %param.6) | copy-start | bytes 393220
  3.1 19.5 %copy-start.3 = (bf16[8,16,512]{2,1,0:T(8,128)(2,1)S(1)}, bf16[8,16,512]{2,1,0:T(8,128)(2,1)}, u32[]{:S(2)}) copy-start(bf16[8,16,512]{2,1,0:T(8,128)(2,1)} %param.5) | copy-start | bytes 393220
  3.1 19.5 %copy-start.4 = (bf16[8,16,512]{2,1,0:T(8,128)(2,1)S(1)}, bf16[8,16,512]{2,1,0:T(8,128)(2,1)}, u32[]{:S(2)}) copy-start(bf16[8,16,512]{2,1,0:T(8,128)(2,1)} %param.8) | copy-start | bytes 393220
  3.5 7.5 %collective-permute-start = (bf16[2,48,512]{2,1,0:T(8,128)(2,1)S(1)}, bf16[2,48,512]{2,1,0:T(8,128)(2,1)S(1)}, u32[]{:S(2)}, u32[]{:S(2)}) collective-permute-start(bf16[2,48,512]{2,1,0:T(8,128)(2,1)S(1)} %get-tuple-element.20), channel_id=1, source_target_pairs={{1,2},{2,1},{3,4},{4,3},{5,6},{6,5},{7,0},{0,7},{9,10},{10,9},{11,... | collective-permute-start | bytes 294920 | tf_op jit(solution)/shard_map/ppermute | solution.py:43
  8.1 8.6 %collective-permute-start.1 = (bf16[2,48,512]{2,1,0:T(8,128)(2,1)S(1)}, bf16[2,48,512]{2,1,0:T(8,128)(2,1)S(1)}, u32[]{:S(2)}, u32[]{:S(2)}) collective-permute-start(bf16[2,48,512]{2,1,0:T(8,128)(2,1)S(1)} %get-tuple-element.21), channel_id=1, source_target_pairs={{0,1},{1,0},{2,3},{3,2},{4,5},{5,4},{6,7},{7,6},{8,9},{9,8},{10,11... | collective-permute-start | bytes 294920 | tf_op jit(solution)/shard_map/ppermute | solution.py:43
  11.0 7.7 %collective-permute-start.6 = (bf16[2,48,512]{2,1,0:T(8,128)(2,1)S(1)}, bf16[2,48,512]{2,1,0:T(8,128)(2,1)S(1)}, u32[]{:S(2)}, u32[]{:S(2)}) collective-permute-start(bf16[2,48,512]{2,1,0:T(8,128)(2,1)S(1)} %collective-permute-done.lon_odd_ref), channel_id=1, source_target_pairs={{8,16},{16,8},{9,17},{17,9},{10,18},{18,10},{11,19},{19,11},{12,20... | collective-permute-start | bytes 294920 | tf_op jit(solution)/shard_map/ppermute | solution.py:43
  12.9 9.8 %collective-permute-start.2 = (bf16[2,96,512]{2,1,0:T(8,128)(2,1)S(1)}, bf16[2,96,512]{2,1,0:T(8,128)(2,1)S(1)}, u32[]{:S(2)}, u32[]{:S(2)}) collective-permute-start(bf16[2,96,512]{2,1,0:T(8,128)(2,1)S(1)} %get-tuple-element.22), channel_id=1, source_target_pairs={{0,8},{8,0},{16,24},{24,16},{1,9},{9,1},{17,25},{25,17},{2,10},{10... | collective-permute-start | bytes 589832 | tf_op jit(solution)/shard_map/ppermute | solution.py:43
  13.0 9.7 %collective-permute-start.3 = (bf16[2,96,512]{2,1,0:T(8,128)(2,1)S(1)}, bf16[2,96,512]{2,1,0:T(8,128)(2,1)S(1)}, u32[]{:S(2)}, u32[]{:S(2)}) collective-permute-start(bf16[2,96,512]{2,1,0:T(8,128)(2,1)S(1)} %get-tuple-element.23), channel_id=1, source_target_pairs={{8,16},{16,8},{9,17},{17,9},{10,18},{18,10},{11,19},{19,11},{12,20... | collective-permute-start | bytes 589832 | tf_op jit(solution)/shard_map/ppermute | solution.py:43
  16.6 4.2 %collective-permute-start.4 = (bf16[2,48,512]{2,1,0:T(8,128)(2,1)S(1)}, bf16[2,48,512]{2,1,0:T(8,128)(2,1)S(1)}, u32[]{:S(2)}, u32[]{:S(2)}) collective-permute-start(bf16[2,48,512]{2,1,0:T(8,128)(2,1)S(1)} %collective-permute-done.lon_odd_ref), channel_id=1, source_target_pairs={{0,8},{8,0},{16,24},{24,16},{1,9},{9,1},{17,25},{25,17},{2,10},{10... | collective-permute-start | bytes 294920 | tf_op jit(solution)/shard_map/ppermute | solution.py:43
  16.7 5.9 %collective-permute-start.7 = (bf16[2,48,512]{2,1,0:T(8,128)(2,1)S(1)}, bf16[2,48,512]{2,1,0:T(8,128)(2,1)S(1)}, u32[]{:S(2)}, u32[]{:S(2)}) collective-permute-start(bf16[2,48,512]{2,1,0:T(8,128)(2,1)S(1)} %collective-permute-done.1.lon_even_ref), channel_id=1, source_target_pairs={{8,16},{16,8},{9,17},{17,9},{10,18},{18,10},{11,19},{19,11},{12,20... | collective-permute-start | bytes 294920 | tf_op jit(solution)/shard_map/ppermute | solution.py:43
  18.6 4.0 %collective-permute-start.5 = (bf16[2,48,512]{2,1,0:T(8,128)(2,1)S(1)}, bf16[2,48,512]{2,1,0:T(8,128)(2,1)S(1)}, u32[]{:S(2)}, u32[]{:S(2)}) collective-permute-start(bf16[2,48,512]{2,1,0:T(8,128)(2,1)S(1)} %collective-permute-done.1.lon_even_ref), channel_id=1, source_target_pairs={{0,8},{8,0},{16,24},{24,16},{1,9},{9,1},{17,25},{25,17},{2,10},{10... | collective-permute-start | bytes 294920 | tf_op jit(solution)/shard_map/ppermute | solution.py:43
  28.2 2.3 %collective-permute-start.8 = (bf16[2,192,512]{2,1,0:T(8,128)(2,1)S(1)}, bf16[2,192,512]{2,1,0:T(8,128)(2,1)S(1)}, u32[]{:S(2)}, u32[]{:S(2)}) collective-permute-start(bf16[2,192,512]{2,1,0:T(8,128)(2,1)S(1)} %get-tuple-element.28), channel_id=1, source_target_pairs={{0,8},{8,0},{16,24},{24,16},{1,9},{9,1},{17,25},{25,17},{2,10},{10... | collective-permute-start | bytes 1179656 | tf_op jit(solution)/shard_map/ppermute | solution.py:43
  28.2 9.1 %collective-permute-start.9 = (bf16[2,192,512]{2,1,0:T(8,128)(2,1)S(1)}, bf16[2,192,512]{2,1,0:T(8,128)(2,1)S(1)}, u32[]{:S(2)}, u32[]{:S(2)}) collective-permute-start(bf16[2,192,512]{2,1,0:T(8,128)(2,1)S(1)} %get-tuple-element.29), channel_id=1, source_target_pairs={{8,16},{16,8},{9,17},{17,9},{10,18},{18,10},{11,19},{19,11},{12,20... | collective-permute-start | bytes 1179656 | tf_op jit(solution)/shard_map/ppermute | solution.py:43
  37.3 7.4 %collective-permute-start.10 = (bf16[2,48,512]{2,1,0:T(8,128)(2,1)S(1)}, bf16[2,48,512]{2,1,0:T(8,128)(2,1)S(1)}, u32[]{:S(2)}, u32[]{:S(2)}) collective-permute-start(bf16[2,48,512]{2,1,0:T(8,128)(2,1)S(1)} %get-tuple-element.32), channel_id=1, source_target_pairs={{1,2},{2,1},{3,4},{4,3},{5,6},{6,5},{7,0},{0,7},{9,10},{10,9},{11,... | collective-permute-start | bytes 294920 | tf_op jit(solution)/shard_map/ppermute | solution.py:43
  41.8 4.6 %collective-permute-start.11 = (bf16[2,48,512]{2,1,0:T(8,128)(2,1)S(1)}, bf16[2,48,512]{2,1,0:T(8,128)(2,1)S(1)}, u32[]{:S(2)}, u32[]{:S(2)}) collective-permute-start(bf16[2,48,512]{2,1,0:T(8,128)(2,1)S(1)} %get-tuple-element.33), channel_id=1, source_target_pairs={{0,1},{1,0},{2,3},{3,2},{4,5},{5,4},{6,7},{7,6},{8,9},{9,8},{10,11... | collective-permute-start | bytes 294920 | tf_op jit(solution)/shard_map/ppermute | solution.py:43

commit v2 on v1

v2 whole, which is shorter than its diff:
```python
import functools

import jax
import jax.numpy as jnp
from jax import lax
from jax.experimental import pallas as pl
from jax.experimental.pallas import tpu as pltpu
from jax.sharding import PartitionSpec as P

HEAD_DIM = 64
RADIUS = 6
SPAN = 2 * RADIUS + 1
ROWS = 8
COLS = 16
CELLS = ROWS * COLS
SIDE = ROWS * RADIUS
BAND = RADIUS * COLS
PAIR = 2 * HEAD_DIM
BASE = 336
TABLE = 512
MASKED = -1e30

OWN_AT = 0
LON_AT = CELLS
LAT_AT = LON_AT + 2 * SIDE
NEAR = LAT_AT + 2 * BAND
CORNERS = 4 * SIDE

F32 = jnp.float32
BF16 = jnp.bfloat16


def pair_exchange(value, axis, odd, wrap):
    count = lax.axis_size(axis)
    pairs = []
    for first in range(odd, count, 2):
        second = first + 1
        if second >= count and not wrap:
            continue
        second %= count
        pairs += [(first, second), (second, first)]
    return lax.ppermute(value, axis, pairs)


def is_odd(axis):
    return lax.axis_index(axis) % 2 == 1


def pick_matrix(first_col):
    shape = (SIDE, CELLS)
    place = lax.broadcasted_iota(jnp.int32, shape, 0)
    cell = lax.broadcasted_iota(jnp.int32, shape, 1)
    source = (place % ROWS) * COLS + first_col + place // ROWS
    return (cell == source).astype(BF16)


def pack_kernel(
    k_hbm, v_hbm, bias_hbm, lon_odd_ref, lon_even_ref, lat_even_ref, lat_odd_ref, line_ref, k_ref, v_ref, bias_ref, sems
):
    copies = [
        pltpu.make_async_copy(source, target, sems.at[index])
        for index, (source, target) in enumerate(((k_hbm, k_ref), (v_hbm, v_ref), (bias_hbm, bias_ref)))
    ]
    for copy in copies:
        copy.start()
    lon_odd = is_odd("lon")
    lat_odd = is_odd("lat")
    pick_odd = pick_matrix(jnp.where(lon_odd, COLS - RADIUS, 0))
    pick_even = pick_matrix(jnp.where(lon_odd, 0, COLS - RADIUS))
    low, high = 0, CELLS - BAND
    start_even = pl.multiple_of(jnp.where(lat_odd, low, high), 32)
    start_odd = pl.multiple_of(jnp.where(lat_odd, high, low), 32)
    shape = (SPAN * SPAN, TABLE)
    entry = lax.broadcasted_iota(jnp.int32, shape, 0)
    offset = BASE - lax.broadcasted_iota(jnp.int32, shape, 1)
    chosen = (offset == (entry // SPAN) * COLS + entry % SPAN).astype(F32)
    for slot, source in ((0, k_ref), (1, v_ref)):
        copies[slot].wait()
        whole = source[...]
        lon_odd_ref[slot] = jnp.dot(pick_odd, whole, preferred_element_type=F32).astype(BF16)
        lon_even_ref[slot] = jnp.dot(pick_even, whole, preferred_element_type=F32).astype(BF16)
        lat_even_ref[slot] = source[pl.ds(start_even, BAND), :]
        lat_odd_ref[slot] = source[pl.ds(start_odd, BAND), :]
    copies[2].wait()
    line = jnp.dot(bias_ref[...], chosen, preferred_element_type=F32, precision=lax.Precision.HIGHEST)
    offset = BASE - lax.broadcasted_iota(jnp.int32, (1, TABLE), 1)
    valid = (offset >= 0) & (offset < SPAN * COLS) & (offset % COLS < SPAN)
    line_ref[...] = jnp.where(valid, line, MASKED)


def bias_kernel(line_ref, table_ref, corner_ref):
    lon_odd = is_odd("lon")
    lat_odd = is_odd("lat")
    has_north = lax.axis_index("lat") > 0
    has_south = lax.axis_index("lat") < lax.axis_size("lat") - 1
    head = pl.program_id(0)
    line = jnp.broadcast_to(line_ref[pl.ds(head, 1), :], (8, TABLE))
    by_one = pltpu.roll(line, 0, 1, stride=1, stride_axis=0)
    by_row = pltpu.roll(line, 0, 1, stride=COLS, stride_axis=0)
    query_col = lax.broadcasted_iota(jnp.int32, (8, CELLS), 1) % COLS
    sub = lax.broadcasted_iota(jnp.int32, (8, CELLS), 0)

    def window(source, row, col):
        first = BASE - (COLS * row + col)
        return source[:, first : first + CELLS]

    def near(delta):
        return (delta >= 0) & (delta < SPAN)

    def put(at, values, target=table_ref):
        target[0, pl.ds(pl.multiple_of(at, 8), 8), :] = values

    def cells(at, row, row_count, there):
        for half in range(COLS // 8):
            allowed = near(RADIUS + 8 * half + sub - query_col)
            if there is not None:
                allowed = allowed & there
            for step in range(row_count):
                values = window(by_one, row + step, RADIUS + 8 * half)
                put(at + step * COLS + 8 * half, jnp.where(allowed, values, MASKED))

    def sides(at, row, first_col, there, target=table_ref):
        for step in range(RADIUS):
            allowed = near(first_col + step - query_col)
            if there is not None:
                allowed = allowed & there
            values = window(by_row, row, first_col + step)
            put(at + step * ROWS, jnp.where(allowed, values, MASKED), target)

    west, east = 0, COLS + RADIUS
    west_slot = jnp.where(lon_odd, SIDE, 0)
    east_slot = SIDE - west_slot
    cells(OWN_AT, RADIUS, ROWS, None)
    sides(LON_AT + west_slot, RADIUS, west, None)
    sides(LON_AT + east_slot, RADIUS, east, None)
    north_slot = jnp.where(lat_odd, 0, 1)
    south_slot = 1 - north_slot
    for slot, row, there in ((north_slot, 0, has_north), (south_slot, ROWS + RADIUS, has_south)):
        cells(LAT_AT + slot * BAND, row, RADIUS, there)
        first = row if row else row - (ROWS - RADIUS)
        sides(slot * 2 * SIDE + west_slot, first, west, there, corner_ref)
        sides(slot * 2 * SIDE + east_slot, first, east, there, corner_ref)


LAST = (((1,), (1,)), ((), ()))
FACTOR = HEAD_DIM ** (-0.5)


def both_heads(block):
    first_head = lax.broadcasted_iota(jnp.int32, block.shape, 1) < HEAD_DIM
    zero = jnp.zeros_like(block)
    return jnp.concatenate([jnp.where(first_head, block, zero), jnp.where(first_head, zero, block)], axis=0)


def scaled_queries(q_ref):
    return both_heads(q_ref[...] * jnp.asarray(FACTOR, BF16))


def pair_scores(keys, values, queries, grads, table_ref):
    scores = lax.dot_general(keys, queries, LAST, preferred_element_type=F32)
    scores = scores + jnp.concatenate([table_ref[0], table_ref[1]], axis=1)
    grad_prob = lax.dot_general(values, grads, LAST, preferred_element_type=F32)
    return scores, grad_prob


def column_sum(x):
    return jnp.sum(x, axis=0, keepdims=True)


def score_gradient(probability, grad_prob, row_dot):
    return probability.astype(BF16), (probability * (grad_prob - row_dot)).astype(BF16)


def near_kernel(
    q_ref, g_ref, k_ref, v_ref, lon_odd_ref, lon_even_ref, lat_even_ref, lat_odd_ref, table_ref,
    own_raised_ref, own_prob_ref, lon_raised_ref, lon_prob_ref, lat_raised_ref, lat_prob_ref, stats_ref,
):
    parts = (lon_odd_ref, lon_even_ref, lat_even_ref, lat_odd_ref)
    keys = jnp.concatenate([k_ref[...]] + [part[0] for part in parts], axis=0)
    values = jnp.concatenate([v_ref[...]] + [part[1] for part in parts], axis=0)
    scores, grad_prob = pair_scores(keys, values, scaled_queries(q_ref), both_heads(g_ref[...]), table_ref)
    largest = jnp.max(scores, axis=0, keepdims=True)
    raised = jnp.exp(scores - largest)
    stats_ref[0, 0:1] = largest
    stats_ref[0, 1:2] = column_sum(raised)
    stats_ref[0, 2:3] = column_sum(raised * grad_prob)
    for at, end, raised_ref, prob_ref in (
        (OWN_AT, LON_AT, own_raised_ref, own_prob_ref),
        (LON_AT, LAT_AT, lon_raised_ref, lon_prob_ref),
        (LAT_AT, NEAR, lat_raised_ref, lat_prob_ref),
    ):
        raised_ref[0] = raised[at:end]
        prob_ref[0] = grad_prob[at:end]


def corner_kernel(
    q_ref, g_ref, c0_ref, c1_ref, c2_ref, c3_ref, table_ref, lon_raised_ref, lon_prob_ref, near_stats_ref,
    back_even_ref, back_odd_ref, dlon_odd_ref, dlon_even_ref, weights_ref, dscore_ref, stats_ref,
):
    parts = (c0_ref, c1_ref, c2_ref, c3_ref)
    keys = jnp.concatenate([part[0] for part in parts], axis=0)
    values = jnp.concatenate([part[1] for part in parts], axis=0)
    queries, grads = scaled_queries(q_ref), both_heads(g_ref[...])
    scores, grad_prob = pair_scores(keys, values, queries, grads, table_ref)
    near_largest = near_stats_ref[0, 0:1]
    largest = jnp.maximum(near_largest, jnp.max(scores, axis=0, keepdims=True))
    raised = jnp.exp(scores - largest)
    shift = jnp.exp(near_largest - largest)
    total = near_stats_ref[0, 1:2] * shift + column_sum(raised)
    inverse = 1.0 / total
    near_scale = shift * inverse
    row_dot = near_stats_ref[0, 2:3] * near_scale + column_sum(raised * grad_prob) * inverse
    stats_ref[0, 0:1] = near_scale
    stats_ref[0, 1:2] = row_dot
    far = score_gradient(raised * inverse, grad_prob, row_dot)
    lon = score_gradient(lon_raised_ref[0] * near_scale, lon_prob_ref[0], row_dot)
    weights = jnp.concatenate([lon[0], far[0]], axis=0)
    dscore = jnp.concatenate([lon[1], far[1]], axis=0)
    weights_ref[0] = weights
    dscore_ref[0] = dscore
    for slot, coefficients, other in ((0, dscore, queries), (1, weights, grads)):
        grad = jnp.dot(coefficients, other, preferred_element_type=F32)
        dlon_odd_ref[slot] = grad[:SIDE]
        dlon_even_ref[slot] = grad[SIDE : 2 * SIDE]
        back_even_ref[slot] = grad[2 * SIDE : 4 * SIDE].astype(BF16)
        back_odd_ref[slot] = grad[4 * SIDE :].astype(BF16)


def lat_kernel(
    q_ref, g_ref, lat_raised_ref, lat_prob_ref, stats_ref, back_even_ref, back_odd_ref, weights_ref, dscore_ref
):
    weights, dscore = score_gradient(lat_raised_ref[0] * stats_ref[0, 0:1], lat_prob_ref[0], stats_ref[0, 1:2])
    weights_ref[0] = weights
    dscore_ref[0] = dscore
    for slot, coefficients, other in ((0, dscore, scaled_queries(q_ref)), (1, weights, both_heads(g_ref[...]))):
        grad = jnp.dot(coefficients, other, preferred_element_type=F32).astype(BF16)
        back_even_ref[slot] = grad[:BAND]
        back_odd_ref[slot] = grad[BAND:]


def own_kernel(
    q_ref, g_ref, k_ref, v_ref, lon_odd_ref, lon_even_ref, lat_even_ref, lat_odd_ref, c0_ref, c1_ref, c2_ref, c3_ref,
    own_raised_ref, own_prob_ref, stats_ref, far_weights_ref, far_dscore_ref, lat_weights_ref, lat_dscore_ref,
    out_ref, dq_ref, own_ref,
):
    own_weights, own_dscore = score_gradient(
        own_raised_ref[0] * stats_ref[0, 0:1], own_prob_ref[0], stats_ref[0, 1:2]
    )
    for slot, coefficients, other in (
        (0, own_dscore, scaled_queries(q_ref)), (1, own_weights, both_heads(g_ref[...]))
    ):
        own_ref[slot] = jnp.dot(coefficients, other, preferred_element_type=F32)
    parts = (lon_odd_ref, lon_even_ref, c0_ref, c1_ref, c2_ref, c3_ref, lat_even_ref, lat_odd_ref)
    keys = jnp.concatenate([k_ref[...]] + [part[0] for part in parts], axis=0)
    values = jnp.concatenate([v_ref[...]] + [part[1] for part in parts], axis=0)
    weights = jnp.concatenate([own_weights, far_weights_ref[0], lat_weights_ref[0]], axis=0)
    dscore = jnp.concatenate([own_dscore, far_dscore_ref[0], lat_dscore_ref[0]], axis=0)

    def per_query(cells, coefficients):
        turned = jnp.dot(cells.T, coefficients, preferred_element_type=F32)
        mine = jnp.concatenate([turned[:HEAD_DIM, :CELLS], turned[HEAD_DIM:, CELLS:]], axis=0)
        return mine.T

    out_ref[...] = per_query(values, weights).astype(BF16)
    dq_ref[...] = (per_query(keys, dscore) * FACTOR).astype(BF16)


def middle_kernel(dlon_odd_ref, dlon_even_ref, back_even_ref, back_odd_ref, send_odd_ref, send_even_ref):
    for index, (mine, send) in enumerate(((dlon_odd_ref, send_odd_ref), (dlon_even_ref, send_even_ref))):
        piece = pl.ds(index * SIDE, SIDE)
        send[...] = (mine[...] + back_even_ref[:, piece].astype(F32) + back_odd_ref[:, piece].astype(F32)).astype(BF16)


def final_kernel(own_ref, back_even_ref, back_odd_ref, side_odd_ref, side_even_ref, dk_ref, dv_ref, sum_ref):
    lon_odd = is_odd("lon")
    lat_odd = is_odd("lat")
    start_even = pl.multiple_of(jnp.where(lat_odd, 0, CELLS - BAND), 32)
    start_odd = pl.multiple_of(jnp.where(lat_odd, CELLS - BAND, 0), 32)
    shape = (CELLS, SIDE)
    cell = lax.broadcasted_iota(jnp.int32, shape, 0)
    place = lax.broadcasted_iota(jnp.int32, shape, 1)

    def spread(first_col):
        return (cell == (place % ROWS) * COLS + first_col + place // ROWS).astype(BF16)

    spread_odd = spread(jnp.where(lon_odd, COLS - RADIUS, 0))
    spread_even = spread(jnp.where(lon_odd, 0, COLS - RADIUS))
    for slot, out in ((0, dk_ref), (1, dv_ref)):
        sum_ref[...] = (
            own_ref[slot]
            + jnp.dot(spread_odd, side_odd_ref[slot], preferred_element_type=F32)
            + jnp.dot(spread_even, side_even_ref[slot], preferred_element_type=F32)
        )
        sum_ref[pl.ds(start_even, BAND), :] += back_even_ref[slot].astype(F32)
        sum_ref[pl.ds(start_odd, BAND), :] += back_odd_ref[slot].astype(F32)
        out[...] = sum_ref[...].astype(BF16)


def arr(shape, dtype):
    return jax.ShapeDtypeStruct(shape, dtype)


PARAMS = pltpu.CompilerParams(vmem_limit_bytes=32 * 1024 * 1024)


def cut(shape):
    if len(shape) == 2:
        return pl.BlockSpec((shape[0], PAIR), lambda i: (0, i))
    return pl.BlockSpec((shape[0], shape[1], PAIR), lambda i: (0, 0, i))


def by_pair(shape):
    return pl.BlockSpec((1, shape[1], shape[2]), lambda i: (i, 0, 0))


def by_two(shape):
    return pl.BlockSpec((2, shape[1], shape[2]), lambda i: (i, 0, 0))


def per_pair_call(kernel, name, operands, results, flops):
    pairs = operands[0][0].shape[1] // PAIR
    moved = sum(x.size * x.dtype.itemsize for x, _ in operands)
    return pl.pallas_call(
        kernel,
        out_shape=[x for x, _ in results],
        grid=(pairs,),
        in_specs=[spec(x.shape) for x, spec in operands],
        out_specs=[spec(x.shape) for x, spec in results],
        compiler_params=PARAMS,
        cost_estimate=pl.CostEstimate(flops=flops, bytes_accessed=moved, transcendentals=0),
        name=name,
    )(*[x for x, _ in operands])


def shards(queries, key_cells, value_cells, grad_output, rel_bias):
    block = queries.shape
    heads = rel_bias.shape[0]
    feat = block[-1]
    pairs = feat // PAIR
    q, k, v, g = (x.reshape(CELLS, feat) for x in (queries, key_cells, value_cells, grad_output))
    side, band = (2, SIDE, feat), (2, BAND, feat)
    work = 2 * CELLS * feat

    hbm = pl.BlockSpec(memory_space=pltpu.HBM)
    lon_odd, lon_even, lat_even, lat_odd, line = pl.pallas_call(
        pack_kernel,
        out_shape=[arr(side, BF16), arr(side, BF16), arr(band, BF16), arr(band, BF16), arr((heads, TABLE), F32)],
        in_specs=[hbm, hbm, hbm],
        scratch_shapes=[
            pltpu.VMEM((CELLS, feat), BF16),
            pltpu.VMEM((CELLS, feat), BF16),
            pltpu.VMEM(rel_bias.shape, F32),
            pltpu.SemaphoreType.DMA((3,)),
        ],
        compiler_params=PARAMS,
        name="pack",
    )(k, v, rel_bias)

    lon_odd = pair_exchange(lon_odd, "lon", 1, True)
    lon_even = pair_exchange(lon_even, "lon", 0, True)
    lat_even = pair_exchange(lat_even, "lat", 0, False)
    lat_odd = pair_exchange(lat_odd, "lat", 1, False)

    table, corner_table = pl.pallas_call(
        bias_kernel,
        out_shape=[arr((heads, NEAR, CELLS), F32), arr((heads, CORNERS, CELLS), F32)],
        grid=(heads,),
        in_specs=[pl.BlockSpec((heads, TABLE), lambda i: (0, 0))],
        out_specs=[
            pl.BlockSpec((1, NEAR, CELLS), lambda i: (i, 0, 0)),
            pl.BlockSpec((1, CORNERS, CELLS), lambda i: (i, 0, 0)),
        ],
        compiler_params=PARAMS,
        cost_estimate=pl.CostEstimate(flops=heads * NEAR * CELLS, bytes_accessed=8 * heads * NEAR * CELLS, transcendentals=0),
        name="bias_table",
    )(line)

    lon_even, table, corner_table = lax.optimization_barrier((lon_even, table, corner_table))
    lon_odd, lat_even, lat_odd = lax.optimization_barrier((lon_odd, lat_even, lat_odd))
    c1 = pair_exchange(lon_even, "lat", 0, False)
    c3 = pair_exchange(lon_even, "lat", 1, False)
    c0 = pair_exchange(lon_odd, "lat", 0, False)
    c2 = pair_exchange(lon_odd, "lat", 1, False)
    corners = [(c, cut) for c in (c0, c1, c2, c3)]

    mine = [(q, cut), (g, cut)]
    near = [(x, cut) for x in (k, v, lon_odd, lon_even, lat_even, lat_odd)]
    stats = (arr((pairs, 8, 2 * CELLS), F32), by_pair)

    def scored(rows, dtype):
        return [(arr((pairs, rows, 2 * CELLS), dtype), by_pair)] * 2

    spans = (CELLS, 2 * SIDE, 2 * BAND)
    own_raised, own_prob, lon_raised, lon_prob, lat_raised, lat_prob, near_stats = per_pair_call(
        near_kernel, "near", mine + near + [(table, by_two)],
        [x for rows in spans for x in scored(rows, F32)] + [stats], 4 * work * NEAR,
    )
    corner_even, corner_odd, dlon_odd, dlon_even, far_weights, far_dscore, all_stats = per_pair_call(
        corner_kernel, "corner",
        mine + corners + [(corner_table, by_two)] + [(x, by_pair) for x in (lon_raised, lon_prob, near_stats)],
        [(arr((2, 2 * SIDE, feat), BF16), cut)] * 2 + [(arr(side, F32), cut)] * 2
        + scored(2 * SIDE + CORNERS, BF16) + [stats], 4 * work * CORNERS,
    )
    corner_even = pair_exchange(corner_even, "lat", 0, False)
    corner_odd = pair_exchange(corner_odd, "lat", 1, False)
    back_even, back_odd, lat_weights, lat_dscore = per_pair_call(
        lat_kernel, "lat_rows", mine + [(x, by_pair) for x in (lat_raised, lat_prob, all_stats)],
        [(arr(band, BF16), cut)] * 2 + scored(2 * BAND, BF16), 4 * work * BAND,
    )
    back_even = pair_exchange(back_even, "lat", 0, False)
    back_odd = pair_exchange(back_odd, "lat", 1, False)
    send_odd, send_even = pl.pallas_call(
        middle_kernel,
        out_shape=[arr(side, BF16), arr(side, BF16)],
        compiler_params=PARAMS,
        name="middle",
    )(dlon_odd, dlon_even, corner_even, corner_odd)
    side_odd = pair_exchange(send_odd, "lon", 1, True)
    side_even = pair_exchange(send_even, "lon", 0, True)
    scores = (own_raised, own_prob, all_stats, far_weights, far_dscore, lat_weights, lat_dscore)
    out, dq, own = per_pair_call(
        own_kernel, "own", mine + near + corners + [(x, by_pair) for x in scores],
        [(arr((CELLS, feat), BF16), cut)] * 2 + [(arr((2, CELLS, feat), F32), cut)], 4 * work * (NEAR + CORNERS),
    )
    dk, dv = pl.pallas_call(
        final_kernel,
        out_shape=[arr((CELLS, feat), BF16), arr((CELLS, feat), BF16)],
        scratch_shapes=[pltpu.VMEM((CELLS, feat), F32)],
        compiler_params=PARAMS,
        name="final",
    )(own, back_even, back_odd, side_odd, side_even)
    return tuple(x.reshape(block) for x in (out, dq, dk, dv))


def solution(mesh):
    spec = P("lat", "lon", None)
    return jax.shard_map(
        shards, mesh=mesh, in_specs=(spec, spec, spec, spec, P()), out_specs=(spec,) * 4, check_vma=False
    )
```

time: 47.7 us -> 46.3 us (0.971)
  the two profiles are of different devices: /device:TPU:2 before, /device:TPU:0 now
where the time goes in v2:
time: 46.3 us; the launch traced here: 45.9 us
  starting transfers between devices  22.9 us (49%)
  Pallas kernels  12.4 us (27%)
  local copies, waits for them, and re-layouts  5.28 us (11%)
  waiting for transfers between devices  4.55 us (10%)
  between operations  0.86 us (2%)
    ppermute x14, starting transfers between devices, pair_exchange(): return lax.ppermute(value, axis, pairs)  22.9 us
    pallas_call x4, Pallas kernels, per_pair_call(): pl.pallas_call(kernel, out_shape=[x for x, _ in results], grid=(pairs,),...  8.15 us
    unnamed x20, local copies, waits for them, and re-layouts  5.28 us
    ppermute x14, waiting for transfers between devices, pair_exchange(): return lax.ppermute(value, axis, pairs)  4.55 us
    pallas_call x1, Pallas kernels, shards(): pl.pallas_call(bias_kernel, out_shape=[arr((heads, NEAR, CELLS), F32), ar...  2.03 us
    pallas_call x1, Pallas kernels, shards(): pl.pallas_call(pack_kernel, out_shape=[arr(side, BF16), arr(side, BF16),...  1.07 us
    pallas_call x1, Pallas kernels, shards(): pl.pallas_call(final_kernel, out_shape=[arr((CELLS, feat), BF16), arr((CE...  1.05 us
  transfers between devices with their start and end apart: 14, of which 2 were waited for; matrix products, arithmetic and copies ran while one was open for 0% of the time, Pallas kernels for 17%

profile of v2, /device:TPU:0, one launch (start us, length us, event | category | flops | bytes accessed | tf_op | source)
XLA Modules:
  0.0 45.9 jit_solution(13179476521088151578)
XLA Ops:
  0.6 0.0 copy-start.3
  0.6 0.0 copy-start.1
  0.7 0.0 copy-start.4
  0.7 0.9 %copy-done.4 = bf16[8,16,512]{2,1,0:T(8,128)(2,1)S(1)} copy-done((bf16[8,16,512]{2,1,0:T(8,128)(2,1)S(1)}, bf16[8,16,512]{2,1,0:T(8,128)(2,1)}, u32[]{:S(2)}) %copy-start.4) | copy-done | bytes 131096
  1.6 0.9 %copy-done.7 = bf16[8,16,512]{2,1,0:T(8,128)(2,1)S(1)} copy-done((bf16[8,16,512]{2,1,0:T(8,128)(2,1)S(1)}, bf16[8,16,512]{2,1,0:T(8,128)(2,1)}, u32[]{:S(2)}) %copy-start.7) | copy-done | bytes 131096
  2.5 0.7 %copy-done.9 = f32[8,169]{1,0:T(8,128)S(1)} copy-done((f32[8,169]{1,0:T(8,128)S(1)}, f32[8,169]{1,0:T(8,128)}, u32[]{:S(2)}) %copy-start.9) | copy-done | bytes 5432
  3.2 1.1 %pack.1 = (bf16[2,48,512]{2,1,0:T(8,128)(2,1)S(1)}, bf16[2,48,512]{2,1,0:T(8,128)(2,1)S(1)}, bf16[2,96,512]{2,1,0:T(8,128)(2,1)S(1)}, bf16[2,96,512]{2,1,0:T(8,128)(2,1)S(1)}, f32[8,512]{1,0:T(8,128)S(1)}) custom-call(bf16[128,512]{1,0:T(8,128)(2,1)S(1)} %bitcast.16, bf16[128,512]{1,0:T(8,128)(2,1)S(1)} %bitcast.19, f32[8,169]{1,0:T(8,128)S(1)} %copy-done.9), custom_call_target="tpu_custom_call" | custom-call | tf_op jit(solution)/shard_map/pack/pallas_call | solution.py:345
  4.3 0.5 %collective-permute-start.1 = (bf16[2,96,512]{2,1,0:T(8,128)(2,1)S(1)}, bf16[2,96,512]{2,1,0:T(8,128)(2,1)S(1)}, u32[]{:S(2)}, u32[]{:S(2)}) collective-permute-start(bf16[2,96,512]{2,1,0:T(8,128)(2,1)S(1)} %get-tuple-element.43), channel_id=1, source_target_pairs={{0,8},{8,0},{16,24},{24,16},{1,9},{9,1},{17,25},{25,17},{2,10},{10... | collective-permute-start | bytes 589832 | tf_op jit(solution)/shard_map/ppermute | solution.py:42
  4.8 0.7 %collective-permute-start.2 = (bf16[2,96,512]{2,1,0:T(8,128)(2,1)S(1)}, bf16[2,96,512]{2,1,0:T(8,128)(2,1)S(1)}, u32[]{:S(2)}, u32[]{:S(2)}) collective-permute-start(bf16[2,96,512]{2,1,0:T(8,128)(2,1)S(1)} %get-tuple-element.44), channel_id=1, source_target_pairs={{8,16},{16,8},{9,17},{17,9},{10,18},{18,10},{11,19},{19,11},{12,20... | collective-permute-start | bytes 589832 | tf_op jit(solution)/shard_map/ppermute | solution.py:42
  5.5 2.6 %collective-permute-start.3 = (bf16[2,48,512]{2,1,0:T(8,128)(2,1)S(1)}, bf16[2,48,512]{2,1,0:T(8,128)(2,1)S(1)}, u32[]{:S(2)}, u32[]{:S(2)}) collective-permute-start(bf16[2,48,512]{2,1,0:T(8,128)(2,1)S(1)} %get-tuple-element.46), channel_id=1, source_target_pairs={{0,1},{1,0},{2,3},{3,2},{4,5},{5,4},{6,7},{7,6},{8,9},{9,8},{10,11... | collective-permute-start | bytes 294920 | tf_op jit(solution)/shard_map/ppermute | solution.py:42
  8.1 3.5 %collective-permute-start = (bf16[2,48,512]{2,1,0:T(8,128)(2,1)S(1)}, bf16[2,48,512]{2,1,0:T(8,128)(2,1)S(1)}, u32[]{:S(2)}, u32[]{:S(2)}) collective-permute-start(bf16[2,48,512]{2,1,0:T(8,128)(2,1)S(1)} %get-tuple-element.42), channel_id=1, source_target_pairs={{1,2},{2,1},{3,4},{4,3},{5,6},{6,5},{7,0},{0,7},{9,10},{10,9},{11,... | collective-permute-start | bytes 294920 | tf_op jit(solution)/shard_map/ppermute | solution.py:42
  11.6 2.0 %bias_table.1 = (f32[8,416,128]{2,1,0:T(8,128)S(1)}, f32[8,192,128]{2,1,0:T(8,128)S(1)}) custom-call(f32[8,512]{1,0:T(8,128)S(1)} %get-tuple-element.47.line_ref), custom_call_target="tpu_custom_call" | custom-call | flops 425984 | bytes 3407872 | tf_op jit(solution)/shard_map/bias_table/pallas_call | solution.py:364
  13.7 0.0 collective-permute-done.3.lon_even_ref
  13.7 0.7 %collective-permute-start.7 = (bf16[2,48,512]{2,1,0:T(8,128)(2,1)S(1)}, bf16[2,48,512]{2,1,0:T(8,128)(2,1)S(1)}, u32[]{:S(2)}, u32[]{:S(2)}) collective-permute-start(bf16[2,48,512]{2,1,0:T(8,128)(2,1)S(1)} %collective-permute-done.3.lon_even_ref), channel_id=1, source_target_pairs={{8,16},{16,8},{9,17},{17,9},{10,18},{18,10},{11,19},{19,11},{12,20... | collective-permute-start | bytes 294920 | tf_op jit(solution)/shard_map/ppermute | solution.py:42
  14.3 4.8 %collective-permute-start.5 = (bf16[2,48,512]{2,1,0:T(8,128)(2,1)S(1)}, bf16[2,48,512]{2,1,0:T(8,128)(2,1)S(1)}, u32[]{:S(2)}, u32[]{:S(2)}) collective-permute-start(bf16[2,48,512]{2,1,0:T(8,128)(2,1)S(1)} %collective-permute-done.3.lon_even_ref), channel_id=1, source_target_pairs={{0,8},{8,0},{16,24},{24,16},{1,9},{9,1},{17,25},{25,17},{2,10},{10... | collective-permute-start | bytes 294920 | tf_op jit(solution)/shard_map/ppermute | solution.py:42
  19.1 0.0 collective-permute-done.lon_odd_ref
  19.1 0.0 collective-permute-done.1.lat_even_ref
  19.1 0.0 collective-permute-done.2.lat_odd_ref
  19.1 0.7 %collective-permute-start.6 = (bf16[2,48,512]{2,1,0:T(8,128)(2,1)S(1)}, bf16[2,48,512]{2,1,0:T(8,128)(2,1)S(1)}, u32[]{:S(2)}, u32[]{:S(2)}) collective-permute-start(bf16[2,48,512]{2,1,0:T(8,128)(2,1)S(1)} %collective-permute-done.lon_odd_ref), channel_id=1, source_target_pairs={{8,16},{16,8},{9,17},{17,9},{10,18},{18,10},{11,19},{19,11},{12,20... | collective-permute-start | bytes 294920 | tf_op jit(solution)/shard_map/ppermute | solution.py:42
  19.8 1.9 %collective-permute-start.4 = (bf16[2,48,512]{2,1,0:T(8,128)(2,1)S(1)}, bf16[2,48,512]{2,1,0:T(8,128)(2,1)S(1)}, u32[]{:S(2)}, u32[]{:S(2)}) collective-permute-start(bf16[2,48,512]{2,1,0:T(8,128)(2,1)S(1)} %collective-permute-done.lon_odd_ref), channel_id=1, source_target_pairs={{0,8},{8,0},{16,24},{24,16},{1,9},{9,1},{17,25},{25,17},{2,10},{10... | collective-permute-start | bytes 294920 | tf_op jit(solution)/shard_map/ppermute | solution.py:42
  21.7 0.9 %copy-done = bf16[8,16,512]{2,1,0:T(8,128)(2,1)S(1)} copy-done((bf16[8,16,512]{2,1,0:T(8,128)(2,1)S(1)}, bf16[8,16,512]{2,1,0:T(8,128)(2,1)}, u32[]{:S(2)}) %copy-start) | copy-done | bytes 131096
  22.6 0.9 %copy-done.2 = bf16[8,16,512]{2,1,0:T(8,128)(2,1)S(1)} copy-done((bf16[8,16,512]{2,1,0:T(8,128)(2,1)S(1)}, bf16[8,16,512]{2,1,0:T(8,128)(2,1)}, u32[]{:S(2)}) %copy-start.2) | copy-done | bytes 131096
  23.5 0.9 %copy-done.5 = bf16[8,16,512]{2,1,0:T(8,128)(2,1)S(1)} copy-done((bf16[8,16,512]{2,1,0:T(8,128)(2,1)S(1)}, bf16[8,16,512]{2,1,0:T(8,128)(2,1)}, u32[]{:S(2)}) %copy-start.5) | copy-done | bytes 131096
  24.4 1.9 %near.1 = (f32[4,128,256]{2,1,0:T(8,128)S(1)}, f32[4,128,256]{2,1,0:T(8,128)S(1)}, f32[4,96,256]{2,1,0:T(8,128)S(1)}, f32[4,96,256]{2,1,0:T(8,128)S(1)}, f32[4,1...) custom-call(bf16[128,512]{1,0:T(8,128)(2,1)S(1)} %bitcast.8, ...), custom_call_target="tpu_custom_call" | custom-call | flops 218103808 | bytes 2818048 | tf_op jit(solution)/shard_map/near/pallas_call | solution.py:323
  26.3 0.0 collective-permute-done.7.c3_ref
  26.3 0.0 collective-permute-done.5.c1_ref
  26.3 0.0 collective-permute-done.6.c2_ref
  26.3 0.0 collective-permute-done.4.c0_ref
  26.3 0.0 copy-done.3
  26.4 2.5 %corner.1 = (bf16[2,96,512]{2,1,0:T(8,128)(2,1)S(1)}, bf16[2,96,512]{2,1,0:T(8,128)(2,1)S(1)}, f32[2,48,512]{2,1,0:T(8,128)S(1)}, f32[2,48,512]{2,1,0:T(8,128)S(...) custom-call(bf16[128,512]{1,0:T(8,128)(2,1)S(1)} %bitcast.9, ...), custom_call_target="tpu_custom_call" | custom-call | flops 100663296 | bytes 2260992 | tf_op jit(solution)/shard_map/corner/pallas_call | solution.py:323
  28.9 0.0 copy-start.6
  28.9 0.0 copy-start.8
  28.9 0.1 collective-permute-start.10
  29.0 0.8 %collective-permute-start.11 = (bf16[2,96,512]{2,1,0:T(8,128)(2,1)S(1)}, bf16[2,96,512]{2,1,0:T(8,128)(2,1)S(1)}, u32[]{:S(2)}, u32[]{:S(2)}) collective-permute-start(bf16[2,96,512]{2,1,0:T(8,128)(2,1)S(1)} %get-tuple-element.75), channel_id=1, source_target_pairs={{8,16},{16,8},{9,17},{17,9},{10,18},{18,10},{11,19},{19,11},{12,20... | collective-permute-start | bytes 589832 | tf_op jit(solution)/shard_map/ppermute | solution.py:42
  29.8 1.0 %lat_rows.1 = (bf16[2,96,512]{2,1,0:T(8,128)(2,1)S(1)}, bf16[2,96,512]{2,1,0:T(8,128)(2,1)S(1)}, bf16[4,192,256]{2,1,0:T(8,128)(2,1)S(1)}, bf16[4,192,256]{2,1,0:T(8,128)(2,1)S(1)}) custom-call(bf16[128,512]{1,0:T(8,128)(2,1)S(1)} %bitcast.10, bf16[128,512]{1,0:T(8,128)(2,1)S(1)} %bitcast.14, f32[4,192,256]{2,1,0:T(8,128)S(1)} %get-tuple-element.63.lat_raised_ref, ...), custom_call_target="tpu_custom_call" | custom-call | flops 50331648 | bytes 1867776 | tf_op jit(solution)/shard_map/lat_rows/pallas_call | solution.py:323
  30.8 2.8 %collective-permute-start.8 = (bf16[2,96,512]{2,1,0:T(8,128)(2,1)S(1)}, bf16[2,96,512]{2,1,0:T(8,128)(2,1)S(1)}, u32[]{:S(2)}, u32[]{:S(2)}) collective-permute-start(bf16[2,96,512]{2,1,0:T(8,128)(2,1)S(1)} %get-tuple-element.70), channel_id=1, source_target_pairs={{0,8},{8,0},{16,24},{24,16},{1,9},{9,1},{17,25},{25,17},{2,10},{10... | collective-permute-start | bytes 589832 | tf_op jit(solution)/shard_map/ppermute | solution.py:42
  33.6 0.7 %collective-permute-start.9 = (bf16[2,96,512]{2,1,0:T(8,128)(2,1)S(1)}, bf16[2,96,512]{2,1,0:T(8,128)(2,1)S(1)}, u32[]{:S(2)}, u32[]{:S(2)}) collective-permute-start(bf16[2,96,512]{2,1,0:T(8,128)(2,1)S(1)} %get-tuple-element.71), channel_id=1, source_target_pairs={{8,16},{16,8},{9,17},{17,9},{10,18},{18,10},{11,19},{19,11},{12,20... | collective-permute-start | bytes 589832 | tf_op jit(solution)/shard_map/ppermute | solution.py:42
  34.3 0.0 collective-permute-done.10.back_even_ref
  34.3 0.0 collective-permute-done.11.back_odd_ref
  34.3 0.1 middle.1
  34.4 3.2 %collective-permute-start.12 = (bf16[2,48,512]{2,1,0:T(8,128)(2,1)S(1)}, bf16[2,48,512]{2,1,0:T(8,128)(2,1)S(1)}, u32[]{:S(2)}, u32[]{:S(2)}) collective-permute-start(bf16[2,48,512]{2,1,0:T(8,128)(2,1)S(1)} %get-tuple-element.76), channel_id=1, source_target_pairs={{1,2},{2,1},{3,4},{4,3},{5,6},{6,5},{7,0},{0,7},{9,10},{10,9},{11,... | collective-permute-start | bytes 294920 | tf_op jit(solution)/shard_map/ppermute | solution.py:42
  37.5 0.0 collective-permute-start.13
  37.5 2.8 %own.1 = (bf16[128,512]{1,0:T(8,128)(2,1)}, bf16[128,512]{1,0:T(8,128)(2,1)}, f32[2,128,512]{2,1,0:T(8,128)S(1)}) custom-call(bf16[128,512]{1,0:T(8,128)(2,1)S(1)} %bitcast.11, bf16[128,512]{1,0:T(8,128)(2,1)S(1)} %bitcast.15, bf16[128,512]{1,0:T(8,128)(2,1)S(1)} %bitcast.18, bf16[128,512]{1,0:T(8,128)(2,1)S(1)} %bitcast.21, ...), custom_call_target="tpu_custom_call" | custom-call | flops 318767104 | bytes 4554752 | tf_op jit(solution)/shard_map/own/pallas_call | solution.py:323
  40.3 0.0 collective-permute-done.8.back_even_ref
  40.3 0.0 collective-permute-done.9.back_odd_ref
  40.4 1.5 %collective-permute-done.12.side_odd_ref = bf16[2,48,512]{2,1,0:T(8,128)(2,1)S(1)} collective-permute-done((bf16[2,48,512]{2,1,0:T(8,128)(2,1)S(1)}, bf16[2,48,512]{2,1,0:T(8,128)(2,1)S(1)}, u32[]{:S(2)}, u32[]{:S(2)}) %collective-permute-start.12) | collective-permute-done | bytes 98336 | tf_op jit(solution)/shard_map/ppermute | solution.py:42
  41.8 3.0 %collective-permute-done.13.side_even_ref = bf16[2,48,512]{2,1,0:T(8,128)(2,1)S(1)} collective-permute-done((bf16[2,48,512]{2,1,0:T(8,128)(2,1)S(1)}, bf16[2,48,512]{2,1,0:T(8,128)(2,1)S(1)}, u32[]{:S(2)}, u32[]{:S(2)}) %collective-permute-start.13) | collective-permute-done | bytes 98336 | tf_op jit(solution)/shard_map/ppermute | solution.py:42
  44.9 1.1 %final.1 = (bf16[128,512]{1,0:T(8,128)(2,1)}, bf16[128,512]{1,0:T(8,128)(2,1)}) custom-call(f32[2,128,512]{2,1,0:T(8,128)S(1)} %get-tuple-element.69.own_ref, bf16[2,96,512]{2,1,0:T(8,128)(2,1)S(1)} %collective-permute-done.8.back_even_ref, bf16[2,96,512]{2,1,0:T(8,128)(2,1)S(1)} %collective-permute-done.9.back_odd_ref, ...), custom_call_target="tpu_custom_call" | custom-call | tf_op jit(solution)/shard_map/final/pallas_call | solution.py:425
  (8 shorter events, 0.0 us)
Async XLA Ops:
  0.6 25.7 %copy-start.3 = (bf16[8,16,512]{2,1,0:T(8,128)(2,1)S(1)}, bf16[8,16,512]{2,1,0:T(8,128)(2,1)}, u32[]{:S(2)}) copy-start(bf16[8,16,512]{2,1,0:T(8,128)(2,1)} %param.8) | copy-start | bytes 393220
  0.6 25.7 %copy-start.1 = (bf16[8,16,512]{2,1,0:T(8,128)(2,1)S(1)}, bf16[8,16,512]{2,1,0:T(8,128)(2,1)}, u32[]{:S(2)}) copy-start(bf16[8,16,512]{2,1,0:T(8,128)(2,1)} %param.5) | copy-start | bytes 393220
  0.7 0.9 %copy-start.4 = (bf16[8,16,512]{2,1,0:T(8,128)(2,1)S(1)}, bf16[8,16,512]{2,1,0:T(8,128)(2,1)}, u32[]{:S(2)}) copy-start(bf16[8,16,512]{2,1,0:T(8,128)(2,1)} %param.6) | copy-start | bytes 393220
  1.6 0.9 %copy-start.7 = (bf16[8,16,512]{2,1,0:T(8,128)(2,1)S(1)}, bf16[8,16,512]{2,1,0:T(8,128)(2,1)}, u32[]{:S(2)}) copy-start(bf16[8,16,512]{2,1,0:T(8,128)(2,1)} %param.7) | copy-start | bytes 393220
  2.5 0.7 %copy-start.9 = (f32[8,169]{1,0:T(8,128)S(1)}, f32[8,169]{1,0:T(8,128)}, u32[]{:S(2)}) copy-start(f32[8,169]{1,0:T(8,128)} %bias_hbm.1) | copy-start | bytes 16228
  4.3 14.8 %collective-permute-start.1 = (bf16[2,96,512]{2,1,0:T(8,128)(2,1)S(1)}, bf16[2,96,512]{2,1,0:T(8,128)(2,1)S(1)}, u32[]{:S(2)}, u32[]{:S(2)}) collective-permute-start(bf16[2,96,512]{2,1,0:T(8,128)(2,1)S(1)} %get-tuple-element.43), channel_id=1, source_target_pairs={{0,8},{8,0},{16,24},{24,16},{1,9},{9,1},{17,25},{25,17},{2,10},{10... | collective-permute-start | bytes 589832 | tf_op jit(solution)/shard_map/ppermute | solution.py:42
  4.8 14.3 %collective-permute-start.2 = (bf16[2,96,512]{2,1,0:T(8,128)(2,1)S(1)}, bf16[2,96,512]{2,1,0:T(8,128)(2,1)S(1)}, u32[]{:S(2)}, u32[]{:S(2)}) collective-permute-start(bf16[2,96,512]{2,1,0:T(8,128)(2,1)S(1)} %get-tuple-element.44), channel_id=1, source_target_pairs={{8,16},{16,8},{9,17},{17,9},{10,18},{18,10},{11,19},{19,11},{12,20... | collective-permute-start | bytes 589832 | tf_op jit(solution)/shard_map/ppermute | solution.py:42
  5.5 8.2 %collective-permute-start.3 = (bf16[2,48,512]{2,1,0:T(8,128)(2,1)S(1)}, bf16[2,48,512]{2,1,0:T(8,128)(2,1)S(1)}, u32[]{:S(2)}, u32[]{:S(2)}) collective-permute-start(bf16[2,48,512]{2,1,0:T(8,128)(2,1)S(1)} %get-tuple-element.46), channel_id=1, source_target_pairs={{0,1},{1,0},{2,3},{3,2},{4,5},{5,4},{6,7},{7,6},{8,9},{9,8},{10,11... | collective-permute-start | bytes 294920 | tf_op jit(solution)/shard_map/ppermute | solution.py:42
  8.1 11.0 %collective-permute-start = (bf16[2,48,512]{2,1,0:T(8,128)(2,1)S(1)}, bf16[2,48,512]{2,1,0:T(8,128)(2,1)S(1)}, u32[]{:S(2)}, u32[]{:S(2)}) collective-permute-start(bf16[2,48,512]{2,1,0:T(8,128)(2,1)S(1)} %get-tuple-element.42), channel_id=1, source_target_pairs={{1,2},{2,1},{3,4},{4,3},{5,6},{6,5},{7,0},{0,7},{9,10},{10,9},{11,... | collective-permute-start | bytes 294920 | tf_op jit(solution)/shard_map/ppermute | solution.py:42
  13.7 12.6 %collective-permute-start.7 = (bf16[2,48,512]{2,1,0:T(8,128)(2,1)S(1)}, bf16[2,48,512]{2,1,0:T(8,128)(2,1)S(1)}, u32[]{:S(2)}, u32[]{:S(2)}) collective-permute-start(bf16[2,48,512]{2,1,0:T(8,128)(2,1)S(1)} %collective-permute-done.3.lon_even_ref), channel_id=1, source_target_pairs={{8,16},{16,8},{9,17},{17,9},{10,18},{18,10},{11,19},{19,11},{12,20... | collective-permute-start | bytes 294920 | tf_op jit(solution)/shard_map/ppermute | solution.py:42
  14.3 12.0 %collective-permute-start.5 = (bf16[2,48,512]{2,1,0:T(8,128)(2,1)S(1)}, bf16[2,48,512]{2,1,0:T(8,128)(2,1)S(1)}, u32[]{:S(2)}, u32[]{:S(2)}) collective-permute-start(bf16[2,48,512]{2,1,0:T(8,128)(2,1)S(1)} %collective-permute-done.3.lon_even_ref), channel_id=1, source_target_pairs={{0,8},{8,0},{16,24},{24,16},{1,9},{9,1},{17,25},{25,17},{2,10},{10... | collective-permute-start | bytes 294920 | tf_op jit(solution)/shard_map/ppermute | solution.py:42
  19.1 7.2 %collective-permute-start.6 = (bf16[2,48,512]{2,1,0:T(8,128)(2,1)S(1)}, bf16[2,48,512]{2,1,0:T(8,128)(2,1)S(1)}, u32[]{:S(2)}, u32[]{:S(2)}) collective-permute-start(bf16[2,48,512]{2,1,0:T(8,128)(2,1)S(1)} %collective-permute-done.lon_odd_ref), channel_id=1, source_target_pairs={{8,16},{16,8},{9,17},{17,9},{10,18},{18,10},{11,19},{19,11},{12,20... | collective-permute-start | bytes 294920 | tf_op jit(solution)/shard_map/ppermute | solution.py:42
  19.8 6.5 %collective-permute-start.4 = (bf16[2,48,512]{2,1,0:T(8,128)(2,1)S(1)}, bf16[2,48,512]{2,1,0:T(8,128)(2,1)S(1)}, u32[]{:S(2)}, u32[]{:S(2)}) collective-permute-start(bf16[2,48,512]{2,1,0:T(8,128)(2,1)S(1)} %collective-permute-done.lon_odd_ref), channel_id=1, source_target_pairs={{0,8},{8,0},{16,24},{24,16},{1,9},{9,1},{17,25},{25,17},{2,10},{10... | collective-permute-start | bytes 294920 | tf_op jit(solution)/shard_map/ppermute | solution.py:42
  21.7 0.9 %copy-start = (bf16[8,16,512]{2,1,0:T(8,128)(2,1)S(1)}, bf16[8,16,512]{2,1,0:T(8,128)(2,1)}, u32[]{:S(2)}) copy-start(bf16[8,16,512]{2,1,0:T(8,128)(2,1)} %param.5) | copy-start | bytes 393220
  22.6 0.9 %copy-start.2 = (bf16[8,16,512]{2,1,0:T(8,128)(2,1)S(1)}, bf16[8,16,512]{2,1,0:T(8,128)(2,1)}, u32[]{:S(2)}) copy-start(bf16[8,16,512]{2,1,0:T(8,128)(2,1)} %param.8) | copy-start | bytes 393220
  23.5 0.9 %copy-start.5 = (bf16[8,16,512]{2,1,0:T(8,128)(2,1)S(1)}, bf16[8,16,512]{2,1,0:T(8,128)(2,1)}, u32[]{:S(2)}) copy-start(bf16[8,16,512]{2,1,0:T(8,128)(2,1)} %param.6) | copy-start | bytes 393220
  28.9 8.7 %copy-start.6 = (bf16[8,16,512]{2,1,0:T(8,128)(2,1)S(1)}, bf16[8,16,512]{2,1,0:T(8,128)(2,1)}, u32[]{:S(2)}) copy-start(bf16[8,16,512]{2,1,0:T(8,128)(2,1)} %param.6) | copy-start | bytes 393220
  28.9 8.7 %copy-start.8 = (bf16[8,16,512]{2,1,0:T(8,128)(2,1)S(1)}, bf16[8,16,512]{2,1,0:T(8,128)(2,1)}, u32[]{:S(2)}) copy-start(bf16[8,16,512]{2,1,0:T(8,128)(2,1)} %param.7) | copy-start | bytes 393220
  28.9 5.4 %collective-permute-start.10 = (bf16[2,96,512]{2,1,0:T(8,128)(2,1)S(1)}, bf16[2,96,512]{2,1,0:T(8,128)(2,1)S(1)}, u32[]{:S(2)}, u32[]{:S(2)}) collective-permute-start(bf16[2,96,512]{2,1,0:T(8,128)(2,1)S(1)} %get-tuple-element.74), channel_id=1, source_target_pairs={{0,8},{8,0},{16,24},{24,16},{1,9},{9,1},{17,25},{25,17},{2,10},{10... | collective-permute-start | bytes 589832 | tf_op jit(solution)/shard_map/ppermute | solution.py:42
  29.0 5.3 %collective-permute-start.11 = (bf16[2,96,512]{2,1,0:T(8,128)(2,1)S(1)}, bf16[2,96,512]{2,1,0:T(8,128)(2,1)S(1)}, u32[]{:S(2)}, u32[]{:S(2)}) collective-permute-start(bf16[2,96,512]{2,1,0:T(8,128)(2,1)S(1)} %get-tuple-element.75), channel_id=1, source_target_pairs={{8,16},{16,8},{9,17},{17,9},{10,18},{18,10},{11,19},{19,11},{12,20... | collective-permute-start | bytes 589832 | tf_op jit(solution)/shard_map/ppermute | solution.py:42
  30.8 9.6 %collective-permute-start.8 = (bf16[2,96,512]{2,1,0:T(8,128)(2,1)S(1)}, bf16[2,96,512]{2,1,0:T(8,128)(2,1)S(1)}, u32[]{:S(2)}, u32[]{:S(2)}) collective-permute-start(bf16[2,96,512]{2,1,0:T(8,128)(2,1)S(1)} %get-tuple-element.70), channel_id=1, source_target_pairs={{0,8},{8,0},{16,24},{24,16},{1,9},{9,1},{17,25},{25,17},{2,10},{10... | collective-permute-start | bytes 589832 | tf_op jit(solution)/shard_map/ppermute | solution.py:42
  33.6 6.7 %collective-permute-start.9 = (bf16[2,96,512]{2,1,0:T(8,128)(2,1)S(1)}, bf16[2,96,512]{2,1,0:T(8,128)(2,1)S(1)}, u32[]{:S(2)}, u32[]{:S(2)}) collective-permute-start(bf16[2,96,512]{2,1,0:T(8,128)(2,1)S(1)} %get-tuple-element.71), channel_id=1, source_target_pairs={{8,16},{16,8},{9,17},{17,9},{10,18},{18,10},{11,19},{19,11},{12,20... | collective-permute-start | bytes 589832 | tf_op jit(solution)/shard_map/ppermute | solution.py:42
  34.4 7.4 %collective-permute-start.12 = (bf16[2,48,512]{2,1,0:T(8,128)(2,1)S(1)}, bf16[2,48,512]{2,1,0:T(8,128)(2,1)S(1)}, u32[]{:S(2)}, u32[]{:S(2)}) collective-permute-start(bf16[2,48,512]{2,1,0:T(8,128)(2,1)S(1)} %get-tuple-element.76), channel_id=1, source_target_pairs={{1,2},{2,1},{3,4},{4,3},{5,6},{6,5},{7,0},{0,7},{9,10},{10,9},{11,... | collective-permute-start | bytes 294920 | tf_op jit(solution)/shard_map/ppermute | solution.py:42
  37.5 7.3 %collective-permute-start.13 = (bf16[2,48,512]{2,1,0:T(8,128)(2,1)S(1)}, bf16[2,48,512]{2,1,0:T(8,128)(2,1)S(1)}, u32[]{:S(2)}, u32[]{:S(2)}) collective-permute-start(bf16[2,48,512]{2,1,0:T(8,128)(2,1)S(1)} %get-tuple-element.77), channel_id=1, source_target_pairs={{0,1},{1,0},{2,3},{3,2},{4,5},{5,4},{6,7},{7,6},{8,9},{9,8},{10,11... | collective-permute-start | bytes 294920 | tf_op jit(solution)/shard_map/ppermute | solution.py:42

commit v3 on v1

v3 whole, which is shorter than its diff:
```python
import jax
import jax.numpy as jnp
from jax import lax
from jax.experimental import pallas as pl
from jax.experimental.pallas import tpu as pltpu
from jax.sharding import PartitionSpec as P

HEAD_DIM = 64
RADIUS = 6
SPAN = 2 * RADIUS + 1
ROWS = 8
COLS = 16
CELLS = ROWS * COLS
SIDE = ROWS * RADIUS
BAND = RADIUS * COLS
PAIR = 2 * HEAD_DIM
BASE = 336
TABLE = 512
MASKED = -1e30

OWN_AT = 0
LON_AT = CELLS
LAT_AT = LON_AT + 2 * SIDE
NEAR = LAT_AT + 2 * BAND
CORNERS = 4 * SIDE

F32 = jnp.float32
BF16 = jnp.bfloat16


def pair_exchange(value, axis, odd, wrap):
    count = lax.axis_size(axis)
    pairs = []
    for first in range(odd, count, 2):
        second = first + 1
        if second >= count and not wrap:
            continue
        second %= count
        pairs += [(first, second), (second, first)]
    return lax.ppermute(value, axis, pairs)


def is_odd(axis):
    return lax.axis_index(axis) % 2 == 1


def pick_matrix(first_col):
    shape = (SIDE, CELLS)
    place = lax.broadcasted_iota(jnp.int32, shape, 0)
    cell = lax.broadcasted_iota(jnp.int32, shape, 1)
    source = (place % ROWS) * COLS + first_col + place // ROWS
    return (cell == source).astype(BF16)


def pack_kernel(k_hbm, v_hbm, q_hbm, g_hbm, lon_odd_ref, lon_even_ref, k_ref, v_ref, q_ref, g_ref, sems):
    copies = [
        pltpu.make_async_copy(source, target, sems.at[index])
        for index, (source, target) in enumerate(((k_hbm, k_ref), (v_hbm, v_ref), (q_hbm, q_ref), (g_hbm, g_ref)))
    ]
    for copy in copies:
        copy.start()
    lon_odd = is_odd("lon")
    pick_odd = pick_matrix(jnp.where(lon_odd, COLS - RADIUS, 0))
    pick_even = pick_matrix(jnp.where(lon_odd, 0, COLS - RADIUS))
    for slot, source in ((0, k_ref), (1, v_ref)):
        copies[slot].wait()
        whole = source[...]
        lon_odd_ref[slot] = jnp.dot(pick_odd, whole, preferred_element_type=F32).astype(BF16)
        lon_even_ref[slot] = jnp.dot(pick_even, whole, preferred_element_type=F32).astype(BF16)
    copies[2].wait()
    copies[3].wait()


def lat_starts():
    lat_odd = is_odd("lat")
    even = jnp.where(lat_odd, 0, CELLS - BAND)
    return pl.multiple_of(even, 32), pl.multiple_of(CELLS - BAND - even, 32)


def rows_kernel(k_ref, v_ref, lat_even_ref, lat_odd_ref):
    for start, out in zip(lat_starts(), (lat_even_ref, lat_odd_ref)):
        out[0] = k_ref[pl.ds(start, BAND), :]
        out[1] = v_ref[pl.ds(start, BAND), :]


def bias_kernel(bias_ref, table_ref, corner_ref, line_ref):
    head = pl.program_id(0)

    @pl.when(head == 0)
    def _():
        shape = (SPAN * SPAN, TABLE)
        entry = lax.broadcasted_iota(jnp.int32, shape, 0)
        offset = BASE - lax.broadcasted_iota(jnp.int32, shape, 1)
        chosen = (offset == (entry // SPAN) * COLS + entry % SPAN).astype(F32)
        line = jnp.dot(bias_ref[...], chosen, preferred_element_type=F32, precision=lax.Precision.HIGHEST)
        offset = BASE - lax.broadcasted_iota(jnp.int32, (1, TABLE), 1)
        valid = (offset >= 0) & (offset < SPAN * COLS) & (offset % COLS < SPAN)
        line_ref[...] = jnp.where(valid, line, MASKED)

    lon_odd = is_odd("lon")
    lat_odd = is_odd("lat")
    has_north = lax.axis_index("lat") > 0
    has_south = lax.axis_index("lat") < lax.axis_size("lat") - 1
    line = jnp.broadcast_to(line_ref[pl.ds(head, 1), :], (8, TABLE))
    by_one = pltpu.roll(line, 0, 1, stride=1, stride_axis=0)
    by_row = pltpu.roll(line, 0, 1, stride=COLS, stride_axis=0)
    query_col = lax.broadcasted_iota(jnp.int32, (8, CELLS), 1) % COLS
    sub = lax.broadcasted_iota(jnp.int32, (8, CELLS), 0)

    def window(source, row, col):
        first = BASE - (COLS * row + col)
        return source[:, first : first + CELLS]

    def near(delta):
        return (delta >= 0) & (delta < SPAN)

    def put(at, values, target=table_ref):
        target[0, pl.ds(pl.multiple_of(at, 8), 8), :] = values

    def cells(at, row, row_count, there):
        for half in range(COLS // 8):
            allowed = near(RADIUS + 8 * half + sub - query_col)
            if there is not None:
                allowed = allowed & there
            for step in range(row_count):
                values = window(by_one, row + step, RADIUS + 8 * half)
                put(at + step * COLS + 8 * half, jnp.where(allowed, values, MASKED))

    def sides(at, row, first_col, there, target=table_ref):
        for step in range(RADIUS):
            allowed = near(first_col + step - query_col)
            if there is not None:
                allowed = allowed & there
            values = window(by_row, row, first_col + step)
            put(at + step * ROWS, jnp.where(allowed, values, MASKED), target)

    west, east = 0, COLS + RADIUS
    west_slot = jnp.where(lon_odd, SIDE, 0)
    east_slot = SIDE - west_slot
    cells(OWN_AT, RADIUS, ROWS, None)
    sides(LON_AT + west_slot, RADIUS, west, None)
    sides(LON_AT + east_slot, RADIUS, east, None)
    north_slot = jnp.where(lat_odd, 0, 1)
    south_slot = 1 - north_slot
    for slot, row, there in ((north_slot, 0, has_north), (south_slot, ROWS + RADIUS, has_south)):
        cells(LAT_AT + slot * BAND, row, RADIUS, there)
        first = row if row else row - (ROWS - RADIUS)
        sides(slot * 2 * SIDE + west_slot, first, west, there, corner_ref)
        sides(slot * 2 * SIDE + east_slot, first, east, there, corner_ref)


LAST = (((1,), (1,)), ((), ()))
FACTOR = HEAD_DIM ** (-0.5)


def join_kernel(lon_odd_ref, lon_even_ref, out_ref):
    out_ref[:, :SIDE] = lon_odd_ref[...]
    out_ref[:, SIDE:] = lon_even_ref[...]


def over_pairs(width, body):
    def step(pair, carry):
        body(pair, pl.ds(pl.multiple_of(pair * PAIR, PAIR), PAIR))
        return carry

    lax.fori_loop(0, width // PAIR, step, 0)


def both_heads(block):
    first_head = lax.broadcasted_iota(jnp.int32, block.shape, 1) < HEAD_DIM
    zero = jnp.zeros_like(block)
    return jnp.concatenate([jnp.where(first_head, block, zero), jnp.where(first_head, zero, block)], axis=0)


def scaled(block):
    return both_heads(block * jnp.asarray(FACTOR, BF16))


def pair_scores(keys, values, queries, grads, table_ref, pair):
    scores = lax.dot_general(keys, queries, LAST, preferred_element_type=F32)
    scores = scores + jnp.concatenate([table_ref[2 * pair], table_ref[2 * pair + 1]], axis=1)
    grad_prob = lax.dot_general(values, grads, LAST, preferred_element_type=F32)
    return scores, grad_prob


def column_sum(x):
    return jnp.sum(x, axis=0, keepdims=True)


def score_gradient(probability, grad_prob, row_dot):
    return probability.astype(BF16), (probability * (grad_prob - row_dot)).astype(BF16)


def near_kernel(
    q_ref, g_ref, k_ref, v_ref, lon_odd_ref, lon_even_ref, lat_even_ref, lat_odd_ref, table_ref,
    raised_ref, prob_ref, stats_ref,
):
    parts = (lon_odd_ref, lon_even_ref, lat_even_ref, lat_odd_ref)

    def body(pair, at):
        keys = jnp.concatenate([k_ref[:, at]] + [part[0, :, at] for part in parts], axis=0)
        values = jnp.concatenate([v_ref[:, at]] + [part[1, :, at] for part in parts], axis=0)
        queries, grads = scaled(q_ref[:, at]), both_heads(g_ref[:, at])
        scores, grad_prob = pair_scores(keys, values, queries, grads, table_ref, pair)
        largest = jnp.max(scores, axis=0, keepdims=True)
        raised = jnp.exp(scores - largest)
        raised_ref[pair] = raised
        prob_ref[pair] = grad_prob
        stats_ref[pair, 0:1] = largest
        stats_ref[pair, 1:2] = column_sum(raised)
        stats_ref[pair, 2:3] = column_sum(raised * grad_prob)

    over_pairs(q_ref.shape[1], body)


def corner_kernel(
    q_ref, g_ref, corner_even_ref, corner_odd_ref, table_ref, near_stats_ref,
    back_even_ref, back_odd_ref, weights_ref, dscore_ref, stats_ref,
):
    def body(pair, at):
        keys = jnp.concatenate([corner_even_ref[0, :, at], corner_odd_ref[0, :, at]], axis=0)
        values = jnp.concatenate([corner_even_ref[1, :, at], corner_odd_ref[1, :, at]], axis=0)
        queries, grads = scaled(q_ref[:, at]), both_heads(g_ref[:, at])
        scores, grad_prob = pair_scores(keys, values, queries, grads, table_ref, pair)
        near_largest = near_stats_ref[pair, 0:1]
        largest = jnp.maximum(near_largest, jnp.max(scores, axis=0, keepdims=True))
        raised = jnp.exp(scores - largest)
        shift = jnp.exp(near_largest - largest)
        total = near_stats_ref[pair, 1:2] * shift + column_sum(raised)
        inverse = 1.0 / total
        near_scale = shift * inverse
        row_dot = near_stats_ref[pair, 2:3] * near_scale + column_sum(raised * grad_prob) * inverse
        stats_ref[pair, 0:1] = near_scale
        stats_ref[pair, 1:2] = row_dot
        weights, dscore = score_gradient(raised * inverse, grad_prob, row_dot)
        weights_ref[pair] = weights
        dscore_ref[pair] = dscore
        for slot, coefficients, other in ((0, dscore, queries), (1, weights, grads)):
            grad = jnp.dot(coefficients, other, preferred_element_type=F32).astype(BF16)
            back_even_ref[slot, :, at] = grad[: 2 * SIDE]
            back_odd_ref[slot, :, at] = grad[2 * SIDE :]

    over_pairs(q_ref.shape[1], body)


def sides_kernel(
    q_ref, g_ref, raised_ref, prob_ref, stats_ref,
    dlon_ref, back_even_ref, back_odd_ref, weights_ref, dscore_ref,
):
    def body(pair, at):
        weights, dscore = score_gradient(
            raised_ref[pair, LON_AT:] * stats_ref[pair, 0:1], prob_ref[pair, LON_AT:], stats_ref[pair, 1:2]
        )
        weights_ref[pair] = weights
        dscore_ref[pair] = dscore
        for slot, coefficients, other in ((0, dscore, scaled(q_ref[:, at])), (1, weights, both_heads(g_ref[:, at]))):
            grad = jnp.dot(coefficients, other, preferred_element_type=F32)
            dlon_ref[slot, :, at] = grad[: 2 * SIDE]
            back_even_ref[slot, :, at] = grad[2 * SIDE : 2 * SIDE + BAND].astype(BF16)
            back_odd_ref[slot, :, at] = grad[2 * SIDE + BAND :].astype(BF16)

    over_pairs(q_ref.shape[1], body)


def own_kernel(
    q_ref, g_ref, k_ref, v_ref, lon_odd_ref, lon_even_ref, lat_even_ref, lat_odd_ref, corner_even_ref, corner_odd_ref,
    raised_ref, prob_ref, stats_ref, side_weights_ref, side_dscore_ref, corner_weights_ref, corner_dscore_ref,
    out_ref, dq_ref, own_ref,
):
    parts = (lon_odd_ref, lon_even_ref, lat_even_ref, lat_odd_ref, corner_even_ref, corner_odd_ref)

    def per_query(cells, coefficients):
        turned = jnp.dot(cells.T, coefficients, preferred_element_type=F32)
        mine = jnp.concatenate([turned[:HEAD_DIM, :CELLS], turned[HEAD_DIM:, CELLS:]], axis=0)
        return mine.T

    def body(pair, at):
        own_weights, own_dscore = score_gradient(
            raised_ref[pair, :LON_AT] * stats_ref[pair, 0:1], prob_ref[pair, :LON_AT], stats_ref[pair, 1:2]
        )
        own_ref[0, :, at] = jnp.dot(own_dscore, scaled(q_ref[:, at]), preferred_element_type=F32)
        own_ref[1, :, at] = jnp.dot(own_weights, both_heads(g_ref[:, at]), preferred_element_type=F32)
        keys = jnp.concatenate([k_ref[:, at]] + [part[0, :, at] for part in parts], axis=0)
        values = jnp.concatenate([v_ref[:, at]] + [part[1, :, at] for part in parts], axis=0)
        weights = jnp.concatenate([own_weights, side_weights_ref[pair], corner_weights_ref[pair]], axis=0)
        dscore = jnp.concatenate([own_dscore, side_dscore_ref[pair], corner_dscore_ref[pair]], axis=0)
        out_ref[:, at] = per_query(values, weights).astype(BF16)
        dq_ref[:, at] = (per_query(keys, dscore) * FACTOR).astype(BF16)

    over_pairs(q_ref.shape[1], body)


def middle_kernel(dlon_ref, back_even_ref, back_odd_ref, send_odd_ref, send_even_ref):
    for index, send in enumerate((send_odd_ref, send_even_ref)):
        piece = pl.ds(index * SIDE, SIDE)
        total = dlon_ref[:, piece] + back_even_ref[:, piece].astype(F32) + back_odd_ref[:, piece].astype(F32)
        send[...] = total.astype(BF16)


def final_kernel(own_ref, back_even_ref, back_odd_ref, side_odd_ref, side_even_ref, dk_ref, dv_ref, sum_ref):
    lon_odd = is_odd("lon")
    start_even, start_odd = lat_starts()
    shape = (CELLS, SIDE)
    cell = lax.broadcasted_iota(jnp.int32, shape, 0)
    place = lax.broadcasted_iota(jnp.int32, shape, 1)

    def spread(first_col):
        return (cell == (place % ROWS) * COLS + first_col + place // ROWS).astype(BF16)

    spread_odd = spread(jnp.where(lon_odd, COLS - RADIUS, 0))
    spread_even = spread(jnp.where(lon_odd, 0, COLS - RADIUS))
    for slot, out in ((0, dk_ref), (1, dv_ref)):
        sum_ref[...] = (
            own_ref[slot]
            + jnp.dot(spread_odd, side_odd_ref[slot], preferred_element_type=F32)
            + jnp.dot(spread_even, side_even_ref[slot], preferred_element_type=F32)
        )
        sum_ref[pl.ds(start_even, BAND), :] += back_even_ref[slot].astype(F32)
        sum_ref[pl.ds(start_odd, BAND), :] += back_odd_ref[slot].astype(F32)
        out[...] = sum_ref[...].astype(BF16)


def arr(shape, dtype):
    return jax.ShapeDtypeStruct(shape, dtype)


def call(kernel, name, operands, results, flops=0, **more):
    moved = sum(x.size * x.dtype.itemsize for x in operands)
    return pl.pallas_call(
        kernel,
        out_shape=results,
        compiler_params=pltpu.CompilerParams(vmem_limit_bytes=32 * 1024 * 1024),
        cost_estimate=pl.CostEstimate(flops=flops, bytes_accessed=moved, transcendentals=0),
        name=name,
        **more,
    )(*operands)


def shards(queries, key_cells, value_cells, grad_output, rel_bias):
    block = queries.shape
    heads = rel_bias.shape[0]
    feat = block[-1]
    pairs = feat // PAIR
    cells = arr((CELLS, feat), BF16)
    side, band, corner = (arr((2, rows, feat), BF16) for rows in (SIDE, BAND, 2 * SIDE))
    work = 2 * CELLS * feat
    barrier = lax.optimization_barrier

    arguments = [
        pltpu.with_memory_space_constraint(x.reshape(CELLS, feat), pltpu.HBM)
        for x in (key_cells, value_cells, queries, grad_output)
    ]
    lon_odd, lon_even, k, v, q, g = call(
        pack_kernel, "pack", arguments, [side, side, cells, cells, cells, cells],
        in_specs=[pl.BlockSpec(memory_space=pltpu.HBM)] * 4,
        scratch_shapes=[pltpu.SemaphoreType.DMA((4,))],
    )
    lon_odd = pair_exchange(lon_odd, "lon", 1, True)
    lon_even = pair_exchange(lon_even, "lon", 0, True)
    lat_even, lat_odd = call(rows_kernel, "rows", [k, v], [band, band])
    lat_even = pair_exchange(lat_even, "lat", 0, False)
    lat_odd = pair_exchange(lat_odd, "lat", 1, True)

    rel_bias, _ = barrier((rel_bias, q))
    table, corner_table = call(
        bias_kernel, "bias_table", [rel_bias],
        [arr((heads, NEAR, CELLS), F32), arr((heads, CORNERS, CELLS), F32)], heads * NEAR * CELLS,
        grid=(heads,),
        in_specs=[pl.BlockSpec(rel_bias.shape, lambda i: (0, 0))],
        out_specs=[
            pl.BlockSpec((1, NEAR, CELLS), lambda i: (i, 0, 0)),
            pl.BlockSpec((1, CORNERS, CELLS), lambda i: (i, 0, 0)),
        ],
        scratch_shapes=[pltpu.VMEM((heads, TABLE), F32)],
    )

    lon_odd, lon_even, table, corner_table = barrier((lon_odd, lon_even, table, corner_table))
    lon_odd, lon_even, lat_even, lat_odd = barrier((lon_odd, lon_even, lat_even, lat_odd))
    joined, = call(join_kernel, "join", [lon_odd, lon_even], [corner])
    corner_even = pair_exchange(joined, "lat", 0, False)
    corner_odd = pair_exchange(joined, "lat", 1, False)

    def scored(rows, dtype):
        return [arr((pairs, rows, 2 * CELLS), dtype)] * 2

    stats = arr((pairs, 8, 2 * CELLS), F32)
    near = [k, v, lon_odd, lon_even, lat_even, lat_odd]
    raised, prob, near_stats = call(
        near_kernel, "near", [q, g, *near, table], scored(NEAR, F32) + [stats], 4 * work * NEAR
    )
    back_corner_even, back_corner_odd, corner_weights, corner_dscore, stats = call(
        corner_kernel, "corner", [q, g, corner_even, corner_odd, corner_table, near_stats],
        [corner, corner] + scored(CORNERS, BF16) + [stats], 4 * work * CORNERS,
    )
    back_corner_even = pair_exchange(back_corner_even, "lat", 0, False)
    back_corner_odd = pair_exchange(back_corner_odd, "lat", 1, False)
    dlon, back_even, back_odd, side_weights, side_dscore = call(
        sides_kernel, "sides", [q, g, raised, prob, stats],
        [arr(corner.shape, F32), band, band] + scored(NEAR - LON_AT, BF16), 4 * work * (NEAR - LON_AT),
    )
    back_even = pair_exchange(back_even, "lat", 0, False)
    back_odd = pair_exchange(back_odd, "lat", 1, False)
    send_odd, send_even = call(middle_kernel, "middle", [dlon, back_corner_even, back_corner_odd], [side, side])
    side_odd = pair_exchange(send_odd, "lon", 1, True)
    side_even = pair_exchange(send_even, "lon", 0, True)
    out, dq, own = call(
        own_kernel, "own",
        [q, g, *near, corner_even, corner_odd, raised, prob, stats, side_weights, side_dscore, corner_weights, corner_dscore],
        [cells, cells, arr((2, CELLS, feat), F32)], 4 * work * (NEAR + CORNERS),
    )
    dk, dv = call(
        final_kernel, "final", [own, back_even, back_odd, side_odd, side_even], [cells, cells],
        scratch_shapes=[pltpu.VMEM((CELLS, feat), F32)],
    )
    return tuple(x.reshape(block) for x in (out, dq, dk, dv))


def solution(mesh):
    spec = P("lat", "lon", None)
    return jax.shard_map(
        shards, mesh=mesh, in_specs=(spec, spec, spec, spec, P()), out_specs=(spec,) * 4, check_vma=False
    )
```

time: 47.7 us -> 39.3 us (0.82)
  the two profiles are of different devices: /device:TPU:2 before, /device:TPU:0 now
where the time goes in v3:
time: 39.3 us; the launch traced here: 39.1 us
  starting transfers between devices  18.8 us (48%)
  Pallas kernels  11.6 us (30%)
  waiting for transfers between devices  7.17 us (18%)
  between operations  0.76 us (2%)
  local copies, waits for them, and re-layouts  0.7 us (2%)
    ppermute x12, starting transfers between devices, pair_exchange(): return lax.ppermute(value, axis, pairs)  18.8 us
    pallas_call x10, Pallas kernels, call(): pl.pallas_call(kernel, out_shape=results, compiler_params=pltpu.CompilerP...  11.6 us
    ppermute x12, waiting for transfers between devices, pair_exchange(): return lax.ppermute(value, axis, pairs)  7.17 us
  transfers between devices with their start and end apart: 12, of which 3 were waited for; matrix products, arithmetic and copies ran while one was open for 0% of the time, Pallas kernels for 19%

profile of v3, /device:TPU:0, one launch (start us, length us, event | category | flops | bytes accessed | tf_op | source)
XLA Modules:
  0.0 39.1 jit_solution(5250592190968084831)
XLA Ops:
  0.6 1.3 %pack.1 = (bf16[2,48,512]{2,1,0:T(8,128)(2,1)S(1)}, bf16[2,48,512]{2,1,0:T(8,128)(2,1)S(1)}, bf16[128,512]{1,0:T(8,128)(2,1)S(1)}, bf16[128,512]{1,0:T(8,128)(2,...) custom-call(bf16[128,512]{1,0:T(8,128)(2,1)} %bitcast.8, bf16[128,512]{1,0:T(8,128)(2,1)} %bitcast.9, ...), custom_call_target="tpu_custom_call" | custom-call | bytes 524288 | tf_op jit(solution)/shard_map/pack/pallas_call | solution.py:329
  2.0 0.5 %collective-permute-start.2 = (bf16[2,96,512]{2,1,0:T(8,128)(2,1)S(1)}, bf16[2,96,512]{2,1,0:T(8,128)(2,1)S(1)}, u32[]{:S(2)}, u32[]{:S(2)}) collective-permute-start(bf16[2,96,512]{2,1,0:T(8,128)(2,1)S(1)} %get-tuple-element.54), channel_id=1, source_target_pairs={{0,8},{8,0},{16,24},{24,16},{1,9},{9,1},{17,25},{25,17},{2,10},{10... | collective-permute-start | bytes 589832 | tf_op jit(solution)/shard_map/ppermute | solution.py:40
  2.5 2.6 %collective-permute-start.3 = (bf16[2,96,512]{2,1,0:T(8,128)(2,1)S(1)}, bf16[2,96,512]{2,1,0:T(8,128)(2,1)S(1)}, u32[]{:S(2)}, u32[]{:S(2)}) collective-permute-start(bf16[2,96,512]{2,1,0:T(8,128)(2,1)S(1)} %get-tuple-element.55), channel_id=1, source_target_pairs={{8,16},{16,8},{24,0},{0,24},{9,17},{17,9},{25,1},{1,25},{10,18},{1... | collective-permute-start | bytes 589832 | tf_op jit(solution)/shard_map/ppermute | solution.py:40
  5.1 4.6 %collective-permute-start = (bf16[2,48,512]{2,1,0:T(8,128)(2,1)S(1)}, bf16[2,48,512]{2,1,0:T(8,128)(2,1)S(1)}, u32[]{:S(2)}, u32[]{:S(2)}) collective-permute-start(bf16[2,48,512]{2,1,0:T(8,128)(2,1)S(1)} %get-tuple-element.47), channel_id=1, source_target_pairs={{1,2},{2,1},{3,4},{4,3},{5,6},{6,5},{7,0},{0,7},{9,10},{10,9},{11,... | collective-permute-start | bytes 294920 | tf_op jit(solution)/shard_map/ppermute | solution.py:40
  9.7 0.0 collective-permute-start.1
  9.7 0.0 copy-start
  9.7 0.7 %copy-done = f32[8,169]{1,0:T(8,128)S(1)} copy-done((f32[8,169]{1,0:T(8,128)S(1)}, f32[8,169]{1,0:T(8,128)}, u32[]{:S(2)}) %copy-start) | copy-done | bytes 5432
  10.4 2.4 %bias_table.1 = (f32[8,416,128]{2,1,0:T(8,128)S(1)}, f32[8,192,128]{2,1,0:T(8,128)S(1)}) custom-call(f32[8,169]{1,0:T(8,128)S(1)} %copy-done), custom_call_target="tpu_custom_call" | custom-call | flops 425984 | bytes 5408 | tf_op jit(solution)/shard_map/bias_table/pallas_call | solution.py:329
  12.8 0.0 collective-permute-done.lon_odd_ref
  12.8 2.0 %collective-permute-done.1.lon_even_ref = bf16[2,48,512]{2,1,0:T(8,128)(2,1)S(1)} collective-permute-done((bf16[2,48,512]{2,1,0:T(8,128)(2,1)S(1)}, bf16[2,48,512]{2,1,0:T(8,128)(2,1)S(1)}, u32[]{:S(2)}, u32[]{:S(2)}) %collective-permute-start.1) | collective-permute-done | bytes 98336 | tf_op jit(solution)/shard_map/ppermute | solution.py:40
  14.8 0.0 collective-permute-done.2.lat_even_ref
  14.8 0.0 collective-permute-done.3.lat_odd_ref
  14.8 0.7 %collective-permute-start.5 = (bf16[2,96,512]{2,1,0:T(8,128)(2,1)S(1)}, bf16[2,96,512]{2,1,0:T(8,128)(2,1)S(1)}, u32[]{:S(2)}, u32[]{:S(2)}) collective-permute-start(bf16[2,96,512]{2,1,0:T(8,128)(2,1)S(1)} %join.1), channel_id=1, source_target_pairs={{8,16},{16,8},{9,17},{17,9},{10,18},{18,10},{11,19},{19,11},{12,20... | collective-permute-start | bytes 589832 | tf_op jit(solution)/shard_map/ppermute | solution.py:40
  15.5 2.0 %collective-permute-start.4 = (bf16[2,96,512]{2,1,0:T(8,128)(2,1)S(1)}, bf16[2,96,512]{2,1,0:T(8,128)(2,1)S(1)}, u32[]{:S(2)}, u32[]{:S(2)}) collective-permute-start(bf16[2,96,512]{2,1,0:T(8,128)(2,1)S(1)} %join.1), channel_id=1, source_target_pairs={{0,8},{8,0},{16,24},{24,16},{1,9},{9,1},{17,25},{25,17},{2,10},{10... | collective-permute-start | bytes 589832 | tf_op jit(solution)/shard_map/ppermute | solution.py:40
  17.5 1.6 %near.1 = (f32[4,416,256]{2,1,0:T(8,128)S(1)}, f32[4,416,256]{2,1,0:T(8,128)S(1)}, f32[4,8,256]{2,1,0:T(8,128)S(1)}) custom-call(bf16[128,512]{1,0:T(8,128)(2,1)S(1)} %get-tuple-element.43.q_ref, bf16[128,512]{1,0:T(8,128)(2,1)S(1)} %get-tuple-element.44.g_ref, bf16[128,512]{1,0:T(8,128)(2,1)S(1)} %get-tuple-element.45.k_ref, ...), custom_call_target="tpu_custom_call" | custom-call | flops 218103808 | bytes 2818048 | tf_op jit(solution)/shard_map/near/pallas_call | solution.py:329
  19.0 0.0 collective-permute-done.5.corner_odd_ref
  19.0 0.0 collective-permute-done.4.corner_even_ref
  19.1 2.0 %corner.1 = (bf16[2,96,512]{2,1,0:T(8,128)(2,1)S(1)}, bf16[2,96,512]{2,1,0:T(8,128)(2,1)S(1)}, bf16[4,192,256]{2,1,0:T(8,128)(2,1)S(1)}, bf16[4,192,256]{2,1,0:T(8,128)(2,1)S(1)}, f32[4,8,256]{2,1,0:T(8,128)S(1)}) custom-call(bf16[128,512]{1,0:T(8,128)(2,1)S(1)} %get-tuple-element.43.q_ref, bf16[128,512]{1,0:T(8,128)(2,1)S(1)} %get-tuple-element.44.g_ref, ...), custom_call_target="tpu_custom_call" | custom-call | flops 100663296 | bytes 1474560 | tf_op jit(solution)/shard_map/corner/pallas_call | solution.py:329
  21.0 2.4 %collective-permute-start.8 = (bf16[2,96,512]{2,1,0:T(8,128)(2,1)S(1)}, bf16[2,96,512]{2,1,0:T(8,128)(2,1)S(1)}, u32[]{:S(2)}, u32[]{:S(2)}) collective-permute-start(bf16[2,96,512]{2,1,0:T(8,128)(2,1)S(1)} %get-tuple-element.76), channel_id=1, source_target_pairs={{0,8},{8,0},{16,24},{24,16},{1,9},{9,1},{17,25},{25,17},{2,10},{10... | collective-permute-start | bytes 589832 | tf_op jit(solution)/shard_map/ppermute | solution.py:40
  23.4 0.7 %collective-permute-start.9 = (bf16[2,96,512]{2,1,0:T(8,128)(2,1)S(1)}, bf16[2,96,512]{2,1,0:T(8,128)(2,1)S(1)}, u32[]{:S(2)}, u32[]{:S(2)}) collective-permute-start(bf16[2,96,512]{2,1,0:T(8,128)(2,1)S(1)} %get-tuple-element.77), channel_id=1, source_target_pairs={{8,16},{16,8},{9,17},{17,9},{10,18},{18,10},{11,19},{19,11},{12,20... | collective-permute-start | bytes 589832 | tf_op jit(solution)/shard_map/ppermute | solution.py:40
  24.1 1.0 %sides.1 = (f32[2,96,512]{2,1,0:T(8,128)S(1)}, bf16[2,96,512]{2,1,0:T(8,128)(2,1)S(1)}, bf16[2,96,512]{2,1,0:T(8,128)(2,1)S(1)}, bf16[4,288,256]{2,1,0:T(8,128)(2,1)S(1)}, bf16[4,288,256]{2,1,0:T(8,128)(2,1)S(1)}) custom-call(bf16[128,512]{1,0:T(8,128)(2,1)S(1)} %get-tuple-element.43.q_ref, bf16[128,512]{1,0:T(8,128)(2,1)S(1)} %get-tuple-element.44.g_ref, ...), custom_call_target="tpu_custom_call" | custom-call | flops 150994944 | bytes 3702784 | tf_op jit(solution)/shard_map/sides/pallas_call | solution.py:329
  25.1 2.4 %collective-permute-start.6 = (bf16[2,96,512]{2,1,0:T(8,128)(2,1)S(1)}, bf16[2,96,512]{2,1,0:T(8,128)(2,1)S(1)}, u32[]{:S(2)}, u32[]{:S(2)}) collective-permute-start(bf16[2,96,512]{2,1,0:T(8,128)(2,1)S(1)} %get-tuple-element.73), channel_id=1, source_target_pairs={{0,8},{8,0},{16,24},{24,16},{1,9},{9,1},{17,25},{25,17},{2,10},{10... | collective-permute-start | bytes 589832 | tf_op jit(solution)/shard_map/ppermute | solution.py:40
  27.5 0.7 %collective-permute-start.7 = (bf16[2,96,512]{2,1,0:T(8,128)(2,1)S(1)}, bf16[2,96,512]{2,1,0:T(8,128)(2,1)S(1)}, u32[]{:S(2)}, u32[]{:S(2)}) collective-permute-start(bf16[2,96,512]{2,1,0:T(8,128)(2,1)S(1)} %get-tuple-element.74), channel_id=1, source_target_pairs={{8,16},{16,8},{9,17},{17,9},{10,18},{18,10},{11,19},{19,11},{12,20... | collective-permute-start | bytes 589832 | tf_op jit(solution)/shard_map/ppermute | solution.py:40
  28.1 0.0 collective-permute-done.8.back_even_ref
  28.2 0.0 collective-permute-done.9.back_odd_ref
  28.2 0.1 middle.1
  28.2 2.4 %collective-permute-start.10 = (bf16[2,48,512]{2,1,0:T(8,128)(2,1)S(1)}, bf16[2,48,512]{2,1,0:T(8,128)(2,1)S(1)}, u32[]{:S(2)}, u32[]{:S(2)}) collective-permute-start(bf16[2,48,512]{2,1,0:T(8,128)(2,1)S(1)} %get-tuple-element.78), channel_id=1, source_target_pairs={{1,2},{2,1},{3,4},{4,3},{5,6},{6,5},{7,0},{0,7},{9,10},{10,9},{11,... | collective-permute-start | bytes 294920 | tf_op jit(solution)/shard_map/ppermute | solution.py:40
  30.6 0.0 collective-permute-start.11
  30.6 2.2 %own.1 = (bf16[128,512]{1,0:T(8,128)(2,1)}, bf16[128,512]{1,0:T(8,128)(2,1)}, f32[2,128,512]{2,1,0:T(8,128)S(1)}) custom-call(bf16[128,512]{1,0:T(8,128)(2,1)S(1)} %get-tuple-element.43.q_ref, bf16[128,512]{1,0:T(8,128)(2,1)S(1)} %get-tuple-element.44.g_ref, bf16[128,512]{1,0:T(8,128)(2,1)S(1)} %get-tuple-element.45.k_ref, ...), custom_call_target="tpu_custom_call" | custom-call | flops 318767104 | bytes 6914048 | tf_op jit(solution)/shard_map/own/pallas_call | solution.py:329
  32.8 0.0 collective-permute-done.6.back_even_ref
  32.8 0.0 collective-permute-done.7.back_odd_ref
  32.9 2.9 %collective-permute-done.10.side_odd_ref = bf16[2,48,512]{2,1,0:T(8,128)(2,1)S(1)} collective-permute-done((bf16[2,48,512]{2,1,0:T(8,128)(2,1)S(1)}, bf16[2,48,512]{2,1,0:T(8,128)(2,1)S(1)}, u32[]{:S(2)}, u32[]{:S(2)}) %collective-permute-start.10) | collective-permute-done | bytes 98336 | tf_op jit(solution)/shard_map/ppermute | solution.py:40
  35.7 2.3 %collective-permute-done.11.side_even_ref = bf16[2,48,512]{2,1,0:T(8,128)(2,1)S(1)} collective-permute-done((bf16[2,48,512]{2,1,0:T(8,128)(2,1)S(1)}, bf16[2,48,512]{2,1,0:T(8,128)(2,1)S(1)}, u32[]{:S(2)}, u32[]{:S(2)}) %collective-permute-start.11) | collective-permute-done | bytes 98336 | tf_op jit(solution)/shard_map/ppermute | solution.py:40
  38.0 1.0 %final.1 = (bf16[128,512]{1,0:T(8,128)(2,1)}, bf16[128,512]{1,0:T(8,128)(2,1)}) custom-call(f32[2,128,512]{2,1,0:T(8,128)S(1)} %get-tuple-element.72.own_ref, bf16[2,96,512]{2,1,0:T(8,128)(2,1)S(1)} %collective-permute-done.6.back_even_ref, bf16[2,96,512]{2,1,0:T(8,128)(2,1)S(1)} %collective-permute-done.7.back_odd_ref, ...), custom_call_target="tpu_custom_call" | custom-call | bytes 1114112 | tf_op jit(solution)/shard_map/final/pallas_call | solution.py:329
  (2 shorter events, 0.1 us)
Async XLA Ops:
  2.0 12.8 %collective-permute-start.2 = (bf16[2,96,512]{2,1,0:T(8,128)(2,1)S(1)}, bf16[2,96,512]{2,1,0:T(8,128)(2,1)S(1)}, u32[]{:S(2)}, u32[]{:S(2)}) collective-permute-start(bf16[2,96,512]{2,1,0:T(8,128)(2,1)S(1)} %get-tuple-element.54), channel_id=1, source_target_pairs={{0,8},{8,0},{16,24},{24,16},{1,9},{9,1},{17,25},{25,17},{2,10},{10... | collective-permute-start | bytes 589832 | tf_op jit(solution)/shard_map/ppermute | solution.py:40
  2.5 12.3 %collective-permute-start.3 = (bf16[2,96,512]{2,1,0:T(8,128)(2,1)S(1)}, bf16[2,96,512]{2,1,0:T(8,128)(2,1)S(1)}, u32[]{:S(2)}, u32[]{:S(2)}) collective-permute-start(bf16[2,96,512]{2,1,0:T(8,128)(2,1)S(1)} %get-tuple-element.55), channel_id=1, source_target_pairs={{8,16},{16,8},{24,0},{0,24},{9,17},{17,9},{25,1},{1,25},{10,18},{1... | collective-permute-start | bytes 589832 | tf_op jit(solution)/shard_map/ppermute | solution.py:40
  5.1 7.7 %collective-permute-start = (bf16[2,48,512]{2,1,0:T(8,128)(2,1)S(1)}, bf16[2,48,512]{2,1,0:T(8,128)(2,1)S(1)}, u32[]{:S(2)}, u32[]{:S(2)}) collective-permute-start(bf16[2,48,512]{2,1,0:T(8,128)(2,1)S(1)} %get-tuple-element.47), channel_id=1, source_target_pairs={{1,2},{2,1},{3,4},{4,3},{5,6},{6,5},{7,0},{0,7},{9,10},{10,9},{11,... | collective-permute-start | bytes 294920 | tf_op jit(solution)/shard_map/ppermute | solution.py:40
  9.7 5.1 %collective-permute-start.1 = (bf16[2,48,512]{2,1,0:T(8,128)(2,1)S(1)}, bf16[2,48,512]{2,1,0:T(8,128)(2,1)S(1)}, u32[]{:S(2)}, u32[]{:S(2)}) collective-permute-start(bf16[2,48,512]{2,1,0:T(8,128)(2,1)S(1)} %get-tuple-element.48), channel_id=1, source_target_pairs={{0,1},{1,0},{2,3},{3,2},{4,5},{5,4},{6,7},{7,6},{8,9},{9,8},{10,11... | collective-permute-start | bytes 294920 | tf_op jit(solution)/shard_map/ppermute | solution.py:40
  9.7 0.7 %copy-start = (f32[8,169]{1,0:T(8,128)S(1)}, f32[8,169]{1,0:T(8,128)}, u32[]{:S(2)}) copy-start(f32[8,169]{1,0:T(8,128)} %bias_ref) | copy-start | bytes 16228
  14.8 4.2 %collective-permute-start.5 = (bf16[2,96,512]{2,1,0:T(8,128)(2,1)S(1)}, bf16[2,96,512]{2,1,0:T(8,128)(2,1)S(1)}, u32[]{:S(2)}, u32[]{:S(2)}) collective-permute-start(bf16[2,96,512]{2,1,0:T(8,128)(2,1)S(1)} %join.1), channel_id=1, source_target_pairs={{8,16},{16,8},{9,17},{17,9},{10,18},{18,10},{11,19},{19,11},{12,20... | collective-permute-start | bytes 589832 | tf_op jit(solution)/shard_map/ppermute | solution.py:40
  15.5 3.5 %collective-permute-start.4 = (bf16[2,96,512]{2,1,0:T(8,128)(2,1)S(1)}, bf16[2,96,512]{2,1,0:T(8,128)(2,1)S(1)}, u32[]{:S(2)}, u32[]{:S(2)}) collective-permute-start(bf16[2,96,512]{2,1,0:T(8,128)(2,1)S(1)} %join.1), channel_id=1, source_target_pairs={{0,8},{8,0},{16,24},{24,16},{1,9},{9,1},{17,25},{25,17},{2,10},{10... | collective-permute-start | bytes 589832 | tf_op jit(solution)/shard_map/ppermute | solution.py:40
  21.0 7.1 %collective-permute-start.8 = (bf16[2,96,512]{2,1,0:T(8,128)(2,1)S(1)}, bf16[2,96,512]{2,1,0:T(8,128)(2,1)S(1)}, u32[]{:S(2)}, u32[]{:S(2)}) collective-permute-start(bf16[2,96,512]{2,1,0:T(8,128)(2,1)S(1)} %get-tuple-element.76), channel_id=1, source_target_pairs={{0,8},{8,0},{16,24},{24,16},{1,9},{9,1},{17,25},{25,17},{2,10},{10... | collective-permute-start | bytes 589832 | tf_op jit(solution)/shard_map/ppermute | solution.py:40
  23.4 4.8 %collective-permute-start.9 = (bf16[2,96,512]{2,1,0:T(8,128)(2,1)S(1)}, bf16[2,96,512]{2,1,0:T(8,128)(2,1)S(1)}, u32[]{:S(2)}, u32[]{:S(2)}) collective-permute-start(bf16[2,96,512]{2,1,0:T(8,128)(2,1)S(1)} %get-tuple-element.77), channel_id=1, source_target_pairs={{8,16},{16,8},{9,17},{17,9},{10,18},{18,10},{11,19},{19,11},{12,20... | collective-permute-start | bytes 589832 | tf_op jit(solution)/shard_map/ppermute | solution.py:40
  25.1 7.8 %collective-permute-start.6 = (bf16[2,96,512]{2,1,0:T(8,128)(2,1)S(1)}, bf16[2,96,512]{2,1,0:T(8,128)(2,1)S(1)}, u32[]{:S(2)}, u32[]{:S(2)}) collective-permute-start(bf16[2,96,512]{2,1,0:T(8,128)(2,1)S(1)} %get-tuple-element.73), channel_id=1, source_target_pairs={{0,8},{8,0},{16,24},{24,16},{1,9},{9,1},{17,25},{25,17},{2,10},{10... | collective-permute-start | bytes 589832 | tf_op jit(solution)/shard_map/ppermute | solution.py:40
  27.5 5.4 %collective-permute-start.7 = (bf16[2,96,512]{2,1,0:T(8,128)(2,1)S(1)}, bf16[2,96,512]{2,1,0:T(8,128)(2,1)S(1)}, u32[]{:S(2)}, u32[]{:S(2)}) collective-permute-start(bf16[2,96,512]{2,1,0:T(8,128)(2,1)S(1)} %get-tuple-element.74), channel_id=1, source_target_pairs={{8,16},{16,8},{9,17},{17,9},{10,18},{18,10},{11,19},{19,11},{12,20... | collective-permute-start | bytes 589832 | tf_op jit(solution)/shard_map/ppermute | solution.py:40
  28.2 7.5 %collective-permute-start.10 = (bf16[2,48,512]{2,1,0:T(8,128)(2,1)S(1)}, bf16[2,48,512]{2,1,0:T(8,128)(2,1)S(1)}, u32[]{:S(2)}, u32[]{:S(2)}) collective-permute-start(bf16[2,48,512]{2,1,0:T(8,128)(2,1)S(1)} %get-tuple-element.78), channel_id=1, source_target_pairs={{1,2},{2,1},{3,4},{4,3},{5,6},{6,5},{7,0},{0,7},{9,10},{10,9},{11,... | collective-permute-start | bytes 294920 | tf_op jit(solution)/shard_map/ppermute | solution.py:40
  30.6 7.4 %collective-permute-start.11 = (bf16[2,48,512]{2,1,0:T(8,128)(2,1)S(1)}, bf16[2,48,512]{2,1,0:T(8,128)(2,1)S(1)}, u32[]{:S(2)}, u32[]{:S(2)}) collective-permute-start(bf16[2,48,512]{2,1,0:T(8,128)(2,1)S(1)} %get-tuple-element.79), channel_id=1, source_target_pairs={{0,1},{1,0},{2,3},{3,2},{4,5},{5,4},{6,7},{7,6},{8,9},{9,8},{10,11... | collective-permute-start | bytes 294920 | tf_op jit(solution)/shard_map/ppermute | solution.py:40

commit v4 on v3

--- a/solution.py
+++ b/solution.py
@@ -38,6 +38,18 @@
         second %= count
         pairs += [(first, second), (second, first)]
     return lax.ppermute(value, axis, pairs)
+
+
+def odd_rows_exchange(value):
+    lats, lons = lax.axis_size("lat"), lax.axis_size("lon")
+    pairs = []
+    for lat in range(lats):
+        for lon in range(lons):
+            other = lat + 1 if lat % 2 else lat - 1
+            inside = 0 <= other < lats
+            target = (other, lon) if inside else (lat, lon ^ 1)
+            pairs.append((lat * lons + lon, target[0] * lons + target[1]))
+    return lax.ppermute(value, ("lat", "lon"), pairs)
 
 
 def is_odd(axis):
@@ -159,11 +171,8 @@
 
 
 def over_pairs(width, body):
-    def step(pair, carry):
-        body(pair, pl.ds(pl.multiple_of(pair * PAIR, PAIR), PAIR))
-        return carry
-
-    lax.fori_loop(0, width // PAIR, step, 0)
+    for pair in range(width // PAIR):
+        body(pair, pl.ds(pair * PAIR, PAIR))
 
 
 def both_heads(block):
@@ -375,10 +384,9 @@
     )
 
     lon_odd, lon_even, table, corner_table = barrier((lon_odd, lon_even, table, corner_table))
-    lon_odd, lon_even, lat_even, lat_odd = barrier((lon_odd, lon_even, lat_even, lat_odd))
     joined, = call(join_kernel, "join", [lon_odd, lon_even], [corner])
     corner_even = pair_exchange(joined, "lat", 0, False)
-    corner_odd = pair_exchange(joined, "lat", 1, False)
+    corner_odd = odd_rows_exchange(joined)
 
     def scored(rows, dtype):
         return [arr((pairs, rows, 2 * CELLS), dtype)] * 2
@@ -393,13 +401,13 @@
         [corner, corner] + scored(CORNERS, BF16) + [stats], 4 * work * CORNERS,
     )
     back_corner_even = pair_exchange(back_corner_even, "lat", 0, False)
-    back_corner_odd = pair_exchange(back_corner_odd, "lat", 1, False)
+    back_corner_odd = odd_rows_exchange(back_corner_odd)
     dlon, back_even, back_odd, side_weights, side_dscore = call(
         sides_kernel, "sides", [q, g, raised, prob, stats],
         [arr(corner.shape, F32), band, band] + scored(NEAR - LON_AT, BF16), 4 * work * (NEAR - LON_AT),
     )
     back_even = pair_exchange(back_even, "lat", 0, False)
-    back_odd = pair_exchange(back_odd, "lat", 1, False)
+    back_odd = odd_rows_exchange(back_odd)
     send_odd, send_even = call(middle_kernel, "middle", [dlon, back_corner_even, back_corner_odd], [side, side])
     side_odd = pair_exchange(send_odd, "lon", 1, True)
     side_even = pair_exchange(send_even, "lon", 0, True)

time: 39.3 us -> 36.4 us (0.926)
  starting transfers between devices: 18.8 us -> 15 us
  waiting for transfers between devices: 7.17 us -> 10.6 us
  Pallas kernels: 11.6 us -> 9.22 us
    ppermute x12 -> x9, starting transfers between devices: 18.8 us -> 10.4 us  [pair_exchange(): return lax.ppermute(value, axis, pairs)]
    ppermute x0 -> x3, waiting for transfers between devices: none -> 5.38 us  [odd_rows_exchange(): return lax.ppermute(value, ('lat', 'lon'), pairs)]
    ppermute x0 -> x3, starting transfers between devices: none -> 4.58 us  [odd_rows_exchange(): return lax.ppermute(value, ('lat', 'lon'), pairs)]
    pallas_call x10, Pallas kernels: 11.6 us -> 9.22 us  [call(): pl.pallas_call(kernel, out_shape=results, compiler_params=pltpu.CompilerP...]
    ppermute x12 -> x9, waiting for transfers between devices: 7.17 us -> 5.23 us  [pair_exchange(): return lax.ppermute(value, axis, pairs)]
  transfers between devices with their start and end apart: 12 -> 12, of which waited for: 3 -> 4; matrix products, arithmetic and copies ran while one was open for 0% -> 0% of each run, Pallas kernels for 19% -> 15%
where the time goes in v4:
time: 36.4 us; the launch traced here: 36.2 us
  starting transfers between devices  15 us (41%)
  waiting for transfers between devices  10.6 us (29%)
  Pallas kernels  9.22 us (25%)
  between operations  0.72 us (2%)
  local copies, waits for them, and re-layouts  0.7 us (2%)
    ppermute x9, starting transfers between devices, pair_exchange(): return lax.ppermute(value, axis, pairs)  10.4 us
    pallas_call x10, Pallas kernels, call(): pl.pallas_call(kernel, out_shape=results, compiler_params=pltpu.CompilerP...  9.22 us
    ppermute x3, waiting for transfers between devices, odd_rows_exchange(): return lax.ppermute(value, ('lat', 'lon'), pairs)  5.38 us
    ppermute x9, waiting for transfers between devices, pair_exchange(): return lax.ppermute(value, axis, pairs)  5.23 us
    ppermute x3, starting transfers between devices, odd_rows_exchange(): return lax.ppermute(value, ('lat', 'lon'), pairs)  4.58 us
  transfers between devices with their start and end apart: 12, of which 4 were waited for; matrix products, arithmetic and copies ran while one was open for 0% of the time, Pallas kernels for 15%

profile of v4, /device:TPU:0, one launch (start us, length us, event | category | flops | bytes accessed | tf_op | source)
XLA Modules:
  0.0 36.2 jit_solution(762726764727577855)
XLA Ops:
  0.6 1.3 %pack.1 = (bf16[2,48,512]{2,1,0:T(8,128)(2,1)S(1)}, bf16[2,48,512]{2,1,0:T(8,128)(2,1)S(1)}, bf16[128,512]{1,0:T(8,128)(2,1)S(1)}, bf16[128,512]{1,0:T(8,128)(2,...) custom-call(bf16[128,512]{1,0:T(8,128)(2,1)} %bitcast.8, bf16[128,512]{1,0:T(8,128)(2,1)} %bitcast.9, ...), custom_call_target="tpu_custom_call" | custom-call | bytes 524288 | tf_op jit(solution)/shard_map/pack/pallas_call | solution.py:338
  1.9 6.1 %collective-permute-start = (bf16[2,48,512]{2,1,0:T(8,128)(2,1)S(1)}, bf16[2,48,512]{2,1,0:T(8,128)(2,1)S(1)}, u32[]{:S(2)}, u32[]{:S(2)}) collective-permute-start(bf16[2,48,512]{2,1,0:T(8,128)(2,1)S(1)} %get-tuple-element.43), channel_id=1, source_target_pairs={{1,2},{2,1},{3,4},{4,3},{5,6},{6,5},{7,0},{0,7},{9,10},{10,9},{11,... | collective-permute-start | bytes 294920 | tf_op jit(solution)/shard_map/ppermute | solution.py:40
  8.0 0.0 collective-permute-start.1
  8.0 0.1 collective-permute-start.2
  8.1 1.6 %collective-permute-start.3 = (bf16[2,96,512]{2,1,0:T(8,128)(2,1)S(1)}, bf16[2,96,512]{2,1,0:T(8,128)(2,1)S(1)}, u32[]{:S(2)}, u32[]{:S(2)}) collective-permute-start(bf16[2,96,512]{2,1,0:T(8,128)(2,1)S(1)} %get-tuple-element.51), channel_id=1, source_target_pairs={{8,16},{16,8},{24,0},{0,24},{9,17},{17,9},{25,1},{1,25},{10,18},{1... | collective-permute-start | bytes 589832 | tf_op jit(solution)/shard_map/ppermute | solution.py:40
  9.7 0.0 copy-start
  9.7 0.7 %copy-done = f32[8,169]{1,0:T(8,128)S(1)} copy-done((f32[8,169]{1,0:T(8,128)S(1)}, f32[8,169]{1,0:T(8,128)}, u32[]{:S(2)}) %copy-start) | copy-done | bytes 5432
  10.4 2.4 %bias_table.1 = (f32[8,416,128]{2,1,0:T(8,128)S(1)}, f32[8,192,128]{2,1,0:T(8,128)S(1)}) custom-call(f32[8,169]{1,0:T(8,128)S(1)} %copy-done), custom_call_target="tpu_custom_call" | custom-call | flops 425984 | bytes 5408 | tf_op jit(solution)/shard_map/bias_table/pallas_call | solution.py:338
  12.9 0.0 collective-permute-done.lon_odd_ref
  12.9 0.0 collective-permute-done.1.lon_even_ref
  12.9 2.1 %collective-permute-start.5 = (bf16[2,96,512]{2,1,0:T(8,128)(2,1)S(1)}, bf16[2,96,512]{2,1,0:T(8,128)(2,1)S(1)}, u32[]{:S(2)}, u32[]{:S(2)}) collective-permute-start(bf16[2,96,512]{2,1,0:T(8,128)(2,1)S(1)} %join.1), channel_id=1, source_target_pairs={{0,1},{1,0},{2,3},{3,2},{4,5},{5,4},{6,7},{7,6},{8,16},{9,17},{10,... | collective-permute-start | bytes 589832 | tf_op jit(solution)/shard_map/ppermute | solution.py:52
  15.0 0.0 collective-permute-start.4
  15.0 0.0 collective-permute-done.2.lat_even_ref
  15.0 0.0 collective-permute-done.3.lat_odd_ref
  15.0 0.9 %near.1 = (f32[4,416,256]{2,1,0:T(8,128)S(1)}, f32[4,416,256]{2,1,0:T(8,128)S(1)}, f32[4,8,256]{2,1,0:T(8,128)S(1)}) custom-call(bf16[128,512]{1,0:T(8,128)(2,1)S(1)} %get-tuple-element.39.q_ref, bf16[128,512]{1,0:T(8,128)(2,1)S(1)} %get-tuple-element.40.g_ref, bf16[128,512]{1,0:T(8,128)(2,1)S(1)} %get-tuple-element.41.k_ref, ...), custom_call_target="tpu_custom_call" | custom-call | flops 218103808 | bytes 2818048 | tf_op jit(solution)/shard_map/near/pallas_call | solution.py:338
  15.9 2.8 %collective-permute-done.5.corner_odd_ref = bf16[2,96,512]{2,1,0:T(8,128)(2,1)S(1)} collective-permute-done((bf16[2,96,512]{2,1,0:T(8,128)(2,1)S(1)}, bf16[2,96,512]{2,1,0:T(8,128)(2,1)S(1)}, u32[]{:S(2)}, u32[]{:S(2)}) %collective-permute-start.5) | collective-permute-done | bytes 196640 | tf_op jit(solution)/shard_map/ppermute | solution.py:52
  18.6 0.0 collective-permute-done.4.corner_even_ref
  18.7 1.4 %corner.1 = (bf16[2,96,512]{2,1,0:T(8,128)(2,1)S(1)}, bf16[2,96,512]{2,1,0:T(8,128)(2,1)S(1)}, bf16[4,192,256]{2,1,0:T(8,128)(2,1)S(1)}, bf16[4,192,256]{2,1,0:T(8,128)(2,1)S(1)}, f32[4,8,256]{2,1,0:T(8,128)S(1)}) custom-call(bf16[128,512]{1,0:T(8,128)(2,1)S(1)} %get-tuple-element.39.q_ref, bf16[128,512]{1,0:T(8,128)(2,1)S(1)} %get-tuple-element.40.g_ref, ...), custom_call_target="tpu_custom_call" | custom-call | flops 100663296 | bytes 1474560 | tf_op jit(solution)/shard_map/corner/pallas_call | solution.py:338
  20.1 0.1 collective-permute-start.8
  20.2 2.1 %collective-permute-start.9 = (bf16[2,96,512]{2,1,0:T(8,128)(2,1)S(1)}, bf16[2,96,512]{2,1,0:T(8,128)(2,1)S(1)}, u32[]{:S(2)}, u32[]{:S(2)}) collective-permute-start(bf16[2,96,512]{2,1,0:T(8,128)(2,1)S(1)} %get-tuple-element.69), channel_id=1, source_target_pairs={{0,1},{1,0},{2,3},{3,2},{4,5},{5,4},{6,7},{7,6},{8,16},{9,17},{10,... | collective-permute-start | bytes 589832 | tf_op jit(solution)/shard_map/ppermute | solution.py:52
  22.2 0.5 %sides.1 = (f32[2,96,512]{2,1,0:T(8,128)S(1)}, bf16[2,96,512]{2,1,0:T(8,128)(2,1)S(1)}, bf16[2,96,512]{2,1,0:T(8,128)(2,1)S(1)}, bf16[4,288,256]{2,1,0:T(8,128)(2,1)S(1)}, bf16[4,288,256]{2,1,0:T(8,128)(2,1)S(1)}) custom-call(bf16[128,512]{1,0:T(8,128)(2,1)S(1)} %get-tuple-element.39.q_ref, bf16[128,512]{1,0:T(8,128)(2,1)S(1)} %get-tuple-element.40.g_ref, ...), custom_call_target="tpu_custom_call" | custom-call | flops 150994944 | bytes 3702784 | tf_op jit(solution)/shard_map/sides/pallas_call | solution.py:338
  22.8 0.1 collective-permute-start.6
  22.9 0.5 %collective-permute-start.7 = (bf16[2,96,512]{2,1,0:T(8,128)(2,1)S(1)}, bf16[2,96,512]{2,1,0:T(8,128)(2,1)S(1)}, u32[]{:S(2)}, u32[]{:S(2)}) collective-permute-start(bf16[2,96,512]{2,1,0:T(8,128)(2,1)S(1)} %get-tuple-element.66), channel_id=1, source_target_pairs={{0,1},{1,0},{2,3},{3,2},{4,5},{5,4},{6,7},{7,6},{8,16},{9,17},{10,... | collective-permute-start | bytes 589832 | tf_op jit(solution)/shard_map/ppermute | solution.py:52
  23.3 0.0 collective-permute-done.8.back_even_ref
  23.3 2.6 %collective-permute-done.9.back_odd_ref = bf16[2,96,512]{2,1,0:T(8,128)(2,1)S(1)} collective-permute-done((bf16[2,96,512]{2,1,0:T(8,128)(2,1)S(1)}, bf16[2,96,512]{2,1,0:T(8,128)(2,1)S(1)}, u32[]{:S(2)}, u32[]{:S(2)}) %collective-permute-start.9) | collective-permute-done | bytes 196640 | tf_op jit(solution)/shard_map/ppermute | solution.py:52
  25.9 0.1 middle.1
  26.0 2.5 %collective-permute-start.10 = (bf16[2,48,512]{2,1,0:T(8,128)(2,1)S(1)}, bf16[2,48,512]{2,1,0:T(8,128)(2,1)S(1)}, u32[]{:S(2)}, u32[]{:S(2)}) collective-permute-start(bf16[2,48,512]{2,1,0:T(8,128)(2,1)S(1)} %get-tuple-element.70), channel_id=1, source_target_pairs={{1,2},{2,1},{3,4},{4,3},{5,6},{6,5},{7,0},{0,7},{9,10},{10,9},{11,... | collective-permute-start | bytes 294920 | tf_op jit(solution)/shard_map/ppermute | solution.py:40
  28.5 0.0 collective-permute-start.11
  28.5 1.5 %own.1 = (bf16[128,512]{1,0:T(8,128)(2,1)}, bf16[128,512]{1,0:T(8,128)(2,1)}, f32[2,128,512]{2,1,0:T(8,128)S(1)}) custom-call(bf16[128,512]{1,0:T(8,128)(2,1)S(1)} %get-tuple-element.39.q_ref, bf16[128,512]{1,0:T(8,128)(2,1)S(1)} %get-tuple-element.40.g_ref, bf16[128,512]{1,0:T(8,128)(2,1)S(1)} %get-tuple-element.41.k_ref, ...), custom_call_target="tpu_custom_call" | custom-call | flops 318767104 | bytes 6914048 | tf_op jit(solution)/shard_map/own/pallas_call | solution.py:338
  30.0 0.0 collective-permute-done.6.back_even_ref
  30.0 0.0 collective-permute-done.7.back_odd_ref
  30.0 3.7 %collective-permute-done.10.side_odd_ref = bf16[2,48,512]{2,1,0:T(8,128)(2,1)S(1)} collective-permute-done((bf16[2,48,512]{2,1,0:T(8,128)(2,1)S(1)}, bf16[2,48,512]{2,1,0:T(8,128)(2,1)S(1)}, u32[]{:S(2)}, u32[]{:S(2)}) %collective-permute-start.10) | collective-permute-done | bytes 98336 | tf_op jit(solution)/shard_map/ppermute | solution.py:40
  33.7 1.5 %collective-permute-done.11.side_even_ref = bf16[2,48,512]{2,1,0:T(8,128)(2,1)S(1)} collective-permute-done((bf16[2,48,512]{2,1,0:T(8,128)(2,1)S(1)}, bf16[2,48,512]{2,1,0:T(8,128)(2,1)S(1)}, u32[]{:S(2)}, u32[]{:S(2)}) %collective-permute-start.11) | collective-permute-done | bytes 98336 | tf_op jit(solution)/shard_map/ppermute | solution.py:40
  35.1 1.1 %final.1 = (bf16[128,512]{1,0:T(8,128)(2,1)}, bf16[128,512]{1,0:T(8,128)(2,1)}) custom-call(f32[2,128,512]{2,1,0:T(8,128)S(1)} %get-tuple-element.64.own_ref, bf16[2,96,512]{2,1,0:T(8,128)(2,1)S(1)} %collective-permute-done.6.back_even_ref, bf16[2,96,512]{2,1,0:T(8,128)(2,1)S(1)} %collective-permute-done.7.back_odd_ref, ...), custom_call_target="tpu_custom_call" | custom-call | bytes 1114112 | tf_op jit(solution)/shard_map/final/pallas_call | solution.py:338
  (2 shorter events, 0.0 us)
Async XLA Ops:
  1.9 10.9 %collective-permute-start = (bf16[2,48,512]{2,1,0:T(8,128)(2,1)S(1)}, bf16[2,48,512]{2,1,0:T(8,128)(2,1)S(1)}, u32[]{:S(2)}, u32[]{:S(2)}) collective-permute-start(bf16[2,48,512]{2,1,0:T(8,128)(2,1)S(1)} %get-tuple-element.43), channel_id=1, source_target_pairs={{1,2},{2,1},{3,4},{4,3},{5,6},{6,5},{7,0},{0,7},{9,10},{10,9},{11,... | collective-permute-start | bytes 294920 | tf_op jit(solution)/shard_map/ppermute | solution.py:40
  8.0 4.9 %collective-permute-start.1 = (bf16[2,48,512]{2,1,0:T(8,128)(2,1)S(1)}, bf16[2,48,512]{2,1,0:T(8,128)(2,1)S(1)}, u32[]{:S(2)}, u32[]{:S(2)}) collective-permute-start(bf16[2,48,512]{2,1,0:T(8,128)(2,1)S(1)} %get-tuple-element.44), channel_id=1, source_target_pairs={{0,1},{1,0},{2,3},{3,2},{4,5},{5,4},{6,7},{7,6},{8,9},{9,8},{10,11... | collective-permute-start | bytes 294920 | tf_op jit(solution)/shard_map/ppermute | solution.py:40
  8.0 7.0 %collective-permute-start.2 = (bf16[2,96,512]{2,1,0:T(8,128)(2,1)S(1)}, bf16[2,96,512]{2,1,0:T(8,128)(2,1)S(1)}, u32[]{:S(2)}, u32[]{:S(2)}) collective-permute-start(bf16[2,96,512]{2,1,0:T(8,128)(2,1)S(1)} %get-tuple-element.50), channel_id=1, source_target_pairs={{0,8},{8,0},{16,24},{24,16},{1,9},{9,1},{17,25},{25,17},{2,10},{10... | collective-permute-start | bytes 589832 | tf_op jit(solution)/shard_map/ppermute | solution.py:40
  8.1 6.9 %collective-permute-start.3 = (bf16[2,96,512]{2,1,0:T(8,128)(2,1)S(1)}, bf16[2,96,512]{2,1,0:T(8,128)(2,1)S(1)}, u32[]{:S(2)}, u32[]{:S(2)}) collective-permute-start(bf16[2,96,512]{2,1,0:T(8,128)(2,1)S(1)} %get-tuple-element.51), channel_id=1, source_target_pairs={{8,16},{16,8},{24,0},{0,24},{9,17},{17,9},{25,1},{1,25},{10,18},{1... | collective-permute-start | bytes 589832 | tf_op jit(solution)/shard_map/ppermute | solution.py:40
  9.7 0.7 %copy-start = (f32[8,169]{1,0:T(8,128)S(1)}, f32[8,169]{1,0:T(8,128)}, u32[]{:S(2)}) copy-start(f32[8,169]{1,0:T(8,128)} %bias_ref) | copy-start | bytes 16228
  12.9 5.7 %collective-permute-start.5 = (bf16[2,96,512]{2,1,0:T(8,128)(2,1)S(1)}, bf16[2,96,512]{2,1,0:T(8,128)(2,1)S(1)}, u32[]{:S(2)}, u32[]{:S(2)}) collective-permute-start(bf16[2,96,512]{2,1,0:T(8,128)(2,1)S(1)} %join.1), channel_id=1, source_target_pairs={{0,1},{1,0},{2,3},{3,2},{4,5},{5,4},{6,7},{7,6},{8,16},{9,17},{10,... | collective-permute-start | bytes 589832 | tf_op jit(solution)/shard_map/ppermute | solution.py:52
  15.0 3.7 %collective-permute-start.4 = (bf16[2,96,512]{2,1,0:T(8,128)(2,1)S(1)}, bf16[2,96,512]{2,1,0:T(8,128)(2,1)S(1)}, u32[]{:S(2)}, u32[]{:S(2)}) collective-permute-start(bf16[2,96,512]{2,1,0:T(8,128)(2,1)S(1)} %join.1), channel_id=1, source_target_pairs={{0,8},{8,0},{16,24},{24,16},{1,9},{9,1},{17,25},{25,17},{2,10},{10... | collective-permute-start | bytes 589832 | tf_op jit(solution)/shard_map/ppermute | solution.py:40
  20.1 3.2 %collective-permute-start.8 = (bf16[2,96,512]{2,1,0:T(8,128)(2,1)S(1)}, bf16[2,96,512]{2,1,0:T(8,128)(2,1)S(1)}, u32[]{:S(2)}, u32[]{:S(2)}) collective-permute-start(bf16[2,96,512]{2,1,0:T(8,128)(2,1)S(1)} %get-tuple-element.68), channel_id=1, source_target_pairs={{0,8},{8,0},{16,24},{24,16},{1,9},{9,1},{17,25},{25,17},{2,10},{10... | collective-permute-start | bytes 589832 | tf_op jit(solution)/shard_map/ppermute | solution.py:40
  20.2 5.7 %collective-permute-start.9 = (bf16[2,96,512]{2,1,0:T(8,128)(2,1)S(1)}, bf16[2,96,512]{2,1,0:T(8,128)(2,1)S(1)}, u32[]{:S(2)}, u32[]{:S(2)}) collective-permute-start(bf16[2,96,512]{2,1,0:T(8,128)(2,1)S(1)} %get-tuple-element.69), channel_id=1, source_target_pairs={{0,1},{1,0},{2,3},{3,2},{4,5},{5,4},{6,7},{7,6},{8,16},{9,17},{10,... | collective-permute-start | bytes 589832 | tf_op jit(solution)/shard_map/ppermute | solution.py:52
  22.8 7.2 %collective-permute-start.6 = (bf16[2,96,512]{2,1,0:T(8,128)(2,1)S(1)}, bf16[2,96,512]{2,1,0:T(8,128)(2,1)S(1)}, u32[]{:S(2)}, u32[]{:S(2)}) collective-permute-start(bf16[2,96,512]{2,1,0:T(8,128)(2,1)S(1)} %get-tuple-element.65), channel_id=1, source_target_pairs={{0,8},{8,0},{16,24},{24,16},{1,9},{9,1},{17,25},{25,17},{2,10},{10... | collective-permute-start | bytes 589832 | tf_op jit(solution)/shard_map/ppermute | solution.py:40
  22.9 7.1 %collective-permute-start.7 = (bf16[2,96,512]{2,1,0:T(8,128)(2,1)S(1)}, bf16[2,96,512]{2,1,0:T(8,128)(2,1)S(1)}, u32[]{:S(2)}, u32[]{:S(2)}) collective-permute-start(bf16[2,96,512]{2,1,0:T(8,128)(2,1)S(1)} %get-tuple-element.66), channel_id=1, source_target_pairs={{0,1},{1,0},{2,3},{3,2},{4,5},{5,4},{6,7},{7,6},{8,16},{9,17},{10,... | collective-permute-start | bytes 589832 | tf_op jit(solution)/shard_map/ppermute | solution.py:52
  26.0 7.7 %collective-permute-start.10 = (bf16[2,48,512]{2,1,0:T(8,128)(2,1)S(1)}, bf16[2,48,512]{2,1,0:T(8,128)(2,1)S(1)}, u32[]{:S(2)}, u32[]{:S(2)}) collective-permute-start(bf16[2,48,512]{2,1,0:T(8,128)(2,1)S(1)} %get-tuple-element.70), channel_id=1, source_target_pairs={{1,2},{2,1},{3,4},{4,3},{5,6},{6,5},{7,0},{0,7},{9,10},{10,9},{11,... | collective-permute-start | bytes 294920 | tf_op jit(solution)/shard_map/ppermute | solution.py:40
  28.5 6.7 %collective-permute-start.11 = (bf16[2,48,512]{2,1,0:T(8,128)(2,1)S(1)}, bf16[2,48,512]{2,1,0:T(8,128)(2,1)S(1)}, u32[]{:S(2)}, u32[]{:S(2)}) collective-permute-start(bf16[2,48,512]{2,1,0:T(8,128)(2,1)S(1)} %get-tuple-element.71), channel_id=1, source_target_pairs={{0,1},{1,0},{2,3},{3,2},{4,5},{5,4},{6,7},{7,6},{8,9},{9,8},{10,11... | collective-permute-start | bytes 294920 | tf_op jit(solution)/shard_map/ppermute | solution.py:40

commit v5 on v4

--- a/solution.py
+++ b/solution.py
@@ -64,10 +64,10 @@
     return (cell == source).astype(BF16)
 
 
-def pack_kernel(k_hbm, v_hbm, q_hbm, g_hbm, lon_odd_ref, lon_even_ref, k_ref, v_ref, q_ref, g_ref, sems):
+def pack_kernel(k_hbm, v_hbm, bias_hbm, lon_odd_ref, lon_even_ref, k_ref, v_ref, bias_ref, sems):
     copies = [
         pltpu.make_async_copy(source, target, sems.at[index])
-        for index, (source, target) in enumerate(((k_hbm, k_ref), (v_hbm, v_ref), (q_hbm, q_ref), (g_hbm, g_ref)))
+        for index, (source, target) in enumerate(((k_hbm, k_ref), (v_hbm, v_ref), (bias_hbm, bias_ref)))
     ]
     for copy in copies:
         copy.start()
@@ -80,7 +80,6 @@
         lon_odd_ref[slot] = jnp.dot(pick_odd, whole, preferred_element_type=F32).astype(BF16)
         lon_even_ref[slot] = jnp.dot(pick_even, whole, preferred_element_type=F32).astype(BF16)
     copies[2].wait()
-    copies[3].wait()
 
 
 def lat_starts():
@@ -95,70 +94,78 @@
         out[1] = v_ref[pl.ds(start, BAND), :]
 
 
-def bias_kernel(bias_ref, table_ref, corner_ref, line_ref):
-    head = pl.program_id(0)
-
-    @pl.when(head == 0)
-    def _():
-        shape = (SPAN * SPAN, TABLE)
-        entry = lax.broadcasted_iota(jnp.int32, shape, 0)
-        offset = BASE - lax.broadcasted_iota(jnp.int32, shape, 1)
-        chosen = (offset == (entry // SPAN) * COLS + entry % SPAN).astype(F32)
-        line = jnp.dot(bias_ref[...], chosen, preferred_element_type=F32, precision=lax.Precision.HIGHEST)
-        offset = BASE - lax.broadcasted_iota(jnp.int32, (1, TABLE), 1)
-        valid = (offset >= 0) & (offset < SPAN * COLS) & (offset % COLS < SPAN)
-        line_ref[...] = jnp.where(valid, line, MASKED)
-
+def bias_kernel(bias_ref, q_hbm, g_hbm, table_ref, corner_ref, q_ref, g_ref, line_ref, sems):
+    copies = [
+        pltpu.make_async_copy(source, target, sems.at[index])
+        for index, (source, target) in enumerate(((q_hbm, q_ref), (g_hbm, g_ref)))
+    ]
+    for copy in copies:
+        copy.start()
     lon_odd = is_odd("lon")
     lat_odd = is_odd("lat")
     has_north = lax.axis_index("lat") > 0
     has_south = lax.axis_index("lat") < lax.axis_size("lat") - 1
-    line = jnp.broadcast_to(line_ref[pl.ds(head, 1), :], (8, TABLE))
-    by_one = pltpu.roll(line, 0, 1, stride=1, stride_axis=0)
-    by_row = pltpu.roll(line, 0, 1, stride=COLS, stride_axis=0)
+    shape = (SPAN * SPAN, TABLE)
+    entry = lax.broadcasted_iota(jnp.int32, shape, 0)
+    offset = BASE - lax.broadcasted_iota(jnp.int32, shape, 1)
+    chosen = (offset == (entry // SPAN) * COLS + entry % SPAN).astype(F32)
+    lines = jnp.dot(bias_ref[...], chosen, preferred_element_type=F32, precision=lax.Precision.HIGHEST)
+    offset = BASE - lax.broadcasted_iota(jnp.int32, (1, TABLE), 1)
+    valid = (offset >= 0) & (offset < SPAN * COLS) & (offset % COLS < SPAN)
+    line_ref[...] = jnp.where(valid, lines, MASKED)
     query_col = lax.broadcasted_iota(jnp.int32, (8, CELLS), 1) % COLS
     sub = lax.broadcasted_iota(jnp.int32, (8, CELLS), 0)
 
-    def window(source, row, col):
-        first = BASE - (COLS * row + col)
-        return source[:, first : first + CELLS]
-
     def near(delta):
         return (delta >= 0) & (delta < SPAN)
-
-    def put(at, values, target=table_ref):
-        target[0, pl.ds(pl.multiple_of(at, 8), 8), :] = values
-
-    def cells(at, row, row_count, there):
-        for half in range(COLS // 8):
-            allowed = near(RADIUS + 8 * half + sub - query_col)
-            if there is not None:
-                allowed = allowed & there
-            for step in range(row_count):
-                values = window(by_one, row + step, RADIUS + 8 * half)
-                put(at + step * COLS + 8 * half, jnp.where(allowed, values, MASKED))
-
-    def sides(at, row, first_col, there, target=table_ref):
-        for step in range(RADIUS):
-            allowed = near(first_col + step - query_col)
-            if there is not None:
-                allowed = allowed & there
-            values = window(by_row, row, first_col + step)
-            put(at + step * ROWS, jnp.where(allowed, values, MASKED), target)
 
     west, east = 0, COLS + RADIUS
     west_slot = jnp.where(lon_odd, SIDE, 0)
     east_slot = SIDE - west_slot
-    cells(OWN_AT, RADIUS, ROWS, None)
-    sides(LON_AT + west_slot, RADIUS, west, None)
-    sides(LON_AT + east_slot, RADIUS, east, None)
     north_slot = jnp.where(lat_odd, 0, 1)
     south_slot = 1 - north_slot
-    for slot, row, there in ((north_slot, 0, has_north), (south_slot, ROWS + RADIUS, has_south)):
-        cells(LAT_AT + slot * BAND, row, RADIUS, there)
-        first = row if row else row - (ROWS - RADIUS)
-        sides(slot * 2 * SIDE + west_slot, first, west, there, corner_ref)
-        sides(slot * 2 * SIDE + east_slot, first, east, there, corner_ref)
+
+    def fill(head, carry):
+        line = jnp.broadcast_to(line_ref[pl.ds(head, 1), :], (8, TABLE))
+        by_one = pltpu.roll(line, 0, 1, stride=1, stride_axis=0)
+        by_row = pltpu.roll(line, 0, 1, stride=COLS, stride_axis=0)
+
+        def window(source, row, col):
+            first = BASE - (COLS * row + col)
+            return source[:, first : first + CELLS]
+
+        def put(at, values, allowed, target):
+            target[head, pl.ds(pl.multiple_of(at, 8), 8), :] = jnp.where(allowed, values, MASKED)
+
+        def cells(at, row, row_count, there):
+            for half in range(COLS // 8):
+                allowed = near(RADIUS + 8 * half + sub - query_col)
+                if there is not None:
+                    allowed = allowed & there
+                for step in range(row_count):
+                    values = window(by_one, row + step, RADIUS + 8 * half)
+                    put(at + step * COLS + 8 * half, values, allowed, table_ref)
+
+        def sides(at, row, first_col, there, target):
+            for step in range(RADIUS):
+                allowed = near(first_col + step - query_col)
+                if there is not None:
+                    allowed = allowed & there
+                put(at + step * ROWS, window(by_row, row, first_col + step), allowed, target)
+
+        cells(OWN_AT, RADIUS, ROWS, None)
+        sides(LON_AT + west_slot, RADIUS, west, None, table_ref)
+        sides(LON_AT + east_slot, RADIUS, east, None, table_ref)
+        for slot, row, there in ((north_slot, 0, has_north), (south_slot, ROWS + RADIUS, has_south)):
+            cells(LAT_AT + slot * BAND, row, RADIUS, there)
+            first = row if row else row - (ROWS - RADIUS)
+            sides(slot * 2 * SIDE + west_slot, first, west, there, corner_ref)
+            sides(slot * 2 * SIDE + east_slot, first, east, there, corner_ref)
+        return carry
+
+    lax.fori_loop(0, bias_ref.shape[0], fill, 0)
+    for copy in copies:
+        copy.wait()
 
 
 LAST = (((1,), (1,)), ((), ()))
@@ -226,11 +233,18 @@
     q_ref, g_ref, corner_even_ref, corner_odd_ref, table_ref, near_stats_ref,
     back_even_ref, back_odd_ref, weights_ref, dscore_ref, stats_ref,
 ):
-    def body(pair, at):
+    scored = []
+
+    def score(pair, at):
         keys = jnp.concatenate([corner_even_ref[0, :, at], corner_odd_ref[0, :, at]], axis=0)
         values = jnp.concatenate([corner_even_ref[1, :, at], corner_odd_ref[1, :, at]], axis=0)
         queries, grads = scaled(q_ref[:, at]), both_heads(g_ref[:, at])
-        scores, grad_prob = pair_scores(keys, values, queries, grads, table_ref, pair)
+        scored.append((queries, grads, *pair_scores(keys, values, queries, grads, table_ref, pair)))
+
+    over_pairs(q_ref.shape[1], score)
+
+    def differentiate(pair, at):
+        queries, grads, scores, grad_prob = scored[pair]
         near_largest = near_stats_ref[pair, 0:1]
         largest = jnp.maximum(near_largest, jnp.max(scores, axis=0, keepdims=True))
         raised = jnp.exp(scores - largest)
@@ -249,7 +263,7 @@
             back_even_ref[slot, :, at] = grad[: 2 * SIDE]
             back_odd_ref[slot, :, at] = grad[2 * SIDE :]
 
-    over_pairs(q_ref.shape[1], body)
+    over_pairs(q_ref.shape[1], differentiate)
 
 
 def sides_kernel(
@@ -355,14 +369,15 @@
     work = 2 * CELLS * feat
     barrier = lax.optimization_barrier
 
-    arguments = [
-        pltpu.with_memory_space_constraint(x.reshape(CELLS, feat), pltpu.HBM)
-        for x in (key_cells, value_cells, queries, grad_output)
-    ]
-    lon_odd, lon_even, k, v, q, g = call(
-        pack_kernel, "pack", arguments, [side, side, cells, cells, cells, cells],
-        in_specs=[pl.BlockSpec(memory_space=pltpu.HBM)] * 4,
-        scratch_shapes=[pltpu.SemaphoreType.DMA((4,))],
+    def in_hbm(x):
+        return pltpu.with_memory_space_constraint(x, pltpu.HBM)
+
+    hbm, vmem = (pl.BlockSpec(memory_space=space) for space in (pltpu.HBM, pltpu.VMEM))
+    arguments = [in_hbm(x) for x in (key_cells.reshape(CELLS, feat), value_cells.reshape(CELLS, feat), rel_bias)]
+    lon_odd, lon_even, k, v, rel_bias = call(
+        pack_kernel, "pack", arguments, [side, side, cells, cells, arr(rel_bias.shape, F32)],
+        in_specs=[hbm] * 3,
+        scratch_shapes=[pltpu.SemaphoreType.DMA((3,))],
     )
     lon_odd = pair_exchange(lon_odd, "lon", 1, True)
     lon_even = pair_exchange(lon_even, "lon", 0, True)
@@ -370,17 +385,12 @@
     lat_even = pair_exchange(lat_even, "lat", 0, False)
     lat_odd = pair_exchange(lat_odd, "lat", 1, True)
 
-    rel_bias, _ = barrier((rel_bias, q))
-    table, corner_table = call(
-        bias_kernel, "bias_table", [rel_bias],
-        [arr((heads, NEAR, CELLS), F32), arr((heads, CORNERS, CELLS), F32)], heads * NEAR * CELLS,
-        grid=(heads,),
-        in_specs=[pl.BlockSpec(rel_bias.shape, lambda i: (0, 0))],
-        out_specs=[
-            pl.BlockSpec((1, NEAR, CELLS), lambda i: (i, 0, 0)),
-            pl.BlockSpec((1, CORNERS, CELLS), lambda i: (i, 0, 0)),
-        ],
-        scratch_shapes=[pltpu.VMEM((heads, TABLE), F32)],
+    table, corner_table, q, g = call(
+        bias_kernel, "bias_table",
+        [rel_bias, in_hbm(queries.reshape(CELLS, feat)), in_hbm(grad_output.reshape(CELLS, feat))],
+        [arr((heads, NEAR, CELLS), F32), arr((heads, CORNERS, CELLS), F32), cells, cells], heads * NEAR * CELLS,
+        in_specs=[vmem, hbm, hbm],
+        scratch_shapes=[pltpu.VMEM((heads, TABLE), F32), pltpu.SemaphoreType.DMA((2,))],
     )
 
     lon_odd, lon_even, table, corner_table = barrier((lon_odd, lon_even, table, corner_table))

time: 36.4 us -> 35.7 us (0.981)
  waiting for transfers between devices: 10.6 us -> 11.8 us
  Pallas kernels: 9.22 us -> 8.48 us
  local copies, waits for them, and re-layouts: 0.7 us -> 0 us
  starting transfers between devices: 15 us -> 14.6 us
    ppermute x9, waiting for transfers between devices: 5.23 us -> 6.2 us  [pair_exchange(): return lax.ppermute(value, axis, pairs)]
    pallas_call x10, Pallas kernels: 9.22 us -> 8.48 us  [call(): pl.pallas_call(kernel, out_shape=results, compiler_params=pltpu.CompilerP...]
    ppermute x3, starting transfers between devices: 4.58 us -> 3.84 us  [odd_rows_exchange(): return lax.ppermute(value, ('lat', 'lon'), pairs)]
    unnamed x2 -> x0, local copies, waits for them, and re-layouts: 0.7 us -> none
  transfers between devices with their start and end apart: 12 -> 12, of which waited for: 4 -> 6; matrix products, arithmetic and copies ran while one was open for 0% -> 0% of each run, Pallas kernels for 15% -> 15%
where the time goes in v5:
time: 35.7 us; the launch traced here: 35.5 us
  starting transfers between devices  14.6 us (41%)
  waiting for transfers between devices  11.8 us (33%)
  Pallas kernels  8.48 us (24%)
  between operations  0.72 us (2%)
    ppermute x9, starting transfers between devices, pair_exchange(): return lax.ppermute(value, axis, pairs)  10.7 us
    pallas_call x10, Pallas kernels, call(): pl.pallas_call(kernel, out_shape=results, compiler_params=pltpu.CompilerP...  8.48 us
    ppermute x9, waiting for transfers between devices, pair_exchange(): return lax.ppermute(value, axis, pairs)  6.2 us
    ppermute x3, waiting for transfers between devices, odd_rows_exchange(): return lax.ppermute(value, ('lat', 'lon'), pairs)  5.57 us
    ppermute x3, starting transfers between devices, odd_rows_exchange(): return lax.ppermute(value, ('lat', 'lon'), pairs)  3.84 us
  transfers between devices with their start and end apart: 12, of which 6 were waited for; matrix products, arithmetic and copies ran while one was open for 0% of the time, Pallas kernels for 15%

profile of v5, /device:TPU:0, one launch (start us, length us, event | category | flops | bytes accessed | tf_op | source)
XLA Modules:
  0.0 35.5 jit_solution(5193313149679521129)
XLA Ops:
  0.6 1.3 %pack.1 = (bf16[2,48,512]{2,1,0:T(8,128)(2,1)S(1)}, bf16[2,48,512]{2,1,0:T(8,128)(2,1)S(1)}, bf16[128,512]{1,0:T(8,128)(2,1)S(1)}, bf16[128,512]{1,0:T(8,128)(2,1)S(1)}, f32[8,169]{1,0:T(8,128)S(1)}) custom-call(bf16[128,512]{1,0:T(8,128)(2,1)} %bitcast.8, bf16[128,512]{1,0:T(8,128)(2,1)} %bitcast.9, f32[8,169]{1,0:T(8,128)} %bias_hbm.1), custom_call_target="tpu_custom_call" | custom-call | bytes 267552 | tf_op jit(solution)/shard_map/pack/pallas_call | solution.py:352
  1.9 6.1 %collective-permute-start = (bf16[2,48,512]{2,1,0:T(8,128)(2,1)S(1)}, bf16[2,48,512]{2,1,0:T(8,128)(2,1)S(1)}, u32[]{:S(2)}, u32[]{:S(2)}) collective-permute-start(bf16[2,48,512]{2,1,0:T(8,128)(2,1)S(1)} %get-tuple-element.44), channel_id=1, source_target_pairs={{1,2},{2,1},{3,4},{4,3},{5,6},{6,5},{7,0},{0,7},{9,10},{10,9},{11,... | collective-permute-start | bytes 294920 | tf_op jit(solution)/shard_map/ppermute | solution.py:40
  8.0 0.0 collective-permute-start.1
  8.0 0.1 collective-permute-start.2
  8.1 1.6 %collective-permute-start.3 = (bf16[2,96,512]{2,1,0:T(8,128)(2,1)S(1)}, bf16[2,96,512]{2,1,0:T(8,128)(2,1)S(1)}, u32[]{:S(2)}, u32[]{:S(2)}) collective-permute-start(bf16[2,96,512]{2,1,0:T(8,128)(2,1)S(1)} %get-tuple-element.51), channel_id=1, source_target_pairs={{8,16},{16,8},{24,0},{0,24},{9,17},{17,9},{25,1},{1,25},{10,18},{1... | collective-permute-start | bytes 589832 | tf_op jit(solution)/shard_map/ppermute | solution.py:40
  9.7 2.4 %bias_table.1 = (f32[8,416,128]{2,1,0:T(8,128)S(1)}, f32[8,192,128]{2,1,0:T(8,128)S(1)}, bf16[128,512]{1,0:T(8,128)(2,1)S(1)}, bf16[128,512]{1,0:T(8,128)(2,1)S(1)}) custom-call(f32[8,169]{1,0:T(8,128)S(1)} %get-tuple-element.39.bias_ref, bf16[128,512]{1,0:T(8,128)(2,1)} %bitcast.10, bf16[128,512]{1,0:T(8,128)(2,1)} %bitcast.11), custom_call_target="tpu_custom_call" | custom-call | flops 425984 | bytes 267552 | tf_op jit(solution)/shard_map/bias_table/pallas_call | solution.py:352
  12.1 0.0 collective-permute-done.lon_odd_ref
  12.1 0.8 %collective-permute-done.1.lon_even_ref = bf16[2,48,512]{2,1,0:T(8,128)(2,1)S(1)} collective-permute-done((bf16[2,48,512]{2,1,0:T(8,128)(2,1)S(1)}, bf16[2,48,512]{2,1,0:T(8,128)(2,1)S(1)}, u32[]{:S(2)}, u32[]{:S(2)}) %collective-permute-start.1) | collective-permute-done | bytes 98336 | tf_op jit(solution)/shard_map/ppermute | solution.py:40
  12.9 1.3 %collective-permute-start.5 = (bf16[2,96,512]{2,1,0:T(8,128)(2,1)S(1)}, bf16[2,96,512]{2,1,0:T(8,128)(2,1)S(1)}, u32[]{:S(2)}, u32[]{:S(2)}) collective-permute-start(bf16[2,96,512]{2,1,0:T(8,128)(2,1)S(1)} %join.1), channel_id=1, source_target_pairs={{0,1},{1,0},{2,3},{3,2},{4,5},{5,4},{6,7},{7,6},{8,16},{9,17},{10,... | collective-permute-start | bytes 589832 | tf_op jit(solution)/shard_map/ppermute | solution.py:52
  14.2 0.4 %collective-permute-start.4 = (bf16[2,96,512]{2,1,0:T(8,128)(2,1)S(1)}, bf16[2,96,512]{2,1,0:T(8,128)(2,1)S(1)}, u32[]{:S(2)}, u32[]{:S(2)}) collective-permute-start(bf16[2,96,512]{2,1,0:T(8,128)(2,1)S(1)} %join.1), channel_id=1, source_target_pairs={{0,8},{8,0},{16,24},{24,16},{1,9},{9,1},{17,25},{25,17},{2,10},{10... | collective-permute-start | bytes 589832 | tf_op jit(solution)/shard_map/ppermute | solution.py:40
  14.6 0.0 collective-permute-done.2.lat_even_ref
  14.6 0.2 collective-permute-done.3.lat_odd_ref
  14.8 0.9 %near.1 = (f32[4,416,256]{2,1,0:T(8,128)S(1)}, f32[4,416,256]{2,1,0:T(8,128)S(1)}, f32[4,8,256]{2,1,0:T(8,128)S(1)}) custom-call(bf16[128,512]{1,0:T(8,128)(2,1)S(1)} %get-tuple-element.40.q_ref, bf16[128,512]{1,0:T(8,128)(2,1)S(1)} %get-tuple-element.41.g_ref, bf16[128,512]{1,0:T(8,128)(2,1)S(1)} %get-tuple-element.42.k_ref, ...), custom_call_target="tpu_custom_call" | custom-call | flops 218103808 | bytes 2818048 | tf_op jit(solution)/shard_map/near/pallas_call | solution.py:352
  15.6 3.0 %collective-permute-done.5.corner_odd_ref = bf16[2,96,512]{2,1,0:T(8,128)(2,1)S(1)} collective-permute-done((bf16[2,96,512]{2,1,0:T(8,128)(2,1)S(1)}, bf16[2,96,512]{2,1,0:T(8,128)(2,1)S(1)}, u32[]{:S(2)}, u32[]{:S(2)}) %collective-permute-start.5) | collective-permute-done | bytes 196640 | tf_op jit(solution)/shard_map/ppermute | solution.py:52
  18.6 0.0 collective-permute-done.4.corner_even_ref
  18.6 0.8 %corner.1 = (bf16[2,96,512]{2,1,0:T(8,128)(2,1)S(1)}, bf16[2,96,512]{2,1,0:T(8,128)(2,1)S(1)}, bf16[4,192,256]{2,1,0:T(8,128)(2,1)S(1)}, bf16[4,192,256]{2,1,0:T(8,128)(2,1)S(1)}, f32[4,8,256]{2,1,0:T(8,128)S(1)}) custom-call(bf16[128,512]{1,0:T(8,128)(2,1)S(1)} %get-tuple-element.40.q_ref, bf16[128,512]{1,0:T(8,128)(2,1)S(1)} %get-tuple-element.41.g_ref, ...), custom_call_target="tpu_custom_call" | custom-call | flops 100663296 | bytes 1474560 | tf_op jit(solution)/shard_map/corner/pallas_call | solution.py:352
  19.4 0.1 collective-permute-start.8
  19.5 1.3 %collective-permute-start.9 = (bf16[2,96,512]{2,1,0:T(8,128)(2,1)S(1)}, bf16[2,96,512]{2,1,0:T(8,128)(2,1)S(1)}, u32[]{:S(2)}, u32[]{:S(2)}) collective-permute-start(bf16[2,96,512]{2,1,0:T(8,128)(2,1)S(1)} %get-tuple-element.69), channel_id=1, source_target_pairs={{0,1},{1,0},{2,3},{3,2},{4,5},{5,4},{6,7},{7,6},{8,16},{9,17},{10,... | collective-permute-start | bytes 589832 | tf_op jit(solution)/shard_map/ppermute | solution.py:52
  20.8 0.5 %sides.1 = (f32[2,96,512]{2,1,0:T(8,128)S(1)}, bf16[2,96,512]{2,1,0:T(8,128)(2,1)S(1)}, bf16[2,96,512]{2,1,0:T(8,128)(2,1)S(1)}, bf16[4,288,256]{2,1,0:T(8,128)(2,1)S(1)}, bf16[4,288,256]{2,1,0:T(8,128)(2,1)S(1)}) custom-call(bf16[128,512]{1,0:T(8,128)(2,1)S(1)} %get-tuple-element.40.q_ref, bf16[128,512]{1,0:T(8,128)(2,1)S(1)} %get-tuple-element.41.g_ref, ...), custom_call_target="tpu_custom_call" | custom-call | flops 150994944 | bytes 3702784 | tf_op jit(solution)/shard_map/sides/pallas_call | solution.py:352
  21.4 0.1 collective-permute-start.6
  21.5 1.2 %collective-permute-start.7 = (bf16[2,96,512]{2,1,0:T(8,128)(2,1)S(1)}, bf16[2,96,512]{2,1,0:T(8,128)(2,1)S(1)}, u32[]{:S(2)}, u32[]{:S(2)}) collective-permute-start(bf16[2,96,512]{2,1,0:T(8,128)(2,1)S(1)} %get-tuple-element.66), channel_id=1, source_target_pairs={{0,1},{1,0},{2,3},{3,2},{4,5},{5,4},{6,7},{7,6},{8,16},{9,17},{10,... | collective-permute-start | bytes 589832 | tf_op jit(solution)/shard_map/ppermute | solution.py:52
  22.7 0.0 collective-permute-done.8.back_even_ref
  22.7 2.6 %collective-permute-done.9.back_odd_ref = bf16[2,96,512]{2,1,0:T(8,128)(2,1)S(1)} collective-permute-done((bf16[2,96,512]{2,1,0:T(8,128)(2,1)S(1)}, bf16[2,96,512]{2,1,0:T(8,128)(2,1)S(1)}, u32[]{:S(2)}, u32[]{:S(2)}) %collective-permute-start.9) | collective-permute-done | bytes 196640 | tf_op jit(solution)/shard_map/ppermute | solution.py:52
  25.3 0.1 middle.1
  25.3 2.5 %collective-permute-start.10 = (bf16[2,48,512]{2,1,0:T(8,128)(2,1)S(1)}, bf16[2,48,512]{2,1,0:T(8,128)(2,1)S(1)}, u32[]{:S(2)}, u32[]{:S(2)}) collective-permute-start(bf16[2,48,512]{2,1,0:T(8,128)(2,1)S(1)} %get-tuple-element.70), channel_id=1, source_target_pairs={{1,2},{2,1},{3,4},{4,3},{5,6},{6,5},{7,0},{0,7},{9,10},{10,9},{11,... | collective-permute-start | bytes 294920 | tf_op jit(solution)/shard_map/ppermute | solution.py:40
  27.8 0.0 collective-permute-start.11
  27.8 1.5 %own.1 = (bf16[128,512]{1,0:T(8,128)(2,1)}, bf16[128,512]{1,0:T(8,128)(2,1)}, f32[2,128,512]{2,1,0:T(8,128)S(1)}) custom-call(bf16[128,512]{1,0:T(8,128)(2,1)S(1)} %get-tuple-element.40.q_ref, bf16[128,512]{1,0:T(8,128)(2,1)S(1)} %get-tuple-element.41.g_ref, bf16[128,512]{1,0:T(8,128)(2,1)S(1)} %get-tuple-element.42.k_ref, ...), custom_call_target="tpu_custom_call" | custom-call | flops 318767104 | bytes 6914048 | tf_op jit(solution)/shard_map/own/pallas_call | solution.py:352
  29.3 0.0 collective-permute-done.6.back_even_ref
  29.3 0.0 collective-permute-done.7.back_odd_ref
  29.3 3.7 %collective-permute-done.10.side_odd_ref = bf16[2,48,512]{2,1,0:T(8,128)(2,1)S(1)} collective-permute-done((bf16[2,48,512]{2,1,0:T(8,128)(2,1)S(1)}, bf16[2,48,512]{2,1,0:T(8,128)(2,1)S(1)}, u32[]{:S(2)}, u32[]{:S(2)}) %collective-permute-start.10) | collective-permute-done | bytes 98336 | tf_op jit(solution)/shard_map/ppermute | solution.py:40
  33.0 1.4 %collective-permute-done.11.side_even_ref = bf16[2,48,512]{2,1,0:T(8,128)(2,1)S(1)} collective-permute-done((bf16[2,48,512]{2,1,0:T(8,128)(2,1)S(1)}, bf16[2,48,512]{2,1,0:T(8,128)(2,1)S(1)}, u32[]{:S(2)}, u32[]{:S(2)}) %collective-permute-start.11) | collective-permute-done | bytes 98336 | tf_op jit(solution)/shard_map/ppermute | solution.py:40
  34.5 1.1 %final.1 = (bf16[128,512]{1,0:T(8,128)(2,1)}, bf16[128,512]{1,0:T(8,128)(2,1)}) custom-call(f32[2,128,512]{2,1,0:T(8,128)S(1)} %get-tuple-element.64.own_ref, bf16[2,96,512]{2,1,0:T(8,128)(2,1)S(1)} %collective-permute-done.6.back_even_ref, bf16[2,96,512]{2,1,0:T(8,128)(2,1)S(1)} %collective-permute-done.7.back_odd_ref, ...), custom_call_target="tpu_custom_call" | custom-call | bytes 1114112 | tf_op jit(solution)/shard_map/final/pallas_call | solution.py:352
  (2 shorter events, 0.0 us)
Async XLA Ops:
  1.9 10.2 %collective-permute-start = (bf16[2,48,512]{2,1,0:T(8,128)(2,1)S(1)}, bf16[2,48,512]{2,1,0:T(8,128)(2,1)S(1)}, u32[]{:S(2)}, u32[]{:S(2)}) collective-permute-start(bf16[2,48,512]{2,1,0:T(8,128)(2,1)S(1)} %get-tuple-element.44), channel_id=1, source_target_pairs={{1,2},{2,1},{3,4},{4,3},{5,6},{6,5},{7,0},{0,7},{9,10},{10,9},{11,... | collective-permute-start | bytes 294920 | tf_op jit(solution)/shard_map/ppermute | solution.py:40
  8.0 4.9 %collective-permute-start.1 = (bf16[2,48,512]{2,1,0:T(8,128)(2,1)S(1)}, bf16[2,48,512]{2,1,0:T(8,128)(2,1)S(1)}, u32[]{:S(2)}, u32[]{:S(2)}) collective-permute-start(bf16[2,48,512]{2,1,0:T(8,128)(2,1)S(1)} %get-tuple-element.45), channel_id=1, source_target_pairs={{0,1},{1,0},{2,3},{3,2},{4,5},{5,4},{6,7},{7,6},{8,9},{9,8},{10,11... | collective-permute-start | bytes 294920 | tf_op jit(solution)/shard_map/ppermute | solution.py:40
  8.0 6.6 %collective-permute-start.2 = (bf16[2,96,512]{2,1,0:T(8,128)(2,1)S(1)}, bf16[2,96,512]{2,1,0:T(8,128)(2,1)S(1)}, u32[]{:S(2)}, u32[]{:S(2)}) collective-permute-start(bf16[2,96,512]{2,1,0:T(8,128)(2,1)S(1)} %get-tuple-element.50), channel_id=1, source_target_pairs={{0,8},{8,0},{16,24},{24,16},{1,9},{9,1},{17,25},{25,17},{2,10},{10... | collective-permute-start | bytes 589832 | tf_op jit(solution)/shard_map/ppermute | solution.py:40
  8.1 6.7 %collective-permute-start.3 = (bf16[2,96,512]{2,1,0:T(8,128)(2,1)S(1)}, bf16[2,96,512]{2,1,0:T(8,128)(2,1)S(1)}, u32[]{:S(2)}, u32[]{:S(2)}) collective-permute-start(bf16[2,96,512]{2,1,0:T(8,128)(2,1)S(1)} %get-tuple-element.51), channel_id=1, source_target_pairs={{8,16},{16,8},{24,0},{0,24},{9,17},{17,9},{25,1},{1,25},{10,18},{1... | collective-permute-start | bytes 589832 | tf_op jit(solution)/shard_map/ppermute | solution.py:40
  12.9 5.7 %collective-permute-start.5 = (bf16[2,96,512]{2,1,0:T(8,128)(2,1)S(1)}, bf16[2,96,512]{2,1,0:T(8,128)(2,1)S(1)}, u32[]{:S(2)}, u32[]{:S(2)}) collective-permute-start(bf16[2,96,512]{2,1,0:T(8,128)(2,1)S(1)} %join.1), channel_id=1, source_target_pairs={{0,1},{1,0},{2,3},{3,2},{4,5},{5,4},{6,7},{7,6},{8,16},{9,17},{10,... | collective-permute-start | bytes 589832 | tf_op jit(solution)/shard_map/ppermute | solution.py:52
  14.2 4.4 %collective-permute-start.4 = (bf16[2,96,512]{2,1,0:T(8,128)(2,1)S(1)}, bf16[2,96,512]{2,1,0:T(8,128)(2,1)S(1)}, u32[]{:S(2)}, u32[]{:S(2)}) collective-permute-start(bf16[2,96,512]{2,1,0:T(8,128)(2,1)S(1)} %join.1), channel_id=1, source_target_pairs={{0,8},{8,0},{16,24},{24,16},{1,9},{9,1},{17,25},{25,17},{2,10},{10... | collective-permute-start | bytes 589832 | tf_op jit(solution)/shard_map/ppermute | solution.py:40
  19.4 3.2 %collective-permute-start.8 = (bf16[2,96,512]{2,1,0:T(8,128)(2,1)S(1)}, bf16[2,96,512]{2,1,0:T(8,128)(2,1)S(1)}, u32[]{:S(2)}, u32[]{:S(2)}) collective-permute-start(bf16[2,96,512]{2,1,0:T(8,128)(2,1)S(1)} %get-tuple-element.68), channel_id=1, source_target_pairs={{0,8},{8,0},{16,24},{24,16},{1,9},{9,1},{17,25},{25,17},{2,10},{10... | collective-permute-start | bytes 589832 | tf_op jit(solution)/shard_map/ppermute | solution.py:40
  19.5 5.7 %collective-permute-start.9 = (bf16[2,96,512]{2,1,0:T(8,128)(2,1)S(1)}, bf16[2,96,512]{2,1,0:T(8,128)(2,1)S(1)}, u32[]{:S(2)}, u32[]{:S(2)}) collective-permute-start(bf16[2,96,512]{2,1,0:T(8,128)(2,1)S(1)} %get-tuple-element.69), channel_id=1, source_target_pairs={{0,1},{1,0},{2,3},{3,2},{4,5},{5,4},{6,7},{7,6},{8,16},{9,17},{10,... | collective-permute-start | bytes 589832 | tf_op jit(solution)/shard_map/ppermute | solution.py:52
  21.4 7.9 %collective-permute-start.6 = (bf16[2,96,512]{2,1,0:T(8,128)(2,1)S(1)}, bf16[2,96,512]{2,1,0:T(8,128)(2,1)S(1)}, u32[]{:S(2)}, u32[]{:S(2)}) collective-permute-start(bf16[2,96,512]{2,1,0:T(8,128)(2,1)S(1)} %get-tuple-element.65), channel_id=1, source_target_pairs={{0,8},{8,0},{16,24},{24,16},{1,9},{9,1},{17,25},{25,17},{2,10},{10... | collective-permute-start | bytes 589832 | tf_op jit(solution)/shard_map/ppermute | solution.py:40
  21.5 7.8 %collective-permute-start.7 = (bf16[2,96,512]{2,1,0:T(8,128)(2,1)S(1)}, bf16[2,96,512]{2,1,0:T(8,128)(2,1)S(1)}, u32[]{:S(2)}, u32[]{:S(2)}) collective-permute-start(bf16[2,96,512]{2,1,0:T(8,128)(2,1)S(1)} %get-tuple-element.66), channel_id=1, source_target_pairs={{0,1},{1,0},{2,3},{3,2},{4,5},{5,4},{6,7},{7,6},{8,16},{9,17},{10,... | collective-permute-start | bytes 589832 | tf_op jit(solution)/shard_map/ppermute | solution.py:52
  25.3 7.7 %collective-permute-start.10 = (bf16[2,48,512]{2,1,0:T(8,128)(2,1)S(1)}, bf16[2,48,512]{2,1,0:T(8,128)(2,1)S(1)}, u32[]{:S(2)}, u32[]{:S(2)}) collective-permute-start(bf16[2,48,512]{2,1,0:T(8,128)(2,1)S(1)} %get-tuple-element.70), channel_id=1, source_target_pairs={{1,2},{2,1},{3,4},{4,3},{5,6},{6,5},{7,0},{0,7},{9,10},{10,9},{11,... | collective-permute-start | bytes 294920 | tf_op jit(solution)/shard_map/ppermute | solution.py:40
  27.8 6.7 %collective-permute-start.11 = (bf16[2,48,512]{2,1,0:T(8,128)(2,1)S(1)}, bf16[2,48,512]{2,1,0:T(8,128)(2,1)S(1)}, u32[]{:S(2)}, u32[]{:S(2)}) collective-permute-start(bf16[2,48,512]{2,1,0:T(8,128)(2,1)S(1)} %get-tuple-element.71), channel_id=1, source_target_pairs={{0,1},{1,0},{2,3},{3,2},{4,5},{5,4},{6,7},{7,6},{8,9},{9,8},{10,11... | collective-permute-start | bytes 294920 | tf_op jit(solution)/shard_map/ppermute | solution.py:40

commit v6 on v5

--- a/solution.py
+++ b/solution.py
@@ -1,3 +1,5 @@
+import functools
+
 import jax
 import jax.numpy as jnp
 from jax import lax
@@ -47,7 +49,7 @@
         for lon in range(lons):
             other = lat + 1 if lat % 2 else lat - 1
             inside = 0 <= other < lats
-            target = (other, lon) if inside else (lat, lon ^ 1)
+            target = (other, lon) if inside else (lat, lon ^ (1 if lons % 4 else 2))
             pairs.append((lat * lons + lon, target[0] * lons + target[1]))
     return lax.ppermute(value, ("lat", "lon"), pairs)
 
@@ -231,7 +233,7 @@
 
 def corner_kernel(
     q_ref, g_ref, corner_even_ref, corner_odd_ref, table_ref, near_stats_ref,
-    back_even_ref, back_odd_ref, weights_ref, dscore_ref, stats_ref,
+    first_even_ref, first_odd_ref, second_even_ref, second_odd_ref, weights_ref, dscore_ref, stats_ref,
 ):
     scored = []
 
@@ -260,8 +262,8 @@
         dscore_ref[pair] = dscore
         for slot, coefficients, other in ((0, dscore, queries), (1, weights, grads)):
             grad = jnp.dot(coefficients, other, preferred_element_type=F32).astype(BF16)
-            back_even_ref[slot, :, at] = grad[: 2 * SIDE]
-            back_odd_ref[slot, :, at] = grad[2 * SIDE :]
+            for index, out in enumerate((second_even_ref, first_even_ref, second_odd_ref, first_odd_ref)):
+                out[slot, :, at] = grad[index * SIDE : (index + 1) * SIDE]
 
     over_pairs(q_ref.shape[1], differentiate)
 
@@ -313,14 +315,12 @@
     over_pairs(q_ref.shape[1], body)
 
 
-def middle_kernel(dlon_ref, back_even_ref, back_odd_ref, send_odd_ref, send_even_ref):
-    for index, send in enumerate((send_odd_ref, send_even_ref)):
-        piece = pl.ds(index * SIDE, SIDE)
-        total = dlon_ref[:, piece] + back_even_ref[:, piece].astype(F32) + back_odd_ref[:, piece].astype(F32)
-        send[...] = total.astype(BF16)
-
-
-def final_kernel(own_ref, back_even_ref, back_odd_ref, side_odd_ref, side_even_ref, dk_ref, dv_ref, sum_ref):
+def middle_kernel(at, dlon_ref, back_even_ref, back_odd_ref, send_ref):
+    total = dlon_ref[:, pl.ds(at, SIDE)] + back_even_ref[...].astype(F32) + back_odd_ref[...].astype(F32)
+    send_ref[...] = total.astype(BF16)
+
+
+def final_kernel(own_ref, back_even_ref, back_odd_ref, side_even_ref, side_odd_ref, dk_ref, dv_ref, sum_ref):
     lon_odd = is_odd("lon")
     start_even, start_odd = lat_starts()
     shape = (CELLS, SIDE)
@@ -406,28 +406,33 @@
     raised, prob, near_stats = call(
         near_kernel, "near", [q, g, *near, table], scored(NEAR, F32) + [stats], 4 * work * NEAR
     )
-    back_corner_even, back_corner_odd, corner_weights, corner_dscore, stats = call(
+    first_even, first_odd, second_even, second_odd, corner_weights, corner_dscore, stats = call(
         corner_kernel, "corner", [q, g, corner_even, corner_odd, corner_table, near_stats],
-        [corner, corner] + scored(CORNERS, BF16) + [stats], 4 * work * CORNERS,
-    )
-    back_corner_even = pair_exchange(back_corner_even, "lat", 0, False)
-    back_corner_odd = odd_rows_exchange(back_corner_odd)
+        [side] * 4 + scored(CORNERS, BF16) + [stats], 4 * work * CORNERS,
+    )
+    first_even = pair_exchange(first_even, "lat", 0, False)
+    first_odd = odd_rows_exchange(first_odd)
+    second_even = pair_exchange(second_even, "lat", 0, False)
+    second_odd = odd_rows_exchange(second_odd)
     dlon, back_even, back_odd, side_weights, side_dscore = call(
         sides_kernel, "sides", [q, g, raised, prob, stats],
         [arr(corner.shape, F32), band, band] + scored(NEAR - LON_AT, BF16), 4 * work * (NEAR - LON_AT),
     )
     back_even = pair_exchange(back_even, "lat", 0, False)
     back_odd = odd_rows_exchange(back_odd)
-    send_odd, send_even = call(middle_kernel, "middle", [dlon, back_corner_even, back_corner_odd], [side, side])
-    side_odd = pair_exchange(send_odd, "lon", 1, True)
-    side_even = pair_exchange(send_even, "lon", 0, True)
+
+    def middle(at, *received):
+        return call(functools.partial(middle_kernel, at), "middle", [dlon, *received], [side])[0]
+
+    side_even = pair_exchange(middle(SIDE, first_even, first_odd), "lon", 0, True)
+    side_odd = pair_exchange(middle(0, second_even, second_odd), "lon", 1, True)
     out, dq, own = call(
         own_kernel, "own",
         [q, g, *near, corner_even, corner_odd, raised, prob, stats, side_weights, side_dscore, corner_weights, corner_dscore],
         [cells, cells, arr((2, CELLS, feat), F32)], 4 * work * (NEAR + CORNERS),
     )
     dk, dv = call(
-        final_kernel, "final", [own, back_even, back_odd, side_odd, side_even], [cells, cells],
+        final_kernel, "final", [own, back_even, back_odd, side_even, side_odd], [cells, cells],
         scratch_shapes=[pltpu.VMEM((CELLS, feat), F32)],
     )
     return tuple(x.reshape(block) for x in (out, dq, dk, dv))

time: 35.7 us -> 34.2 us (0.958)
  waiting for transfers between devices: 11.8 us -> 8.51 us
  starting transfers between devices: 14.6 us -> 16.3 us
    ppermute x9 -> x10, starting transfers between devices: 10.7 us -> 14.1 us  [pair_exchange(): return lax.ppermute(value, axis, pairs)]
    ppermute x3 -> x4, waiting for transfers between devices: 5.57 us -> 3.78 us  [odd_rows_exchange(): return lax.ppermute(value, ('lat', 'lon'), pairs)]
    ppermute x3 -> x4, starting transfers between devices: 3.84 us -> 2.18 us  [odd_rows_exchange(): return lax.ppermute(value, ('lat', 'lon'), pairs)]
    ppermute x9 -> x10, waiting for transfers between devices: 6.2 us -> 4.73 us  [pair_exchange(): return lax.ppermute(value, axis, pairs)]
    pallas_call x10 -> x11, Pallas kernels: 8.48 us -> 8.49 us  [call(): pl.pallas_call(kernel, out_shape=results, compiler_params=pltpu.CompilerP...]
  transfers between devices with their start and end apart: 12 -> 14, of which waited for: 6 -> 5; matrix products, arithmetic and copies ran while one was open for 0% -> 0% of each run, Pallas kernels for 15% -> 16%
where the time goes in v6:
time: 34.2 us; the launch traced here: 34 us
  starting transfers between devices  16.3 us (48%)
  waiting for transfers between devices  8.51 us (25%)
  Pallas kernels  8.49 us (25%)
  between operations  0.72 us (2%)
    ppermute x10, starting transfers between devices, pair_exchange(): return lax.ppermute(value, axis, pairs)  14.1 us
    pallas_call x11, Pallas kernels, call(): pl.pallas_call(kernel, out_shape=results, compiler_params=pltpu.CompilerP...  8.49 us
    ppermute x10, waiting for transfers between devices, pair_exchange(): return lax.ppermute(value, axis, pairs)  4.73 us
    ppermute x4, waiting for transfers between devices, odd_rows_exchange(): return lax.ppermute(value, ('lat', 'lon'), pairs)  3.78 us
    ppermute x4, starting transfers between devices, odd_rows_exchange(): return lax.ppermute(value, ('lat', 'lon'), pairs)  2.18 us
  transfers between devices with their start and end apart: 14, of which 5 were waited for; matrix products, arithmetic and copies ran while one was open for 0% of the time, Pallas kernels for 16%

profile of v6, /device:TPU:0, one launch (start us, length us, event | category | flops | bytes accessed | tf_op | source)
XLA Modules:
  0.0 34.0 jit_solution(5334958640405785282)
XLA Ops:
  0.6 1.3 %pack.1 = (bf16[2,48,512]{2,1,0:T(8,128)(2,1)S(1)}, bf16[2,48,512]{2,1,0:T(8,128)(2,1)S(1)}, bf16[128,512]{1,0:T(8,128)(2,1)S(1)}, bf16[128,512]{1,0:T(8,128)(2,1)S(1)}, f32[8,169]{1,0:T(8,128)S(1)}) custom-call(bf16[128,512]{1,0:T(8,128)(2,1)} %bitcast.8, bf16[128,512]{1,0:T(8,128)(2,1)} %bitcast.9, f32[8,169]{1,0:T(8,128)} %bias_hbm.1), custom_call_target="tpu_custom_call" | custom-call | bytes 267552 | tf_op jit(solution)/shard_map/pack/pallas_call | solution.py:352
  1.9 6.1 %collective-permute-start = (bf16[2,48,512]{2,1,0:T(8,128)(2,1)S(1)}, bf16[2,48,512]{2,1,0:T(8,128)(2,1)S(1)}, u32[]{:S(2)}, u32[]{:S(2)}) collective-permute-start(bf16[2,48,512]{2,1,0:T(8,128)(2,1)S(1)} %get-tuple-element.44), channel_id=1, source_target_pairs={{1,2},{2,1},{3,4},{4,3},{5,6},{6,5},{7,0},{0,7},{9,10},{10,9},{11,... | collective-permute-start | bytes 294920 | tf_op jit(solution)/shard_map/ppermute | solution.py:42
  8.0 0.0 collective-permute-start.1
  8.0 0.1 collective-permute-start.2
  8.1 1.6 %collective-permute-start.3 = (bf16[2,96,512]{2,1,0:T(8,128)(2,1)S(1)}, bf16[2,96,512]{2,1,0:T(8,128)(2,1)S(1)}, u32[]{:S(2)}, u32[]{:S(2)}) collective-permute-start(bf16[2,96,512]{2,1,0:T(8,128)(2,1)S(1)} %get-tuple-element.51), channel_id=1, source_target_pairs={{8,16},{16,8},{24,0},{0,24},{9,17},{17,9},{25,1},{1,25},{10,18},{1... | collective-permute-start | bytes 589832 | tf_op jit(solution)/shard_map/ppermute | solution.py:42
  9.7 2.4 %bias_table.1 = (f32[8,416,128]{2,1,0:T(8,128)S(1)}, f32[8,192,128]{2,1,0:T(8,128)S(1)}, bf16[128,512]{1,0:T(8,128)(2,1)S(1)}, bf16[128,512]{1,0:T(8,128)(2,1)S(1)}) custom-call(f32[8,169]{1,0:T(8,128)S(1)} %get-tuple-element.39.bias_ref, bf16[128,512]{1,0:T(8,128)(2,1)} %bitcast.10, bf16[128,512]{1,0:T(8,128)(2,1)} %bitcast.11), custom_call_target="tpu_custom_call" | custom-call | flops 425984 | bytes 267552 | tf_op jit(solution)/shard_map/bias_table/pallas_call | solution.py:352
  12.1 0.0 collective-permute-done.lon_odd_ref
  12.1 0.8 %collective-permute-done.1.lon_even_ref = bf16[2,48,512]{2,1,0:T(8,128)(2,1)S(1)} collective-permute-done((bf16[2,48,512]{2,1,0:T(8,128)(2,1)S(1)}, bf16[2,48,512]{2,1,0:T(8,128)(2,1)S(1)}, u32[]{:S(2)}, u32[]{:S(2)}) %collective-permute-start.1) | collective-permute-done | bytes 98336 | tf_op jit(solution)/shard_map/ppermute | solution.py:42
  12.9 0.1 collective-permute-start.5
  13.0 1.6 %collective-permute-start.4 = (bf16[2,96,512]{2,1,0:T(8,128)(2,1)S(1)}, bf16[2,96,512]{2,1,0:T(8,128)(2,1)S(1)}, u32[]{:S(2)}, u32[]{:S(2)}) collective-permute-start(bf16[2,96,512]{2,1,0:T(8,128)(2,1)S(1)} %join.1), channel_id=1, source_target_pairs={{0,8},{8,0},{16,24},{24,16},{1,9},{9,1},{17,25},{25,17},{2,10},{10... | collective-permute-start | bytes 589832 | tf_op jit(solution)/shard_map/ppermute | solution.py:42
  14.6 0.0 collective-permute-done.2.lat_even_ref
  14.6 0.2 collective-permute-done.3.lat_odd_ref
  14.8 0.9 %near.1 = (f32[4,416,256]{2,1,0:T(8,128)S(1)}, f32[4,416,256]{2,1,0:T(8,128)S(1)}, f32[4,8,256]{2,1,0:T(8,128)S(1)}) custom-call(bf16[128,512]{1,0:T(8,128)(2,1)S(1)} %get-tuple-element.40.q_ref, bf16[128,512]{1,0:T(8,128)(2,1)S(1)} %get-tuple-element.41.g_ref, bf16[128,512]{1,0:T(8,128)(2,1)S(1)} %get-tuple-element.42.k_ref, ...), custom_call_target="tpu_custom_call" | custom-call | flops 218103808 | bytes 2818048 | tf_op jit(solution)/shard_map/near/pallas_call | solution.py:352
  15.6 3.0 %collective-permute-done.5.corner_odd_ref = bf16[2,96,512]{2,1,0:T(8,128)(2,1)S(1)} collective-permute-done((bf16[2,96,512]{2,1,0:T(8,128)(2,1)S(1)}, bf16[2,96,512]{2,1,0:T(8,128)(2,1)S(1)}, u32[]{:S(2)}, u32[]{:S(2)}) %collective-permute-start.5) | collective-permute-done | bytes 196640 | tf_op jit(solution)/shard_map/ppermute | solution.py:54
  18.6 0.0 collective-permute-done.4.corner_even_ref
  18.6 0.8 %corner.1 = (bf16[2,48,512]{2,1,0:T(8,128)(2,1)S(1)}, bf16[2,48,512]{2,1,0:T(8,128)(2,1)S(1)}, bf16[2,48,512]{2,1,0:T(8,128)(2,1)S(1)}, bf16[2,48,512]{2,1,0:T(8...) custom-call(bf16[128,512]{1,0:T(8,128)(2,1)S(1)} %get-tuple-element.40., ...), custom_call_target="tpu_custom_call" | custom-call | flops 100663296 | bytes 1474560 | tf_op jit(solution)/shard_map/corner/pallas_call | solution.py:352
  19.4 0.1 collective-permute-start.8
  19.5 0.1 collective-permute-start.9
  19.6 1.0 %collective-permute-start.11 = (bf16[2,48,512]{2,1,0:T(8,128)(2,1)S(1)}, bf16[2,48,512]{2,1,0:T(8,128)(2,1)S(1)}, u32[]{:S(2)}, u32[]{:S(2)}) collective-permute-start(bf16[2,48,512]{2,1,0:T(8,128)(2,1)S(1)} %get-tuple-element.70), channel_id=1, source_target_pairs={{0,8},{8,0},{16,24},{24,16},{1,9},{9,1},{17,25},{25,17},{2,10},{10... | collective-permute-start | bytes 294920 | tf_op jit(solution)/shard_map/ppermute | solution.py:42
  20.6 1.0 %collective-permute-start.12 = (bf16[2,48,512]{2,1,0:T(8,128)(2,1)S(1)}, bf16[2,48,512]{2,1,0:T(8,128)(2,1)S(1)}, u32[]{:S(2)}, u32[]{:S(2)}) collective-permute-start(bf16[2,48,512]{2,1,0:T(8,128)(2,1)S(1)} %get-tuple-element.71), channel_id=1, source_target_pairs={{0,2},{1,3},{2,0},{3,1},{4,6},{5,7},{6,4},{7,5},{8,16},{9,17},{10,... | collective-permute-start | bytes 294920 | tf_op jit(solution)/shard_map/ppermute | solution.py:54
  21.6 0.5 %sides.1 = (f32[2,96,512]{2,1,0:T(8,128)S(1)}, bf16[2,96,512]{2,1,0:T(8,128)(2,1)S(1)}, bf16[2,96,512]{2,1,0:T(8,128)(2,1)S(1)}, bf16[4,288,256]{2,1,0:T(8,128)(2,1)S(1)}, bf16[4,288,256]{2,1,0:T(8,128)(2,1)S(1)}) custom-call(bf16[128,512]{1,0:T(8,128)(2,1)S(1)} %get-tuple-element.40.q_ref, bf16[128,512]{1,0:T(8,128)(2,1)S(1)} %get-tuple-element.41.g_ref, ...), custom_call_target="tpu_custom_call" | custom-call | flops 150994944 | bytes 3702784 | tf_op jit(solution)/shard_map/sides/pallas_call | solution.py:352
  22.2 0.2 collective-permute-start.6
  22.4 0.0 collective-permute-done.8.back_even_ref
  22.4 1.0 %collective-permute-start.7 = (bf16[2,96,512]{2,1,0:T(8,128)(2,1)S(1)}, bf16[2,96,512]{2,1,0:T(8,128)(2,1)S(1)}, u32[]{:S(2)}, u32[]{:S(2)}) collective-permute-start(bf16[2,96,512]{2,1,0:T(8,128)(2,1)S(1)} %get-tuple-element.66), channel_id=1, source_target_pairs={{0,2},{1,3},{2,0},{3,1},{4,6},{5,7},{6,4},{7,5},{8,16},{9,17},{10,... | collective-permute-start | bytes 589832 | tf_op jit(solution)/shard_map/ppermute | solution.py:54
  23.4 0.8 %collective-permute-done.9.back_odd_ref = bf16[2,48,512]{2,1,0:T(8,128)(2,1)S(1)} collective-permute-done((bf16[2,48,512]{2,1,0:T(8,128)(2,1)S(1)}, bf16[2,48,512]{2,1,0:T(8,128)(2,1)S(1)}, u32[]{:S(2)}, u32[]{:S(2)}) %collective-permute-start.9) | collective-permute-done | bytes 98336 | tf_op jit(solution)/shard_map/ppermute | solution.py:54
  24.2 1.3 %collective-permute-start.10 = (bf16[2,48,512]{2,1,0:T(8,128)(2,1)S(1)}, bf16[2,48,512]{2,1,0:T(8,128)(2,1)S(1)}, u32[]{:S(2)}, u32[]{:S(2)}) collective-permute-start(bf16[2,48,512]{2,1,0:T(8,128)(2,1)S(1)} %middle.2), channel_id=1, source_target_pairs={{0,1},{1,0},{2,3},{3,2},{4,5},{5,4},{6,7},{7,6},{8,9},{9,8},{10,11... | collective-permute-start | bytes 294920 | tf_op jit(solution)/shard_map/ppermute | solution.py:42
  25.6 0.0 collective-permute-done.11.back_even_ref
  25.6 0.0 collective-permute-done.12.back_odd_ref
  25.6 2.2 %collective-permute-start.13 = (bf16[2,48,512]{2,1,0:T(8,128)(2,1)S(1)}, bf16[2,48,512]{2,1,0:T(8,128)(2,1)S(1)}, u32[]{:S(2)}, u32[]{:S(2)}) collective-permute-start(bf16[2,48,512]{2,1,0:T(8,128)(2,1)S(1)} %middle.3), channel_id=1, source_target_pairs={{1,2},{2,1},{3,4},{4,3},{5,6},{6,5},{7,0},{0,7},{9,10},{10,9},{11,... | collective-permute-start | bytes 294920 | tf_op jit(solution)/shard_map/ppermute | solution.py:42
  27.8 1.5 %own.1 = (bf16[128,512]{1,0:T(8,128)(2,1)}, bf16[128,512]{1,0:T(8,128)(2,1)}, f32[2,128,512]{2,1,0:T(8,128)S(1)}) custom-call(bf16[128,512]{1,0:T(8,128)(2,1)S(1)} %get-tuple-element.40.q_ref, bf16[128,512]{1,0:T(8,128)(2,1)S(1)} %get-tuple-element.41.g_ref, bf16[128,512]{1,0:T(8,128)(2,1)S(1)} %get-tuple-element.42.k_ref, ...), custom_call_target="tpu_custom_call" | custom-call | flops 318767104 | bytes 6914048 | tf_op jit(solution)/shard_map/own/pallas_call | solution.py:352
  29.3 0.0 collective-permute-done.10.side_even_ref
  29.3 3.7 %collective-permute-done.13.side_odd_ref = bf16[2,48,512]{2,1,0:T(8,128)(2,1)S(1)} collective-permute-done((bf16[2,48,512]{2,1,0:T(8,128)(2,1)S(1)}, bf16[2,48,512]{2,1,0:T(8,128)(2,1)S(1)}, u32[]{:S(2)}, u32[]{:S(2)}) %collective-permute-start.13) | collective-permute-done | bytes 98336 | tf_op jit(solution)/shard_map/ppermute | solution.py:42
  33.0 0.0 collective-permute-done.6.back_even_ref
  33.0 0.0 collective-permute-done.7.back_odd_ref
  33.0 1.1 %final.1 = (bf16[128,512]{1,0:T(8,128)(2,1)}, bf16[128,512]{1,0:T(8,128)(2,1)}) custom-call(f32[2,128,512]{2,1,0:T(8,128)S(1)} %get-tuple-element.64.own_ref, bf16[2,96,512]{2,1,0:T(8,128)(2,1)S(1)} %collective-permute-done.6.back_even_ref, bf16[2,96,512]{2,1,0:T(8,128)(2,1)S(1)} %collective-permute-done.7.back_odd_ref, ...), custom_call_target="tpu_custom_call" | custom-call | bytes 1114112 | tf_op jit(solution)/shard_map/final/pallas_call | solution.py:352
  (4 shorter events, 0.1 us)
Async XLA Ops:
  1.9 10.2 %collective-permute-start = (bf16[2,48,512]{2,1,0:T(8,128)(2,1)S(1)}, bf16[2,48,512]{2,1,0:T(8,128)(2,1)S(1)}, u32[]{:S(2)}, u32[]{:S(2)}) collective-permute-start(bf16[2,48,512]{2,1,0:T(8,128)(2,1)S(1)} %get-tuple-element.44), channel_id=1, source_target_pairs={{1,2},{2,1},{3,4},{4,3},{5,6},{6,5},{7,0},{0,7},{9,10},{10,9},{11,... | collective-permute-start | bytes 294920 | tf_op jit(solution)/shard_map/ppermute | solution.py:42
  8.0 4.9 %collective-permute-start.1 = (bf16[2,48,512]{2,1,0:T(8,128)(2,1)S(1)}, bf16[2,48,512]{2,1,0:T(8,128)(2,1)S(1)}, u32[]{:S(2)}, u32[]{:S(2)}) collective-permute-start(bf16[2,48,512]{2,1,0:T(8,128)(2,1)S(1)} %get-tuple-element.45), channel_id=1, source_target_pairs={{0,1},{1,0},{2,3},{3,2},{4,5},{5,4},{6,7},{7,6},{8,9},{9,8},{10,11... | collective-permute-start | bytes 294920 | tf_op jit(solution)/shard_map/ppermute | solution.py:42
  8.0 6.6 %collective-permute-start.2 = (bf16[2,96,512]{2,1,0:T(8,128)(2,1)S(1)}, bf16[2,96,512]{2,1,0:T(8,128)(2,1)S(1)}, u32[]{:S(2)}, u32[]{:S(2)}) collective-permute-start(bf16[2,96,512]{2,1,0:T(8,128)(2,1)S(1)} %get-tuple-element.50), channel_id=1, source_target_pairs={{0,8},{8,0},{16,24},{24,16},{1,9},{9,1},{17,25},{25,17},{2,10},{10... | collective-permute-start | bytes 589832 | tf_op jit(solution)/shard_map/ppermute | solution.py:42
  8.1 6.7 %collective-permute-start.3 = (bf16[2,96,512]{2,1,0:T(8,128)(2,1)S(1)}, bf16[2,96,512]{2,1,0:T(8,128)(2,1)S(1)}, u32[]{:S(2)}, u32[]{:S(2)}) collective-permute-start(bf16[2,96,512]{2,1,0:T(8,128)(2,1)S(1)} %get-tuple-element.51), channel_id=1, source_target_pairs={{8,16},{16,8},{24,0},{0,24},{9,17},{17,9},{25,1},{1,25},{10,18},{1... | collective-permute-start | bytes 589832 | tf_op jit(solution)/shard_map/ppermute | solution.py:42
  12.9 5.7 %collective-permute-start.5 = (bf16[2,96,512]{2,1,0:T(8,128)(2,1)S(1)}, bf16[2,96,512]{2,1,0:T(8,128)(2,1)S(1)}, u32[]{:S(2)}, u32[]{:S(2)}) collective-permute-start(bf16[2,96,512]{2,1,0:T(8,128)(2,1)S(1)} %join.1), channel_id=1, source_target_pairs={{0,2},{1,3},{2,0},{3,1},{4,6},{5,7},{6,4},{7,5},{8,16},{9,17},{10,... | collective-permute-start | bytes 589832 | tf_op jit(solution)/shard_map/ppermute | solution.py:54
  13.0 5.7 %collective-permute-start.4 = (bf16[2,96,512]{2,1,0:T(8,128)(2,1)S(1)}, bf16[2,96,512]{2,1,0:T(8,128)(2,1)S(1)}, u32[]{:S(2)}, u32[]{:S(2)}) collective-permute-start(bf16[2,96,512]{2,1,0:T(8,128)(2,1)S(1)} %join.1), channel_id=1, source_target_pairs={{0,8},{8,0},{16,24},{24,16},{1,9},{9,1},{17,25},{25,17},{2,10},{10... | collective-permute-start | bytes 589832 | tf_op jit(solution)/shard_map/ppermute | solution.py:42
  19.4 2.9 %collective-permute-start.8 = (bf16[2,48,512]{2,1,0:T(8,128)(2,1)S(1)}, bf16[2,48,512]{2,1,0:T(8,128)(2,1)S(1)}, u32[]{:S(2)}, u32[]{:S(2)}) collective-permute-start(bf16[2,48,512]{2,1,0:T(8,128)(2,1)S(1)} %get-tuple-element.68), channel_id=1, source_target_pairs={{0,8},{8,0},{16,24},{24,16},{1,9},{9,1},{17,25},{25,17},{2,10},{10... | collective-permute-start | bytes 294920 | tf_op jit(solution)/shard_map/ppermute | solution.py:42
  19.5 4.7 %collective-permute-start.9 = (bf16[2,48,512]{2,1,0:T(8,128)(2,1)S(1)}, bf16[2,48,512]{2,1,0:T(8,128)(2,1)S(1)}, u32[]{:S(2)}, u32[]{:S(2)}) collective-permute-start(bf16[2,48,512]{2,1,0:T(8,128)(2,1)S(1)} %get-tuple-element.69), channel_id=1, source_target_pairs={{0,2},{1,3},{2,0},{3,1},{4,6},{5,7},{6,4},{7,5},{8,16},{9,17},{10,... | collective-permute-start | bytes 294920 | tf_op jit(solution)/shard_map/ppermute | solution.py:54
  19.6 6.0 %collective-permute-start.11 = (bf16[2,48,512]{2,1,0:T(8,128)(2,1)S(1)}, bf16[2,48,512]{2,1,0:T(8,128)(2,1)S(1)}, u32[]{:S(2)}, u32[]{:S(2)}) collective-permute-start(bf16[2,48,512]{2,1,0:T(8,128)(2,1)S(1)} %get-tuple-element.70), channel_id=1, source_target_pairs={{0,8},{8,0},{16,24},{24,16},{1,9},{9,1},{17,25},{25,17},{2,10},{10... | collective-permute-start | bytes 294920 | tf_op jit(solution)/shard_map/ppermute | solution.py:42
  20.6 4.9 %collective-permute-start.12 = (bf16[2,48,512]{2,1,0:T(8,128)(2,1)S(1)}, bf16[2,48,512]{2,1,0:T(8,128)(2,1)S(1)}, u32[]{:S(2)}, u32[]{:S(2)}) collective-permute-start(bf16[2,48,512]{2,1,0:T(8,128)(2,1)S(1)} %get-tuple-element.71), channel_id=1, source_target_pairs={{0,2},{1,3},{2,0},{3,1},{4,6},{5,7},{6,4},{7,5},{8,16},{9,17},{10,... | collective-permute-start | bytes 294920 | tf_op jit(solution)/shard_map/ppermute | solution.py:54
  22.2 10.8 %collective-permute-start.6 = (bf16[2,96,512]{2,1,0:T(8,128)(2,1)S(1)}, bf16[2,96,512]{2,1,0:T(8,128)(2,1)S(1)}, u32[]{:S(2)}, u32[]{:S(2)}) collective-permute-start(bf16[2,96,512]{2,1,0:T(8,128)(2,1)S(1)} %get-tuple-element.65), channel_id=1, source_target_pairs={{0,8},{8,0},{16,24},{24,16},{1,9},{9,1},{17,25},{25,17},{2,10},{10... | collective-permute-start | bytes 589832 | tf_op jit(solution)/shard_map/ppermute | solution.py:42
  22.4 10.6 %collective-permute-start.7 = (bf16[2,96,512]{2,1,0:T(8,128)(2,1)S(1)}, bf16[2,96,512]{2,1,0:T(8,128)(2,1)S(1)}, u32[]{:S(2)}, u32[]{:S(2)}) collective-permute-start(bf16[2,96,512]{2,1,0:T(8,128)(2,1)S(1)} %get-tuple-element.66), channel_id=1, source_target_pairs={{0,2},{1,3},{2,0},{3,1},{4,6},{5,7},{6,4},{7,5},{8,16},{9,17},{10,... | collective-permute-start | bytes 589832 | tf_op jit(solution)/shard_map/ppermute | solution.py:54
  24.2 5.0 %collective-permute-start.10 = (bf16[2,48,512]{2,1,0:T(8,128)(2,1)S(1)}, bf16[2,48,512]{2,1,0:T(8,128)(2,1)S(1)}, u32[]{:S(2)}, u32[]{:S(2)}) collective-permute-start(bf16[2,48,512]{2,1,0:T(8,128)(2,1)S(1)} %middle.2), channel_id=1, source_target_pairs={{0,1},{1,0},{2,3},{3,2},{4,5},{5,4},{6,7},{7,6},{8,9},{9,8},{10,11... | collective-permute-start | bytes 294920 | tf_op jit(solution)/shard_map/ppermute | solution.py:42
  25.6 7.4 %collective-permute-start.13 = (bf16[2,48,512]{2,1,0:T(8,128)(2,1)S(1)}, bf16[2,48,512]{2,1,0:T(8,128)(2,1)S(1)}, u32[]{:S(2)}, u32[]{:S(2)}) collective-permute-start(bf16[2,48,512]{2,1,0:T(8,128)(2,1)S(1)} %middle.3), channel_id=1, source_target_pairs={{1,2},{2,1},{3,4},{4,3},{5,6},{6,5},{7,0},{0,7},{9,10},{10,9},{11,... | collective-permute-start | bytes 294920 | tf_op jit(solution)/shard_map/ppermute | solution.py:42

commit v7 on v6

v7 whole, which is shorter than its diff:
```python
import functools

import jax
import jax.numpy as jnp
from jax import lax
from jax.experimental import pallas as pl
from jax.experimental.pallas import tpu as pltpu
from jax.sharding import PartitionSpec as P

HEAD_DIM = 64
RADIUS = 6
SPAN = 2 * RADIUS + 1
ROWS = 8
COLS = 16
CELLS = ROWS * COLS
SIDE = ROWS * RADIUS
BAND = RADIUS * COLS
PAIR = 2 * HEAD_DIM
BASE = 336
TABLE = 512
MASKED = -1e30

OWN_AT = 0
LON_AT = CELLS
LAT_AT = LON_AT + 2 * SIDE
NEAR = LAT_AT + 2 * BAND
AROUND = NEAR + 4 * SIDE
LANES = 128

F32 = jnp.float32
BF16 = jnp.bfloat16


def pair_exchange(value, axis, odd, wrap):
    count = lax.axis_size(axis)
    pairs = []
    for first in range(odd, count, 2):
        second = first + 1
        if second >= count and not wrap:
            continue
        second %= count
        pairs += [(first, second), (second, first)]
    return lax.ppermute(value, axis, pairs)


def odd_rows_exchange(value):
    lats, lons = lax.axis_size("lat"), lax.axis_size("lon")
    pairs = []
    for lat in range(lats):
        for lon in range(lons):
            other = lat + 1 if lat % 2 else lat - 1
            inside = 0 <= other < lats
            target = (other, lon) if inside else (lat, lon ^ (1 if lons % 4 else 2))
            pairs.append((lat * lons + lon, target[0] * lons + target[1]))
    return lax.ppermute(value, ("lat", "lon"), pairs)


def is_odd(axis):
    return lax.axis_index(axis) % 2 == 1


def pick_matrix(first_col):
    shape = (SIDE, CELLS)
    place = lax.broadcasted_iota(jnp.int32, shape, 0)
    cell = lax.broadcasted_iota(jnp.int32, shape, 1)
    source = (place % ROWS) * COLS + first_col + place // ROWS
    return (cell == source).astype(BF16)


def pack_kernel(k_hbm, v_hbm, bias_hbm, lon_odd_ref, lon_even_ref, k_ref, v_ref, bias_ref, sems):
    copies = [
        pltpu.make_async_copy(source, target, sems.at[index])
        for index, (source, target) in enumerate(((k_hbm, k_ref), (v_hbm, v_ref), (bias_hbm, bias_ref)))
    ]
    for copy in copies:
        copy.start()
    lon_odd = is_odd("lon")
    first_cols = (jnp.where(lon_odd, COLS - RADIUS, 0), jnp.where(lon_odd, 0, COLS - RADIUS))
    picks = jnp.concatenate([pick_matrix(first_col) for first_col in first_cols], axis=0)
    for slot, source in ((0, k_ref), (1, v_ref)):
        copies[slot].wait()
        both = jnp.dot(picks, source[...], preferred_element_type=F32).astype(BF16)
        lon_odd_ref[slot] = both[:SIDE]
        lon_even_ref[slot] = both[SIDE:]
    copies[2].wait()


def lat_starts():
    lat_odd = is_odd("lat")
    even = jnp.where(lat_odd, 0, CELLS - BAND)
    return pl.multiple_of(even, 32), pl.multiple_of(CELLS - BAND - even, 32)


def rows_kernel(k_ref, v_ref, lat_even_ref, lat_odd_ref):
    for start, out in zip(lat_starts(), (lat_even_ref, lat_odd_ref)):
        out[0] = k_ref[pl.ds(start, BAND), :]
        out[1] = v_ref[pl.ds(start, BAND), :]


def bias_lines(bias_ref, line_ref):
    offset = BASE - lax.broadcasted_iota(jnp.int32, (1, TABLE), 1)
    row, col = offset // COLS, offset % COLS
    valid = (offset >= 0) & (row < SPAN) & (col < SPAN)
    entry = lax.broadcasted_iota(jnp.int32, (SPAN * SPAN, TABLE), 0)
    chosen = jnp.where(entry == jnp.where(valid, row * SPAN + col, -1), 1.0, 0.0).astype(BF16)
    rest = bias_ref[...]
    total = jnp.zeros((rest.shape[0], TABLE), F32)
    for _ in range(3):
        part = rest.astype(BF16)
        total = total + jnp.dot(part, chosen, preferred_element_type=F32)
        rest = rest - part.astype(F32)
    line_ref[...] = jnp.where(valid, total, MASKED)


def spread_rows(line_ref, spread_ref):
    heads = line_ref.shape[0]
    lines = [jnp.broadcast_to(line_ref[head : head + 1], (8, TABLE)) for head in range(heads)]
    x = jnp.concatenate(lines, axis=0)
    sub = lax.broadcasted_iota(jnp.int32, x.shape, 0)
    for index, stride in enumerate((1, COLS)):
        turned = x
        for bit in (1, 2, 4):
            turned = jnp.where((sub & bit) != 0, pltpu.roll(turned, bit * stride, 1), turned)
        for head in range(heads):
            spread_ref[index, head] = turned[8 * head : 8 * head + 8]


def windows(source, col, rows):
    firsts = [BASE - (COLS * row + col) for row in rows]
    turn = firsts[0] % LANES
    turned = pltpu.roll(source, TABLE - turn, 1) if turn else source
    return [turned[:, first - turn : first - turn + CELLS] for first in firsts]


def near(delta, there=None):
    allowed = (delta >= 0) & (delta < SPAN)
    return allowed if there is None else allowed & there


def places():
    west_slot = jnp.where(is_odd("lon"), SIDE, 0)
    north_slot = jnp.where(is_odd("lat"), 0, 1)
    has_north = lax.axis_index("lat") > 0
    has_south = lax.axis_index("lat") < lax.axis_size("lat") - 1
    sides = ((0, west_slot), (COLS + RADIUS, SIDE - west_slot))
    own_col = lax.broadcasted_iota(jnp.int32, (8, CELLS), 1) % COLS
    sub = lax.broadcasted_iota(jnp.int32, (8, CELLS), 0)
    return sides, north_slot, 1 - north_slot, has_north, has_south, own_col, sub


def bias_kernel(bias_ref, q_hbm, g_hbm, table_ref, q_ref, g_ref, line_ref, spread_ref, sems):
    copies = [
        pltpu.make_async_copy(source, target, sems.at[index])
        for index, (source, target) in enumerate(((q_hbm, q_ref), (g_hbm, g_ref)))
    ]
    for copy in copies:
        copy.start()
    bias_lines(bias_ref, line_ref)
    spread_rows(line_ref, spread_ref)
    sides, north_slot, south_slot, has_north, has_south, own_col, sub = places()

    def fill(head, carry):
        def put(at, values, allowed):
            table_ref[head, pl.ds(pl.multiple_of(at, 8), 8), :] = jnp.where(allowed, values, MASKED)

        by_one = spread_ref[0, head]
        for half in range(COLS // 8):
            delta = RADIUS + 8 * half + sub - own_col
            own, north, south = near(delta), near(delta, has_north), near(delta, has_south)
            for step in range(8):
                rows = [row for row in (step, step + 8, step + 16) if row < 2 * RADIUS + ROWS]
                for row, values in zip(rows, windows(by_one, RADIUS + 8 * half, rows)):
                    if row < RADIUS:
                        put(LAT_AT + north_slot * BAND + row * COLS + 8 * half, values, north)
                    elif row < RADIUS + ROWS:
                        put(OWN_AT + (row - RADIUS) * COLS + 8 * half, values, own)
                    else:
                        put(LAT_AT + south_slot * BAND + (row - RADIUS - ROWS) * COLS + 8 * half, values, south)
        by_row = spread_ref[1, head]
        rows = (RADIUS - ROWS, RADIUS, RADIUS + ROWS)
        for first_col, lon_slot in sides:
            for step in range(RADIUS):
                delta = first_col + step - own_col
                above, beside, below = windows(by_row, first_col + step, rows)
                at = lon_slot + step * ROWS
                put(LON_AT + at, beside, near(delta))
                put(NEAR + north_slot * 2 * SIDE + at, above, near(delta, has_north))
                put(NEAR + south_slot * 2 * SIDE + at, below, near(delta, has_south))
        return carry

    lax.fori_loop(0, bias_ref.shape[0], fill, 0, unroll=8)
    for copy in copies:
        copy.wait()


def band_bias_kernel(bias_ref, after_ref, table_ref, line_ref, spread_ref):
    del after_ref
    bias_lines(bias_ref, line_ref)
    spread_rows(line_ref, spread_ref)
    sides, north_slot, south_slot, has_north, has_south, own_col, sub = places()
    lane = lax.broadcasted_iota(jnp.int32, (8, CELLS), 1)
    bands = ((north_slot, RADIUS, has_north & (lane < BAND)), (south_slot, -ROWS, has_south & (lane < BAND)))

    def fill(head, carry):
        def put(slot, at, values, allowed):
            table_ref[slot, head, pl.ds(pl.multiple_of(at, 8), 8), :] = jnp.where(allowed, values, MASKED)

        by_one = spread_ref[0, head]
        for half in range(COLS // 8):
            delta = RADIUS + 8 * half + sub - own_col
            masks = [near(delta, there) for _, _, there in bands]
            for step in range(ROWS):
                rows = [next(row for row in range(ROWS) if (RADIUS + row + shift - step) % 8 == 0) for _, shift, _ in bands]
                found = windows(by_one, RADIUS + 8 * half, [RADIUS + row + band[1] for row, band in zip(rows, bands)])
                for row, band, mask, values in zip(rows, bands, masks, found):
                    put(band[0], OWN_AT + row * COLS + 8 * half, values, mask)
        by_row = spread_ref[1, head]
        for slot, shift, there in bands:
            for first_col, lon_slot in sides:
                for step in range(RADIUS):
                    (values,) = windows(by_row, first_col + step, (RADIUS + shift,))
                    put(slot, LON_AT + lon_slot + step * ROWS, values, near(first_col + step - own_col, there))
        return carry

    lax.fori_loop(0, bias_ref.shape[0], fill, 0, unroll=8)


LAST = (((1,), (1,)), ((), ()))
FACTOR = HEAD_DIM ** (-0.5)


def join_kernel(lon_odd_ref, lon_even_ref, out_ref):
    out_ref[:, :SIDE] = lon_odd_ref[...]
    out_ref[:, SIDE:] = lon_even_ref[...]


def over_pairs(width, body):
    return [body(pair, pl.ds(pair * PAIR, PAIR)) for pair in range(width // PAIR)]


def stacked(slot, at, own_ref, *refs):
    return jnp.concatenate([own_ref[:, at]] + [ref[slot, :, at] for ref in refs], axis=0)


def both_heads(block):
    first_head = lax.broadcasted_iota(jnp.int32, block.shape, 1) < HEAD_DIM
    zero = jnp.zeros_like(block)
    return jnp.concatenate([jnp.where(first_head, block, zero), jnp.where(first_head, zero, block)], axis=0)


def scaled(block):
    return both_heads(block * jnp.asarray(FACTOR, BF16))


def two_tables(table_ref, pair, rows):
    return jnp.concatenate([table_ref[2 * pair, rows], table_ref[2 * pair + 1, rows]], axis=1)


def times(left, right):
    return lax.dot_general(left, right, LAST, preferred_element_type=F32)


def column_sum(x):
    return jnp.sum(x, axis=0, keepdims=True)


def score_gradient(probability, grad_prob, row_dot):
    return probability.astype(BF16), (probability * (grad_prob - row_dot)).astype(BF16)


def near_kernel(
    q_ref, g_ref, k_ref, v_ref, lon_odd_ref, lon_even_ref, lat_even_ref, lat_odd_ref, table_ref,
    raised_ref, prob_ref, stats_ref,
):
    parts = (lon_odd_ref, lon_even_ref, lat_even_ref, lat_odd_ref)

    def body(pair, at):
        scores = times(stacked(0, at, k_ref, *parts), scaled(q_ref[:, at])) + two_tables(table_ref, pair, pl.ds(0, NEAR))
        grad_prob = times(stacked(1, at, v_ref, *parts), both_heads(g_ref[:, at]))
        largest = jnp.max(scores, axis=0, keepdims=True)
        raised = jnp.exp(scores - largest)
        raised_ref[pair] = raised
        prob_ref[pair] = grad_prob
        stats_ref[pair, 0:1] = largest
        stats_ref[pair, 1:2] = column_sum(raised)
        stats_ref[pair, 2:3] = column_sum(raised * grad_prob)

    over_pairs(q_ref.shape[1], body)


def corner_kernel(
    q_ref, g_ref, corner_even_ref, corner_odd_ref, table_ref, near_stats_ref,
    raised_ref, prob_ref, stats_ref, send_even_ref, send_odd_ref, lines_ref,
):
    def score(pair, at):
        keys, values = (
            jnp.concatenate([corner_even_ref[slot, :, at], corner_odd_ref[slot, :, at]], axis=0) for slot in (0, 1)
        )
        scores = times(keys, scaled(q_ref[:, at])) + two_tables(table_ref, pair, pl.ds(NEAR, AROUND - NEAR))
        return scores, times(values, both_heads(g_ref[:, at]))

    scored = over_pairs(q_ref.shape[1], score)
    for pair, (scores, grad_prob) in enumerate(scored):
        near_largest = near_stats_ref[pair, 0:1]
        largest = jnp.maximum(near_largest, jnp.max(scores, axis=0, keepdims=True))
        raised = jnp.exp(scores - largest)
        shift = jnp.exp(near_largest - largest)
        total = near_stats_ref[pair, 1:2] * shift + column_sum(raised)
        inverse = 1.0 / total
        near_scale = shift * inverse
        row_dot = near_stats_ref[pair, 2:3] * near_scale + column_sum(raised * grad_prob) * inverse
        raised_ref[pair] = raised
        prob_ref[pair] = grad_prob
        stats_ref[pair, 0:1] = near_scale
        stats_ref[pair, 1:2] = row_dot
        stats_ref[pair, 2:3] = inverse
        for index, line in enumerate((largest + jnp.log(total), row_dot)):
            for head in (0, 1):
                at = 4 * pair + 2 * index + head
                lines_ref[at : at + 1] = line[:, head * CELLS : (head + 1) * CELLS]
    lines = lines_ref[...]
    low_rows = pltpu.roll(lines, BAND, 1)
    lat_odd = is_odd("lat")
    send_even_ref[...] = jnp.where(lat_odd, lines, low_rows)
    send_odd_ref[...] = jnp.where(lat_odd, low_rows, lines)


def near_gradient(raised_ref, prob_ref, stats_ref, pair, rows):
    return score_gradient(raised_ref[pair, rows] * stats_ref[pair, 0:1], prob_ref[pair, rows], stats_ref[pair, 1:2])


def band_lines(lines_refs, pair):
    def row(first):
        return jnp.concatenate([ref[line : line + 1] for ref in lines_refs for line in (first, first + 1)], axis=1)

    return row(4 * pair), row(4 * pair + 2)


def band_queries(queries_refs, slot, at, prepare):
    empty = jnp.zeros((CELLS - BAND, PAIR), BF16)
    return jnp.concatenate([prepare(jnp.concatenate([ref[slot, :, at], empty], axis=0)) for ref in queries_refs], axis=0)


def band_tables(table_ref, pair, rows):
    return jnp.concatenate([table_ref[slot, 2 * pair + head, rows] for slot in (0, 1) for head in (0, 1)], axis=1)


def side_scores_kernel(
    q_ref, g_ref, raised_ref, prob_ref, stats_ref, lon_odd_ref, lon_even_ref, queries_even_ref, queries_odd_ref, table_ref,
    dlon_ref, scores_ref, prob_out_ref, band_q_ref, band_g_ref,
):
    queries_refs = (queries_even_ref, queries_odd_ref)

    def body(pair, at):
        keys, values = (
            jnp.concatenate([lon_odd_ref[slot, :, at], lon_even_ref[slot, :, at]], axis=0) for slot in (0, 1)
        )
        queries = band_queries(queries_refs, 0, at, scaled)
        grads = band_queries(queries_refs, 1, at, both_heads)
        band_q_ref[pair] = queries
        band_g_ref[pair] = grads
        scores_ref[pair] = times(keys, queries) + band_tables(table_ref, pair, pl.ds(LON_AT, 2 * SIDE))
        prob_out_ref[pair] = times(values, grads)
        weights, dscore = near_gradient(raised_ref, prob_ref, stats_ref, pair, pl.ds(LON_AT, LAT_AT - LON_AT))
        dlon_ref[0, :, at] = jnp.dot(dscore, scaled(q_ref[:, at]), preferred_element_type=F32)
        dlon_ref[1, :, at] = jnp.dot(weights, both_heads(g_ref[:, at]), preferred_element_type=F32)

    over_pairs(q_ref.shape[1], body)


def side_band_kernel(
    dlon_ref, scores_ref, prob_ref, band_q_ref, band_g_ref, lines_even_ref, lines_odd_ref, send_odd_ref, send_even_ref
):
    lines_refs = (lines_even_ref, lines_odd_ref)

    def score(pair, at):
        log_total, row_dot = band_lines(lines_refs, pair)
        return score_gradient(jnp.exp(scores_ref[pair] - log_total), prob_ref[pair], row_dot)

    width = dlon_ref.shape[2]
    scored = over_pairs(width, score)

    def finish(pair, at):
        weights, dscore = scored[pair]
        for slot, coefficients, other in ((0, dscore, band_q_ref), (1, weights, band_g_ref)):
            total = dlon_ref[slot, :, at] + jnp.dot(coefficients, other[pair], preferred_element_type=F32)
            send_odd_ref[slot, :, at] = total[:SIDE].astype(BF16)
            send_even_ref[slot, :, at] = total[SIDE:].astype(BF16)

    over_pairs(width, finish)


def own_kernel(
    q_ref, g_ref, k_ref, v_ref, lon_odd_ref, lon_even_ref, lat_even_ref, lat_odd_ref, corner_even_ref, corner_odd_ref,
    raised_ref, prob_ref, corner_raised_ref, corner_prob_ref, stats_ref, out_ref, dq_ref, own_ref,
):
    parts = (lon_odd_ref, lon_even_ref, lat_even_ref, lat_odd_ref, corner_even_ref, corner_odd_ref)

    def per_query(cells, coefficients):
        turned = jnp.dot(cells.T, coefficients, preferred_element_type=F32)
        mine = jnp.concatenate([turned[:HEAD_DIM, :CELLS], turned[HEAD_DIM:, CELLS:]], axis=0)
        return mine.T

    def body(pair, at):
        nearby = near_gradient(raised_ref, prob_ref, stats_ref, pair, pl.ds(0, NEAR))
        far = score_gradient(
            corner_raised_ref[pair] * stats_ref[pair, 2:3], corner_prob_ref[pair], stats_ref[pair, 1:2]
        )
        weights, dscore = (jnp.concatenate(x, axis=0) for x in zip(nearby, far))
        own_ref[0, :, at] = jnp.dot(dscore[:LON_AT], scaled(q_ref[:, at]), preferred_element_type=F32)
        own_ref[1, :, at] = jnp.dot(weights[:LON_AT], both_heads(g_ref[:, at]), preferred_element_type=F32)
        out_ref[:, at] = per_query(stacked(1, at, v_ref, *parts), weights).astype(BF16)
        dq_ref[:, at] = (per_query(stacked(0, at, k_ref, *parts), dscore) * FACTOR).astype(BF16)

    over_pairs(q_ref.shape[1], body)


def own_band_kernel(
    k_ref, v_ref, band_q_ref, band_g_ref, table_ref, lines_even_ref, lines_odd_ref, own_ref, total_ref
):
    def score(pair, at):
        log_total, row_dot = band_lines((lines_even_ref, lines_odd_ref), pair)
        scores = times(k_ref[:, at], band_q_ref[pair]) + band_tables(table_ref, pair, pl.ds(OWN_AT, CELLS))
        return score_gradient(jnp.exp(scores - log_total), times(v_ref[:, at], band_g_ref[pair]), row_dot)

    scored = over_pairs(k_ref.shape[1], score)

    def finish(pair, at):
        weights, dscore = scored[pair]
        for slot, coefficients, other in ((0, dscore, band_q_ref), (1, weights, band_g_ref)):
            grad = jnp.dot(coefficients, other[pair], preferred_element_type=F32)
            total_ref[slot, :, at] = own_ref[slot, :, at] + grad

    over_pairs(k_ref.shape[1], finish)


def final_kernel(total_ref, side_even_ref, side_odd_ref, dk_ref, dv_ref):
    lon_odd = is_odd("lon")
    shape = (CELLS, SIDE)
    cell = lax.broadcasted_iota(jnp.int32, shape, 0)
    place = lax.broadcasted_iota(jnp.int32, shape, 1)

    def spread(first_col):
        return (cell == (place % ROWS) * COLS + first_col + place // ROWS).astype(BF16)

    spread_odd = spread(jnp.where(lon_odd, COLS - RADIUS, 0))
    spread_even = spread(jnp.where(lon_odd, 0, COLS - RADIUS))
    for slot, out in ((0, dk_ref), (1, dv_ref)):
        total = (
            total_ref[slot]
            + jnp.dot(spread_odd, side_odd_ref[slot], preferred_element_type=F32)
            + jnp.dot(spread_even, side_even_ref[slot], preferred_element_type=F32)
        )
        out[...] = total.astype(BF16)


def arr(shape, dtype):
    return jax.ShapeDtypeStruct(shape, dtype)


def call(kernel, name, operands, results, flops=0, **more):
    moved = sum(x.size * x.dtype.itemsize for x in operands)
    return pl.pallas_call(
        kernel,
        out_shape=results,
        compiler_params=pltpu.CompilerParams(vmem_limit_bytes=32 * 1024 * 1024),
        cost_estimate=pl.CostEstimate(flops=flops, bytes_accessed=moved, transcendentals=0),
        name=name,
        **more,
    )(*operands)


def shards(queries, key_cells, value_cells, grad_output, rel_bias):
    block = queries.shape
    heads = rel_bias.shape[0]
    feat = block[-1]
    pairs = feat // PAIR
    cells = arr((CELLS, feat), BF16)
    side, band, corner = (arr((2, rows, feat), BF16) for rows in (SIDE, BAND, 2 * SIDE))
    work = 2 * CELLS * feat
    barrier = lax.optimization_barrier

    def in_hbm(x):
        return pltpu.with_memory_space_constraint(x, pltpu.HBM)

    hbm, vmem = (pl.BlockSpec(memory_space=space) for space in (pltpu.HBM, pltpu.VMEM))
    arguments = [in_hbm(x) for x in (key_cells.reshape(CELLS, feat), value_cells.reshape(CELLS, feat), rel_bias)]
    lon_odd, lon_even, k, v, rel_bias = call(
        pack_kernel, "pack", arguments, [side, side, cells, cells, arr(rel_bias.shape, F32)],
        in_specs=[hbm] * 3,
        scratch_shapes=[pltpu.SemaphoreType.DMA((3,))],
    )
    lon_odd = pair_exchange(lon_odd, "lon", 1, True)
    lon_even = pair_exchange(lon_even, "lon", 0, True)
    lat_even, lat_odd = call(rows_kernel, "rows", [k, v], [band, band])
    lat_even = pair_exchange(lat_even, "lat", 0, False)
    lat_odd = pair_exchange(lat_odd, "lat", 1, True)

    spread = [pltpu.VMEM((heads, TABLE), F32), pltpu.VMEM((2, heads, 8, TABLE), F32)]
    table, q, g = call(
        bias_kernel, "bias_table",
        [rel_bias, in_hbm(queries.reshape(CELLS, feat)), in_hbm(grad_output.reshape(CELLS, feat))],
        [arr((heads, AROUND, CELLS), F32), cells, cells], heads * AROUND * CELLS,
        in_specs=[vmem, hbm, hbm],
        scratch_shapes=[*spread, pltpu.SemaphoreType.DMA((2,))],
    )

    lon_odd, lon_even, table = barrier((lon_odd, lon_even, table))
    joined, = call(join_kernel, "join", [lon_odd, lon_even], [corner], int(2e9))
    corner_even = pair_exchange(joined, "lat", 0, False)
    corner_odd = odd_rows_exchange(joined)

    def scored(rows):
        return [arr((pairs, rows, 2 * CELLS), F32)] * 2 + [arr((pairs, 8, 2 * CELLS), F32)]

    near = [k, v, lon_odd, lon_even, lat_even, lat_odd]
    raised, prob, near_stats = call(near_kernel, "near", [q, g, *near, table], scored(NEAR), 4 * work * NEAR)
    late_q, late_g, _ = barrier((q, g, joined))
    queries_even, queries_odd = call(rows_kernel, "query_rows", [late_q, late_g], [band, band])
    queries_even = pair_exchange(queries_even, "lat", 0, False)
    queries_odd = odd_rows_exchange(queries_odd)
    lines = arr((4 * pairs, LANES), F32)
    corner_raised, corner_prob, stats, lines_even, lines_odd = call(
        corner_kernel, "corner", [q, g, corner_even, corner_odd, table, near_stats],
        scored(AROUND - NEAR) + [lines, lines], 4 * work * (AROUND - NEAR),
        scratch_shapes=[pltpu.VMEM(lines.shape, F32)],
    )
    lines_even = pair_exchange(lines_even, "lat", 0, False)
    lines_odd = odd_rows_exchange(lines_odd)
    band_table, = call(
        band_bias_kernel, "band_table", [rel_bias, stats], [arr((2, heads, LAT_AT, CELLS), F32)],
        2 * heads * LAT_AT * CELLS,
        scratch_shapes=spread,
    )
    band_scores = [arr((pairs, 2 * SIDE, 4 * CELLS), F32)] * 2
    masked = [arr((pairs, 4 * CELLS, PAIR), BF16)] * 2
    dlon, side_scores, side_prob, band_q, band_g = call(
        side_scores_kernel, "side_scores",
        [q, g, raised, prob, stats, lon_odd, lon_even, queries_even, queries_odd, band_table],
        [arr(corner.shape, F32), *band_scores, *masked], 16 * work * SIDE,
    )
    lines_odd, dlon = barrier((lines_odd, dlon))
    send_odd, send_even = call(
        side_band_kernel, "side_band", [dlon, side_scores, side_prob, band_q, band_g, lines_even, lines_odd], [side, side],
        16 * work * SIDE,
    )
    side_even = pair_exchange(send_even, "lon", 0, True)
    side_odd = pair_exchange(send_odd, "lon", 1, True)
    out, dq, own = call(
        own_kernel, "own", [q, g, *near, corner_even, corner_odd, raised, prob, corner_raised, corner_prob, stats],
        [cells, cells, arr((2, CELLS, feat), F32)], 4 * work * AROUND,
    )
    total, = call(
        own_band_kernel, "own_band", [k, v, band_q, band_g, band_table, lines_even, lines_odd, own],
        [arr((2, CELLS, feat), F32)], 8 * work * CELLS,
    )
    dk, dv = call(final_kernel, "final", [total, side_even, side_odd], [cells, cells])
    return tuple(x.reshape(block) for x in (out, dq, dk, dv))


def solution(mesh):
    spec = P("lat", "lon", None)
    return jax.shard_map(
        shards, mesh=mesh, in_specs=(spec, spec, spec, spec, P()), out_specs=(spec,) * 4, check_vma=False
    )
```

time: 34.2 us -> 33 us (0.965)
  Pallas kernels: 8.49 us -> 11.1 us
  starting transfers between devices: 16.3 us -> 13.7 us
  waiting for transfers between devices: 8.51 us -> 7.36 us
    pallas_call x11 -> x13, Pallas kernels: 8.49 us -> 11.1 us  [call(): pl.pallas_call(kernel, out_shape=results, compiler_params=pltpu.CompilerP...]
    ppermute x10 -> x9, starting transfers between devices: 14.1 us -> 12.6 us  [pair_exchange(): return lax.ppermute(value, axis, pairs)]
    ppermute x4 -> x3, starting transfers between devices: 2.18 us -> 1.05 us  [odd_rows_exchange(): return lax.ppermute(value, ('lat', 'lon'), pairs)]
    ppermute x10 -> x9, waiting for transfers between devices: 4.73 us -> 3.91 us  [pair_exchange(): return lax.ppermute(value, axis, pairs)]
    ppermute x4 -> x3, waiting for transfers between devices: 3.78 us -> 3.44 us  [odd_rows_exchange(): return lax.ppermute(value, ('lat', 'lon'), pairs)]
  transfers between devices with their start and end apart: 14 -> 12, of which waited for: 5 -> 5; matrix products, arithmetic and copies ran while one was open for 0% -> 0% of each run, Pallas kernels for 16% -> 26%
where the time goes in v7:
time: 33 us; the launch traced here: 32.9 us
  starting transfers between devices  13.7 us (42%)
  Pallas kernels  11.1 us (34%)
  waiting for transfers between devices  7.36 us (22%)
  between operations  0.76 us (2%)
    ppermute x9, starting transfers between devices, pair_exchange(): return lax.ppermute(value, axis, pairs)  12.6 us
    pallas_call x13, Pallas kernels, call(): pl.pallas_call(kernel, out_shape=results, compiler_params=pltpu.CompilerP...  11.1 us
    ppermute x9, waiting for transfers between devices, pair_exchange(): return lax.ppermute(value, axis, pairs)  3.91 us
    ppermute x3, waiting for transfers between devices, odd_rows_exchange(): return lax.ppermute(value, ('lat', 'lon'), pairs)  3.44 us
    ppermute x3, starting transfers between devices, odd_rows_exchange(): return lax.ppermute(value, ('lat', 'lon'), pairs)  1.05 us
  transfers between devices with their start and end apart: 12, of which 5 were waited for; matrix products, arithmetic and copies ran while one was open for 0% of the time, Pallas kernels for 26%

profile of v7, /device:TPU:0, one launch (start us, length us, event | category | flops | bytes accessed | tf_op | source)
XLA Modules:
  0.0 32.9 jit_solution(1100630662759195167)
XLA Ops:
  0.6 1.3 %pack.1 = (bf16[2,48,512]{2,1,0:T(8,128)(2,1)S(1)}, bf16[2,48,512]{2,1,0:T(8,128)(2,1)S(1)}, bf16[128,512]{1,0:T(8,128)(2,1)S(1)}, bf16[128,512]{1,0:T(8,128)(2,1)S(1)}, f32[8,169]{1,0:T(8,128)S(1)}) custom-call(bf16[128,512]{1,0:T(8,128)(2,1)} %bitcast.8, bf16[128,512]{1,0:T(8,128)(2,1)} %bitcast.9, f32[8,169]{1,0:T(8,128)} %bias_hbm.1), custom_call_target="tpu_custom_call" | custom-call | bytes 267552 | tf_op jit(solution)/shard_map/pack/pallas_call | solution.py:463
  1.9 6.1 %collective-permute-start = (bf16[2,48,512]{2,1,0:T(8,128)(2,1)S(1)}, bf16[2,48,512]{2,1,0:T(8,128)(2,1)S(1)}, u32[]{:S(2)}, u32[]{:S(2)}) collective-permute-start(bf16[2,48,512]{2,1,0:T(8,128)(2,1)S(1)} %get-tuple-element.48), channel_id=1, source_target_pairs={{1,2},{2,1},{3,4},{4,3},{5,6},{6,5},{7,0},{0,7},{9,10},{10,9},{11,... | collective-permute-start | bytes 294920 | tf_op jit(solution)/shard_map/ppermute | solution.py:43
  8.0 0.0 collective-permute-start.1
  8.0 0.1 collective-permute-start.2
  8.1 1.6 %collective-permute-start.3 = (bf16[2,96,512]{2,1,0:T(8,128)(2,1)S(1)}, bf16[2,96,512]{2,1,0:T(8,128)(2,1)S(1)}, u32[]{:S(2)}, u32[]{:S(2)}) collective-permute-start(bf16[2,96,512]{2,1,0:T(8,128)(2,1)S(1)} %get-tuple-element.54), channel_id=1, source_target_pairs={{8,16},{16,8},{24,0},{0,24},{9,17},{17,9},{25,1},{1,25},{10,18},{1... | collective-permute-start | bytes 589832 | tf_op jit(solution)/shard_map/ppermute | solution.py:43
  9.7 2.3 %bias_table.1 = (f32[8,608,128]{2,1,0:T(8,128)S(1)}, bf16[128,512]{1,0:T(8,128)(2,1)S(1)}, bf16[128,512]{1,0:T(8,128)(2,1)S(1)}) custom-call(f32[8,169]{1,0:T(8,128)S(1)} %get-tuple-element.43.bias_ref, bf16[128,512]{1,0:T(8,128)(2,1)} %bitcast.10, bf16[128,512]{1,0:T(8,128)(2,1)} %bitcast.11), custom_call_target="tpu_custom_call" | custom-call | flops 622592 | bytes 267552 | tf_op jit(solution)/shard_map/bias_table/pallas_call | solution.py:463
  12.0 0.0 collective-permute-done.lon_odd_ref
  12.0 0.8 %collective-permute-done.1.lon_even_ref = bf16[2,48,512]{2,1,0:T(8,128)(2,1)S(1)} collective-permute-done((bf16[2,48,512]{2,1,0:T(8,128)(2,1)S(1)}, bf16[2,48,512]{2,1,0:T(8,128)(2,1)S(1)}, u32[]{:S(2)}, u32[]{:S(2)}) %collective-permute-start.1) | collective-permute-done | bytes 98336 | tf_op jit(solution)/shard_map/ppermute | solution.py:43
  12.9 0.1 collective-permute-start.5
  13.0 1.6 %collective-permute-start.4 = (bf16[2,96,512]{2,1,0:T(8,128)(2,1)S(1)}, bf16[2,96,512]{2,1,0:T(8,128)(2,1)S(1)}, u32[]{:S(2)}, u32[]{:S(2)}) collective-permute-start(bf16[2,96,512]{2,1,0:T(8,128)(2,1)S(1)} %join.1), channel_id=1, source_target_pairs={{0,8},{8,0},{16,24},{24,16},{1,9},{9,1},{17,25},{25,17},{2,10},{10... | collective-permute-start | bytes 589832 | tf_op jit(solution)/shard_map/ppermute | solution.py:43
  14.6 0.1 collective-permute-start.6
  14.7 0.0 collective-permute-done.2.lat_even_ref
  14.7 0.9 %collective-permute-start.7 = (bf16[2,96,512]{2,1,0:T(8,128)(2,1)S(1)}, bf16[2,96,512]{2,1,0:T(8,128)(2,1)S(1)}, u32[]{:S(2)}, u32[]{:S(2)}) collective-permute-start(bf16[2,96,512]{2,1,0:T(8,128)(2,1)S(1)} %get-tuple-element.67), channel_id=1, source_target_pairs={{0,2},{1,3},{2,0},{3,1},{4,6},{5,7},{6,4},{7,5},{8,16},{9,17},{10,... | collective-permute-start | bytes 589832 | tf_op jit(solution)/shard_map/ppermute | solution.py:55
  15.6 0.0 collective-permute-done.3.lat_odd_ref
  15.6 0.9 %near.1 = (f32[4,416,256]{2,1,0:T(8,128)S(1)}, f32[4,416,256]{2,1,0:T(8,128)S(1)}, f32[4,8,256]{2,1,0:T(8,128)S(1)}) custom-call(bf16[128,512]{1,0:T(8,128)(2,1)S(1)} %get-tuple-element.64.q_ref.k_ref, bf16[128,512]{1,0:T(8,128)(2,1)S(1)} %get-tuple-element.65.g_ref.v_ref, bf16[128,512]{1,0:T(8,128)(2,1)S(1)} %get-tuple-element.46.k_ref, ...), custom_call_target="tpu_custom_call" | custom-call | flops 218103808 | bytes 3604480 | tf_op jit(solution)/shard_map/near/pallas_call | solution.py:463
  16.5 2.2 %collective-permute-done.5.corner_odd_ref = bf16[2,96,512]{2,1,0:T(8,128)(2,1)S(1)} collective-permute-done((bf16[2,96,512]{2,1,0:T(8,128)(2,1)S(1)}, bf16[2,96,512]{2,1,0:T(8,128)(2,1)S(1)}, u32[]{:S(2)}, u32[]{:S(2)}) %collective-permute-start.5) | collective-permute-done | bytes 196640 | tf_op jit(solution)/shard_map/ppermute | solution.py:55
  18.6 0.0 collective-permute-done.4.corner_even_ref
  18.6 0.6 %corner.1 = (f32[4,192,256]{2,1,0:T(8,128)S(1)}, f32[4,192,256]{2,1,0:T(8,128)S(1)}, f32[4,8,256]{2,1,0:T(8,128)S(1)}, f32[16,128]{1,0:T(8,128)S(1)}, f32[16,128]{1,0:T(8,128)S(1)}) custom-call(bf16[128,512]{1,0:T(8,128)(2,1)S(1)} %get-tuple-element.64.q_ref.k_ref, bf16[128,512]{1,0:T(8,128)(2,1)S(1)} %get-tuple-element.65.g_ref.v_ref, ...), custom_call_target="tpu_custom_call" | custom-call | flops 100663296 | bytes 3178496 | tf_op jit(solution)/shard_map/corner/pallas_call | solution.py:463
  19.2 0.0 collective-permute-start.8
  19.2 0.1 collective-permute-start.9
  19.3 1.4 %band_table.1.table_ref = f32[2,8,224,128]{3,2,1,0:T(8,128)S(1)} custom-call(f32[8,169]{1,0:T(8,128)S(1)} %get-tuple-element.43.bias_ref, f32[4,8,256]{2,1,0:T(8,128)S(1)} %get-tuple-element.61.stats_ref.after_ref), custom_call_target="tpu_custom_call" | custom-call | flops 458752 | bytes 38176 | tf_op jit(solution)/shard_map/band_table/pallas_call | solution.py:463
  20.7 0.0 collective-permute-done.6.queries_even_ref
  20.7 0.0 collective-permute-done.7.queries_odd_ref
  20.8 0.9 %side_scores.1 = (f32[2,96,512]{2,1,0:T(8,128)S(1)}, f32[4,96,512]{2,1,0:T(8,128)S(1)}, f32[4,96,512]{2,1,0:T(8,128)S(1)}, bf16[4,512,128]{2,1,0:T(8,128)(2,1)S(1)}, bf16[4,512,128]{2,1,0:T(8,128)(2,1)S(1)}) custom-call(bf16[128,512]{1,0:T(8,128)(2,1)S(1)} %get-tuple-element.64.q_ref.k_ref, bf16[128,512]{1,0:T(8,128)(2,1)S(1)} %get-tuple-element.65.g_ref.v_ref, ...), custom_call_target="tpu_custom_call" | custom-call | flops 100663296 | bytes 6127616 | tf_op jit(solution)/shard_map/side_scores/pallas_call | solution.py:463
  21.7 1.3 %collective-permute-done.9.lines_odd_ref = f32[16,128]{1,0:T(8,128)S(1)} collective-permute-done((f32[16,128]{1,0:T(8,128)S(1)}, f32[16,128]{1,0:T(8,128)S(1)}, u32[]{:S(2)}, u32[]{:S(2)}) %collective-permute-start.9) | collective-permute-done | bytes 8224 | tf_op jit(solution)/shard_map/ppermute | solution.py:55
  22.9 0.0 collective-permute-done.8.lines_even_ref
  22.9 0.4 %side_band.1 = (bf16[2,48,512]{2,1,0:T(8,128)(2,1)S(1)}, bf16[2,48,512]{2,1,0:T(8,128)(2,1)S(1)}) custom-call(f32[2,96,512]{2,1,0:T(8,128)S(1)} %get-tuple-element.75.dlon_ref, f32[4,96,512]{2,1,0:T(8,128)S(1)} %get-tuple-element.76.scores_ref, f32[4,96,512]{2,1,0:T(8,128)S(1)} %get-tuple-element.77.prob_ref, ...), custom_call_target="tpu_custom_call" | custom-call | flops 100663296 | bytes 3031040 | tf_op jit(solution)/shard_map/side_band/pallas_call | solution.py:463
  23.3 1.3 %collective-permute-start.10 = (bf16[2,48,512]{2,1,0:T(8,128)(2,1)S(1)}, bf16[2,48,512]{2,1,0:T(8,128)(2,1)S(1)}, u32[]{:S(2)}, u32[]{:S(2)}) collective-permute-start(bf16[2,48,512]{2,1,0:T(8,128)(2,1)S(1)} %get-tuple-element.78), channel_id=1, source_target_pairs={{0,1},{1,0},{2,3},{3,2},{4,5},{5,4},{6,7},{7,6},{8,9},{9,8},{10,11... | collective-permute-start | bytes 294920 | tf_op jit(solution)/shard_map/ppermute | solution.py:43
  24.6 1.9 %collective-permute-start.11 = (bf16[2,48,512]{2,1,0:T(8,128)(2,1)S(1)}, bf16[2,48,512]{2,1,0:T(8,128)(2,1)S(1)}, u32[]{:S(2)}, u32[]{:S(2)}) collective-permute-start(bf16[2,48,512]{2,1,0:T(8,128)(2,1)S(1)} %get-tuple-element.79), channel_id=1, source_target_pairs={{1,2},{2,1},{3,4},{4,3},{5,6},{6,5},{7,0},{0,7},{9,10},{10,9},{11,... | collective-permute-start | bytes 294920 | tf_op jit(solution)/shard_map/ppermute | solution.py:43
  26.5 1.6 %own.1 = (bf16[128,512]{1,0:T(8,128)(2,1)}, bf16[128,512]{1,0:T(8,128)(2,1)}, f32[2,128,512]{2,1,0:T(8,128)S(1)}) custom-call(bf16[128,512]{1,0:T(8,128)(2,1)S(1)} %get-tuple-element.64.q_ref.k_ref, bf16[128,512]{1,0:T(8,128)(2,1)S(1)} %get-tuple-element.65.g_ref.v_ref, bf16[128,512]{1,0:T(8,128)(2,1)S(1)} %get-tuple-element.46.k_ref, ...), custom_call_target="tpu_custom_call" | custom-call | flops 318767104 | bytes 6520832 | tf_op jit(solution)/shard_map/own/pallas_call | solution.py:463
  28.1 0.7 %own_band.1.total_ref = f32[2,128,512]{2,1,0:T(8,128)S(1)} custom-call(bf16[128,512]{1,0:T(8,128)(2,1)S(1)} %get-tuple-element.46.k_ref, bf16[128,512]{1,0:T(8,128)(2,1)S(1)} %get-tuple-element.47.v_ref, bf16[4,512,128]{2,1,0:T(8,128)(2,1)S(1)} %get-tuple-element.68.band_q_ref, bf16[4,512,128]{2,1,0:T(8,128)(2,1)S(1)} %get-tuple-element.69.band_g_ref, ...), custom_call_target="tpu_custom_call" | custom-call | flops 134217728 | bytes 3686400 | tf_op jit(solution)/shard_map/own_band/pallas_call | solution.py:463
  28.9 0.2 collective-permute-done.10.side_even_ref
  29.1 2.8 %collective-permute-done.11.side_odd_ref = bf16[2,48,512]{2,1,0:T(8,128)(2,1)S(1)} collective-permute-done((bf16[2,48,512]{2,1,0:T(8,128)(2,1)S(1)}, bf16[2,48,512]{2,1,0:T(8,128)(2,1)S(1)}, u32[]{:S(2)}, u32[]{:S(2)}) %collective-permute-start.11) | collective-permute-done | bytes 98336 | tf_op jit(solution)/shard_map/ppermute | solution.py:43
  31.9 0.9 %final.1 = (bf16[128,512]{1,0:T(8,128)(2,1)}, bf16[128,512]{1,0:T(8,128)(2,1)}) custom-call(f32[2,128,512]{2,1,0:T(8,128)S(1)} %own_band.1.total_ref, bf16[2,48,512]{2,1,0:T(8,128)(2,1)S(1)} %collective-permute-done.10.side_even_ref, bf16[2,48,512]{2,1,0:T(8,128)(2,1)S(1)} %collective-permute-done.11.side_odd_ref), custom_call_target="tpu_custom_call" | custom-call | bytes 720896 | tf_op jit(solution)/shard_map/final/pallas_call | solution.py:463
  (3 shorter events, 0.1 us)
Async XLA Ops:
  1.9 10.1 %collective-permute-start = (bf16[2,48,512]{2,1,0:T(8,128)(2,1)S(1)}, bf16[2,48,512]{2,1,0:T(8,128)(2,1)S(1)}, u32[]{:S(2)}, u32[]{:S(2)}) collective-permute-start(bf16[2,48,512]{2,1,0:T(8,128)(2,1)S(1)} %get-tuple-element.48), channel_id=1, source_target_pairs={{1,2},{2,1},{3,4},{4,3},{5,6},{6,5},{7,0},{0,7},{9,10},{10,9},{11,... | collective-permute-start | bytes 294920 | tf_op jit(solution)/shard_map/ppermute | solution.py:43
  8.0 4.9 %collective-permute-start.1 = (bf16[2,48,512]{2,1,0:T(8,128)(2,1)S(1)}, bf16[2,48,512]{2,1,0:T(8,128)(2,1)S(1)}, u32[]{:S(2)}, u32[]{:S(2)}) collective-permute-start(bf16[2,48,512]{2,1,0:T(8,128)(2,1)S(1)} %get-tuple-element.49), channel_id=1, source_target_pairs={{0,1},{1,0},{2,3},{3,2},{4,5},{5,4},{6,7},{7,6},{8,9},{9,8},{10,11... | collective-permute-start | bytes 294920 | tf_op jit(solution)/shard_map/ppermute | solution.py:43
  8.0 6.7 %collective-permute-start.2 = (bf16[2,96,512]{2,1,0:T(8,128)(2,1)S(1)}, bf16[2,96,512]{2,1,0:T(8,128)(2,1)S(1)}, u32[]{:S(2)}, u32[]{:S(2)}) collective-permute-start(bf16[2,96,512]{2,1,0:T(8,128)(2,1)S(1)} %get-tuple-element.53), channel_id=1, source_target_pairs={{0,8},{8,0},{16,24},{24,16},{1,9},{9,1},{17,25},{25,17},{2,10},{10... | collective-permute-start | bytes 589832 | tf_op jit(solution)/shard_map/ppermute | solution.py:43
  8.1 7.5 %collective-permute-start.3 = (bf16[2,96,512]{2,1,0:T(8,128)(2,1)S(1)}, bf16[2,96,512]{2,1,0:T(8,128)(2,1)S(1)}, u32[]{:S(2)}, u32[]{:S(2)}) collective-permute-start(bf16[2,96,512]{2,1,0:T(8,128)(2,1)S(1)} %get-tuple-element.54), channel_id=1, source_target_pairs={{8,16},{16,8},{24,0},{0,24},{9,17},{17,9},{25,1},{1,25},{10,18},{1... | collective-permute-start | bytes 589832 | tf_op jit(solution)/shard_map/ppermute | solution.py:43
  12.9 5.7 %collective-permute-start.5 = (bf16[2,96,512]{2,1,0:T(8,128)(2,1)S(1)}, bf16[2,96,512]{2,1,0:T(8,128)(2,1)S(1)}, u32[]{:S(2)}, u32[]{:S(2)}) collective-permute-start(bf16[2,96,512]{2,1,0:T(8,128)(2,1)S(1)} %join.1), channel_id=1, source_target_pairs={{0,2},{1,3},{2,0},{3,1},{4,6},{5,7},{6,4},{7,5},{8,16},{9,17},{10,... | collective-permute-start | bytes 589832 | tf_op jit(solution)/shard_map/ppermute | solution.py:55
  13.0 5.7 %collective-permute-start.4 = (bf16[2,96,512]{2,1,0:T(8,128)(2,1)S(1)}, bf16[2,96,512]{2,1,0:T(8,128)(2,1)S(1)}, u32[]{:S(2)}, u32[]{:S(2)}) collective-permute-start(bf16[2,96,512]{2,1,0:T(8,128)(2,1)S(1)} %join.1), channel_id=1, source_target_pairs={{0,8},{8,0},{16,24},{24,16},{1,9},{9,1},{17,25},{25,17},{2,10},{10... | collective-permute-start | bytes 589832 | tf_op jit(solution)/shard_map/ppermute | solution.py:43
  14.6 6.1 %collective-permute-start.6 = (bf16[2,96,512]{2,1,0:T(8,128)(2,1)S(1)}, bf16[2,96,512]{2,1,0:T(8,128)(2,1)S(1)}, u32[]{:S(2)}, u32[]{:S(2)}) collective-permute-start(bf16[2,96,512]{2,1,0:T(8,128)(2,1)S(1)} %get-tuple-element.66), channel_id=1, source_target_pairs={{0,8},{8,0},{16,24},{24,16},{1,9},{9,1},{17,25},{25,17},{2,10},{10... | collective-permute-start | bytes 589832 | tf_op jit(solution)/shard_map/ppermute | solution.py:43
  14.7 6.1 %collective-permute-start.7 = (bf16[2,96,512]{2,1,0:T(8,128)(2,1)S(1)}, bf16[2,96,512]{2,1,0:T(8,128)(2,1)S(1)}, u32[]{:S(2)}, u32[]{:S(2)}) collective-permute-start(bf16[2,96,512]{2,1,0:T(8,128)(2,1)S(1)} %get-tuple-element.67), channel_id=1, source_target_pairs={{0,2},{1,3},{2,0},{3,1},{4,6},{5,7},{6,4},{7,5},{8,16},{9,17},{10,... | collective-permute-start | bytes 589832 | tf_op jit(solution)/shard_map/ppermute | solution.py:55
  19.2 3.7 %collective-permute-start.8 = (f32[16,128]{1,0:T(8,128)S(1)}, f32[16,128]{1,0:T(8,128)S(1)}, u32[]{:S(2)}, u32[]{:S(2)}) collective-permute-start(f32[16,128]{1,0:T(8,128)S(1)} %get-tuple-element.70), channel_id=1, source_target_pairs={{0,8},{8,0},{16,24},{24,16},{1,9},{9,1},{17,25},{25,17},{2,10},{10... | collective-permute-start | bytes 24584 | tf_op jit(solution)/shard_map/ppermute | solution.py:43
  19.2 3.7 %collective-permute-start.9 = (f32[16,128]{1,0:T(8,128)S(1)}, f32[16,128]{1,0:T(8,128)S(1)}, u32[]{:S(2)}, u32[]{:S(2)}) collective-permute-start(f32[16,128]{1,0:T(8,128)S(1)} %get-tuple-element.71), channel_id=1, source_target_pairs={{0,2},{1,3},{2,0},{3,1},{4,6},{5,7},{6,4},{7,5},{8,16},{9,17},{10,... | collective-permute-start | bytes 24584 | tf_op jit(solution)/shard_map/ppermute | solution.py:55
  23.3 5.7 %collective-permute-start.10 = (bf16[2,48,512]{2,1,0:T(8,128)(2,1)S(1)}, bf16[2,48,512]{2,1,0:T(8,128)(2,1)S(1)}, u32[]{:S(2)}, u32[]{:S(2)}) collective-permute-start(bf16[2,48,512]{2,1,0:T(8,128)(2,1)S(1)} %get-tuple-element.78), channel_id=1, source_target_pairs={{0,1},{1,0},{2,3},{3,2},{4,5},{5,4},{6,7},{7,6},{8,9},{9,8},{10,11... | collective-permute-start | bytes 294920 | tf_op jit(solution)/shard_map/ppermute | solution.py:43
  24.6 7.3 %collective-permute-start.11 = (bf16[2,48,512]{2,1,0:T(8,128)(2,1)S(1)}, bf16[2,48,512]{2,1,0:T(8,128)(2,1)S(1)}, u32[]{:S(2)}, u32[]{:S(2)}) collective-permute-start(bf16[2,48,512]{2,1,0:T(8,128)(2,1)S(1)} %get-tuple-element.79), channel_id=1, source_target_pairs={{1,2},{2,1},{3,4},{4,3},{5,6},{6,5},{7,0},{0,7},{9,10},{10,9},{11,... | collective-permute-start | bytes 294920 | tf_op jit(solution)/shard_map/ppermute | solution.py:43

commit v8 on v7

--- a/solution.py
+++ b/solution.py
@@ -322,7 +322,8 @@
     low_rows = pltpu.roll(lines, BAND, 1)
     lat_odd = is_odd("lat")
     send_even_ref[...] = jnp.where(lat_odd, lines, low_rows)
-    send_odd_ref[...] = jnp.where(lat_odd, low_rows, lines)
+    odd_lines = jnp.where(lat_odd, low_rows, lines)
+    send_odd_ref[...] = jnp.concatenate([odd_lines] * (send_odd_ref.shape[0] // lines.shape[0]), axis=0)
 
 
 def near_gradient(raised_ref, prob_ref, stats_ref, pair, rows):
@@ -519,19 +520,20 @@
     queries_even, queries_odd = call(rows_kernel, "query_rows", [late_q, late_g], [band, band])
     queries_even = pair_exchange(queries_even, "lat", 0, False)
     queries_odd = odd_rows_exchange(queries_odd)
+    band_table, = call(
+        band_bias_kernel, "band_table", [rel_bias, near_stats], [arr((2, heads, LAT_AT, CELLS), F32)],
+        2 * heads * LAT_AT * CELLS,
+        scratch_shapes=spread,
+    )
+    corner_odd, band_table = barrier((corner_odd, band_table))
     lines = arr((4 * pairs, LANES), F32)
     corner_raised, corner_prob, stats, lines_even, lines_odd = call(
         corner_kernel, "corner", [q, g, corner_even, corner_odd, table, near_stats],
-        scored(AROUND - NEAR) + [lines, lines], 4 * work * (AROUND - NEAR),
+        scored(AROUND - NEAR) + [lines, arr((2 * lines.shape[0], LANES), F32)], 4 * work * (AROUND - NEAR),
         scratch_shapes=[pltpu.VMEM(lines.shape, F32)],
     )
     lines_even = pair_exchange(lines_even, "lat", 0, False)
-    lines_odd = odd_rows_exchange(lines_odd)
-    band_table, = call(
-        band_bias_kernel, "band_table", [rel_bias, stats], [arr((2, heads, LAT_AT, CELLS), F32)],
-        2 * heads * LAT_AT * CELLS,
-        scratch_shapes=spread,
-    )
+    lines_odd = pair_exchange(lines_odd, "lat", 1, True)
     band_scores = [arr((pairs, 2 * SIDE, 4 * CELLS), F32)] * 2
     masked = [arr((pairs, 4 * CELLS, PAIR), BF16)] * 2
     dlon, side_scores, side_prob, band_q, band_g = call(

time: 33 us -> 32.6 us (0.988)
  waiting for transfers between devices: 7.36 us -> 5.91 us
  starting transfers between devices: 13.7 us -> 14.7 us
    ppermute x3 -> x2, waiting for transfers between devices: 3.44 us -> 1.22 us  [odd_rows_exchange(): return lax.ppermute(value, ('lat', 'lon'), pairs)]
    ppermute x9 -> x10, starting transfers between devices: 12.6 us -> 13.7 us  [pair_exchange(): return lax.ppermute(value, axis, pairs)]
    ppermute x9 -> x10, waiting for transfers between devices: 3.91 us -> 4.7 us  [pair_exchange(): return lax.ppermute(value, axis, pairs)]
    ppermute x3 -> x2, starting transfers between devices: 1.05 us -> 0.98 us  [odd_rows_exchange(): return lax.ppermute(value, ('lat', 'lon'), pairs)]
  transfers between devices with their start and end apart: 12 -> 12, of which waited for: 5 -> 6; matrix products, arithmetic and copies ran while one was open for 0% -> 0% of each run, Pallas kernels for 26% -> 26%
where the time goes in v8:
time: 32.6 us; the launch traced here: 32.4 us
  starting transfers between devices  14.7 us (45%)
  Pallas kernels  11.1 us (34%)
  waiting for transfers between devices  5.91 us (18%)
  between operations  0.74 us (2%)
    ppermute x10, starting transfers between devices, pair_exchange(): return lax.ppermute(value, axis, pairs)  13.7 us
    pallas_call x13, Pallas kernels, call(): pl.pallas_call(kernel, out_shape=results, compiler_params=pltpu.CompilerP...  11.1 us
    ppermute x10, waiting for transfers between devices, pair_exchange(): return lax.ppermute(value, axis, pairs)  4.7 us
    ppermute x2, waiting for transfers between devices, odd_rows_exchange(): return lax.ppermute(value, ('lat', 'lon'), pairs)  1.22 us
    ppermute x2, starting transfers between devices, odd_rows_exchange(): return lax.ppermute(value, ('lat', 'lon'), pairs)  0.98 us
  transfers between devices with their start and end apart: 12, of which 6 were waited for; matrix products, arithmetic and copies ran while one was open for 0% of the time, Pallas kernels for 26%

profile of v8, /device:TPU:0, one launch (start us, length us, event | category | flops | bytes accessed | tf_op | source)
XLA Modules:
  0.0 32.4 jit_solution(4151505002527685070)
XLA Ops:
  0.6 1.3 %pack.1 = (bf16[2,48,512]{2,1,0:T(8,128)(2,1)S(1)}, bf16[2,48,512]{2,1,0:T(8,128)(2,1)S(1)}, bf16[128,512]{1,0:T(8,128)(2,1)S(1)}, bf16[128,512]{1,0:T(8,128)(2,1)S(1)}, f32[8,169]{1,0:T(8,128)S(1)}) custom-call(bf16[128,512]{1,0:T(8,128)(2,1)} %bitcast.8, bf16[128,512]{1,0:T(8,128)(2,1)} %bitcast.9, f32[8,169]{1,0:T(8,128)} %bias_hbm.1), custom_call_target="tpu_custom_call" | custom-call | bytes 267552 | tf_op jit(solution)/shard_map/pack/pallas_call | solution.py:464
  1.9 6.1 %collective-permute-start = (bf16[2,48,512]{2,1,0:T(8,128)(2,1)S(1)}, bf16[2,48,512]{2,1,0:T(8,128)(2,1)S(1)}, u32[]{:S(2)}, u32[]{:S(2)}) collective-permute-start(bf16[2,48,512]{2,1,0:T(8,128)(2,1)S(1)} %get-tuple-element.50), channel_id=1, source_target_pairs={{1,2},{2,1},{3,4},{4,3},{5,6},{6,5},{7,0},{0,7},{9,10},{10,9},{11,... | collective-permute-start | bytes 294920 | tf_op jit(solution)/shard_map/ppermute | solution.py:43
  8.0 0.0 collective-permute-start.1
  8.0 0.1 collective-permute-start.2
  8.1 1.6 %collective-permute-start.3 = (bf16[2,96,512]{2,1,0:T(8,128)(2,1)S(1)}, bf16[2,96,512]{2,1,0:T(8,128)(2,1)S(1)}, u32[]{:S(2)}, u32[]{:S(2)}) collective-permute-start(bf16[2,96,512]{2,1,0:T(8,128)(2,1)S(1)} %get-tuple-element.56), channel_id=1, source_target_pairs={{8,16},{16,8},{24,0},{0,24},{9,17},{17,9},{25,1},{1,25},{10,18},{1... | collective-permute-start | bytes 589832 | tf_op jit(solution)/shard_map/ppermute | solution.py:43
  9.7 2.3 %bias_table.1 = (f32[8,608,128]{2,1,0:T(8,128)S(1)}, bf16[128,512]{1,0:T(8,128)(2,1)S(1)}, bf16[128,512]{1,0:T(8,128)(2,1)S(1)}) custom-call(f32[8,169]{1,0:T(8,128)S(1)} %get-tuple-element.45.bias_ref, bf16[128,512]{1,0:T(8,128)(2,1)} %bitcast.10, bf16[128,512]{1,0:T(8,128)(2,1)} %bitcast.11), custom_call_target="tpu_custom_call" | custom-call | flops 622592 | bytes 267552 | tf_op jit(solution)/shard_map/bias_table/pallas_call | solution.py:464
  12.0 0.0 collective-permute-done.lon_odd_ref
  12.0 0.8 %collective-permute-done.1.lon_even_ref = bf16[2,48,512]{2,1,0:T(8,128)(2,1)S(1)} collective-permute-done((bf16[2,48,512]{2,1,0:T(8,128)(2,1)S(1)}, bf16[2,48,512]{2,1,0:T(8,128)(2,1)S(1)}, u32[]{:S(2)}, u32[]{:S(2)}) %collective-permute-start.1) | collective-permute-done | bytes 98336 | tf_op jit(solution)/shard_map/ppermute | solution.py:43
  12.9 0.1 collective-permute-start.5
  13.0 1.6 %collective-permute-start.4 = (bf16[2,96,512]{2,1,0:T(8,128)(2,1)S(1)}, bf16[2,96,512]{2,1,0:T(8,128)(2,1)S(1)}, u32[]{:S(2)}, u32[]{:S(2)}) collective-permute-start(bf16[2,96,512]{2,1,0:T(8,128)(2,1)S(1)} %join.1), channel_id=1, source_target_pairs={{0,8},{8,0},{16,24},{24,16},{1,9},{9,1},{17,25},{25,17},{2,10},{10... | collective-permute-start | bytes 589832 | tf_op jit(solution)/shard_map/ppermute | solution.py:43
  14.6 0.1 collective-permute-start.6
  14.7 0.0 collective-permute-done.2.lat_even_ref
  14.7 0.9 %collective-permute-start.7 = (bf16[2,96,512]{2,1,0:T(8,128)(2,1)S(1)}, bf16[2,96,512]{2,1,0:T(8,128)(2,1)S(1)}, u32[]{:S(2)}, u32[]{:S(2)}) collective-permute-start(bf16[2,96,512]{2,1,0:T(8,128)(2,1)S(1)} %get-tuple-element.70), channel_id=1, source_target_pairs={{0,2},{1,3},{2,0},{3,1},{4,6},{5,7},{6,4},{7,5},{8,16},{9,17},{10,... | collective-permute-start | bytes 589832 | tf_op jit(solution)/shard_map/ppermute | solution.py:55
  15.6 0.0 collective-permute-done.3.lat_odd_ref
  15.6 0.9 %near.1 = (f32[4,416,256]{2,1,0:T(8,128)S(1)}, f32[4,416,256]{2,1,0:T(8,128)S(1)}, f32[4,8,256]{2,1,0:T(8,128)S(1)}) custom-call(bf16[128,512]{1,0:T(8,128)(2,1)S(1)} %get-tuple-element.67.q_ref.k_ref, bf16[128,512]{1,0:T(8,128)(2,1)S(1)} %get-tuple-element.68.g_ref.v_ref, bf16[128,512]{1,0:T(8,128)(2,1)S(1)} %get-tuple-element.48.k_ref, ...), custom_call_target="tpu_custom_call" | custom-call | flops 218103808 | bytes 3604480 | tf_op jit(solution)/shard_map/near/pallas_call | solution.py:464
  16.5 1.4 %band_table.1.table_ref = f32[2,8,224,128]{3,2,1,0:T(8,128)S(1)} custom-call(f32[8,169]{1,0:T(8,128)S(1)} %get-tuple-element.45.bias_ref, f32[4,8,256]{2,1,0:T(8,128)S(1)} %get-tuple-element.58.after_ref.near_stats_ref), custom_call_target="tpu_custom_call" | custom-call | flops 458752 | bytes 38176 | tf_op jit(solution)/shard_map/band_table/pallas_call | solution.py:464
  17.9 0.7 %collective-permute-done.5.corner_odd_ref = bf16[2,96,512]{2,1,0:T(8,128)(2,1)S(1)} collective-permute-done((bf16[2,96,512]{2,1,0:T(8,128)(2,1)S(1)}, bf16[2,96,512]{2,1,0:T(8,128)(2,1)S(1)}, u32[]{:S(2)}, u32[]{:S(2)}) %collective-permute-start.5) | collective-permute-done | bytes 196640 | tf_op jit(solution)/shard_map/ppermute | solution.py:55
  18.6 0.0 collective-permute-done.4.corner_even_ref
  18.6 0.6 %corner.1 = (f32[4,192,256]{2,1,0:T(8,128)S(1)}, f32[4,192,256]{2,1,0:T(8,128)S(1)}, f32[4,8,256]{2,1,0:T(8,128)S(1)}, f32[16,128]{1,0:T(8,128)S(1)}, f32[32,128]{1,0:T(8,128)S(1)}) custom-call(bf16[128,512]{1,0:T(8,128)(2,1)S(1)} %get-tuple-element.67.q_ref.k_ref, bf16[128,512]{1,0:T(8,128)(2,1)S(1)} %get-tuple-element.68.g_ref.v_ref, ...), custom_call_target="tpu_custom_call" | custom-call | flops 100663296 | bytes 3178496 | tf_op jit(solution)/shard_map/corner/pallas_call | solution.py:464
  19.2 0.0 collective-permute-start.9
  19.2 1.0 %collective-permute-start.8 = (f32[16,128]{1,0:T(8,128)S(1)}, f32[16,128]{1,0:T(8,128)S(1)}, u32[]{:S(2)}, u32[]{:S(2)}) collective-permute-start(f32[16,128]{1,0:T(8,128)S(1)} %get-tuple-element.74), channel_id=1, source_target_pairs={{0,8},{8,0},{16,24},{24,16},{1,9},{9,1},{17,25},{25,17},{2,10},{10... | collective-permute-start | bytes 24584 | tf_op jit(solution)/shard_map/ppermute | solution.py:43
  20.2 0.0 collective-permute-done.6.queries_even_ref
  20.2 0.5 %collective-permute-done.7.queries_odd_ref = bf16[2,96,512]{2,1,0:T(8,128)(2,1)S(1)} collective-permute-done((bf16[2,96,512]{2,1,0:T(8,128)(2,1)S(1)}, bf16[2,96,512]{2,1,0:T(8,128)(2,1)S(1)}, u32[]{:S(2)}, u32[]{:S(2)}) %collective-permute-start.7) | collective-permute-done | bytes 196640 | tf_op jit(solution)/shard_map/ppermute | solution.py:55
  20.7 0.9 %side_scores.1 = (f32[2,96,512]{2,1,0:T(8,128)S(1)}, f32[4,96,512]{2,1,0:T(8,128)S(1)}, f32[4,96,512]{2,1,0:T(8,128)S(1)}, bf16[4,512,128]{2,1,0:T(8,128)(2,1)S(1)}, bf16[4,512,128]{2,1,0:T(8,128)(2,1)S(1)}) custom-call(bf16[128,512]{1,0:T(8,128)(2,1)S(1)} %get-tuple-element.67.q_ref.k_ref, bf16[128,512]{1,0:T(8,128)(2,1)S(1)} %get-tuple-element.68.g_ref.v_ref, ...), custom_call_target="tpu_custom_call" | custom-call | flops 100663296 | bytes 6127616 | tf_op jit(solution)/shard_map/side_scores/pallas_call | solution.py:464
  21.6 0.7 %collective-permute-done.9.lines_odd_ref = f32[32,128]{1,0:T(8,128)S(1)} collective-permute-done((f32[32,128]{1,0:T(8,128)S(1)}, f32[32,128]{1,0:T(8,128)S(1)}, u32[]{:S(2)}, u32[]{:S(2)}) %collective-permute-start.9) | collective-permute-done | bytes 16416 | tf_op jit(solution)/shard_map/ppermute | solution.py:43
  22.4 0.0 collective-permute-done.8.lines_even_ref
  22.4 0.4 %side_band.1 = (bf16[2,48,512]{2,1,0:T(8,128)(2,1)S(1)}, bf16[2,48,512]{2,1,0:T(8,128)(2,1)S(1)}) custom-call(f32[2,96,512]{2,1,0:T(8,128)S(1)} %get-tuple-element.79.dlon_ref, f32[4,96,512]{2,1,0:T(8,128)S(1)} %get-tuple-element.80.scores_ref, f32[4,96,512]{2,1,0:T(8,128)S(1)} %get-tuple-element.81.prob_ref, ...), custom_call_target="tpu_custom_call" | custom-call | flops 100663296 | bytes 3039232 | tf_op jit(solution)/shard_map/side_band/pallas_call | solution.py:464
  22.8 1.4 %collective-permute-start.10 = (bf16[2,48,512]{2,1,0:T(8,128)(2,1)S(1)}, bf16[2,48,512]{2,1,0:T(8,128)(2,1)S(1)}, u32[]{:S(2)}, u32[]{:S(2)}) collective-permute-start(bf16[2,48,512]{2,1,0:T(8,128)(2,1)S(1)} %get-tuple-element.82), channel_id=1, source_target_pairs={{0,1},{1,0},{2,3},{3,2},{4,5},{5,4},{6,7},{7,6},{8,9},{9,8},{10,11... | collective-permute-start | bytes 294920 | tf_op jit(solution)/shard_map/ppermute | solution.py:43
  24.2 1.9 %collective-permute-start.11 = (bf16[2,48,512]{2,1,0:T(8,128)(2,1)S(1)}, bf16[2,48,512]{2,1,0:T(8,128)(2,1)S(1)}, u32[]{:S(2)}, u32[]{:S(2)}) collective-permute-start(bf16[2,48,512]{2,1,0:T(8,128)(2,1)S(1)} %get-tuple-element.83), channel_id=1, source_target_pairs={{1,2},{2,1},{3,4},{4,3},{5,6},{6,5},{7,0},{0,7},{9,10},{10,9},{11,... | collective-permute-start | bytes 294920 | tf_op jit(solution)/shard_map/ppermute | solution.py:43
  26.0 1.6 %own.1 = (bf16[128,512]{1,0:T(8,128)(2,1)}, bf16[128,512]{1,0:T(8,128)(2,1)}, f32[2,128,512]{2,1,0:T(8,128)S(1)}) custom-call(bf16[128,512]{1,0:T(8,128)(2,1)S(1)} %get-tuple-element.67.q_ref.k_ref, bf16[128,512]{1,0:T(8,128)(2,1)S(1)} %get-tuple-element.68.g_ref.v_ref, bf16[128,512]{1,0:T(8,128)(2,1)S(1)} %get-tuple-element.48.k_ref, ...), custom_call_target="tpu_custom_call" | custom-call | flops 318767104 | bytes 6520832 | tf_op jit(solution)/shard_map/own/pallas_call | solution.py:464
  27.7 0.7 %own_band.1.total_ref = f32[2,128,512]{2,1,0:T(8,128)S(1)} custom-call(bf16[128,512]{1,0:T(8,128)(2,1)S(1)} %get-tuple-element.48.k_ref, bf16[128,512]{1,0:T(8,128)(2,1)S(1)} %get-tuple-element.49.v_ref, bf16[4,512,128]{2,1,0:T(8,128)(2,1)S(1)} %get-tuple-element.72.band_q_ref, bf16[4,512,128]{2,1,0:T(8,128)(2,1)S(1)} %get-tuple-element.73.band_g_ref, ...), custom_call_target="tpu_custom_call" | custom-call | flops 134217728 | bytes 3694592 | tf_op jit(solution)/shard_map/own_band/pallas_call | solution.py:464
  28.4 0.2 collective-permute-done.10.side_even_ref
  28.6 2.9 %collective-permute-done.11.side_odd_ref = bf16[2,48,512]{2,1,0:T(8,128)(2,1)S(1)} collective-permute-done((bf16[2,48,512]{2,1,0:T(8,128)(2,1)S(1)}, bf16[2,48,512]{2,1,0:T(8,128)(2,1)S(1)}, u32[]{:S(2)}, u32[]{:S(2)}) %collective-permute-start.11) | collective-permute-done | bytes 98336 | tf_op jit(solution)/shard_map/ppermute | solution.py:43
  31.5 0.9 %final.1 = (bf16[128,512]{1,0:T(8,128)(2,1)}, bf16[128,512]{1,0:T(8,128)(2,1)}) custom-call(f32[2,128,512]{2,1,0:T(8,128)S(1)} %own_band.1.total_ref, bf16[2,48,512]{2,1,0:T(8,128)(2,1)S(1)} %collective-permute-done.10.side_even_ref, bf16[2,48,512]{2,1,0:T(8,128)(2,1)S(1)} %collective-permute-done.11.side_odd_ref), custom_call_target="tpu_custom_call" | custom-call | bytes 720896 | tf_op jit(solution)/shard_map/final/pallas_call | solution.py:464
  (3 shorter events, 0.1 us)
Async XLA Ops:
  1.9 10.1 %collective-permute-start = (bf16[2,48,512]{2,1,0:T(8,128)(2,1)S(1)}, bf16[2,48,512]{2,1,0:T(8,128)(2,1)S(1)}, u32[]{:S(2)}, u32[]{:S(2)}) collective-permute-start(bf16[2,48,512]{2,1,0:T(8,128)(2,1)S(1)} %get-tuple-element.50), channel_id=1, source_target_pairs={{1,2},{2,1},{3,4},{4,3},{5,6},{6,5},{7,0},{0,7},{9,10},{10,9},{11,... | collective-permute-start | bytes 294920 | tf_op jit(solution)/shard_map/ppermute | solution.py:43
  8.0 4.9 %collective-permute-start.1 = (bf16[2,48,512]{2,1,0:T(8,128)(2,1)S(1)}, bf16[2,48,512]{2,1,0:T(8,128)(2,1)S(1)}, u32[]{:S(2)}, u32[]{:S(2)}) collective-permute-start(bf16[2,48,512]{2,1,0:T(8,128)(2,1)S(1)} %get-tuple-element.51), channel_id=1, source_target_pairs={{0,1},{1,0},{2,3},{3,2},{4,5},{5,4},{6,7},{7,6},{8,9},{9,8},{10,11... | collective-permute-start | bytes 294920 | tf_op jit(solution)/shard_map/ppermute | solution.py:43
  8.0 6.7 %collective-permute-start.2 = (bf16[2,96,512]{2,1,0:T(8,128)(2,1)S(1)}, bf16[2,96,512]{2,1,0:T(8,128)(2,1)S(1)}, u32[]{:S(2)}, u32[]{:S(2)}) collective-permute-start(bf16[2,96,512]{2,1,0:T(8,128)(2,1)S(1)} %get-tuple-element.55), channel_id=1, source_target_pairs={{0,8},{8,0},{16,24},{24,16},{1,9},{9,1},{17,25},{25,17},{2,10},{10... | collective-permute-start | bytes 589832 | tf_op jit(solution)/shard_map/ppermute | solution.py:43
  8.1 7.5 %collective-permute-start.3 = (bf16[2,96,512]{2,1,0:T(8,128)(2,1)S(1)}, bf16[2,96,512]{2,1,0:T(8,128)(2,1)S(1)}, u32[]{:S(2)}, u32[]{:S(2)}) collective-permute-start(bf16[2,96,512]{2,1,0:T(8,128)(2,1)S(1)} %get-tuple-element.56), channel_id=1, source_target_pairs={{8,16},{16,8},{24,0},{0,24},{9,17},{17,9},{25,1},{1,25},{10,18},{1... | collective-permute-start | bytes 589832 | tf_op jit(solution)/shard_map/ppermute | solution.py:43
  12.9 5.7 %collective-permute-start.5 = (bf16[2,96,512]{2,1,0:T(8,128)(2,1)S(1)}, bf16[2,96,512]{2,1,0:T(8,128)(2,1)S(1)}, u32[]{:S(2)}, u32[]{:S(2)}) collective-permute-start(bf16[2,96,512]{2,1,0:T(8,128)(2,1)S(1)} %join.1), channel_id=1, source_target_pairs={{0,2},{1,3},{2,0},{3,1},{4,6},{5,7},{6,4},{7,5},{8,16},{9,17},{10,... | collective-permute-start | bytes 589832 | tf_op jit(solution)/shard_map/ppermute | solution.py:55
  13.0 5.7 %collective-permute-start.4 = (bf16[2,96,512]{2,1,0:T(8,128)(2,1)S(1)}, bf16[2,96,512]{2,1,0:T(8,128)(2,1)S(1)}, u32[]{:S(2)}, u32[]{:S(2)}) collective-permute-start(bf16[2,96,512]{2,1,0:T(8,128)(2,1)S(1)} %join.1), channel_id=1, source_target_pairs={{0,8},{8,0},{16,24},{24,16},{1,9},{9,1},{17,25},{25,17},{2,10},{10... | collective-permute-start | bytes 589832 | tf_op jit(solution)/shard_map/ppermute | solution.py:43
  14.6 5.6 %collective-permute-start.6 = (bf16[2,96,512]{2,1,0:T(8,128)(2,1)S(1)}, bf16[2,96,512]{2,1,0:T(8,128)(2,1)S(1)}, u32[]{:S(2)}, u32[]{:S(2)}) collective-permute-start(bf16[2,96,512]{2,1,0:T(8,128)(2,1)S(1)} %get-tuple-element.69), channel_id=1, source_target_pairs={{0,8},{8,0},{16,24},{24,16},{1,9},{9,1},{17,25},{25,17},{2,10},{10... | collective-permute-start | bytes 589832 | tf_op jit(solution)/shard_map/ppermute | solution.py:43
  14.7 6.1 %collective-permute-start.7 = (bf16[2,96,512]{2,1,0:T(8,128)(2,1)S(1)}, bf16[2,96,512]{2,1,0:T(8,128)(2,1)S(1)}, u32[]{:S(2)}, u32[]{:S(2)}) collective-permute-start(bf16[2,96,512]{2,1,0:T(8,128)(2,1)S(1)} %get-tuple-element.70), channel_id=1, source_target_pairs={{0,2},{1,3},{2,0},{3,1},{4,6},{5,7},{6,4},{7,5},{8,16},{9,17},{10,... | collective-permute-start | bytes 589832 | tf_op jit(solution)/shard_map/ppermute | solution.py:55
  19.2 3.2 %collective-permute-start.9 = (f32[32,128]{1,0:T(8,128)S(1)}, f32[32,128]{1,0:T(8,128)S(1)}, u32[]{:S(2)}, u32[]{:S(2)}) collective-permute-start(f32[32,128]{1,0:T(8,128)S(1)} %get-tuple-element.75), channel_id=1, source_target_pairs={{8,16},{16,8},{24,0},{0,24},{9,17},{17,9},{25,1},{1,25},{10,18},{1... | collective-permute-start | bytes 49160 | tf_op jit(solution)/shard_map/ppermute | solution.py:43
  19.2 3.2 %collective-permute-start.8 = (f32[16,128]{1,0:T(8,128)S(1)}, f32[16,128]{1,0:T(8,128)S(1)}, u32[]{:S(2)}, u32[]{:S(2)}) collective-permute-start(f32[16,128]{1,0:T(8,128)S(1)} %get-tuple-element.74), channel_id=1, source_target_pairs={{0,8},{8,0},{16,24},{24,16},{1,9},{9,1},{17,25},{25,17},{2,10},{10... | collective-permute-start | bytes 24584 | tf_op jit(solution)/shard_map/ppermute | solution.py:43
  22.8 5.8 %collective-permute-start.10 = (bf16[2,48,512]{2,1,0:T(8,128)(2,1)S(1)}, bf16[2,48,512]{2,1,0:T(8,128)(2,1)S(1)}, u32[]{:S(2)}, u32[]{:S(2)}) collective-permute-start(bf16[2,48,512]{2,1,0:T(8,128)(2,1)S(1)} %get-tuple-element.82), channel_id=1, source_target_pairs={{0,1},{1,0},{2,3},{3,2},{4,5},{5,4},{6,7},{7,6},{8,9},{9,8},{10,11... | collective-permute-start | bytes 294920 | tf_op jit(solution)/shard_map/ppermute | solution.py:43
  24.2 7.3 %collective-permute-start.11 = (bf16[2,48,512]{2,1,0:T(8,128)(2,1)S(1)}, bf16[2,48,512]{2,1,0:T(8,128)(2,1)S(1)}, u32[]{:S(2)}, u32[]{:S(2)}) collective-permute-start(bf16[2,48,512]{2,1,0:T(8,128)(2,1)S(1)} %get-tuple-element.83), channel_id=1, source_target_pairs={{1,2},{2,1},{3,4},{4,3},{5,6},{6,5},{7,0},{0,7},{9,10},{10,9},{11,... | collective-permute-start | bytes 294920 | tf_op jit(solution)/shard_map/ppermute | solution.py:43

commit v9 on v8

--- a/solution.py
+++ b/solution.py
@@ -24,7 +24,8 @@
 LON_AT = CELLS
 LAT_AT = LON_AT + 2 * SIDE
 NEAR = LAT_AT + 2 * BAND
-AROUND = NEAR + 4 * SIDE
+EARLY = NEAR + 2 * SIDE
+AROUND = EARLY + 2 * SIDE
 LANES = 128
 
 F32 = jnp.float32
@@ -188,7 +189,7 @@
                 put(NEAR + south_slot * 2 * SIDE + at, below, near(delta, has_south))
         return carry
 
-    lax.fori_loop(0, bias_ref.shape[0], fill, 0, unroll=8)
+    lax.fori_loop(0, bias_ref.shape[0], fill, 0, unroll=4)
     for copy in copies:
         copy.wait()
 
@@ -269,13 +270,13 @@
 
 
 def near_kernel(
-    q_ref, g_ref, k_ref, v_ref, lon_odd_ref, lon_even_ref, lat_even_ref, lat_odd_ref, table_ref,
+    q_ref, g_ref, k_ref, v_ref, lon_odd_ref, lon_even_ref, lat_even_ref, lat_odd_ref, corner_even_ref, table_ref,
     raised_ref, prob_ref, stats_ref,
 ):
-    parts = (lon_odd_ref, lon_even_ref, lat_even_ref, lat_odd_ref)
+    parts = (lon_odd_ref, lon_even_ref, lat_even_ref, lat_odd_ref, corner_even_ref)
 
     def body(pair, at):
-        scores = times(stacked(0, at, k_ref, *parts), scaled(q_ref[:, at])) + two_tables(table_ref, pair, pl.ds(0, NEAR))
+        scores = times(stacked(0, at, k_ref, *parts), scaled(q_ref[:, at])) + two_tables(table_ref, pair, pl.ds(0, EARLY))
         grad_prob = times(stacked(1, at, v_ref, *parts), both_heads(g_ref[:, at]))
         largest = jnp.max(scores, axis=0, keepdims=True)
         raised = jnp.exp(scores - largest)
@@ -289,15 +290,11 @@
 
 
 def corner_kernel(
-    q_ref, g_ref, corner_even_ref, corner_odd_ref, table_ref, near_stats_ref,
-    raised_ref, prob_ref, stats_ref, send_even_ref, send_odd_ref, lines_ref,
+    q_ref, g_ref, corner_ref, table_ref, near_stats_ref, raised_ref, prob_ref, stats_ref, send_even_ref, send_odd_ref, lines_ref
 ):
     def score(pair, at):
-        keys, values = (
-            jnp.concatenate([corner_even_ref[slot, :, at], corner_odd_ref[slot, :, at]], axis=0) for slot in (0, 1)
-        )
-        scores = times(keys, scaled(q_ref[:, at])) + two_tables(table_ref, pair, pl.ds(NEAR, AROUND - NEAR))
-        return scores, times(values, both_heads(g_ref[:, at]))
+        scores = times(corner_ref[0, :, at], scaled(q_ref[:, at])) + two_tables(table_ref, pair, pl.ds(EARLY, AROUND - EARLY))
+        return scores, times(corner_ref[1, :, at], both_heads(g_ref[:, at]))
 
     scored = over_pairs(q_ref.shape[1], score)
     for pair, (scores, grad_prob) in enumerate(scored):
@@ -369,26 +366,40 @@
     over_pairs(q_ref.shape[1], body)
 
 
+def side_terms(pair, at, lanes, scores_ref, prob_ref, lines_ref, band_q_ref, band_g_ref):
+    log_total, row_dot = band_lines((lines_ref,), pair)
+    weights, dscore = score_gradient(
+        jnp.exp(scores_ref[pair, :, lanes] - log_total), prob_ref[pair, :, lanes], row_dot
+    )
+    return [
+        jnp.dot(coefficients, other[pair, lanes], preferred_element_type=F32)
+        for coefficients, other in ((dscore, band_q_ref), (weights, band_g_ref))
+    ]
+
+
+def side_even_kernel(dlon_ref, scores_ref, prob_ref, band_q_ref, band_g_ref, lines_ref, sum_ref):
+    def body(pair, at):
+        terms = side_terms(pair, at, pl.ds(0, 2 * CELLS), scores_ref, prob_ref, lines_ref, band_q_ref, band_g_ref)
+        for slot, term in enumerate(terms):
+            sum_ref[slot, :, at] = dlon_ref[slot, :, at] + term
+
+    over_pairs(dlon_ref.shape[2], body)
+
+
 def side_band_kernel(
-    dlon_ref, scores_ref, prob_ref, band_q_ref, band_g_ref, lines_even_ref, lines_odd_ref, send_odd_ref, send_even_ref
+    sum_ref, scores_ref, prob_ref, band_q_ref, band_g_ref, lines_ref, send_odd_ref, send_even_ref
 ):
-    lines_refs = (lines_even_ref, lines_odd_ref)
-
-    def score(pair, at):
-        log_total, row_dot = band_lines(lines_refs, pair)
-        return score_gradient(jnp.exp(scores_ref[pair] - log_total), prob_ref[pair], row_dot)
-
-    width = dlon_ref.shape[2]
-    scored = over_pairs(width, score)
-
-    def finish(pair, at):
-        weights, dscore = scored[pair]
-        for slot, coefficients, other in ((0, dscore, band_q_ref), (1, weights, band_g_ref)):
-            total = dlon_ref[slot, :, at] + jnp.dot(coefficients, other[pair], preferred_element_type=F32)
-            send_odd_ref[slot, :, at] = total[:SIDE].astype(BF16)
-            send_even_ref[slot, :, at] = total[SIDE:].astype(BF16)
-
-    over_pairs(width, finish)
+    def body(pair, at):
+        return side_terms(
+            pair, at, pl.ds(2 * CELLS, 2 * CELLS), scores_ref, prob_ref, lines_ref, band_q_ref, band_g_ref
+        )
+
+    for pair, terms in enumerate(over_pairs(sum_ref.shape[2], body)):
+        at = pl.ds(pair * PAIR, PAIR)
+        for slot, term in enumerate(terms):
+            total = (sum_ref[slot, :, at] + term).astype(BF16)
+            send_odd_ref[slot, :, at] = total[:SIDE]
+            send_even_ref[slot, :, at] = total[SIDE:]
 
 
 def own_kernel(
@@ -403,7 +414,7 @@
         return mine.T
 
     def body(pair, at):
-        nearby = near_gradient(raised_ref, prob_ref, stats_ref, pair, pl.ds(0, NEAR))
+        nearby = near_gradient(raised_ref, prob_ref, stats_ref, pair, pl.ds(0, EARLY))
         far = score_gradient(
             corner_raised_ref[pair] * stats_ref[pair, 2:3], corner_prob_ref[pair], stats_ref[pair, 1:2]
         )
@@ -435,23 +446,23 @@
     over_pairs(k_ref.shape[1], finish)
 
 
-def final_kernel(total_ref, side_even_ref, side_odd_ref, dk_ref, dv_ref):
-    lon_odd = is_odd("lon")
+def spread_matrix(first_col):
     shape = (CELLS, SIDE)
     cell = lax.broadcasted_iota(jnp.int32, shape, 0)
     place = lax.broadcasted_iota(jnp.int32, shape, 1)
-
-    def spread(first_col):
-        return (cell == (place % ROWS) * COLS + first_col + place // ROWS).astype(BF16)
-
-    spread_odd = spread(jnp.where(lon_odd, COLS - RADIUS, 0))
-    spread_even = spread(jnp.where(lon_odd, 0, COLS - RADIUS))
+    return (cell == (place % ROWS) * COLS + first_col + place // ROWS).astype(BF16)
+
+
+def blend_kernel(total_ref, side_even_ref, blended_ref):
+    spread = spread_matrix(jnp.where(is_odd("lon"), 0, COLS - RADIUS))
+    for slot in (0, 1):
+        blended_ref[slot] = total_ref[slot] + jnp.dot(spread, side_even_ref[slot], preferred_element_type=F32)
+
+
+def final_kernel(blended_ref, side_odd_ref, dk_ref, dv_ref):
+    spread = spread_matrix(jnp.where(is_odd("lon"), COLS - RADIUS, 0))
     for slot, out in ((0, dk_ref), (1, dv_ref)):
-        total = (
-            total_ref[slot]
-            + jnp.dot(spread_odd, side_odd_ref[slot], preferred_element_type=F32)
-            + jnp.dot(spread_even, side_even_ref[slot], preferred_element_type=F32)
-        )
+        total = blended_ref[slot] + jnp.dot(spread, side_odd_ref[slot], preferred_element_type=F32)
         out[...] = total.astype(BF16)
 
 
@@ -515,21 +526,21 @@
         return [arr((pairs, rows, 2 * CELLS), F32)] * 2 + [arr((pairs, 8, 2 * CELLS), F32)]
 
     near = [k, v, lon_odd, lon_even, lat_even, lat_odd]
-    raised, prob, near_stats = call(near_kernel, "near", [q, g, *near, table], scored(NEAR), 4 * work * NEAR)
+    raised, prob, near_stats = call(near_kernel, "near", [q, g, *near, corner_even, table], scored(EARLY), 4 * work * EARLY)
     late_q, late_g, _ = barrier((q, g, joined))
     queries_even, queries_odd = call(rows_kernel, "query_rows", [late_q, late_g], [band, band])
+    band_table, = call(
+        band_bias_kernel, "band_table", [rel_bias, queries_odd], [arr((2, heads, LAT_AT, CELLS), F32)],
+        2 * heads * LAT_AT * CELLS,
+        scratch_shapes=spread,
+    )
+    table, band_table = barrier((table, band_table))
     queries_even = pair_exchange(queries_even, "lat", 0, False)
     queries_odd = odd_rows_exchange(queries_odd)
-    band_table, = call(
-        band_bias_kernel, "band_table", [rel_bias, near_stats], [arr((2, heads, LAT_AT, CELLS), F32)],
-        2 * heads * LAT_AT * CELLS,
-        scratch_shapes=spread,
-    )
-    corner_odd, band_table = barrier((corner_odd, band_table))
     lines = arr((4 * pairs, LANES), F32)
     corner_raised, corner_prob, stats, lines_even, lines_odd = call(
-        corner_kernel, "corner", [q, g, corner_even, corner_odd, table, near_stats],
-        scored(AROUND - NEAR) + [lines, arr((2 * lines.shape[0], LANES), F32)], 4 * work * (AROUND - NEAR),
+        corner_kernel, "corner", [q, g, corner_odd, table, near_stats],
+        scored(AROUND - EARLY) + [lines, arr((2 * lines.shape[0], LANES), F32)], 4 * work * (AROUND - EARLY),
         scratch_shapes=[pltpu.VMEM(lines.shape, F32)],
     )
     lines_even = pair_exchange(lines_even, "lat", 0, False)
@@ -541,10 +552,14 @@
         [q, g, raised, prob, stats, lon_odd, lon_even, queries_even, queries_odd, band_table],
         [arr(corner.shape, F32), *band_scores, *masked], 16 * work * SIDE,
     )
+    dlon, = call(
+        side_even_kernel, "side_even", [dlon, side_scores, side_prob, band_q, band_g, lines_even],
+        [arr(corner.shape, F32)], 8 * work * SIDE,
+    )
     lines_odd, dlon = barrier((lines_odd, dlon))
     send_odd, send_even = call(
-        side_band_kernel, "side_band", [dlon, side_scores, side_prob, band_q, band_g, lines_even, lines_odd], [side, side],
-        16 * work * SIDE,
+        side_band_kernel, "side_band", [dlon, side_scores, side_prob, band_q, band_g, lines_odd], [side, side],
+        8 * work * SIDE,
     )
     side_even = pair_exchange(send_even, "lon", 0, True)
     side_odd = pair_exchange(send_odd, "lon", 1, True)
@@ -556,7 +571,8 @@
         own_band_kernel, "own_band", [k, v, band_q, band_g, band_table, lines_even, lines_odd, own],
         [arr((2, CELLS, feat), F32)], 8 * work * CELLS,
     )
-    dk, dv = call(final_kernel, "final", [total, side_even, side_odd], [cells, cells])
+    blended, = call(blend_kernel, "blend", [total, side_even], [arr((2, CELLS, feat), F32)])
+    dk, dv = call(final_kernel, "final", [blended, side_odd], [cells, cells])
     return tuple(x.reshape(block) for x in (out, dq, dk, dv))
 
 

time: 32.6 us -> 31.7 us (0.972)
  Pallas kernels: 11.1 us -> 10.7 us
  starting transfers between devices: 14.7 us -> 14.3 us
    ppermute x10, waiting for transfers between devices: 4.7 us -> 4.29 us  [pair_exchange(): return lax.ppermute(value, axis, pairs)]
    ppermute x2, starting transfers between devices: 0.98 us -> 0.58 us  [odd_rows_exchange(): return lax.ppermute(value, ('lat', 'lon'), pairs)]
    pallas_call x13 -> x15, Pallas kernels: 11.1 us -> 10.7 us  [call(): pl.pallas_call(kernel, out_shape=results, compiler_params=pltpu.CompilerP...]
  transfers between devices with their start and end apart: 12 -> 12, of which waited for: 6 -> 5; matrix products, arithmetic and copies ran while one was open for 0% -> 0% of each run, Pallas kernels for 26% -> 26%
where the time goes in v9:
time: 31.7 us; the launch traced here: 31.6 us
  starting transfers between devices  14.3 us (45%)
  Pallas kernels  10.7 us (34%)
  waiting for transfers between devices  5.77 us (18%)
  between operations  0.78 us (2%)
    ppermute x10, starting transfers between devices, pair_exchange(): return lax.ppermute(value, axis, pairs)  13.7 us
    pallas_call x15, Pallas kernels, call(): pl.pallas_call(kernel, out_shape=results, compiler_params=pltpu.CompilerP...  10.7 us
    ppermute x10, waiting for transfers between devices, pair_exchange(): return lax.ppermute(value, axis, pairs)  4.29 us
    ppermute x2, waiting for transfers between devices, odd_rows_exchange(): return lax.ppermute(value, ('lat', 'lon'), pairs)  1.49 us
  transfers between devices with their start and end apart: 12, of which 5 were waited for; matrix products, arithmetic and copies ran while one was open for 0% of the time, Pallas kernels for 26%

profile of v9, /device:TPU:0, one launch (start us, length us, event | category | flops | bytes accessed | tf_op | source)
XLA Modules:
  0.0 31.6 jit_solution(11177904897998276747)
XLA Ops:
  0.6 1.3 %pack.1 = (bf16[2,48,512]{2,1,0:T(8,128)(2,1)S(1)}, bf16[2,48,512]{2,1,0:T(8,128)(2,1)S(1)}, bf16[128,512]{1,0:T(8,128)(2,1)S(1)}, bf16[128,512]{1,0:T(8,128)(2,1)S(1)}, f32[8,169]{1,0:T(8,128)S(1)}) custom-call(bf16[128,512]{1,0:T(8,128)(2,1)} %bitcast.8, bf16[128,512]{1,0:T(8,128)(2,1)} %bitcast.9, f32[8,169]{1,0:T(8,128)} %bias_hbm.1), custom_call_target="tpu_custom_call" | custom-call | bytes 267552 | tf_op jit(solution)/shard_map/pack/pallas_call | solution.py:475
  1.9 6.1 %collective-permute-start = (bf16[2,48,512]{2,1,0:T(8,128)(2,1)S(1)}, bf16[2,48,512]{2,1,0:T(8,128)(2,1)S(1)}, u32[]{:S(2)}, u32[]{:S(2)}) collective-permute-start(bf16[2,48,512]{2,1,0:T(8,128)(2,1)S(1)} %get-tuple-element.50), channel_id=1, source_target_pairs={{1,2},{2,1},{3,4},{4,3},{5,6},{6,5},{7,0},{0,7},{9,10},{10,9},{11,... | collective-permute-start | bytes 294920 | tf_op jit(solution)/shard_map/ppermute | solution.py:44
  8.0 0.0 collective-permute-start.1
  8.0 0.1 collective-permute-start.2
  8.1 1.6 %collective-permute-start.3 = (bf16[2,96,512]{2,1,0:T(8,128)(2,1)S(1)}, bf16[2,96,512]{2,1,0:T(8,128)(2,1)S(1)}, u32[]{:S(2)}, u32[]{:S(2)}) collective-permute-start(bf16[2,96,512]{2,1,0:T(8,128)(2,1)S(1)} %get-tuple-element.56), channel_id=1, source_target_pairs={{8,16},{16,8},{24,0},{0,24},{9,17},{17,9},{25,1},{1,25},{10,18},{1... | collective-permute-start | bytes 589832 | tf_op jit(solution)/shard_map/ppermute | solution.py:44
  9.7 1.6 %bias_table.1 = (f32[8,608,128]{2,1,0:T(8,128)S(1)}, bf16[128,512]{1,0:T(8,128)(2,1)S(1)}, bf16[128,512]{1,0:T(8,128)(2,1)S(1)}) custom-call(f32[8,169]{1,0:T(8,128)S(1)} %get-tuple-element.45.bias_ref, bf16[128,512]{1,0:T(8,128)(2,1)} %bitcast.10, bf16[128,512]{1,0:T(8,128)(2,1)} %bitcast.11), custom_call_target="tpu_custom_call" | custom-call | flops 622592 | bytes 267552 | tf_op jit(solution)/shard_map/bias_table/pallas_call | solution.py:475
  11.3 0.0 collective-permute-done.lon_odd_ref
  11.3 1.6 %collective-permute-done.1.lon_even_ref = bf16[2,48,512]{2,1,0:T(8,128)(2,1)S(1)} collective-permute-done((bf16[2,48,512]{2,1,0:T(8,128)(2,1)S(1)}, bf16[2,48,512]{2,1,0:T(8,128)(2,1)S(1)}, u32[]{:S(2)}, u32[]{:S(2)}) %collective-permute-start.1) | collective-permute-done | bytes 98336 | tf_op jit(solution)/shard_map/ppermute | solution.py:44
  12.9 0.1 collective-permute-start.4
  13.0 0.1 collective-permute-start.5
  13.1 1.6 %collective-permute-start.6 = (bf16[2,96,512]{2,1,0:T(8,128)(2,1)S(1)}, bf16[2,96,512]{2,1,0:T(8,128)(2,1)S(1)}, u32[]{:S(2)}, u32[]{:S(2)}) collective-permute-start(bf16[2,96,512]{2,1,0:T(8,128)(2,1)S(1)} %get-tuple-element.70), channel_id=1, source_target_pairs={{0,8},{8,0},{16,24},{24,16},{1,9},{9,1},{17,25},{25,17},{2,10},{10... | collective-permute-start | bytes 589832 | tf_op jit(solution)/shard_map/ppermute | solution.py:44
  14.7 0.0 collective-permute-done.2.lat_even_ref
  14.7 0.5 %collective-permute-start.7 = (bf16[2,96,512]{2,1,0:T(8,128)(2,1)S(1)}, bf16[2,96,512]{2,1,0:T(8,128)(2,1)S(1)}, u32[]{:S(2)}, u32[]{:S(2)}) collective-permute-start(bf16[2,96,512]{2,1,0:T(8,128)(2,1)S(1)} %get-tuple-element.62.after_ref), channel_id=1, source_target_pairs={{0,2},{1,3},{2,0},{3,1},{4,6},{5,7},{6,4},{7,5},{8,16},{9,17},{10,... | collective-permute-start | bytes 589832 | tf_op jit(solution)/shard_map/ppermute | solution.py:56
  15.2 1.4 %band_table.1.table_ref = f32[2,8,224,128]{3,2,1,0:T(8,128)S(1)} custom-call(f32[8,169]{1,0:T(8,128)S(1)} %get-tuple-element.45.bias_ref, bf16[2,96,512]{2,1,0:T(8,128)(2,1)S(1)} %get-tuple-element.62.after_ref), custom_call_target="tpu_custom_call" | custom-call | flops 458752 | bytes 202016 | tf_op jit(solution)/shard_map/band_table/pallas_call | solution.py:475
  16.7 0.0 collective-permute-done.3.lat_odd_ref
  16.7 0.0 collective-permute-done.4.corner_even_ref
  16.7 1.1 %near.1 = (f32[4,512,256]{2,1,0:T(8,128)S(1)}, f32[4,512,256]{2,1,0:T(8,128)S(1)}, f32[4,8,256]{2,1,0:T(8,128)S(1)}) custom-call(bf16[128,512]{1,0:T(8,128)(2,1)S(1)} %get-tuple-element.60.q_ref.k_ref, bf16[128,512]{1,0:T(8,128)(2,1)S(1)} %get-tuple-element.61.g_ref.v_ref, bf16[128,512]{1,0:T(8,128)(2,1)S(1)} %get-tuple-element.48.k_ref, ...), custom_call_target="tpu_custom_call" | custom-call | flops 268435456 | bytes 3801088 | tf_op jit(solution)/shard_map/near/pallas_call | solution.py:475
  17.8 0.9 %collective-permute-done.5.corner_ref.corner_odd_ref = bf16[2,96,512]{2,1,0:T(8,128)(2,1)S(1)} collective-permute-done((bf16[2,96,512]{2,1,0:T(8,128)(2,1)S(1)}, bf16[2,96,512]{2,1,0:T(8,128)(2,1)S(1)}, u32[]{:S(2)}, u32[]{:S(2)}) %collective-permute-start.5) | collective-permute-done | bytes 196640 | tf_op jit(solution)/shard_map/ppermute | solution.py:56
  18.7 0.5 %corner.1 = (f32[4,96,256]{2,1,0:T(8,128)S(1)}, f32[4,96,256]{2,1,0:T(8,128)S(1)}, f32[4,8,256]{2,1,0:T(8,128)S(1)}, f32[16,128]{1,0:T(8,128)S(1)}, f32[32,128]{1,0:T(8,128)S(1)}) custom-call(bf16[128,512]{1,0:T(8,128)(2,1)S(1)} %get-tuple-element.60.q_ref.k_ref, bf16[128,512]{1,0:T(8,128)(2,1)S(1)} %get-tuple-element.61.g_ref.v_ref, ...), custom_call_target="tpu_custom_call" | custom-call | flops 50331648 | bytes 2981888 | tf_op jit(solution)/shard_map/corner/pallas_call | solution.py:475
  19.2 0.7 %collective-permute-start.9 = (f32[32,128]{1,0:T(8,128)S(1)}, f32[32,128]{1,0:T(8,128)S(1)}, u32[]{:S(2)}, u32[]{:S(2)}) collective-permute-start(f32[32,128]{1,0:T(8,128)S(1)} %get-tuple-element.75), channel_id=1, source_target_pairs={{8,16},{16,8},{24,0},{0,24},{9,17},{17,9},{25,1},{1,25},{10,18},{1... | collective-permute-start | bytes 49160 | tf_op jit(solution)/shard_map/ppermute | solution.py:44
  19.9 0.4 %collective-permute-start.8 = (f32[16,128]{1,0:T(8,128)S(1)}, f32[16,128]{1,0:T(8,128)S(1)}, u32[]{:S(2)}, u32[]{:S(2)}) collective-permute-start(f32[16,128]{1,0:T(8,128)S(1)} %get-tuple-element.74), channel_id=1, source_target_pairs={{0,8},{8,0},{16,24},{24,16},{1,9},{9,1},{17,25},{25,17},{2,10},{10... | collective-permute-start | bytes 24584 | tf_op jit(solution)/shard_map/ppermute | solution.py:44
  20.2 0.0 collective-permute-done.6.queries_even_ref
  20.2 0.6 %collective-permute-done.7.queries_odd_ref = bf16[2,96,512]{2,1,0:T(8,128)(2,1)S(1)} collective-permute-done((bf16[2,96,512]{2,1,0:T(8,128)(2,1)S(1)}, bf16[2,96,512]{2,1,0:T(8,128)(2,1)S(1)}, u32[]{:S(2)}, u32[]{:S(2)}) %collective-permute-start.7) | collective-permute-done | bytes 196640 | tf_op jit(solution)/shard_map/ppermute | solution.py:56
  20.8 0.9 %side_scores.1 = (f32[2,96,512]{2,1,0:T(8,128)S(1)}, f32[4,96,512]{2,1,0:T(8,128)S(1)}, f32[4,96,512]{2,1,0:T(8,128)S(1)}, bf16[4,512,128]{2,1,0:T(8,128)(2,1)S(1)}, bf16[4,512,128]{2,1,0:T(8,128)(2,1)S(1)}) custom-call(bf16[128,512]{1,0:T(8,128)(2,1)S(1)} %get-tuple-element.60.q_ref.k_ref, bf16[128,512]{1,0:T(8,128)(2,1)S(1)} %get-tuple-element.61.g_ref.v_ref, ...), custom_call_target="tpu_custom_call" | custom-call | flops 100663296 | bytes 6914048 | tf_op jit(solution)/shard_map/side_scores/pallas_call | solution.py:475
  21.7 0.0 collective-permute-done.8.lines_ref.lines_even_ref
  21.7 0.3 side_even.1.sum_ref
  22.0 0.4 %collective-permute-done.9.lines_odd_ref.lines_ref = f32[32,128]{1,0:T(8,128)S(1)} collective-permute-done((f32[32,128]{1,0:T(8,128)S(1)}, f32[32,128]{1,0:T(8,128)S(1)}, u32[]{:S(2)}, u32[]{:S(2)}) %collective-permute-start.9) | collective-permute-done | bytes 16416 | tf_op jit(solution)/shard_map/ppermute | solution.py:44
  22.3 0.3 side_band.1
  22.6 0.5 %collective-permute-start.10 = (bf16[2,48,512]{2,1,0:T(8,128)(2,1)S(1)}, bf16[2,48,512]{2,1,0:T(8,128)(2,1)S(1)}, u32[]{:S(2)}, u32[]{:S(2)}) collective-permute-start(bf16[2,48,512]{2,1,0:T(8,128)(2,1)S(1)} %get-tuple-element.82), channel_id=1, source_target_pairs={{0,1},{1,0},{2,3},{3,2},{4,5},{5,4},{6,7},{7,6},{8,9},{9,8},{10,11... | collective-permute-start | bytes 294920 | tf_op jit(solution)/shard_map/ppermute | solution.py:44
  23.1 2.7 %collective-permute-start.11 = (bf16[2,48,512]{2,1,0:T(8,128)(2,1)S(1)}, bf16[2,48,512]{2,1,0:T(8,128)(2,1)S(1)}, u32[]{:S(2)}, u32[]{:S(2)}) collective-permute-start(bf16[2,48,512]{2,1,0:T(8,128)(2,1)S(1)} %get-tuple-element.83), channel_id=1, source_target_pairs={{1,2},{2,1},{3,4},{4,3},{5,6},{6,5},{7,0},{0,7},{9,10},{10,9},{11,... | collective-permute-start | bytes 294920 | tf_op jit(solution)/shard_map/ppermute | solution.py:44
  25.8 1.6 %own.1 = (bf16[128,512]{1,0:T(8,128)(2,1)}, bf16[128,512]{1,0:T(8,128)(2,1)}, f32[2,128,512]{2,1,0:T(8,128)S(1)}) custom-call(bf16[128,512]{1,0:T(8,128)(2,1)S(1)} %get-tuple-element.60.q_ref.k_ref, bf16[128,512]{1,0:T(8,128)(2,1)S(1)} %get-tuple-element.61.g_ref.v_ref, bf16[128,512]{1,0:T(8,128)(2,1)S(1)} %get-tuple-element.48.k_ref, ...), custom_call_target="tpu_custom_call" | custom-call | flops 318767104 | bytes 6520832 | tf_op jit(solution)/shard_map/own/pallas_call | solution.py:475
  27.4 0.7 %own_band.1.total_ref = f32[2,128,512]{2,1,0:T(8,128)S(1)} custom-call(bf16[128,512]{1,0:T(8,128)(2,1)S(1)} %get-tuple-element.48.k_ref, bf16[128,512]{1,0:T(8,128)(2,1)S(1)} %get-tuple-element.49.v_ref, bf16[4,512,128]{2,1,0:T(8,128)(2,1)S(1)} %get-tuple-element.72.band_q_ref, bf16[4,512,128]{2,1,0:T(8,128)(2,1)S(1)} %get-tuple-element.73.band_g_ref, ...), custom_call_target="tpu_custom_call" | custom-call | flops 134217728 | bytes 3694592 | tf_op jit(solution)/shard_map/own_band/pallas_call | solution.py:475
  28.1 0.0 collective-permute-done.10.side_even_ref
  28.2 0.2 blend.1.blended_ref
  28.4 2.3 %collective-permute-done.11.side_odd_ref = bf16[2,48,512]{2,1,0:T(8,128)(2,1)S(1)} collective-permute-done((bf16[2,48,512]{2,1,0:T(8,128)(2,1)S(1)}, bf16[2,48,512]{2,1,0:T(8,128)(2,1)S(1)}, u32[]{:S(2)}, u32[]{:S(2)}) %collective-permute-start.11) | collective-permute-done | bytes 98336 | tf_op jit(solution)/shard_map/ppermute | solution.py:44
  30.7 0.9 %final.1 = (bf16[128,512]{1,0:T(8,128)(2,1)}, bf16[128,512]{1,0:T(8,128)(2,1)}) custom-call(f32[2,128,512]{2,1,0:T(8,128)S(1)} %blend.1.blended_ref, bf16[2,48,512]{2,1,0:T(8,128)(2,1)S(1)} %collective-permute-done.11.side_odd_ref), custom_call_target="tpu_custom_call" | custom-call | bytes 622592 | tf_op jit(solution)/shard_map/final/pallas_call | solution.py:475
  (3 shorter events, 0.1 us)
Async XLA Ops:
  1.9 9.4 %collective-permute-start = (bf16[2,48,512]{2,1,0:T(8,128)(2,1)S(1)}, bf16[2,48,512]{2,1,0:T(8,128)(2,1)S(1)}, u32[]{:S(2)}, u32[]{:S(2)}) collective-permute-start(bf16[2,48,512]{2,1,0:T(8,128)(2,1)S(1)} %get-tuple-element.50), channel_id=1, source_target_pairs={{1,2},{2,1},{3,4},{4,3},{5,6},{6,5},{7,0},{0,7},{9,10},{10,9},{11,... | collective-permute-start | bytes 294920 | tf_op jit(solution)/shard_map/ppermute | solution.py:44
  8.0 4.9 %collective-permute-start.1 = (bf16[2,48,512]{2,1,0:T(8,128)(2,1)S(1)}, bf16[2,48,512]{2,1,0:T(8,128)(2,1)S(1)}, u32[]{:S(2)}, u32[]{:S(2)}) collective-permute-start(bf16[2,48,512]{2,1,0:T(8,128)(2,1)S(1)} %get-tuple-element.51), channel_id=1, source_target_pairs={{0,1},{1,0},{2,3},{3,2},{4,5},{5,4},{6,7},{7,6},{8,9},{9,8},{10,11... | collective-permute-start | bytes 294920 | tf_op jit(solution)/shard_map/ppermute | solution.py:44
  8.0 6.7 %collective-permute-start.2 = (bf16[2,96,512]{2,1,0:T(8,128)(2,1)S(1)}, bf16[2,96,512]{2,1,0:T(8,128)(2,1)S(1)}, u32[]{:S(2)}, u32[]{:S(2)}) collective-permute-start(bf16[2,96,512]{2,1,0:T(8,128)(2,1)S(1)} %get-tuple-element.55), channel_id=1, source_target_pairs={{0,8},{8,0},{16,24},{24,16},{1,9},{9,1},{17,25},{25,17},{2,10},{10... | collective-permute-start | bytes 589832 | tf_op jit(solution)/shard_map/ppermute | solution.py:44
  8.1 8.6 %collective-permute-start.3 = (bf16[2,96,512]{2,1,0:T(8,128)(2,1)S(1)}, bf16[2,96,512]{2,1,0:T(8,128)(2,1)S(1)}, u32[]{:S(2)}, u32[]{:S(2)}) collective-permute-start(bf16[2,96,512]{2,1,0:T(8,128)(2,1)S(1)} %get-tuple-element.56), channel_id=1, source_target_pairs={{8,16},{16,8},{24,0},{0,24},{9,17},{17,9},{25,1},{1,25},{10,18},{1... | collective-permute-start | bytes 589832 | tf_op jit(solution)/shard_map/ppermute | solution.py:44
  12.9 3.8 %collective-permute-start.4 = (bf16[2,96,512]{2,1,0:T(8,128)(2,1)S(1)}, bf16[2,96,512]{2,1,0:T(8,128)(2,1)S(1)}, u32[]{:S(2)}, u32[]{:S(2)}) collective-permute-start(bf16[2,96,512]{2,1,0:T(8,128)(2,1)S(1)} %join.1), channel_id=1, source_target_pairs={{0,8},{8,0},{16,24},{24,16},{1,9},{9,1},{17,25},{25,17},{2,10},{10... | collective-permute-start | bytes 589832 | tf_op jit(solution)/shard_map/ppermute | solution.py:44
  13.0 5.7 %collective-permute-start.5 = (bf16[2,96,512]{2,1,0:T(8,128)(2,1)S(1)}, bf16[2,96,512]{2,1,0:T(8,128)(2,1)S(1)}, u32[]{:S(2)}, u32[]{:S(2)}) collective-permute-start(bf16[2,96,512]{2,1,0:T(8,128)(2,1)S(1)} %join.1), channel_id=1, source_target_pairs={{0,2},{1,3},{2,0},{3,1},{4,6},{5,7},{6,4},{7,5},{8,16},{9,17},{10,... | collective-permute-start | bytes 589832 | tf_op jit(solution)/shard_map/ppermute | solution.py:56
  13.1 7.1 %collective-permute-start.6 = (bf16[2,96,512]{2,1,0:T(8,128)(2,1)S(1)}, bf16[2,96,512]{2,1,0:T(8,128)(2,1)S(1)}, u32[]{:S(2)}, u32[]{:S(2)}) collective-permute-start(bf16[2,96,512]{2,1,0:T(8,128)(2,1)S(1)} %get-tuple-element.70), channel_id=1, source_target_pairs={{0,8},{8,0},{16,24},{24,16},{1,9},{9,1},{17,25},{25,17},{2,10},{10... | collective-permute-start | bytes 589832 | tf_op jit(solution)/shard_map/ppermute | solution.py:44
  14.7 6.1 %collective-permute-start.7 = (bf16[2,96,512]{2,1,0:T(8,128)(2,1)S(1)}, bf16[2,96,512]{2,1,0:T(8,128)(2,1)S(1)}, u32[]{:S(2)}, u32[]{:S(2)}) collective-permute-start(bf16[2,96,512]{2,1,0:T(8,128)(2,1)S(1)} %get-tuple-element.62.after_ref), channel_id=1, source_target_pairs={{0,2},{1,3},{2,0},{3,1},{4,6},{5,7},{6,4},{7,5},{8,16},{9,17},{10,... | collective-permute-start | bytes 589832 | tf_op jit(solution)/shard_map/ppermute | solution.py:56
  19.2 3.2 %collective-permute-start.9 = (f32[32,128]{1,0:T(8,128)S(1)}, f32[32,128]{1,0:T(8,128)S(1)}, u32[]{:S(2)}, u32[]{:S(2)}) collective-permute-start(f32[32,128]{1,0:T(8,128)S(1)} %get-tuple-element.75), channel_id=1, source_target_pairs={{8,16},{16,8},{24,0},{0,24},{9,17},{17,9},{25,1},{1,25},{10,18},{1... | collective-permute-start | bytes 49160 | tf_op jit(solution)/shard_map/ppermute | solution.py:44
  19.9 1.9 %collective-permute-start.8 = (f32[16,128]{1,0:T(8,128)S(1)}, f32[16,128]{1,0:T(8,128)S(1)}, u32[]{:S(2)}, u32[]{:S(2)}) collective-permute-start(f32[16,128]{1,0:T(8,128)S(1)} %get-tuple-element.74), channel_id=1, source_target_pairs={{0,8},{8,0},{16,24},{24,16},{1,9},{9,1},{17,25},{25,17},{2,10},{10... | collective-permute-start | bytes 24584 | tf_op jit(solution)/shard_map/ppermute | solution.py:44
  22.6 5.5 %collective-permute-start.10 = (bf16[2,48,512]{2,1,0:T(8,128)(2,1)S(1)}, bf16[2,48,512]{2,1,0:T(8,128)(2,1)S(1)}, u32[]{:S(2)}, u32[]{:S(2)}) collective-permute-start(bf16[2,48,512]{2,1,0:T(8,128)(2,1)S(1)} %get-tuple-element.82), channel_id=1, source_target_pairs={{0,1},{1,0},{2,3},{3,2},{4,5},{5,4},{6,7},{7,6},{8,9},{9,8},{10,11... | collective-permute-start | bytes 294920 | tf_op jit(solution)/shard_map/ppermute | solution.py:44
  23.1 7.6 %collective-permute-start.11 = (bf16[2,48,512]{2,1,0:T(8,128)(2,1)S(1)}, bf16[2,48,512]{2,1,0:T(8,128)(2,1)S(1)}, u32[]{:S(2)}, u32[]{:S(2)}) collective-permute-start(bf16[2,48,512]{2,1,0:T(8,128)(2,1)S(1)} %get-tuple-element.83), channel_id=1, source_target_pairs={{1,2},{2,1},{3,4},{4,3},{5,6},{6,5},{7,0},{0,7},{9,10},{10,9},{11,... | collective-permute-start | bytes 294920 | tf_op jit(solution)/shard_map/ppermute | solution.py:44

commit v10 on v9

--- a/solution.py
+++ b/solution.py
@@ -230,7 +230,7 @@
 FACTOR = HEAD_DIM ** (-0.5)
 
 
-def join_kernel(lon_odd_ref, lon_even_ref, out_ref):
+def join_kernel(lon_even_ref, lon_odd_ref, out_ref):
     out_ref[:, :SIDE] = lon_odd_ref[...]
     out_ref[:, SIDE:] = lon_even_ref[...]
 
@@ -502,8 +502,8 @@
         in_specs=[hbm] * 3,
         scratch_shapes=[pltpu.SemaphoreType.DMA((3,))],
     )
+    lon_even = pair_exchange(lon_even, "lon", 0, True)
     lon_odd = pair_exchange(lon_odd, "lon", 1, True)
-    lon_even = pair_exchange(lon_even, "lon", 0, True)
     lat_even, lat_odd = call(rows_kernel, "rows", [k, v], [band, band])
     lat_even = pair_exchange(lat_even, "lat", 0, False)
     lat_odd = pair_exchange(lat_odd, "lat", 1, True)
@@ -517,8 +517,8 @@
         scratch_shapes=[*spread, pltpu.SemaphoreType.DMA((2,))],
     )
 
-    lon_odd, lon_even, table = barrier((lon_odd, lon_even, table))
-    joined, = call(join_kernel, "join", [lon_odd, lon_even], [corner], int(2e9))
+    lon_even, lon_odd, table = barrier((lon_even, lon_odd, table))
+    joined, = call(join_kernel, "join", [lon_even, lon_odd], [corner], int(2e9))
     corner_even = pair_exchange(joined, "lat", 0, False)
     corner_odd = odd_rows_exchange(joined)
 

time: 31.7 us -> 30.7 us (0.968)
  waiting for transfers between devices: 5.77 us -> 3.35 us
  starting transfers between devices: 14.3 us -> 15.7 us
    ppermute x10, waiting for transfers between devices: 4.29 us -> 2.32 us  [pair_exchange(): return lax.ppermute(value, axis, pairs)]
    ppermute x10, starting transfers between devices: 13.7 us -> 15.1 us  [pair_exchange(): return lax.ppermute(value, axis, pairs)]
    ppermute x2, waiting for transfers between devices: 1.49 us -> 1.03 us  [odd_rows_exchange(): return lax.ppermute(value, ('lat', 'lon'), pairs)]
  transfers between devices with their start and end apart: 12 -> 12, of which waited for: 5 -> 5; matrix products, arithmetic and copies ran while one was open for 0% -> 0% of each run, Pallas kernels for 26% -> 27%
where the time goes in v10:
time: 30.7 us; the launch traced here: 30.6 us
  starting transfers between devices  15.7 us (51%)
  Pallas kernels  10.7 us (35%)
  waiting for transfers between devices  3.35 us (11%)
  between operations  0.79 us (3%)
    ppermute x10, starting transfers between devices, pair_exchange(): return lax.ppermute(value, axis, pairs)  15.1 us
    pallas_call x15, Pallas kernels, call(): pl.pallas_call(kernel, out_shape=results, compiler_params=pltpu.CompilerP...  10.7 us
    ppermute x10, waiting for transfers between devices, pair_exchange(): return lax.ppermute(value, axis, pairs)  2.32 us
    ppermute x2, waiting for transfers between devices, odd_rows_exchange(): return lax.ppermute(value, ('lat', 'lon'), pairs)  1.03 us
  transfers between devices with their start and end apart: 12, of which 5 were waited for; matrix products, arithmetic and copies ran while one was open for 0% of the time, Pallas kernels for 27%

profile of v10, /device:TPU:0, one launch (start us, length us, event | category | flops | bytes accessed | tf_op | source)
XLA Modules:
  0.0 30.6 jit_solution(8316305131455957491)
XLA Ops:
  0.6 1.3 %pack.1 = (bf16[2,48,512]{2,1,0:T(8,128)(2,1)S(1)}, bf16[2,48,512]{2,1,0:T(8,128)(2,1)S(1)}, bf16[128,512]{1,0:T(8,128)(2,1)S(1)}, bf16[128,512]{1,0:T(8,128)(2,1)S(1)}, f32[8,169]{1,0:T(8,128)S(1)}) custom-call(bf16[128,512]{1,0:T(8,128)(2,1)} %bitcast.8, bf16[128,512]{1,0:T(8,128)(2,1)} %bitcast.9, f32[8,169]{1,0:T(8,128)} %bias_hbm.1), custom_call_target="tpu_custom_call" | custom-call | bytes 267552 | tf_op jit(solution)/shard_map/pack/pallas_call | solution.py:475
  1.9 3.0 %collective-permute-start = (bf16[2,48,512]{2,1,0:T(8,128)(2,1)S(1)}, bf16[2,48,512]{2,1,0:T(8,128)(2,1)S(1)}, u32[]{:S(2)}, u32[]{:S(2)}) collective-permute-start(bf16[2,48,512]{2,1,0:T(8,128)(2,1)S(1)} %get-tuple-element.50), channel_id=1, source_target_pairs={{0,1},{1,0},{2,3},{3,2},{4,5},{5,4},{6,7},{7,6},{8,9},{9,8},{10,11... | collective-permute-start | bytes 294920 | tf_op jit(solution)/shard_map/ppermute | solution.py:44
  4.9 3.5 %collective-permute-start.1 = (bf16[2,48,512]{2,1,0:T(8,128)(2,1)S(1)}, bf16[2,48,512]{2,1,0:T(8,128)(2,1)S(1)}, u32[]{:S(2)}, u32[]{:S(2)}) collective-permute-start(bf16[2,48,512]{2,1,0:T(8,128)(2,1)S(1)} %get-tuple-element.51), channel_id=1, source_target_pairs={{1,2},{2,1},{3,4},{4,3},{5,6},{6,5},{7,0},{0,7},{9,10},{10,9},{11,... | collective-permute-start | bytes 294920 | tf_op jit(solution)/shard_map/ppermute | solution.py:44
  8.5 0.1 collective-permute-start.2
  8.6 1.6 %collective-permute-start.3 = (bf16[2,96,512]{2,1,0:T(8,128)(2,1)S(1)}, bf16[2,96,512]{2,1,0:T(8,128)(2,1)S(1)}, u32[]{:S(2)}, u32[]{:S(2)}) collective-permute-start(bf16[2,96,512]{2,1,0:T(8,128)(2,1)S(1)} %get-tuple-element.56), channel_id=1, source_target_pairs={{8,16},{16,8},{24,0},{0,24},{9,17},{17,9},{25,1},{1,25},{10,18},{1... | collective-permute-start | bytes 589832 | tf_op jit(solution)/shard_map/ppermute | solution.py:44
  10.2 1.6 %bias_table.1 = (f32[8,608,128]{2,1,0:T(8,128)S(1)}, bf16[128,512]{1,0:T(8,128)(2,1)S(1)}, bf16[128,512]{1,0:T(8,128)(2,1)S(1)}) custom-call(f32[8,169]{1,0:T(8,128)S(1)} %get-tuple-element.45.bias_ref, bf16[128,512]{1,0:T(8,128)(2,1)} %bitcast.10, bf16[128,512]{1,0:T(8,128)(2,1)} %bitcast.11), custom_call_target="tpu_custom_call" | custom-call | flops 622592 | bytes 267552 | tf_op jit(solution)/shard_map/bias_table/pallas_call | solution.py:475
  11.8 0.0 collective-permute-done.lon_even_ref
  11.8 0.5 %collective-permute-done.1.lon_odd_ref = bf16[2,48,512]{2,1,0:T(8,128)(2,1)S(1)} collective-permute-done((bf16[2,48,512]{2,1,0:T(8,128)(2,1)S(1)}, bf16[2,48,512]{2,1,0:T(8,128)(2,1)S(1)}, u32[]{:S(2)}, u32[]{:S(2)}) %collective-permute-start.1) | collective-permute-done | bytes 98336 | tf_op jit(solution)/shard_map/ppermute | solution.py:44
  12.3 0.1 collective-permute-start.4
  12.3 0.1 collective-permute-start.5
  12.5 1.6 %collective-permute-start.6 = (bf16[2,96,512]{2,1,0:T(8,128)(2,1)S(1)}, bf16[2,96,512]{2,1,0:T(8,128)(2,1)S(1)}, u32[]{:S(2)}, u32[]{:S(2)}) collective-permute-start(bf16[2,96,512]{2,1,0:T(8,128)(2,1)S(1)} %get-tuple-element.70), channel_id=1, source_target_pairs={{0,8},{8,0},{16,24},{24,16},{1,9},{9,1},{17,25},{25,17},{2,10},{10... | collective-permute-start | bytes 589832 | tf_op jit(solution)/shard_map/ppermute | solution.py:44
  14.1 0.0 collective-permute-done.2.lat_even_ref
  14.1 0.5 %collective-permute-start.7 = (bf16[2,96,512]{2,1,0:T(8,128)(2,1)S(1)}, bf16[2,96,512]{2,1,0:T(8,128)(2,1)S(1)}, u32[]{:S(2)}, u32[]{:S(2)}) collective-permute-start(bf16[2,96,512]{2,1,0:T(8,128)(2,1)S(1)} %get-tuple-element.62.after_ref), channel_id=1, source_target_pairs={{0,2},{1,3},{2,0},{3,1},{4,6},{5,7},{6,4},{7,5},{8,16},{9,17},{10,... | collective-permute-start | bytes 589832 | tf_op jit(solution)/shard_map/ppermute | solution.py:56
  14.6 1.4 %band_table.1.table_ref = f32[2,8,224,128]{3,2,1,0:T(8,128)S(1)} custom-call(f32[8,169]{1,0:T(8,128)S(1)} %get-tuple-element.45.bias_ref, bf16[2,96,512]{2,1,0:T(8,128)(2,1)S(1)} %get-tuple-element.62.after_ref), custom_call_target="tpu_custom_call" | custom-call | flops 458752 | bytes 202016 | tf_op jit(solution)/shard_map/band_table/pallas_call | solution.py:475
  16.1 0.0 collective-permute-done.3.lat_odd_ref
  16.1 0.0 collective-permute-done.4.corner_even_ref
  16.1 1.1 %near.1 = (f32[4,512,256]{2,1,0:T(8,128)S(1)}, f32[4,512,256]{2,1,0:T(8,128)S(1)}, f32[4,8,256]{2,1,0:T(8,128)S(1)}) custom-call(bf16[128,512]{1,0:T(8,128)(2,1)S(1)} %get-tuple-element.60.q_ref.k_ref, bf16[128,512]{1,0:T(8,128)(2,1)S(1)} %get-tuple-element.61.g_ref.v_ref, bf16[128,512]{1,0:T(8,128)(2,1)S(1)} %get-tuple-element.48.k_ref, ...), custom_call_target="tpu_custom_call" | custom-call | flops 268435456 | bytes 3801088 | tf_op jit(solution)/shard_map/near/pallas_call | solution.py:475
  17.2 0.9 %collective-permute-done.5.corner_ref.corner_odd_ref = bf16[2,96,512]{2,1,0:T(8,128)(2,1)S(1)} collective-permute-done((bf16[2,96,512]{2,1,0:T(8,128)(2,1)S(1)}, bf16[2,96,512]{2,1,0:T(8,128)(2,1)S(1)}, u32[]{:S(2)}, u32[]{:S(2)}) %collective-permute-start.5) | collective-permute-done | bytes 196640 | tf_op jit(solution)/shard_map/ppermute | solution.py:56
  18.1 0.5 %corner.1 = (f32[4,96,256]{2,1,0:T(8,128)S(1)}, f32[4,96,256]{2,1,0:T(8,128)S(1)}, f32[4,8,256]{2,1,0:T(8,128)S(1)}, f32[16,128]{1,0:T(8,128)S(1)}, f32[32,128]{1,0:T(8,128)S(1)}) custom-call(bf16[128,512]{1,0:T(8,128)(2,1)S(1)} %get-tuple-element.60.q_ref.k_ref, bf16[128,512]{1,0:T(8,128)(2,1)S(1)} %get-tuple-element.61.g_ref.v_ref, ...), custom_call_target="tpu_custom_call" | custom-call | flops 50331648 | bytes 2981888 | tf_op jit(solution)/shard_map/corner/pallas_call | solution.py:475
  18.5 0.7 %collective-permute-start.9 = (f32[32,128]{1,0:T(8,128)S(1)}, f32[32,128]{1,0:T(8,128)S(1)}, u32[]{:S(2)}, u32[]{:S(2)}) collective-permute-start(f32[32,128]{1,0:T(8,128)S(1)} %get-tuple-element.75), channel_id=1, source_target_pairs={{8,16},{16,8},{24,0},{0,24},{9,17},{17,9},{25,1},{1,25},{10,18},{1... | collective-permute-start | bytes 49160 | tf_op jit(solution)/shard_map/ppermute | solution.py:44
  19.2 0.8 %collective-permute-start.8 = (f32[16,128]{1,0:T(8,128)S(1)}, f32[16,128]{1,0:T(8,128)S(1)}, u32[]{:S(2)}, u32[]{:S(2)}) collective-permute-start(f32[16,128]{1,0:T(8,128)S(1)} %get-tuple-element.74), channel_id=1, source_target_pairs={{0,8},{8,0},{16,24},{24,16},{1,9},{9,1},{17,25},{25,17},{2,10},{10... | collective-permute-start | bytes 24584 | tf_op jit(solution)/shard_map/ppermute | solution.py:44
  20.0 0.0 collective-permute-done.6.queries_even_ref
  20.0 0.1 collective-permute-done.7.queries_odd_ref
  20.2 0.9 %side_scores.1 = (f32[2,96,512]{2,1,0:T(8,128)S(1)}, f32[4,96,512]{2,1,0:T(8,128)S(1)}, f32[4,96,512]{2,1,0:T(8,128)S(1)}, bf16[4,512,128]{2,1,0:T(8,128)(2,1)S(1)}, bf16[4,512,128]{2,1,0:T(8,128)(2,1)S(1)}) custom-call(bf16[128,512]{1,0:T(8,128)(2,1)S(1)} %get-tuple-element.60.q_ref.k_ref, bf16[128,512]{1,0:T(8,128)(2,1)S(1)} %get-tuple-element.61.g_ref.v_ref, ...), custom_call_target="tpu_custom_call" | custom-call | flops 100663296 | bytes 6914048 | tf_op jit(solution)/shard_map/side_scores/pallas_call | solution.py:475
  21.1 0.0 collective-permute-done.8.lines_ref.lines_even_ref
  21.1 0.3 side_even.1.sum_ref
  21.4 0.4 %collective-permute-done.9.lines_odd_ref.lines_ref = f32[32,128]{1,0:T(8,128)S(1)} collective-permute-done((f32[32,128]{1,0:T(8,128)S(1)}, f32[32,128]{1,0:T(8,128)S(1)}, u32[]{:S(2)}, u32[]{:S(2)}) %collective-permute-start.9) | collective-permute-done | bytes 16416 | tf_op jit(solution)/shard_map/ppermute | solution.py:44
  21.7 0.3 side_band.1
  22.0 0.1 collective-permute-start.10
  22.1 3.6 %collective-permute-start.11 = (bf16[2,48,512]{2,1,0:T(8,128)(2,1)S(1)}, bf16[2,48,512]{2,1,0:T(8,128)(2,1)S(1)}, u32[]{:S(2)}, u32[]{:S(2)}) collective-permute-start(bf16[2,48,512]{2,1,0:T(8,128)(2,1)S(1)} %get-tuple-element.83), channel_id=1, source_target_pairs={{1,2},{2,1},{3,4},{4,3},{5,6},{6,5},{7,0},{0,7},{9,10},{10,9},{11,... | collective-permute-start | bytes 294920 | tf_op jit(solution)/shard_map/ppermute | solution.py:44
  25.7 1.6 %own.1 = (bf16[128,512]{1,0:T(8,128)(2,1)}, bf16[128,512]{1,0:T(8,128)(2,1)}, f32[2,128,512]{2,1,0:T(8,128)S(1)}) custom-call(bf16[128,512]{1,0:T(8,128)(2,1)S(1)} %get-tuple-element.60.q_ref.k_ref, bf16[128,512]{1,0:T(8,128)(2,1)S(1)} %get-tuple-element.61.g_ref.v_ref, bf16[128,512]{1,0:T(8,128)(2,1)S(1)} %get-tuple-element.48.k_ref, ...), custom_call_target="tpu_custom_call" | custom-call | flops 318767104 | bytes 6520832 | tf_op jit(solution)/shard_map/own/pallas_call | solution.py:475
  27.3 0.7 %own_band.1.total_ref = f32[2,128,512]{2,1,0:T(8,128)S(1)} custom-call(bf16[128,512]{1,0:T(8,128)(2,1)S(1)} %get-tuple-element.48.k_ref, bf16[128,512]{1,0:T(8,128)(2,1)S(1)} %get-tuple-element.49.v_ref, bf16[4,512,128]{2,1,0:T(8,128)(2,1)S(1)} %get-tuple-element.72.band_q_ref, bf16[4,512,128]{2,1,0:T(8,128)(2,1)S(1)} %get-tuple-element.73.band_g_ref, ...), custom_call_target="tpu_custom_call" | custom-call | flops 134217728 | bytes 3694592 | tf_op jit(solution)/shard_map/own_band/pallas_call | solution.py:475
  28.0 0.0 collective-permute-done.10.side_even_ref
  28.0 0.2 blend.1.blended_ref
  28.2 1.5 %collective-permute-done.11.side_odd_ref = bf16[2,48,512]{2,1,0:T(8,128)(2,1)S(1)} collective-permute-done((bf16[2,48,512]{2,1,0:T(8,128)(2,1)S(1)}, bf16[2,48,512]{2,1,0:T(8,128)(2,1)S(1)}, u32[]{:S(2)}, u32[]{:S(2)}) %collective-permute-start.11) | collective-permute-done | bytes 98336 | tf_op jit(solution)/shard_map/ppermute | solution.py:44
  29.7 0.9 %final.1 = (bf16[128,512]{1,0:T(8,128)(2,1)}, bf16[128,512]{1,0:T(8,128)(2,1)}) custom-call(f32[2,128,512]{2,1,0:T(8,128)S(1)} %blend.1.blended_ref, bf16[2,48,512]{2,1,0:T(8,128)(2,1)S(1)} %collective-permute-done.11.side_odd_ref), custom_call_target="tpu_custom_call" | custom-call | bytes 622592 | tf_op jit(solution)/shard_map/final/pallas_call | solution.py:475
  (3 shorter events, 0.1 us)
Async XLA Ops:
  1.9 9.9 %collective-permute-start = (bf16[2,48,512]{2,1,0:T(8,128)(2,1)S(1)}, bf16[2,48,512]{2,1,0:T(8,128)(2,1)S(1)}, u32[]{:S(2)}, u32[]{:S(2)}) collective-permute-start(bf16[2,48,512]{2,1,0:T(8,128)(2,1)S(1)} %get-tuple-element.50), channel_id=1, source_target_pairs={{0,1},{1,0},{2,3},{3,2},{4,5},{5,4},{6,7},{7,6},{8,9},{9,8},{10,11... | collective-permute-start | bytes 294920 | tf_op jit(solution)/shard_map/ppermute | solution.py:44
  4.9 7.3 %collective-permute-start.1 = (bf16[2,48,512]{2,1,0:T(8,128)(2,1)S(1)}, bf16[2,48,512]{2,1,0:T(8,128)(2,1)S(1)}, u32[]{:S(2)}, u32[]{:S(2)}) collective-permute-start(bf16[2,48,512]{2,1,0:T(8,128)(2,1)S(1)} %get-tuple-element.51), channel_id=1, source_target_pairs={{1,2},{2,1},{3,4},{4,3},{5,6},{6,5},{7,0},{0,7},{9,10},{10,9},{11,... | collective-permute-start | bytes 294920 | tf_op jit(solution)/shard_map/ppermute | solution.py:44
  8.5 5.6 %collective-permute-start.2 = (bf16[2,96,512]{2,1,0:T(8,128)(2,1)S(1)}, bf16[2,96,512]{2,1,0:T(8,128)(2,1)S(1)}, u32[]{:S(2)}, u32[]{:S(2)}) collective-permute-start(bf16[2,96,512]{2,1,0:T(8,128)(2,1)S(1)} %get-tuple-element.55), channel_id=1, source_target_pairs={{0,8},{8,0},{16,24},{24,16},{1,9},{9,1},{17,25},{25,17},{2,10},{10... | collective-permute-start | bytes 589832 | tf_op jit(solution)/shard_map/ppermute | solution.py:44
  8.6 7.5 %collective-permute-start.3 = (bf16[2,96,512]{2,1,0:T(8,128)(2,1)S(1)}, bf16[2,96,512]{2,1,0:T(8,128)(2,1)S(1)}, u32[]{:S(2)}, u32[]{:S(2)}) collective-permute-start(bf16[2,96,512]{2,1,0:T(8,128)(2,1)S(1)} %get-tuple-element.56), channel_id=1, source_target_pairs={{8,16},{16,8},{24,0},{0,24},{9,17},{17,9},{25,1},{1,25},{10,18},{1... | collective-permute-start | bytes 589832 | tf_op jit(solution)/shard_map/ppermute | solution.py:44
  12.3 3.8 %collective-permute-start.4 = (bf16[2,96,512]{2,1,0:T(8,128)(2,1)S(1)}, bf16[2,96,512]{2,1,0:T(8,128)(2,1)S(1)}, u32[]{:S(2)}, u32[]{:S(2)}) collective-permute-start(bf16[2,96,512]{2,1,0:T(8,128)(2,1)S(1)} %join.1), channel_id=1, source_target_pairs={{0,8},{8,0},{16,24},{24,16},{1,9},{9,1},{17,25},{25,17},{2,10},{10... | collective-permute-start | bytes 589832 | tf_op jit(solution)/shard_map/ppermute | solution.py:44
  12.3 5.7 %collective-permute-start.5 = (bf16[2,96,512]{2,1,0:T(8,128)(2,1)S(1)}, bf16[2,96,512]{2,1,0:T(8,128)(2,1)S(1)}, u32[]{:S(2)}, u32[]{:S(2)}) collective-permute-start(bf16[2,96,512]{2,1,0:T(8,128)(2,1)S(1)} %join.1), channel_id=1, source_target_pairs={{0,2},{1,3},{2,0},{3,1},{4,6},{5,7},{6,4},{7,5},{8,16},{9,17},{10,... | collective-permute-start | bytes 589832 | tf_op jit(solution)/shard_map/ppermute | solution.py:56
  12.5 7.6 %collective-permute-start.6 = (bf16[2,96,512]{2,1,0:T(8,128)(2,1)S(1)}, bf16[2,96,512]{2,1,0:T(8,128)(2,1)S(1)}, u32[]{:S(2)}, u32[]{:S(2)}) collective-permute-start(bf16[2,96,512]{2,1,0:T(8,128)(2,1)S(1)} %get-tuple-element.70), channel_id=1, source_target_pairs={{0,8},{8,0},{16,24},{24,16},{1,9},{9,1},{17,25},{25,17},{2,10},{10... | collective-permute-start | bytes 589832 | tf_op jit(solution)/shard_map/ppermute | solution.py:44
  14.1 6.1 %collective-permute-start.7 = (bf16[2,96,512]{2,1,0:T(8,128)(2,1)S(1)}, bf16[2,96,512]{2,1,0:T(8,128)(2,1)S(1)}, u32[]{:S(2)}, u32[]{:S(2)}) collective-permute-start(bf16[2,96,512]{2,1,0:T(8,128)(2,1)S(1)} %get-tuple-element.62.after_ref), channel_id=1, source_target_pairs={{0,2},{1,3},{2,0},{3,1},{4,6},{5,7},{6,4},{7,5},{8,16},{9,17},{10,... | collective-permute-start | bytes 589832 | tf_op jit(solution)/shard_map/ppermute | solution.py:56
  18.5 3.2 %collective-permute-start.9 = (f32[32,128]{1,0:T(8,128)S(1)}, f32[32,128]{1,0:T(8,128)S(1)}, u32[]{:S(2)}, u32[]{:S(2)}) collective-permute-start(f32[32,128]{1,0:T(8,128)S(1)} %get-tuple-element.75), channel_id=1, source_target_pairs={{8,16},{16,8},{24,0},{0,24},{9,17},{17,9},{25,1},{1,25},{10,18},{1... | collective-permute-start | bytes 49160 | tf_op jit(solution)/shard_map/ppermute | solution.py:44
  19.2 1.9 %collective-permute-start.8 = (f32[16,128]{1,0:T(8,128)S(1)}, f32[16,128]{1,0:T(8,128)S(1)}, u32[]{:S(2)}, u32[]{:S(2)}) collective-permute-start(f32[16,128]{1,0:T(8,128)S(1)} %get-tuple-element.74), channel_id=1, source_target_pairs={{0,8},{8,0},{16,24},{24,16},{1,9},{9,1},{17,25},{25,17},{2,10},{10... | collective-permute-start | bytes 24584 | tf_op jit(solution)/shard_map/ppermute | solution.py:44
  22.0 6.0 %collective-permute-start.10 = (bf16[2,48,512]{2,1,0:T(8,128)(2,1)S(1)}, bf16[2,48,512]{2,1,0:T(8,128)(2,1)S(1)}, u32[]{:S(2)}, u32[]{:S(2)}) collective-permute-start(bf16[2,48,512]{2,1,0:T(8,128)(2,1)S(1)} %get-tuple-element.82), channel_id=1, source_target_pairs={{0,1},{1,0},{2,3},{3,2},{4,5},{5,4},{6,7},{7,6},{8,9},{9,8},{10,11... | collective-permute-start | bytes 294920 | tf_op jit(solution)/shard_map/ppermute | solution.py:44
  22.1 7.6 %collective-permute-start.11 = (bf16[2,48,512]{2,1,0:T(8,128)(2,1)S(1)}, bf16[2,48,512]{2,1,0:T(8,128)(2,1)S(1)}, u32[]{:S(2)}, u32[]{:S(2)}) collective-permute-start(bf16[2,48,512]{2,1,0:T(8,128)(2,1)S(1)} %get-tuple-element.83), channel_id=1, source_target_pairs={{1,2},{2,1},{3,4},{4,3},{5,6},{6,5},{7,0},{0,7},{9,10},{10,9},{11,... | collective-permute-start | bytes 294920 | tf_op jit(solution)/shard_map/ppermute | solution.py:44

commit v11 on v10

--- a/solution.py
+++ b/solution.py
@@ -265,6 +265,10 @@
     return jnp.sum(x, axis=0, keepdims=True)
 
 
+def rounded_dot(probability, grad_prob):
+    return column_sum(probability.astype(BF16).astype(F32) * grad_prob)
+
+
 def score_gradient(probability, grad_prob, row_dot):
     return probability.astype(BF16), (probability * (grad_prob - row_dot)).astype(BF16)
 
@@ -280,11 +284,14 @@
         grad_prob = times(stacked(1, at, v_ref, *parts), both_heads(g_ref[:, at]))
         largest = jnp.max(scores, axis=0, keepdims=True)
         raised = jnp.exp(scores - largest)
+        total = column_sum(raised)
         raised_ref[pair] = raised
         prob_ref[pair] = grad_prob
         stats_ref[pair, 0:1] = largest
-        stats_ref[pair, 1:2] = column_sum(raised)
-        stats_ref[pair, 2:3] = column_sum(raised * grad_prob)
+        stats_ref[pair, 1:2] = total
+        log_total = largest + jnp.log(total)
+        stats_ref[pair, 2:3] = rounded_dot(raised * jnp.exp(largest - log_total), grad_prob)
+        stats_ref[pair, 3:4] = log_total
 
     over_pairs(q_ref.shape[1], body)
 
@@ -303,15 +310,17 @@
         raised = jnp.exp(scores - largest)
         shift = jnp.exp(near_largest - largest)
         total = near_stats_ref[pair, 1:2] * shift + column_sum(raised)
-        inverse = 1.0 / total
-        near_scale = shift * inverse
-        row_dot = near_stats_ref[pair, 2:3] * near_scale + column_sum(raised * grad_prob) * inverse
+        log_total = largest + jnp.log(total)
+        scale = jnp.exp(largest - log_total)
+        near_scale = jnp.exp(near_largest - log_total)
+        row_dot = near_stats_ref[pair, 2:3] * jnp.exp(near_stats_ref[pair, 3:4] - log_total)
+        row_dot = row_dot + rounded_dot(raised * scale, grad_prob)
         raised_ref[pair] = raised
         prob_ref[pair] = grad_prob
         stats_ref[pair, 0:1] = near_scale
         stats_ref[pair, 1:2] = row_dot
-        stats_ref[pair, 2:3] = inverse
-        for index, line in enumerate((largest + jnp.log(total), row_dot)):
+        stats_ref[pair, 2:3] = scale
+        for index, line in enumerate((log_total, row_dot)):
             for head in (0, 1):
                 at = 4 * pair + 2 * index + head
                 lines_ref[at : at + 1] = line[:, head * CELLS : (head + 1) * CELLS]

time: 30.7 us -> 30.7 us (level)
  transfers between devices with their start and end apart: 12 -> 12, of which waited for: 5 -> 5; matrix products, arithmetic and copies ran while one was open for 0% -> 0% of each run, Pallas kernels for 27% -> 28%
where the time goes in v11:
time: 30.7 us; the launch traced here: 30.6 us
  starting transfers between devices  15.7 us (51%)
  Pallas kernels  10.9 us (36%)
  waiting for transfers between devices  3.16 us (10%)
  between operations  0.78 us (3%)
    ppermute x10, starting transfers between devices, pair_exchange(): return lax.ppermute(value, axis, pairs)  15.1 us
    pallas_call x15, Pallas kernels, call(): pl.pallas_call(kernel, out_shape=results, compiler_params=pltpu.CompilerP...  10.9 us
    ppermute x10, waiting for transfers between devices, pair_exchange(): return lax.ppermute(value, axis, pairs)  2.35 us
    ppermute x2, waiting for transfers between devices, odd_rows_exchange(): return lax.ppermute(value, ('lat', 'lon'), pairs)  0.81 us
  transfers between devices with their start and end apart: 12, of which 5 were waited for; matrix products, arithmetic and copies ran while one was open for 0% of the time, Pallas kernels for 28%

profile of v11, /device:TPU:0, one launch (start us, length us, event | category | flops | bytes accessed | tf_op | source)
XLA Modules:
  0.0 30.6 jit_solution(15144615847783417953)
XLA Ops:
  0.6 1.3 %pack.1 = (bf16[2,48,512]{2,1,0:T(8,128)(2,1)S(1)}, bf16[2,48,512]{2,1,0:T(8,128)(2,1)S(1)}, bf16[128,512]{1,0:T(8,128)(2,1)S(1)}, bf16[128,512]{1,0:T(8,128)(2,1)S(1)}, f32[8,169]{1,0:T(8,128)S(1)}) custom-call(bf16[128,512]{1,0:T(8,128)(2,1)} %bitcast.8, bf16[128,512]{1,0:T(8,128)(2,1)} %bitcast.9, f32[8,169]{1,0:T(8,128)} %bias_hbm.1), custom_call_target="tpu_custom_call" | custom-call | bytes 267552 | tf_op jit(solution)/shard_map/pack/pallas_call | solution.py:484
  1.9 3.0 %collective-permute-start = (bf16[2,48,512]{2,1,0:T(8,128)(2,1)S(1)}, bf16[2,48,512]{2,1,0:T(8,128)(2,1)S(1)}, u32[]{:S(2)}, u32[]{:S(2)}) collective-permute-start(bf16[2,48,512]{2,1,0:T(8,128)(2,1)S(1)} %get-tuple-element.50), channel_id=1, source_target_pairs={{0,1},{1,0},{2,3},{3,2},{4,5},{5,4},{6,7},{7,6},{8,9},{9,8},{10,11... | collective-permute-start | bytes 294920 | tf_op jit(solution)/shard_map/ppermute | solution.py:44
  4.9 3.5 %collective-permute-start.1 = (bf16[2,48,512]{2,1,0:T(8,128)(2,1)S(1)}, bf16[2,48,512]{2,1,0:T(8,128)(2,1)S(1)}, u32[]{:S(2)}, u32[]{:S(2)}) collective-permute-start(bf16[2,48,512]{2,1,0:T(8,128)(2,1)S(1)} %get-tuple-element.51), channel_id=1, source_target_pairs={{1,2},{2,1},{3,4},{4,3},{5,6},{6,5},{7,0},{0,7},{9,10},{10,9},{11,... | collective-permute-start | bytes 294920 | tf_op jit(solution)/shard_map/ppermute | solution.py:44
  8.5 0.1 collective-permute-start.2
  8.6 1.6 %collective-permute-start.3 = (bf16[2,96,512]{2,1,0:T(8,128)(2,1)S(1)}, bf16[2,96,512]{2,1,0:T(8,128)(2,1)S(1)}, u32[]{:S(2)}, u32[]{:S(2)}) collective-permute-start(bf16[2,96,512]{2,1,0:T(8,128)(2,1)S(1)} %get-tuple-element.56), channel_id=1, source_target_pairs={{8,16},{16,8},{24,0},{0,24},{9,17},{17,9},{25,1},{1,25},{10,18},{1... | collective-permute-start | bytes 589832 | tf_op jit(solution)/shard_map/ppermute | solution.py:44
  10.2 1.6 %bias_table.1 = (f32[8,608,128]{2,1,0:T(8,128)S(1)}, bf16[128,512]{1,0:T(8,128)(2,1)S(1)}, bf16[128,512]{1,0:T(8,128)(2,1)S(1)}) custom-call(f32[8,169]{1,0:T(8,128)S(1)} %get-tuple-element.45.bias_ref, bf16[128,512]{1,0:T(8,128)(2,1)} %bitcast.10, bf16[128,512]{1,0:T(8,128)(2,1)} %bitcast.11), custom_call_target="tpu_custom_call" | custom-call | flops 622592 | bytes 267552 | tf_op jit(solution)/shard_map/bias_table/pallas_call | solution.py:484
  11.8 0.0 collective-permute-done.lon_even_ref
  11.8 0.5 %collective-permute-done.1.lon_odd_ref = bf16[2,48,512]{2,1,0:T(8,128)(2,1)S(1)} collective-permute-done((bf16[2,48,512]{2,1,0:T(8,128)(2,1)S(1)}, bf16[2,48,512]{2,1,0:T(8,128)(2,1)S(1)}, u32[]{:S(2)}, u32[]{:S(2)}) %collective-permute-start.1) | collective-permute-done | bytes 98336 | tf_op jit(solution)/shard_map/ppermute | solution.py:44
  12.3 0.1 collective-permute-start.4
  12.3 0.1 collective-permute-start.5
  12.5 1.6 %collective-permute-start.6 = (bf16[2,96,512]{2,1,0:T(8,128)(2,1)S(1)}, bf16[2,96,512]{2,1,0:T(8,128)(2,1)S(1)}, u32[]{:S(2)}, u32[]{:S(2)}) collective-permute-start(bf16[2,96,512]{2,1,0:T(8,128)(2,1)S(1)} %get-tuple-element.70), channel_id=1, source_target_pairs={{0,8},{8,0},{16,24},{24,16},{1,9},{9,1},{17,25},{25,17},{2,10},{10... | collective-permute-start | bytes 589832 | tf_op jit(solution)/shard_map/ppermute | solution.py:44
  14.1 0.0 collective-permute-done.2.lat_even_ref
  14.1 0.5 %collective-permute-start.7 = (bf16[2,96,512]{2,1,0:T(8,128)(2,1)S(1)}, bf16[2,96,512]{2,1,0:T(8,128)(2,1)S(1)}, u32[]{:S(2)}, u32[]{:S(2)}) collective-permute-start(bf16[2,96,512]{2,1,0:T(8,128)(2,1)S(1)} %get-tuple-element.62.after_ref), channel_id=1, source_target_pairs={{0,2},{1,3},{2,0},{3,1},{4,6},{5,7},{6,4},{7,5},{8,16},{9,17},{10,... | collective-permute-start | bytes 589832 | tf_op jit(solution)/shard_map/ppermute | solution.py:56
  14.6 1.4 %band_table.1.table_ref = f32[2,8,224,128]{3,2,1,0:T(8,128)S(1)} custom-call(f32[8,169]{1,0:T(8,128)S(1)} %get-tuple-element.45.bias_ref, bf16[2,96,512]{2,1,0:T(8,128)(2,1)S(1)} %get-tuple-element.62.after_ref), custom_call_target="tpu_custom_call" | custom-call | flops 458752 | bytes 202016 | tf_op jit(solution)/shard_map/band_table/pallas_call | solution.py:484
  16.1 0.0 collective-permute-done.3.lat_odd_ref
  16.1 0.0 collective-permute-done.4.corner_even_ref
  16.1 1.3 %near.1 = (f32[4,512,256]{2,1,0:T(8,128)S(1)}, f32[4,512,256]{2,1,0:T(8,128)S(1)}, f32[4,8,256]{2,1,0:T(8,128)S(1)}) custom-call(bf16[128,512]{1,0:T(8,128)(2,1)S(1)} %get-tuple-element.60.q_ref.k_ref, bf16[128,512]{1,0:T(8,128)(2,1)S(1)} %get-tuple-element.61.g_ref.v_ref, bf16[128,512]{1,0:T(8,128)(2,1)S(1)} %get-tuple-element.48.k_ref, ...), custom_call_target="tpu_custom_call" | custom-call | flops 268435456 | bytes 3801088 | tf_op jit(solution)/shard_map/near/pallas_call | solution.py:484
  17.4 0.7 %collective-permute-done.5.corner_ref.corner_odd_ref = bf16[2,96,512]{2,1,0:T(8,128)(2,1)S(1)} collective-permute-done((bf16[2,96,512]{2,1,0:T(8,128)(2,1)S(1)}, bf16[2,96,512]{2,1,0:T(8,128)(2,1)S(1)}, u32[]{:S(2)}, u32[]{:S(2)}) %collective-permute-start.5) | collective-permute-done | bytes 196640 | tf_op jit(solution)/shard_map/ppermute | solution.py:56
  18.1 0.5 %corner.1 = (f32[4,96,256]{2,1,0:T(8,128)S(1)}, f32[4,96,256]{2,1,0:T(8,128)S(1)}, f32[4,8,256]{2,1,0:T(8,128)S(1)}, f32[16,128]{1,0:T(8,128)S(1)}, f32[32,128]{1,0:T(8,128)S(1)}) custom-call(bf16[128,512]{1,0:T(8,128)(2,1)S(1)} %get-tuple-element.60.q_ref.k_ref, bf16[128,512]{1,0:T(8,128)(2,1)S(1)} %get-tuple-element.61.g_ref.v_ref, ...), custom_call_target="tpu_custom_call" | custom-call | flops 50331648 | bytes 2981888 | tf_op jit(solution)/shard_map/corner/pallas_call | solution.py:484
  18.6 0.7 %collective-permute-start.9 = (f32[32,128]{1,0:T(8,128)S(1)}, f32[32,128]{1,0:T(8,128)S(1)}, u32[]{:S(2)}, u32[]{:S(2)}) collective-permute-start(f32[32,128]{1,0:T(8,128)S(1)} %get-tuple-element.75), channel_id=1, source_target_pairs={{8,16},{16,8},{24,0},{0,24},{9,17},{17,9},{25,1},{1,25},{10,18},{1... | collective-permute-start | bytes 49160 | tf_op jit(solution)/shard_map/ppermute | solution.py:44
  19.3 0.8 %collective-permute-start.8 = (f32[16,128]{1,0:T(8,128)S(1)}, f32[16,128]{1,0:T(8,128)S(1)}, u32[]{:S(2)}, u32[]{:S(2)}) collective-permute-start(f32[16,128]{1,0:T(8,128)S(1)} %get-tuple-element.74), channel_id=1, source_target_pairs={{0,8},{8,0},{16,24},{24,16},{1,9},{9,1},{17,25},{25,17},{2,10},{10... | collective-permute-start | bytes 24584 | tf_op jit(solution)/shard_map/ppermute | solution.py:44
  20.1 0.0 collective-permute-done.6.queries_even_ref
  20.1 0.1 collective-permute-done.7.queries_odd_ref
  20.2 0.9 %side_scores.1 = (f32[2,96,512]{2,1,0:T(8,128)S(1)}, f32[4,96,512]{2,1,0:T(8,128)S(1)}, f32[4,96,512]{2,1,0:T(8,128)S(1)}, bf16[4,512,128]{2,1,0:T(8,128)(2,1)S(1)}, bf16[4,512,128]{2,1,0:T(8,128)(2,1)S(1)}) custom-call(bf16[128,512]{1,0:T(8,128)(2,1)S(1)} %get-tuple-element.60.q_ref.k_ref, bf16[128,512]{1,0:T(8,128)(2,1)S(1)} %get-tuple-element.61.g_ref.v_ref, ...), custom_call_target="tpu_custom_call" | custom-call | flops 100663296 | bytes 6914048 | tf_op jit(solution)/shard_map/side_scores/pallas_call | solution.py:484
  21.1 0.0 collective-permute-done.8.lines_ref.lines_even_ref
  21.1 0.3 side_even.1.sum_ref
  21.4 0.4 %collective-permute-done.9.lines_odd_ref.lines_ref = f32[32,128]{1,0:T(8,128)S(1)} collective-permute-done((f32[32,128]{1,0:T(8,128)S(1)}, f32[32,128]{1,0:T(8,128)S(1)}, u32[]{:S(2)}, u32[]{:S(2)}) %collective-permute-start.9) | collective-permute-done | bytes 16416 | tf_op jit(solution)/shard_map/ppermute | solution.py:44
  21.8 0.3 side_band.1
  22.0 0.1 collective-permute-start.10
  22.1 3.6 %collective-permute-start.11 = (bf16[2,48,512]{2,1,0:T(8,128)(2,1)S(1)}, bf16[2,48,512]{2,1,0:T(8,128)(2,1)S(1)}, u32[]{:S(2)}, u32[]{:S(2)}) collective-permute-start(bf16[2,48,512]{2,1,0:T(8,128)(2,1)S(1)} %get-tuple-element.83), channel_id=1, source_target_pairs={{1,2},{2,1},{3,4},{4,3},{5,6},{6,5},{7,0},{0,7},{9,10},{10,9},{11,... | collective-permute-start | bytes 294920 | tf_op jit(solution)/shard_map/ppermute | solution.py:44
  25.7 1.6 %own.1 = (bf16[128,512]{1,0:T(8,128)(2,1)}, bf16[128,512]{1,0:T(8,128)(2,1)}, f32[2,128,512]{2,1,0:T(8,128)S(1)}) custom-call(bf16[128,512]{1,0:T(8,128)(2,1)S(1)} %get-tuple-element.60.q_ref.k_ref, bf16[128,512]{1,0:T(8,128)(2,1)S(1)} %get-tuple-element.61.g_ref.v_ref, bf16[128,512]{1,0:T(8,128)(2,1)S(1)} %get-tuple-element.48.k_ref, ...), custom_call_target="tpu_custom_call" | custom-call | flops 318767104 | bytes 6520832 | tf_op jit(solution)/shard_map/own/pallas_call | solution.py:484
  27.3 0.7 %own_band.1.total_ref = f32[2,128,512]{2,1,0:T(8,128)S(1)} custom-call(bf16[128,512]{1,0:T(8,128)(2,1)S(1)} %get-tuple-element.48.k_ref, bf16[128,512]{1,0:T(8,128)(2,1)S(1)} %get-tuple-element.49.v_ref, bf16[4,512,128]{2,1,0:T(8,128)(2,1)S(1)} %get-tuple-element.72.band_q_ref, bf16[4,512,128]{2,1,0:T(8,128)(2,1)S(1)} %get-tuple-element.73.band_g_ref, ...), custom_call_target="tpu_custom_call" | custom-call | flops 134217728 | bytes 3694592 | tf_op jit(solution)/shard_map/own_band/pallas_call | solution.py:484
  28.0 0.0 collective-permute-done.10.side_even_ref
  28.1 0.2 blend.1.blended_ref
  28.3 1.5 %collective-permute-done.11.side_odd_ref = bf16[2,48,512]{2,1,0:T(8,128)(2,1)S(1)} collective-permute-done((bf16[2,48,512]{2,1,0:T(8,128)(2,1)S(1)}, bf16[2,48,512]{2,1,0:T(8,128)(2,1)S(1)}, u32[]{:S(2)}, u32[]{:S(2)}) %collective-permute-start.11) | collective-permute-done | bytes 98336 | tf_op jit(solution)/shard_map/ppermute | solution.py:44
  29.7 0.9 %final.1 = (bf16[128,512]{1,0:T(8,128)(2,1)}, bf16[128,512]{1,0:T(8,128)(2,1)}) custom-call(f32[2,128,512]{2,1,0:T(8,128)S(1)} %blend.1.blended_ref, bf16[2,48,512]{2,1,0:T(8,128)(2,1)S(1)} %collective-permute-done.11.side_odd_ref), custom_call_target="tpu_custom_call" | custom-call | bytes 622592 | tf_op jit(solution)/shard_map/final/pallas_call | solution.py:484
  (3 shorter events, 0.1 us)
Async XLA Ops:
  1.9 9.9 %collective-permute-start = (bf16[2,48,512]{2,1,0:T(8,128)(2,1)S(1)}, bf16[2,48,512]{2,1,0:T(8,128)(2,1)S(1)}, u32[]{:S(2)}, u32[]{:S(2)}) collective-permute-start(bf16[2,48,512]{2,1,0:T(8,128)(2,1)S(1)} %get-tuple-element.50), channel_id=1, source_target_pairs={{0,1},{1,0},{2,3},{3,2},{4,5},{5,4},{6,7},{7,6},{8,9},{9,8},{10,11... | collective-permute-start | bytes 294920 | tf_op jit(solution)/shard_map/ppermute | solution.py:44
  4.9 7.3 %collective-permute-start.1 = (bf16[2,48,512]{2,1,0:T(8,128)(2,1)S(1)}, bf16[2,48,512]{2,1,0:T(8,128)(2,1)S(1)}, u32[]{:S(2)}, u32[]{:S(2)}) collective-permute-start(bf16[2,48,512]{2,1,0:T(8,128)(2,1)S(1)} %get-tuple-element.51), channel_id=1, source_target_pairs={{1,2},{2,1},{3,4},{4,3},{5,6},{6,5},{7,0},{0,7},{9,10},{10,9},{11,... | collective-permute-start | bytes 294920 | tf_op jit(solution)/shard_map/ppermute | solution.py:44
  8.5 5.6 %collective-permute-start.2 = (bf16[2,96,512]{2,1,0:T(8,128)(2,1)S(1)}, bf16[2,96,512]{2,1,0:T(8,128)(2,1)S(1)}, u32[]{:S(2)}, u32[]{:S(2)}) collective-permute-start(bf16[2,96,512]{2,1,0:T(8,128)(2,1)S(1)} %get-tuple-element.55), channel_id=1, source_target_pairs={{0,8},{8,0},{16,24},{24,16},{1,9},{9,1},{17,25},{25,17},{2,10},{10... | collective-permute-start | bytes 589832 | tf_op jit(solution)/shard_map/ppermute | solution.py:44
  8.6 7.5 %collective-permute-start.3 = (bf16[2,96,512]{2,1,0:T(8,128)(2,1)S(1)}, bf16[2,96,512]{2,1,0:T(8,128)(2,1)S(1)}, u32[]{:S(2)}, u32[]{:S(2)}) collective-permute-start(bf16[2,96,512]{2,1,0:T(8,128)(2,1)S(1)} %get-tuple-element.56), channel_id=1, source_target_pairs={{8,16},{16,8},{24,0},{0,24},{9,17},{17,9},{25,1},{1,25},{10,18},{1... | collective-permute-start | bytes 589832 | tf_op jit(solution)/shard_map/ppermute | solution.py:44
  12.3 3.8 %collective-permute-start.4 = (bf16[2,96,512]{2,1,0:T(8,128)(2,1)S(1)}, bf16[2,96,512]{2,1,0:T(8,128)(2,1)S(1)}, u32[]{:S(2)}, u32[]{:S(2)}) collective-permute-start(bf16[2,96,512]{2,1,0:T(8,128)(2,1)S(1)} %join.1), channel_id=1, source_target_pairs={{0,8},{8,0},{16,24},{24,16},{1,9},{9,1},{17,25},{25,17},{2,10},{10... | collective-permute-start | bytes 589832 | tf_op jit(solution)/shard_map/ppermute | solution.py:44
  12.3 5.7 %collective-permute-start.5 = (bf16[2,96,512]{2,1,0:T(8,128)(2,1)S(1)}, bf16[2,96,512]{2,1,0:T(8,128)(2,1)S(1)}, u32[]{:S(2)}, u32[]{:S(2)}) collective-permute-start(bf16[2,96,512]{2,1,0:T(8,128)(2,1)S(1)} %join.1), channel_id=1, source_target_pairs={{0,2},{1,3},{2,0},{3,1},{4,6},{5,7},{6,4},{7,5},{8,16},{9,17},{10,... | collective-permute-start | bytes 589832 | tf_op jit(solution)/shard_map/ppermute | solution.py:56
  12.5 7.6 %collective-permute-start.6 = (bf16[2,96,512]{2,1,0:T(8,128)(2,1)S(1)}, bf16[2,96,512]{2,1,0:T(8,128)(2,1)S(1)}, u32[]{:S(2)}, u32[]{:S(2)}) collective-permute-start(bf16[2,96,512]{2,1,0:T(8,128)(2,1)S(1)} %get-tuple-element.70), channel_id=1, source_target_pairs={{0,8},{8,0},{16,24},{24,16},{1,9},{9,1},{17,25},{25,17},{2,10},{10... | collective-permute-start | bytes 589832 | tf_op jit(solution)/shard_map/ppermute | solution.py:44
  14.1 6.1 %collective-permute-start.7 = (bf16[2,96,512]{2,1,0:T(8,128)(2,1)S(1)}, bf16[2,96,512]{2,1,0:T(8,128)(2,1)S(1)}, u32[]{:S(2)}, u32[]{:S(2)}) collective-permute-start(bf16[2,96,512]{2,1,0:T(8,128)(2,1)S(1)} %get-tuple-element.62.after_ref), channel_id=1, source_target_pairs={{0,2},{1,3},{2,0},{3,1},{4,6},{5,7},{6,4},{7,5},{8,16},{9,17},{10,... | collective-permute-start | bytes 589832 | tf_op jit(solution)/shard_map/ppermute | solution.py:56
  18.6 3.2 %collective-permute-start.9 = (f32[32,128]{1,0:T(8,128)S(1)}, f32[32,128]{1,0:T(8,128)S(1)}, u32[]{:S(2)}, u32[]{:S(2)}) collective-permute-start(f32[32,128]{1,0:T(8,128)S(1)} %get-tuple-element.75), channel_id=1, source_target_pairs={{8,16},{16,8},{24,0},{0,24},{9,17},{17,9},{25,1},{1,25},{10,18},{1... | collective-permute-start | bytes 49160 | tf_op jit(solution)/shard_map/ppermute | solution.py:44
  19.3 1.8 %collective-permute-start.8 = (f32[16,128]{1,0:T(8,128)S(1)}, f32[16,128]{1,0:T(8,128)S(1)}, u32[]{:S(2)}, u32[]{:S(2)}) collective-permute-start(f32[16,128]{1,0:T(8,128)S(1)} %get-tuple-element.74), channel_id=1, source_target_pairs={{0,8},{8,0},{16,24},{24,16},{1,9},{9,1},{17,25},{25,17},{2,10},{10... | collective-permute-start | bytes 24584 | tf_op jit(solution)/shard_map/ppermute | solution.py:44
  22.0 6.0 %collective-permute-start.10 = (bf16[2,48,512]{2,1,0:T(8,128)(2,1)S(1)}, bf16[2,48,512]{2,1,0:T(8,128)(2,1)S(1)}, u32[]{:S(2)}, u32[]{:S(2)}) collective-permute-start(bf16[2,48,512]{2,1,0:T(8,128)(2,1)S(1)} %get-tuple-element.82), channel_id=1, source_target_pairs={{0,1},{1,0},{2,3},{3,2},{4,5},{5,4},{6,7},{7,6},{8,9},{9,8},{10,11... | collective-permute-start | bytes 294920 | tf_op jit(solution)/shard_map/ppermute | solution.py:44
  22.1 7.6 %collective-permute-start.11 = (bf16[2,48,512]{2,1,0:T(8,128)(2,1)S(1)}, bf16[2,48,512]{2,1,0:T(8,128)(2,1)S(1)}, u32[]{:S(2)}, u32[]{:S(2)}) collective-permute-start(bf16[2,48,512]{2,1,0:T(8,128)(2,1)S(1)} %get-tuple-element.83), channel_id=1, source_target_pairs={{1,2},{2,1},{3,4},{4,3},{5,6},{6,5},{7,0},{0,7},{9,10},{10,9},{11,... | collective-permute-start | bytes 294920 | tf_op jit(solution)/shard_map/ppermute | solution.py:44

commit v12 on v11

--- a/solution.py
+++ b/solution.py
@@ -44,6 +44,11 @@
     return lax.ppermute(value, axis, pairs)
 
 
+def ring_shift(value, by):
+    count = lax.axis_size("lon")
+    return lax.ppermute(value, "lon", [(lon, (lon + by) % count) for lon in range(count)])
+
+
 def odd_rows_exchange(value):
     lats, lons = lax.axis_size("lat"), lax.axis_size("lon")
     pairs = []
@@ -68,21 +73,19 @@
     return (cell == source).astype(BF16)
 
 
-def pack_kernel(k_hbm, v_hbm, bias_hbm, lon_odd_ref, lon_even_ref, k_ref, v_ref, bias_ref, sems):
+def pack_kernel(k_hbm, v_hbm, bias_hbm, lon_west_ref, lon_east_ref, k_ref, v_ref, bias_ref, sems):
     copies = [
         pltpu.make_async_copy(source, target, sems.at[index])
         for index, (source, target) in enumerate(((k_hbm, k_ref), (v_hbm, v_ref), (bias_hbm, bias_ref)))
     ]
     for copy in copies:
         copy.start()
-    lon_odd = is_odd("lon")
-    first_cols = (jnp.where(lon_odd, COLS - RADIUS, 0), jnp.where(lon_odd, 0, COLS - RADIUS))
-    picks = jnp.concatenate([pick_matrix(first_col) for first_col in first_cols], axis=0)
+    picks = jnp.concatenate([pick_matrix(first_col) for first_col in (COLS - RADIUS, 0)], axis=0)
     for slot, source in ((0, k_ref), (1, v_ref)):
         copies[slot].wait()
         both = jnp.dot(picks, source[...], preferred_element_type=F32).astype(BF16)
-        lon_odd_ref[slot] = both[:SIDE]
-        lon_even_ref[slot] = both[SIDE:]
+        lon_west_ref[slot] = both[:SIDE]
+        lon_east_ref[slot] = both[SIDE:]
     copies[2].wait()
 
 
@@ -139,11 +142,10 @@
 
 
 def places():
-    west_slot = jnp.where(is_odd("lon"), SIDE, 0)
     north_slot = jnp.where(is_odd("lat"), 0, 1)
     has_north = lax.axis_index("lat") > 0
     has_south = lax.axis_index("lat") < lax.axis_size("lat") - 1
-    sides = ((0, west_slot), (COLS + RADIUS, SIDE - west_slot))
+    sides = ((0, 0), (COLS + RADIUS, SIDE))
     own_col = lax.broadcasted_iota(jnp.int32, (8, CELLS), 1) % COLS
     sub = lax.broadcasted_iota(jnp.int32, (8, CELLS), 0)
     return sides, north_slot, 1 - north_slot, has_north, has_south, own_col, sub
@@ -230,9 +232,9 @@
 FACTOR = HEAD_DIM ** (-0.5)
 
 
-def join_kernel(lon_even_ref, lon_odd_ref, out_ref):
-    out_ref[:, :SIDE] = lon_odd_ref[...]
-    out_ref[:, SIDE:] = lon_even_ref[...]
+def join_kernel(lon_west_ref, lon_east_ref, out_ref):
+    out_ref[:, :SIDE] = lon_west_ref[...]
+    out_ref[:, SIDE:] = lon_east_ref[...]
 
 
 def over_pairs(width, body):
@@ -274,10 +276,10 @@
 
 
 def near_kernel(
-    q_ref, g_ref, k_ref, v_ref, lon_odd_ref, lon_even_ref, lat_even_ref, lat_odd_ref, corner_even_ref, table_ref,
+    q_ref, g_ref, k_ref, v_ref, lon_west_ref, lon_east_ref, lat_even_ref, lat_odd_ref, corner_even_ref, table_ref,
     raised_ref, prob_ref, stats_ref,
 ):
-    parts = (lon_odd_ref, lon_even_ref, lat_even_ref, lat_odd_ref, corner_even_ref)
+    parts = (lon_west_ref, lon_east_ref, lat_even_ref, lat_odd_ref, corner_even_ref)
 
     def body(pair, at):
         scores = times(stacked(0, at, k_ref, *parts), scaled(q_ref[:, at])) + two_tables(table_ref, pair, pl.ds(0, EARLY))
@@ -353,14 +355,14 @@
 
 
 def side_scores_kernel(
-    q_ref, g_ref, raised_ref, prob_ref, stats_ref, lon_odd_ref, lon_even_ref, queries_even_ref, queries_odd_ref, table_ref,
+    q_ref, g_ref, raised_ref, prob_ref, stats_ref, lon_west_ref, lon_east_ref, queries_even_ref, queries_odd_ref, table_ref,
     dlon_ref, scores_ref, prob_out_ref, band_q_ref, band_g_ref,
 ):
     queries_refs = (queries_even_ref, queries_odd_ref)
 
     def body(pair, at):
         keys, values = (
-            jnp.concatenate([lon_odd_ref[slot, :, at], lon_even_ref[slot, :, at]], axis=0) for slot in (0, 1)
+            jnp.concatenate([lon_west_ref[slot, :, at], lon_east_ref[slot, :, at]], axis=0) for slot in (0, 1)
         )
         queries = band_queries(queries_refs, 0, at, scaled)
         grads = band_queries(queries_refs, 1, at, both_heads)
@@ -412,10 +414,10 @@
 
 
 def own_kernel(
-    q_ref, g_ref, k_ref, v_ref, lon_odd_ref, lon_even_ref, lat_even_ref, lat_odd_ref, corner_even_ref, corner_odd_ref,
+    q_ref, g_ref, k_ref, v_ref, lon_west_ref, lon_east_ref, lat_even_ref, lat_odd_ref, corner_even_ref, corner_odd_ref,
     raised_ref, prob_ref, corner_raised_ref, corner_prob_ref, stats_ref, out_ref, dq_ref, own_ref,
 ):
-    parts = (lon_odd_ref, lon_even_ref, lat_even_ref, lat_odd_ref, corner_even_ref, corner_odd_ref)
+    parts = (lon_west_ref, lon_east_ref, lat_even_ref, lat_odd_ref, corner_even_ref, corner_odd_ref)
 
     def per_query(cells, coefficients):
         turned = jnp.dot(cells.T, coefficients, preferred_element_type=F32)
@@ -462,16 +464,16 @@
     return (cell == (place % ROWS) * COLS + first_col + place // ROWS).astype(BF16)
 
 
-def blend_kernel(total_ref, side_even_ref, blended_ref):
-    spread = spread_matrix(jnp.where(is_odd("lon"), 0, COLS - RADIUS))
+def blend_kernel(total_ref, side_east_ref, blended_ref):
+    spread = spread_matrix(0)
     for slot in (0, 1):
-        blended_ref[slot] = total_ref[slot] + jnp.dot(spread, side_even_ref[slot], preferred_element_type=F32)
-
-
-def final_kernel(blended_ref, side_odd_ref, dk_ref, dv_ref):
-    spread = spread_matrix(jnp.where(is_odd("lon"), COLS - RADIUS, 0))
+        blended_ref[slot] = total_ref[slot] + jnp.dot(spread, side_east_ref[slot], preferred_element_type=F32)
+
+
+def final_kernel(blended_ref, side_west_ref, dk_ref, dv_ref):
+    spread = spread_matrix(COLS - RADIUS)
     for slot, out in ((0, dk_ref), (1, dv_ref)):
-        total = blended_ref[slot] + jnp.dot(spread, side_odd_ref[slot], preferred_element_type=F32)
+        total = blended_ref[slot] + jnp.dot(spread, side_west_ref[slot], preferred_element_type=F32)
         out[...] = total.astype(BF16)
 
 
@@ -506,13 +508,13 @@
 
     hbm, vmem = (pl.BlockSpec(memory_space=space) for space in (pltpu.HBM, pltpu.VMEM))
     arguments = [in_hbm(x) for x in (key_cells.reshape(CELLS, feat), value_cells.reshape(CELLS, feat), rel_bias)]
-    lon_odd, lon_even, k, v, rel_bias = call(
+    lon_west, lon_east, k, v, rel_bias = call(
         pack_kernel, "pack", arguments, [side, side, cells, cells, arr(rel_bias.shape, F32)],
         in_specs=[hbm] * 3,
         scratch_shapes=[pltpu.SemaphoreType.DMA((3,))],
     )
-    lon_even = pair_exchange(lon_even, "lon", 0, True)
-    lon_odd = pair_exchange(lon_odd, "lon", 1, True)
+    lon_west = ring_shift(lon_west, 1)
+    lon_east = ring_shift(lon_east, -1)
     lat_even, lat_odd = call(rows_kernel, "rows", [k, v], [band, band])
     lat_even = pair_exchange(lat_even, "lat", 0, False)
     lat_odd = pair_exchange(lat_odd, "lat", 1, True)
@@ -526,15 +528,15 @@
         scratch_shapes=[*spread, pltpu.SemaphoreType.DMA((2,))],
     )
 
-    lon_even, lon_odd, table = barrier((lon_even, lon_odd, table))
-    joined, = call(join_kernel, "join", [lon_even, lon_odd], [corner], int(2e9))
+    lon_west, lon_east, table = barrier((lon_west, lon_east, table))
+    joined, = call(join_kernel, "join", [lon_west, lon_east], [corner], int(2e9))
     corner_even = pair_exchange(joined, "lat", 0, False)
     corner_odd = odd_rows_exchange(joined)
 
     def scored(rows):
         return [arr((pairs, rows, 2 * CELLS), F32)] * 2 + [arr((pairs, 8, 2 * CELLS), F32)]
 
-    near = [k, v, lon_odd, lon_even, lat_even, lat_odd]
+    near = [k, v, lon_west, lon_east, lat_even, lat_odd]
     raised, prob, near_stats = call(near_kernel, "near", [q, g, *near, corner_even, table], scored(EARLY), 4 * work * EARLY)
     late_q, late_g, _ = barrier((q, g, joined))
     queries_even, queries_odd = call(rows_kernel, "query_rows", [late_q, late_g], [band, band])
@@ -558,7 +560,7 @@
     masked = [arr((pairs, 4 * CELLS, PAIR), BF16)] * 2
     dlon, side_scores, side_prob, band_q, band_g = call(
         side_scores_kernel, "side_scores",
-        [q, g, raised, prob, stats, lon_odd, lon_even, queries_even, queries_odd, band_table],
+        [q, g, raised, prob, stats, lon_west, lon_east, queries_even, queries_odd, band_table],
         [arr(corner.shape, F32), *band_scores, *masked], 16 * work * SIDE,
     )
     dlon, = call(
@@ -566,12 +568,12 @@
         [arr(corner.shape, F32)], 8 * work * SIDE,
     )
     lines_odd, dlon = barrier((lines_odd, dlon))
-    send_odd, send_even = call(
+    send_west, send_east = call(
         side_band_kernel, "side_band", [dlon, side_scores, side_prob, band_q, band_g, lines_odd], [side, side],
         8 * work * SIDE,
     )
-    side_even = pair_exchange(send_even, "lon", 0, True)
-    side_odd = pair_exchange(send_odd, "lon", 1, True)
+    side_east = ring_shift(send_east, 1)
+    side_west = ring_shift(send_west, -1)
     out, dq, own = call(
         own_kernel, "own", [q, g, *near, corner_even, corner_odd, raised, prob, corner_raised, corner_prob, stats],
         [cells, cells, arr((2, CELLS, feat), F32)], 4 * work * AROUND,
@@ -580,8 +582,8 @@
         own_band_kernel, "own_band", [k, v, band_q, band_g, band_table, lines_even, lines_odd, own],
         [arr((2, CELLS, feat), F32)], 8 * work * CELLS,
     )
-    blended, = call(blend_kernel, "blend", [total, side_even], [arr((2, CELLS, feat), F32)])
-    dk, dv = call(final_kernel, "final", [blended, side_odd], [cells, cells])
+    blended, = call(blend_kernel, "blend", [total, side_east], [arr((2, CELLS, feat), F32)])
+    dk, dv = call(final_kernel, "final", [blended, side_west], [cells, cells])
     return tuple(x.reshape(block) for x in (out, dq, dk, dv))
 
 

time: 30.7 us -> 30.3 us (0.987)
  waiting for transfers between devices: 3.16 us -> 1.33 us
  starting transfers between devices: 15.7 us -> 17.1 us
    ppermute x0 -> x4, starting transfers between devices: none -> 10.9 us  [ring_shift(): lax.ppermute(value, 'lon', [(lon, (lon + by) % count) for lon in range(co...]
    ppermute x10 -> x6, starting transfers between devices: 15.1 us -> 4.39 us  [pair_exchange(): return lax.ppermute(value, axis, pairs)]
    ppermute x10 -> x6, waiting for transfers between devices: 2.35 us -> 0.25 us  [pair_exchange(): return lax.ppermute(value, axis, pairs)]
    ppermute x2, starting transfers between devices: 0.58 us -> 1.81 us  [odd_rows_exchange(): return lax.ppermute(value, ('lat', 'lon'), pairs)]
    ppermute x0 -> x4, waiting for transfers between devices: none -> 0.74 us  [ring_shift(): lax.ppermute(value, 'lon', [(lon, (lon + by) % count) for lon in range(co...]
    ppermute x2, waiting for transfers between devices: 0.81 us -> 0.34 us  [odd_rows_exchange(): return lax.ppermute(value, ('lat', 'lon'), pairs)]
  transfers between devices with their start and end apart: 12 -> 12, of which waited for: 5 -> 4; matrix products, arithmetic and copies ran while one was open for 0% -> 0% of each run, Pallas kernels for 28% -> 28%
where the time goes in v12:
time: 30.3 us; the launch traced here: 30.1 us
  starting transfers between devices  17.1 us (56%)
  Pallas kernels  10.9 us (36%)
  waiting for transfers between devices  1.33 us (4%)
  between operations  0.77 us (3%)
    pallas_call x15, Pallas kernels, call(): pl.pallas_call(kernel, out_shape=results, compiler_params=pltpu.CompilerP...  10.9 us
    ppermute x4, starting transfers between devices, ring_shift(): lax.ppermute(value, 'lon', [(lon, (lon + by) % count) for lon in range(co...  10.9 us
    ppermute x6, starting transfers between devices, pair_exchange(): return lax.ppermute(value, axis, pairs)  4.39 us
    ppermute x2, starting transfers between devices, odd_rows_exchange(): return lax.ppermute(value, ('lat', 'lon'), pairs)  1.81 us
    ppermute x4, waiting for transfers between devices, ring_shift(): lax.ppermute(value, 'lon', [(lon, (lon + by) % count) for lon in range(co...  0.74 us
  transfers between devices with their start and end apart: 12, of which 4 were waited for; matrix products, arithmetic and copies ran while one was open for 0% of the time, Pallas kernels for 28%

profile of v12, /device:TPU:0, one launch (start us, length us, event | category | flops | bytes accessed | tf_op | source)
XLA Modules:
  0.0 30.1 jit_solution(16318735030114244982)
XLA Ops:
  0.6 1.3 %pack.1 = (bf16[2,48,512]{2,1,0:T(8,128)(2,1)S(1)}, bf16[2,48,512]{2,1,0:T(8,128)(2,1)S(1)}, bf16[128,512]{1,0:T(8,128)(2,1)S(1)}, bf16[128,512]{1,0:T(8,128)(2,1)S(1)}, f32[8,169]{1,0:T(8,128)S(1)}) custom-call(bf16[128,512]{1,0:T(8,128)(2,1)} %bitcast.8, bf16[128,512]{1,0:T(8,128)(2,1)} %bitcast.9, f32[8,169]{1,0:T(8,128)} %bias_hbm.1), custom_call_target="tpu_custom_call" | custom-call | bytes 267552 | tf_op jit(solution)/shard_map/pack/pallas_call | solution.py:486
  1.9 3.0 %collective-permute-start = (bf16[2,48,512]{2,1,0:T(8,128)(2,1)S(1)}, bf16[2,48,512]{2,1,0:T(8,128)(2,1)S(1)}, u32[]{:S(2)}, u32[]{:S(2)}) collective-permute-start(bf16[2,48,512]{2,1,0:T(8,128)(2,1)S(1)} %get-tuple-element.50), channel_id=1, source_target_pairs={{0,1},{1,2},{2,3},{3,4},{4,5},{5,6},{6,7},{7,0},{8,9},{9,10},{10,1... | collective-permute-start | bytes 294920 | tf_op jit(solution)/shard_map/ppermute | solution.py:49
  4.9 3.1 %collective-permute-start.1 = (bf16[2,48,512]{2,1,0:T(8,128)(2,1)S(1)}, bf16[2,48,512]{2,1,0:T(8,128)(2,1)S(1)}, u32[]{:S(2)}, u32[]{:S(2)}) collective-permute-start(bf16[2,48,512]{2,1,0:T(8,128)(2,1)S(1)} %get-tuple-element.51), channel_id=1, source_target_pairs={{0,7},{1,0},{2,1},{3,2},{4,3},{5,4},{6,5},{7,6},{8,15},{9,8},{10,9... | collective-permute-start | bytes 294920 | tf_op jit(solution)/shard_map/ppermute | solution.py:49
  8.1 0.1 collective-permute-start.2
  8.1 1.7 %collective-permute-start.3 = (bf16[2,96,512]{2,1,0:T(8,128)(2,1)S(1)}, bf16[2,96,512]{2,1,0:T(8,128)(2,1)S(1)}, u32[]{:S(2)}, u32[]{:S(2)}) collective-permute-start(bf16[2,96,512]{2,1,0:T(8,128)(2,1)S(1)} %get-tuple-element.56), channel_id=1, source_target_pairs={{8,16},{16,8},{24,0},{0,24},{9,17},{17,9},{25,1},{1,25},{10,18},{1... | collective-permute-start | bytes 589832 | tf_op jit(solution)/shard_map/ppermute | solution.py:44
  9.8 1.6 %bias_table.1 = (f32[8,608,128]{2,1,0:T(8,128)S(1)}, bf16[128,512]{1,0:T(8,128)(2,1)S(1)}, bf16[128,512]{1,0:T(8,128)(2,1)S(1)}) custom-call(f32[8,169]{1,0:T(8,128)S(1)} %get-tuple-element.45.bias_ref, bf16[128,512]{1,0:T(8,128)(2,1)} %bitcast.10, bf16[128,512]{1,0:T(8,128)(2,1)} %bitcast.11), custom_call_target="tpu_custom_call" | custom-call | flops 622592 | bytes 267552 | tf_op jit(solution)/shard_map/bias_table/pallas_call | solution.py:486
  11.4 0.0 collective-permute-done.lon_west_ref
  11.4 0.2 collective-permute-done.1.lon_east_ref
  11.7 0.1 collective-permute-start.4
  11.7 0.9 %collective-permute-start.5 = (bf16[2,96,512]{2,1,0:T(8,128)(2,1)S(1)}, bf16[2,96,512]{2,1,0:T(8,128)(2,1)S(1)}, u32[]{:S(2)}, u32[]{:S(2)}) collective-permute-start(bf16[2,96,512]{2,1,0:T(8,128)(2,1)S(1)} %join.1), channel_id=1, source_target_pairs={{0,2},{1,3},{2,0},{3,1},{4,6},{5,7},{6,4},{7,5},{8,16},{9,17},{10,... | collective-permute-start | bytes 589832 | tf_op jit(solution)/shard_map/ppermute | solution.py:61
  12.7 0.8 %collective-permute-start.6 = (bf16[2,96,512]{2,1,0:T(8,128)(2,1)S(1)}, bf16[2,96,512]{2,1,0:T(8,128)(2,1)S(1)}, u32[]{:S(2)}, u32[]{:S(2)}) collective-permute-start(bf16[2,96,512]{2,1,0:T(8,128)(2,1)S(1)} %get-tuple-element.70), channel_id=1, source_target_pairs={{0,8},{8,0},{16,24},{24,16},{1,9},{9,1},{17,25},{25,17},{2,10},{10... | collective-permute-start | bytes 589832 | tf_op jit(solution)/shard_map/ppermute | solution.py:44
  13.5 0.0 collective-permute-done.2.lat_even_ref
  13.5 0.9 %collective-permute-start.7 = (bf16[2,96,512]{2,1,0:T(8,128)(2,1)S(1)}, bf16[2,96,512]{2,1,0:T(8,128)(2,1)S(1)}, u32[]{:S(2)}, u32[]{:S(2)}) collective-permute-start(bf16[2,96,512]{2,1,0:T(8,128)(2,1)S(1)} %get-tuple-element.62.after_ref), channel_id=1, source_target_pairs={{0,2},{1,3},{2,0},{3,1},{4,6},{5,7},{6,4},{7,5},{8,16},{9,17},{10,... | collective-permute-start | bytes 589832 | tf_op jit(solution)/shard_map/ppermute | solution.py:61
  14.4 1.4 %band_table.1.table_ref = f32[2,8,224,128]{3,2,1,0:T(8,128)S(1)} custom-call(f32[8,169]{1,0:T(8,128)S(1)} %get-tuple-element.45.bias_ref, bf16[2,96,512]{2,1,0:T(8,128)(2,1)S(1)} %get-tuple-element.62.after_ref), custom_call_target="tpu_custom_call" | custom-call | flops 458752 | bytes 202016 | tf_op jit(solution)/shard_map/band_table/pallas_call | solution.py:486
  15.8 0.0 collective-permute-done.3.lat_odd_ref
  15.9 0.0 collective-permute-done.4.corner_even_ref
  15.9 1.3 %near.1 = (f32[4,512,256]{2,1,0:T(8,128)S(1)}, f32[4,512,256]{2,1,0:T(8,128)S(1)}, f32[4,8,256]{2,1,0:T(8,128)S(1)}) custom-call(bf16[128,512]{1,0:T(8,128)(2,1)S(1)} %get-tuple-element.60.q_ref.k_ref, bf16[128,512]{1,0:T(8,128)(2,1)S(1)} %get-tuple-element.61.g_ref.v_ref, bf16[128,512]{1,0:T(8,128)(2,1)S(1)} %get-tuple-element.48.k_ref, ...), custom_call_target="tpu_custom_call" | custom-call | flops 268435456 | bytes 3801088 | tf_op jit(solution)/shard_map/near/pallas_call | solution.py:486
  17.1 0.3 %collective-permute-done.5.corner_ref.corner_odd_ref = bf16[2,96,512]{2,1,0:T(8,128)(2,1)S(1)} collective-permute-done((bf16[2,96,512]{2,1,0:T(8,128)(2,1)S(1)}, bf16[2,96,512]{2,1,0:T(8,128)(2,1)S(1)}, u32[]{:S(2)}, u32[]{:S(2)}) %collective-permute-start.5) | collective-permute-done | bytes 196640 | tf_op jit(solution)/shard_map/ppermute | solution.py:61
  17.5 0.5 %corner.1 = (f32[4,96,256]{2,1,0:T(8,128)S(1)}, f32[4,96,256]{2,1,0:T(8,128)S(1)}, f32[4,8,256]{2,1,0:T(8,128)S(1)}, f32[16,128]{1,0:T(8,128)S(1)}, f32[32,128]{1,0:T(8,128)S(1)}) custom-call(bf16[128,512]{1,0:T(8,128)(2,1)S(1)} %get-tuple-element.60.q_ref.k_ref, bf16[128,512]{1,0:T(8,128)(2,1)S(1)} %get-tuple-element.61.g_ref.v_ref, ...), custom_call_target="tpu_custom_call" | custom-call | flops 50331648 | bytes 2981888 | tf_op jit(solution)/shard_map/corner/pallas_call | solution.py:486
  18.0 1.1 %collective-permute-start.9 = (f32[32,128]{1,0:T(8,128)S(1)}, f32[32,128]{1,0:T(8,128)S(1)}, u32[]{:S(2)}, u32[]{:S(2)}) collective-permute-start(f32[32,128]{1,0:T(8,128)S(1)} %get-tuple-element.75), channel_id=1, source_target_pairs={{8,16},{16,8},{24,0},{0,24},{9,17},{17,9},{25,1},{1,25},{10,18},{1... | collective-permute-start | bytes 49160 | tf_op jit(solution)/shard_map/ppermute | solution.py:44
  19.1 0.6 %collective-permute-start.8 = (f32[16,128]{1,0:T(8,128)S(1)}, f32[16,128]{1,0:T(8,128)S(1)}, u32[]{:S(2)}, u32[]{:S(2)}) collective-permute-start(f32[16,128]{1,0:T(8,128)S(1)} %get-tuple-element.74), channel_id=1, source_target_pairs={{0,8},{8,0},{16,24},{24,16},{1,9},{9,1},{17,25},{25,17},{2,10},{10... | collective-permute-start | bytes 24584 | tf_op jit(solution)/shard_map/ppermute | solution.py:44
  19.7 0.0 collective-permute-done.6.queries_even_ref
  19.7 0.0 collective-permute-done.7.queries_odd_ref
  19.7 0.9 %side_scores.1 = (f32[2,96,512]{2,1,0:T(8,128)S(1)}, f32[4,96,512]{2,1,0:T(8,128)S(1)}, f32[4,96,512]{2,1,0:T(8,128)S(1)}, bf16[4,512,128]{2,1,0:T(8,128)(2,1)S(1)}, bf16[4,512,128]{2,1,0:T(8,128)(2,1)S(1)}) custom-call(bf16[128,512]{1,0:T(8,128)(2,1)S(1)} %get-tuple-element.60.q_ref.k_ref, bf16[128,512]{1,0:T(8,128)(2,1)S(1)} %get-tuple-element.61.g_ref.v_ref, ...), custom_call_target="tpu_custom_call" | custom-call | flops 100663296 | bytes 6914048 | tf_op jit(solution)/shard_map/side_scores/pallas_call | solution.py:486
  20.6 0.0 collective-permute-done.8.lines_ref.lines_even_ref
  20.6 0.3 side_even.1.sum_ref
  20.9 0.2 collective-permute-done.9.lines_odd_ref.lines_ref
  21.2 0.3 side_band.1
  21.4 0.7 %collective-permute-start.10 = (bf16[2,48,512]{2,1,0:T(8,128)(2,1)S(1)}, bf16[2,48,512]{2,1,0:T(8,128)(2,1)S(1)}, u32[]{:S(2)}, u32[]{:S(2)}) collective-permute-start(bf16[2,48,512]{2,1,0:T(8,128)(2,1)S(1)} %get-tuple-element.82), channel_id=1, source_target_pairs={{0,1},{1,2},{2,3},{3,4},{4,5},{5,6},{6,7},{7,0},{8,9},{9,10},{10,1... | collective-permute-start | bytes 294920 | tf_op jit(solution)/shard_map/ppermute | solution.py:49
  22.2 4.0 %collective-permute-start.11 = (bf16[2,48,512]{2,1,0:T(8,128)(2,1)S(1)}, bf16[2,48,512]{2,1,0:T(8,128)(2,1)S(1)}, u32[]{:S(2)}, u32[]{:S(2)}) collective-permute-start(bf16[2,48,512]{2,1,0:T(8,128)(2,1)S(1)} %get-tuple-element.83), channel_id=1, source_target_pairs={{0,7},{1,0},{2,1},{3,2},{4,3},{5,4},{6,5},{7,6},{8,15},{9,8},{10,9... | collective-permute-start | bytes 294920 | tf_op jit(solution)/shard_map/ppermute | solution.py:49
  26.2 1.6 %own.1 = (bf16[128,512]{1,0:T(8,128)(2,1)}, bf16[128,512]{1,0:T(8,128)(2,1)}, f32[2,128,512]{2,1,0:T(8,128)S(1)}) custom-call(bf16[128,512]{1,0:T(8,128)(2,1)S(1)} %get-tuple-element.60.q_ref.k_ref, bf16[128,512]{1,0:T(8,128)(2,1)S(1)} %get-tuple-element.61.g_ref.v_ref, bf16[128,512]{1,0:T(8,128)(2,1)S(1)} %get-tuple-element.48.k_ref, ...), custom_call_target="tpu_custom_call" | custom-call | flops 318767104 | bytes 6520832 | tf_op jit(solution)/shard_map/own/pallas_call | solution.py:486
  27.8 0.7 %own_band.1.total_ref = f32[2,128,512]{2,1,0:T(8,128)S(1)} custom-call(bf16[128,512]{1,0:T(8,128)(2,1)S(1)} %get-tuple-element.48.k_ref, bf16[128,512]{1,0:T(8,128)(2,1)S(1)} %get-tuple-element.49.v_ref, bf16[4,512,128]{2,1,0:T(8,128)(2,1)S(1)} %get-tuple-element.72.band_q_ref, bf16[4,512,128]{2,1,0:T(8,128)(2,1)S(1)} %get-tuple-element.73.band_g_ref, ...), custom_call_target="tpu_custom_call" | custom-call | flops 134217728 | bytes 3694592 | tf_op jit(solution)/shard_map/own_band/pallas_call | solution.py:486
  28.5 0.5 %collective-permute-done.10.side_east_ref = bf16[2,48,512]{2,1,0:T(8,128)(2,1)S(1)} collective-permute-done((bf16[2,48,512]{2,1,0:T(8,128)(2,1)S(1)}, bf16[2,48,512]{2,1,0:T(8,128)(2,1)S(1)}, u32[]{:S(2)}, u32[]{:S(2)}) %collective-permute-start.10) | collective-permute-done | bytes 98336 | tf_op jit(solution)/shard_map/ppermute | solution.py:49
  29.0 0.2 blend.1.blended_ref
  29.2 0.0 collective-permute-done.11.side_west_ref
  29.2 0.9 %final.1 = (bf16[128,512]{1,0:T(8,128)(2,1)}, bf16[128,512]{1,0:T(8,128)(2,1)}) custom-call(f32[2,128,512]{2,1,0:T(8,128)S(1)} %blend.1.blended_ref, bf16[2,48,512]{2,1,0:T(8,128)(2,1)S(1)} %collective-permute-done.11.side_west_ref), custom_call_target="tpu_custom_call" | custom-call | bytes 622592 | tf_op jit(solution)/shard_map/final/pallas_call | solution.py:486
  (3 shorter events, 0.1 us)
Async XLA Ops:
  1.9 9.5 %collective-permute-start = (bf16[2,48,512]{2,1,0:T(8,128)(2,1)S(1)}, bf16[2,48,512]{2,1,0:T(8,128)(2,1)S(1)}, u32[]{:S(2)}, u32[]{:S(2)}) collective-permute-start(bf16[2,48,512]{2,1,0:T(8,128)(2,1)S(1)} %get-tuple-element.50), channel_id=1, source_target_pairs={{0,1},{1,2},{2,3},{3,4},{4,5},{5,6},{6,7},{7,0},{8,9},{9,10},{10,1... | collective-permute-start | bytes 294920 | tf_op jit(solution)/shard_map/ppermute | solution.py:49
  4.9 6.7 %collective-permute-start.1 = (bf16[2,48,512]{2,1,0:T(8,128)(2,1)S(1)}, bf16[2,48,512]{2,1,0:T(8,128)(2,1)S(1)}, u32[]{:S(2)}, u32[]{:S(2)}) collective-permute-start(bf16[2,48,512]{2,1,0:T(8,128)(2,1)S(1)} %get-tuple-element.51), channel_id=1, source_target_pairs={{0,7},{1,0},{2,1},{3,2},{4,3},{5,4},{6,5},{7,6},{8,15},{9,8},{10,9... | collective-permute-start | bytes 294920 | tf_op jit(solution)/shard_map/ppermute | solution.py:49
  8.1 5.5 %collective-permute-start.2 = (bf16[2,96,512]{2,1,0:T(8,128)(2,1)S(1)}, bf16[2,96,512]{2,1,0:T(8,128)(2,1)S(1)}, u32[]{:S(2)}, u32[]{:S(2)}) collective-permute-start(bf16[2,96,512]{2,1,0:T(8,128)(2,1)S(1)} %get-tuple-element.55), channel_id=1, source_target_pairs={{0,8},{8,0},{16,24},{24,16},{1,9},{9,1},{17,25},{25,17},{2,10},{10... | collective-permute-start | bytes 589832 | tf_op jit(solution)/shard_map/ppermute | solution.py:44
  8.1 7.7 %collective-permute-start.3 = (bf16[2,96,512]{2,1,0:T(8,128)(2,1)S(1)}, bf16[2,96,512]{2,1,0:T(8,128)(2,1)S(1)}, u32[]{:S(2)}, u32[]{:S(2)}) collective-permute-start(bf16[2,96,512]{2,1,0:T(8,128)(2,1)S(1)} %get-tuple-element.56), channel_id=1, source_target_pairs={{8,16},{16,8},{24,0},{0,24},{9,17},{17,9},{25,1},{1,25},{10,18},{1... | collective-permute-start | bytes 589832 | tf_op jit(solution)/shard_map/ppermute | solution.py:44
  11.7 4.2 %collective-permute-start.4 = (bf16[2,96,512]{2,1,0:T(8,128)(2,1)S(1)}, bf16[2,96,512]{2,1,0:T(8,128)(2,1)S(1)}, u32[]{:S(2)}, u32[]{:S(2)}) collective-permute-start(bf16[2,96,512]{2,1,0:T(8,128)(2,1)S(1)} %join.1), channel_id=1, source_target_pairs={{0,8},{8,0},{16,24},{24,16},{1,9},{9,1},{17,25},{25,17},{2,10},{10... | collective-permute-start | bytes 589832 | tf_op jit(solution)/shard_map/ppermute | solution.py:44
  11.7 5.7 %collective-permute-start.5 = (bf16[2,96,512]{2,1,0:T(8,128)(2,1)S(1)}, bf16[2,96,512]{2,1,0:T(8,128)(2,1)S(1)}, u32[]{:S(2)}, u32[]{:S(2)}) collective-permute-start(bf16[2,96,512]{2,1,0:T(8,128)(2,1)S(1)} %join.1), channel_id=1, source_target_pairs={{0,2},{1,3},{2,0},{3,1},{4,6},{5,7},{6,4},{7,5},{8,16},{9,17},{10,... | collective-permute-start | bytes 589832 | tf_op jit(solution)/shard_map/ppermute | solution.py:61
  12.7 7.0 %collective-permute-start.6 = (bf16[2,96,512]{2,1,0:T(8,128)(2,1)S(1)}, bf16[2,96,512]{2,1,0:T(8,128)(2,1)S(1)}, u32[]{:S(2)}, u32[]{:S(2)}) collective-permute-start(bf16[2,96,512]{2,1,0:T(8,128)(2,1)S(1)} %get-tuple-element.70), channel_id=1, source_target_pairs={{0,8},{8,0},{16,24},{24,16},{1,9},{9,1},{17,25},{25,17},{2,10},{10... | collective-permute-start | bytes 589832 | tf_op jit(solution)/shard_map/ppermute | solution.py:44
  13.5 6.2 %collective-permute-start.7 = (bf16[2,96,512]{2,1,0:T(8,128)(2,1)S(1)}, bf16[2,96,512]{2,1,0:T(8,128)(2,1)S(1)}, u32[]{:S(2)}, u32[]{:S(2)}) collective-permute-start(bf16[2,96,512]{2,1,0:T(8,128)(2,1)S(1)} %get-tuple-element.62.after_ref), channel_id=1, source_target_pairs={{0,2},{1,3},{2,0},{3,1},{4,6},{5,7},{6,4},{7,5},{8,16},{9,17},{10,... | collective-permute-start | bytes 589832 | tf_op jit(solution)/shard_map/ppermute | solution.py:61
  18.0 3.2 %collective-permute-start.9 = (f32[32,128]{1,0:T(8,128)S(1)}, f32[32,128]{1,0:T(8,128)S(1)}, u32[]{:S(2)}, u32[]{:S(2)}) collective-permute-start(f32[32,128]{1,0:T(8,128)S(1)} %get-tuple-element.75), channel_id=1, source_target_pairs={{8,16},{16,8},{24,0},{0,24},{9,17},{17,9},{25,1},{1,25},{10,18},{1... | collective-permute-start | bytes 49160 | tf_op jit(solution)/shard_map/ppermute | solution.py:44
  19.1 1.6 %collective-permute-start.8 = (f32[16,128]{1,0:T(8,128)S(1)}, f32[16,128]{1,0:T(8,128)S(1)}, u32[]{:S(2)}, u32[]{:S(2)}) collective-permute-start(f32[16,128]{1,0:T(8,128)S(1)} %get-tuple-element.74), channel_id=1, source_target_pairs={{0,8},{8,0},{16,24},{24,16},{1,9},{9,1},{17,25},{25,17},{2,10},{10... | collective-permute-start | bytes 24584 | tf_op jit(solution)/shard_map/ppermute | solution.py:44
  21.4 7.6 %collective-permute-start.10 = (bf16[2,48,512]{2,1,0:T(8,128)(2,1)S(1)}, bf16[2,48,512]{2,1,0:T(8,128)(2,1)S(1)}, u32[]{:S(2)}, u32[]{:S(2)}) collective-permute-start(bf16[2,48,512]{2,1,0:T(8,128)(2,1)S(1)} %get-tuple-element.82), channel_id=1, source_target_pairs={{0,1},{1,2},{2,3},{3,4},{4,5},{5,6},{6,7},{7,0},{8,9},{9,10},{10,1... | collective-permute-start | bytes 294920 | tf_op jit(solution)/shard_map/ppermute | solution.py:49
  22.2 7.1 %collective-permute-start.11 = (bf16[2,48,512]{2,1,0:T(8,128)(2,1)S(1)}, bf16[2,48,512]{2,1,0:T(8,128)(2,1)S(1)}, u32[]{:S(2)}, u32[]{:S(2)}) collective-permute-start(bf16[2,48,512]{2,1,0:T(8,128)(2,1)S(1)} %get-tuple-element.83), channel_id=1, source_target_pairs={{0,7},{1,0},{2,1},{3,2},{4,3},{5,4},{6,5},{7,6},{8,15},{9,8},{10,9... | collective-permute-start | bytes 294920 | tf_op jit(solution)/shard_map/ppermute | solution.py:49

commit v13 on v12

--- a/solution.py
+++ b/solution.py
@@ -464,17 +464,11 @@
     return (cell == (place % ROWS) * COLS + first_col + place // ROWS).astype(BF16)
 
 
-def blend_kernel(total_ref, side_east_ref, blended_ref):
-    spread = spread_matrix(0)
-    for slot in (0, 1):
-        blended_ref[slot] = total_ref[slot] + jnp.dot(spread, side_east_ref[slot], preferred_element_type=F32)
-
-
-def final_kernel(blended_ref, side_west_ref, dk_ref, dv_ref):
-    spread = spread_matrix(COLS - RADIUS)
+def final_kernel(total_ref, side_east_ref, side_west_ref, dk_ref, dv_ref):
+    spread = jnp.concatenate([spread_matrix(0), spread_matrix(COLS - RADIUS)], axis=1)
     for slot, out in ((0, dk_ref), (1, dv_ref)):
-        total = blended_ref[slot] + jnp.dot(spread, side_west_ref[slot], preferred_element_type=F32)
-        out[...] = total.astype(BF16)
+        sides = jnp.concatenate([side_east_ref[slot], side_west_ref[slot]], axis=0)
+        out[...] = (total_ref[slot] + jnp.dot(spread, sides, preferred_element_type=F32)).astype(BF16)
 
 
 def arr(shape, dtype):
@@ -582,8 +576,7 @@
         own_band_kernel, "own_band", [k, v, band_q, band_g, band_table, lines_even, lines_odd, own],
         [arr((2, CELLS, feat), F32)], 8 * work * CELLS,
     )
-    blended, = call(blend_kernel, "blend", [total, side_east], [arr((2, CELLS, feat), F32)])
-    dk, dv = call(final_kernel, "final", [blended, side_west], [cells, cells])
+    dk, dv = call(final_kernel, "final", [total, side_east, side_west], [cells, cells])
     return tuple(x.reshape(block) for x in (out, dq, dk, dv))
 
 

time: 30.3 us -> 30.1 us (level)
    pallas_call x15 -> x14, Pallas kernels: 10.9 us -> 10.8 us  [call(): pl.pallas_call(kernel, out_shape=results, compiler_params=pltpu.CompilerP...]
where the time goes in v13:
time: 30.1 us; the launch traced here: 30 us
  starting transfers between devices  17.1 us (57%)
  Pallas kernels  10.8 us (36%)
  waiting for transfers between devices  1.34 us (4%)
  between operations  0.75 us (2%)
    ppermute x4, starting transfers between devices, ring_shift(): lax.ppermute(value, 'lon', [(lon, (lon + by) % count) for lon in range(co...  10.9 us
    pallas_call x14, Pallas kernels, call(): pl.pallas_call(kernel, out_shape=results, compiler_params=pltpu.CompilerP...  10.8 us
    ppermute x6, starting transfers between devices, pair_exchange(): return lax.ppermute(value, axis, pairs)  4.39 us
    ppermute x2, starting transfers between devices, odd_rows_exchange(): return lax.ppermute(value, ('lat', 'lon'), pairs)  1.81 us
    ppermute x4, waiting for transfers between devices, ring_shift(): lax.ppermute(value, 'lon', [(lon, (lon + by) % count) for lon in range(co...  0.75 us
  transfers between devices with their start and end apart: 12, of which 4 were waited for; matrix products, arithmetic and copies ran while one was open for 0% of the time, Pallas kernels for 28%

profile of v13, /device:TPU:0, one launch (start us, length us, event | category | flops | bytes accessed | tf_op | source)
XLA Modules:
  0.0 30.0 jit_solution(12435855198852526739)
XLA Ops:
  0.6 1.3 %pack.1 = (bf16[2,48,512]{2,1,0:T(8,128)(2,1)S(1)}, bf16[2,48,512]{2,1,0:T(8,128)(2,1)S(1)}, bf16[128,512]{1,0:T(8,128)(2,1)S(1)}, bf16[128,512]{1,0:T(8,128)(2,1)S(1)}, f32[8,169]{1,0:T(8,128)S(1)}) custom-call(bf16[128,512]{1,0:T(8,128)(2,1)} %bitcast.8, bf16[128,512]{1,0:T(8,128)(2,1)} %bitcast.9, f32[8,169]{1,0:T(8,128)} %bias_hbm.1), custom_call_target="tpu_custom_call" | custom-call | bytes 267552 | tf_op jit(solution)/shard_map/pack/pallas_call | solution.py:480
  1.9 3.0 %collective-permute-start = (bf16[2,48,512]{2,1,0:T(8,128)(2,1)S(1)}, bf16[2,48,512]{2,1,0:T(8,128)(2,1)S(1)}, u32[]{:S(2)}, u32[]{:S(2)}) collective-permute-start(bf16[2,48,512]{2,1,0:T(8,128)(2,1)S(1)} %get-tuple-element.50), channel_id=1, source_target_pairs={{0,1},{1,2},{2,3},{3,4},{4,5},{5,6},{6,7},{7,0},{8,9},{9,10},{10,1... | collective-permute-start | bytes 294920 | tf_op jit(solution)/shard_map/ppermute | solution.py:49
  4.9 3.1 %collective-permute-start.1 = (bf16[2,48,512]{2,1,0:T(8,128)(2,1)S(1)}, bf16[2,48,512]{2,1,0:T(8,128)(2,1)S(1)}, u32[]{:S(2)}, u32[]{:S(2)}) collective-permute-start(bf16[2,48,512]{2,1,0:T(8,128)(2,1)S(1)} %get-tuple-element.51), channel_id=1, source_target_pairs={{0,7},{1,0},{2,1},{3,2},{4,3},{5,4},{6,5},{7,6},{8,15},{9,8},{10,9... | collective-permute-start | bytes 294920 | tf_op jit(solution)/shard_map/ppermute | solution.py:49
  8.1 0.1 collective-permute-start.2
  8.1 1.7 %collective-permute-start.3 = (bf16[2,96,512]{2,1,0:T(8,128)(2,1)S(1)}, bf16[2,96,512]{2,1,0:T(8,128)(2,1)S(1)}, u32[]{:S(2)}, u32[]{:S(2)}) collective-permute-start(bf16[2,96,512]{2,1,0:T(8,128)(2,1)S(1)} %get-tuple-element.56), channel_id=1, source_target_pairs={{8,16},{16,8},{24,0},{0,24},{9,17},{17,9},{25,1},{1,25},{10,18},{1... | collective-permute-start | bytes 589832 | tf_op jit(solution)/shard_map/ppermute | solution.py:44
  9.8 1.6 %bias_table.1 = (f32[8,608,128]{2,1,0:T(8,128)S(1)}, bf16[128,512]{1,0:T(8,128)(2,1)S(1)}, bf16[128,512]{1,0:T(8,128)(2,1)S(1)}) custom-call(f32[8,169]{1,0:T(8,128)S(1)} %get-tuple-element.45.bias_ref, bf16[128,512]{1,0:T(8,128)(2,1)} %bitcast.10, bf16[128,512]{1,0:T(8,128)(2,1)} %bitcast.11), custom_call_target="tpu_custom_call" | custom-call | flops 622592 | bytes 267552 | tf_op jit(solution)/shard_map/bias_table/pallas_call | solution.py:480
  11.4 0.0 collective-permute-done.lon_west_ref
  11.4 0.2 collective-permute-done.1.lon_east_ref
  11.7 0.1 collective-permute-start.4
  11.7 0.9 %collective-permute-start.5 = (bf16[2,96,512]{2,1,0:T(8,128)(2,1)S(1)}, bf16[2,96,512]{2,1,0:T(8,128)(2,1)S(1)}, u32[]{:S(2)}, u32[]{:S(2)}) collective-permute-start(bf16[2,96,512]{2,1,0:T(8,128)(2,1)S(1)} %join.1), channel_id=1, source_target_pairs={{0,2},{1,3},{2,0},{3,1},{4,6},{5,7},{6,4},{7,5},{8,16},{9,17},{10,... | collective-permute-start | bytes 589832 | tf_op jit(solution)/shard_map/ppermute | solution.py:61
  12.7 0.8 %collective-permute-start.6 = (bf16[2,96,512]{2,1,0:T(8,128)(2,1)S(1)}, bf16[2,96,512]{2,1,0:T(8,128)(2,1)S(1)}, u32[]{:S(2)}, u32[]{:S(2)}) collective-permute-start(bf16[2,96,512]{2,1,0:T(8,128)(2,1)S(1)} %get-tuple-element.70), channel_id=1, source_target_pairs={{0,8},{8,0},{16,24},{24,16},{1,9},{9,1},{17,25},{25,17},{2,10},{10... | collective-permute-start | bytes 589832 | tf_op jit(solution)/shard_map/ppermute | solution.py:44
  13.5 0.0 collective-permute-done.2.lat_even_ref
  13.5 0.9 %collective-permute-start.7 = (bf16[2,96,512]{2,1,0:T(8,128)(2,1)S(1)}, bf16[2,96,512]{2,1,0:T(8,128)(2,1)S(1)}, u32[]{:S(2)}, u32[]{:S(2)}) collective-permute-start(bf16[2,96,512]{2,1,0:T(8,128)(2,1)S(1)} %get-tuple-element.62.after_ref), channel_id=1, source_target_pairs={{0,2},{1,3},{2,0},{3,1},{4,6},{5,7},{6,4},{7,5},{8,16},{9,17},{10,... | collective-permute-start | bytes 589832 | tf_op jit(solution)/shard_map/ppermute | solution.py:61
  14.4 1.4 %band_table.1.table_ref = f32[2,8,224,128]{3,2,1,0:T(8,128)S(1)} custom-call(f32[8,169]{1,0:T(8,128)S(1)} %get-tuple-element.45.bias_ref, bf16[2,96,512]{2,1,0:T(8,128)(2,1)S(1)} %get-tuple-element.62.after_ref), custom_call_target="tpu_custom_call" | custom-call | flops 458752 | bytes 202016 | tf_op jit(solution)/shard_map/band_table/pallas_call | solution.py:480
  15.8 0.0 collective-permute-done.3.lat_odd_ref
  15.9 0.0 collective-permute-done.4.corner_even_ref
  15.9 1.3 %near.1 = (f32[4,512,256]{2,1,0:T(8,128)S(1)}, f32[4,512,256]{2,1,0:T(8,128)S(1)}, f32[4,8,256]{2,1,0:T(8,128)S(1)}) custom-call(bf16[128,512]{1,0:T(8,128)(2,1)S(1)} %get-tuple-element.60.q_ref.k_ref, bf16[128,512]{1,0:T(8,128)(2,1)S(1)} %get-tuple-element.61.g_ref.v_ref, bf16[128,512]{1,0:T(8,128)(2,1)S(1)} %get-tuple-element.48.k_ref, ...), custom_call_target="tpu_custom_call" | custom-call | flops 268435456 | bytes 3801088 | tf_op jit(solution)/shard_map/near/pallas_call | solution.py:480
  17.1 0.3 %collective-permute-done.5.corner_ref.corner_odd_ref = bf16[2,96,512]{2,1,0:T(8,128)(2,1)S(1)} collective-permute-done((bf16[2,96,512]{2,1,0:T(8,128)(2,1)S(1)}, bf16[2,96,512]{2,1,0:T(8,128)(2,1)S(1)}, u32[]{:S(2)}, u32[]{:S(2)}) %collective-permute-start.5) | collective-permute-done | bytes 196640 | tf_op jit(solution)/shard_map/ppermute | solution.py:61
  17.5 0.5 %corner.1 = (f32[4,96,256]{2,1,0:T(8,128)S(1)}, f32[4,96,256]{2,1,0:T(8,128)S(1)}, f32[4,8,256]{2,1,0:T(8,128)S(1)}, f32[16,128]{1,0:T(8,128)S(1)}, f32[32,128]{1,0:T(8,128)S(1)}) custom-call(bf16[128,512]{1,0:T(8,128)(2,1)S(1)} %get-tuple-element.60.q_ref.k_ref, bf16[128,512]{1,0:T(8,128)(2,1)S(1)} %get-tuple-element.61.g_ref.v_ref, ...), custom_call_target="tpu_custom_call" | custom-call | flops 50331648 | bytes 2981888 | tf_op jit(solution)/shard_map/corner/pallas_call | solution.py:480
  18.0 1.1 %collective-permute-start.9 = (f32[32,128]{1,0:T(8,128)S(1)}, f32[32,128]{1,0:T(8,128)S(1)}, u32[]{:S(2)}, u32[]{:S(2)}) collective-permute-start(f32[32,128]{1,0:T(8,128)S(1)} %get-tuple-element.75), channel_id=1, source_target_pairs={{8,16},{16,8},{24,0},{0,24},{9,17},{17,9},{25,1},{1,25},{10,18},{1... | collective-permute-start | bytes 49160 | tf_op jit(solution)/shard_map/ppermute | solution.py:44
  19.1 0.6 %collective-permute-start.8 = (f32[16,128]{1,0:T(8,128)S(1)}, f32[16,128]{1,0:T(8,128)S(1)}, u32[]{:S(2)}, u32[]{:S(2)}) collective-permute-start(f32[16,128]{1,0:T(8,128)S(1)} %get-tuple-element.74), channel_id=1, source_target_pairs={{0,8},{8,0},{16,24},{24,16},{1,9},{9,1},{17,25},{25,17},{2,10},{10... | collective-permute-start | bytes 24584 | tf_op jit(solution)/shard_map/ppermute | solution.py:44
  19.7 0.0 collective-permute-done.6.queries_even_ref
  19.7 0.0 collective-permute-done.7.queries_odd_ref
  19.7 0.9 %side_scores.1 = (f32[2,96,512]{2,1,0:T(8,128)S(1)}, f32[4,96,512]{2,1,0:T(8,128)S(1)}, f32[4,96,512]{2,1,0:T(8,128)S(1)}, bf16[4,512,128]{2,1,0:T(8,128)(2,1)S(1)}, bf16[4,512,128]{2,1,0:T(8,128)(2,1)S(1)}) custom-call(bf16[128,512]{1,0:T(8,128)(2,1)S(1)} %get-tuple-element.60.q_ref.k_ref, bf16[128,512]{1,0:T(8,128)(2,1)S(1)} %get-tuple-element.61.g_ref.v_ref, ...), custom_call_target="tpu_custom_call" | custom-call | flops 100663296 | bytes 6914048 | tf_op jit(solution)/shard_map/side_scores/pallas_call | solution.py:480
  20.6 0.0 collective-permute-done.8.lines_ref.lines_even_ref
  20.6 0.3 side_even.1.sum_ref
  20.9 0.2 collective-permute-done.9.lines_odd_ref.lines_ref
  21.2 0.3 side_band.1
  21.4 0.7 %collective-permute-start.10 = (bf16[2,48,512]{2,1,0:T(8,128)(2,1)S(1)}, bf16[2,48,512]{2,1,0:T(8,128)(2,1)S(1)}, u32[]{:S(2)}, u32[]{:S(2)}) collective-permute-start(bf16[2,48,512]{2,1,0:T(8,128)(2,1)S(1)} %get-tuple-element.82), channel_id=1, source_target_pairs={{0,1},{1,2},{2,3},{3,4},{4,5},{5,6},{6,7},{7,0},{8,9},{9,10},{10,1... | collective-permute-start | bytes 294920 | tf_op jit(solution)/shard_map/ppermute | solution.py:49
  22.2 4.0 %collective-permute-start.11 = (bf16[2,48,512]{2,1,0:T(8,128)(2,1)S(1)}, bf16[2,48,512]{2,1,0:T(8,128)(2,1)S(1)}, u32[]{:S(2)}, u32[]{:S(2)}) collective-permute-start(bf16[2,48,512]{2,1,0:T(8,128)(2,1)S(1)} %get-tuple-element.83), channel_id=1, source_target_pairs={{0,7},{1,0},{2,1},{3,2},{4,3},{5,4},{6,5},{7,6},{8,15},{9,8},{10,9... | collective-permute-start | bytes 294920 | tf_op jit(solution)/shard_map/ppermute | solution.py:49
  26.2 1.6 %own.1 = (bf16[128,512]{1,0:T(8,128)(2,1)}, bf16[128,512]{1,0:T(8,128)(2,1)}, f32[2,128,512]{2,1,0:T(8,128)S(1)}) custom-call(bf16[128,512]{1,0:T(8,128)(2,1)S(1)} %get-tuple-element.60.q_ref.k_ref, bf16[128,512]{1,0:T(8,128)(2,1)S(1)} %get-tuple-element.61.g_ref.v_ref, bf16[128,512]{1,0:T(8,128)(2,1)S(1)} %get-tuple-element.48.k_ref, ...), custom_call_target="tpu_custom_call" | custom-call | flops 318767104 | bytes 6520832 | tf_op jit(solution)/shard_map/own/pallas_call | solution.py:480
  27.8 0.7 %own_band.1.total_ref = f32[2,128,512]{2,1,0:T(8,128)S(1)} custom-call(bf16[128,512]{1,0:T(8,128)(2,1)S(1)} %get-tuple-element.48.k_ref, bf16[128,512]{1,0:T(8,128)(2,1)S(1)} %get-tuple-element.49.v_ref, bf16[4,512,128]{2,1,0:T(8,128)(2,1)S(1)} %get-tuple-element.72.band_q_ref, bf16[4,512,128]{2,1,0:T(8,128)(2,1)S(1)} %get-tuple-element.73.band_g_ref, ...), custom_call_target="tpu_custom_call" | custom-call | flops 134217728 | bytes 3694592 | tf_op jit(solution)/shard_map/own_band/pallas_call | solution.py:480
  28.5 0.5 %collective-permute-done.10.side_east_ref = bf16[2,48,512]{2,1,0:T(8,128)(2,1)S(1)} collective-permute-done((bf16[2,48,512]{2,1,0:T(8,128)(2,1)S(1)}, bf16[2,48,512]{2,1,0:T(8,128)(2,1)S(1)}, u32[]{:S(2)}, u32[]{:S(2)}) %collective-permute-start.10) | collective-permute-done | bytes 98336 | tf_op jit(solution)/shard_map/ppermute | solution.py:49
  29.0 0.0 collective-permute-done.11.side_west_ref
  29.0 0.9 %final.1 = (bf16[128,512]{1,0:T(8,128)(2,1)}, bf16[128,512]{1,0:T(8,128)(2,1)}) custom-call(f32[2,128,512]{2,1,0:T(8,128)S(1)} %own_band.1.total_ref, bf16[2,48,512]{2,1,0:T(8,128)(2,1)S(1)} %collective-permute-done.10.side_east_ref, bf16[2,48,512]{2,1,0:T(8,128)(2,1)S(1)} %collective-permute-done.11.side_west_ref), custom_call_target="tpu_custom_call" | custom-call | bytes 720896 | tf_op jit(solution)/shard_map/final/pallas_call | solution.py:480
  (3 shorter events, 0.1 us)
Async XLA Ops:
  1.9 9.5 %collective-permute-start = (bf16[2,48,512]{2,1,0:T(8,128)(2,1)S(1)}, bf16[2,48,512]{2,1,0:T(8,128)(2,1)S(1)}, u32[]{:S(2)}, u32[]{:S(2)}) collective-permute-start(bf16[2,48,512]{2,1,0:T(8,128)(2,1)S(1)} %get-tuple-element.50), channel_id=1, source_target_pairs={{0,1},{1,2},{2,3},{3,4},{4,5},{5,6},{6,7},{7,0},{8,9},{9,10},{10,1... | collective-permute-start | bytes 294920 | tf_op jit(solution)/shard_map/ppermute | solution.py:49
  4.9 6.7 %collective-permute-start.1 = (bf16[2,48,512]{2,1,0:T(8,128)(2,1)S(1)}, bf16[2,48,512]{2,1,0:T(8,128)(2,1)S(1)}, u32[]{:S(2)}, u32[]{:S(2)}) collective-permute-start(bf16[2,48,512]{2,1,0:T(8,128)(2,1)S(1)} %get-tuple-element.51), channel_id=1, source_target_pairs={{0,7},{1,0},{2,1},{3,2},{4,3},{5,4},{6,5},{7,6},{8,15},{9,8},{10,9... | collective-permute-start | bytes 294920 | tf_op jit(solution)/shard_map/ppermute | solution.py:49
  8.1 5.5 %collective-permute-start.2 = (bf16[2,96,512]{2,1,0:T(8,128)(2,1)S(1)}, bf16[2,96,512]{2,1,0:T(8,128)(2,1)S(1)}, u32[]{:S(2)}, u32[]{:S(2)}) collective-permute-start(bf16[2,96,512]{2,1,0:T(8,128)(2,1)S(1)} %get-tuple-element.55), channel_id=1, source_target_pairs={{0,8},{8,0},{16,24},{24,16},{1,9},{9,1},{17,25},{25,17},{2,10},{10... | collective-permute-start | bytes 589832 | tf_op jit(solution)/shard_map/ppermute | solution.py:44
  8.1 7.7 %collective-permute-start.3 = (bf16[2,96,512]{2,1,0:T(8,128)(2,1)S(1)}, bf16[2,96,512]{2,1,0:T(8,128)(2,1)S(1)}, u32[]{:S(2)}, u32[]{:S(2)}) collective-permute-start(bf16[2,96,512]{2,1,0:T(8,128)(2,1)S(1)} %get-tuple-element.56), channel_id=1, source_target_pairs={{8,16},{16,8},{24,0},{0,24},{9,17},{17,9},{25,1},{1,25},{10,18},{1... | collective-permute-start | bytes 589832 | tf_op jit(solution)/shard_map/ppermute | solution.py:44
  11.7 4.2 %collective-permute-start.4 = (bf16[2,96,512]{2,1,0:T(8,128)(2,1)S(1)}, bf16[2,96,512]{2,1,0:T(8,128)(2,1)S(1)}, u32[]{:S(2)}, u32[]{:S(2)}) collective-permute-start(bf16[2,96,512]{2,1,0:T(8,128)(2,1)S(1)} %join.1), channel_id=1, source_target_pairs={{0,8},{8,0},{16,24},{24,16},{1,9},{9,1},{17,25},{25,17},{2,10},{10... | collective-permute-start | bytes 589832 | tf_op jit(solution)/shard_map/ppermute | solution.py:44
  11.7 5.7 %collective-permute-start.5 = (bf16[2,96,512]{2,1,0:T(8,128)(2,1)S(1)}, bf16[2,96,512]{2,1,0:T(8,128)(2,1)S(1)}, u32[]{:S(2)}, u32[]{:S(2)}) collective-permute-start(bf16[2,96,512]{2,1,0:T(8,128)(2,1)S(1)} %join.1), channel_id=1, source_target_pairs={{0,2},{1,3},{2,0},{3,1},{4,6},{5,7},{6,4},{7,5},{8,16},{9,17},{10,... | collective-permute-start | bytes 589832 | tf_op jit(solution)/shard_map/ppermute | solution.py:61
  12.7 7.0 %collective-permute-start.6 = (bf16[2,96,512]{2,1,0:T(8,128)(2,1)S(1)}, bf16[2,96,512]{2,1,0:T(8,128)(2,1)S(1)}, u32[]{:S(2)}, u32[]{:S(2)}) collective-permute-start(bf16[2,96,512]{2,1,0:T(8,128)(2,1)S(1)} %get-tuple-element.70), channel_id=1, source_target_pairs={{0,8},{8,0},{16,24},{24,16},{1,9},{9,1},{17,25},{25,17},{2,10},{10... | collective-permute-start | bytes 589832 | tf_op jit(solution)/shard_map/ppermute | solution.py:44
  13.5 6.2 %collective-permute-start.7 = (bf16[2,96,512]{2,1,0:T(8,128)(2,1)S(1)}, bf16[2,96,512]{2,1,0:T(8,128)(2,1)S(1)}, u32[]{:S(2)}, u32[]{:S(2)}) collective-permute-start(bf16[2,96,512]{2,1,0:T(8,128)(2,1)S(1)} %get-tuple-element.62.after_ref), channel_id=1, source_target_pairs={{0,2},{1,3},{2,0},{3,1},{4,6},{5,7},{6,4},{7,5},{8,16},{9,17},{10,... | collective-permute-start | bytes 589832 | tf_op jit(solution)/shard_map/ppermute | solution.py:61
  18.0 3.2 %collective-permute-start.9 = (f32[32,128]{1,0:T(8,128)S(1)}, f32[32,128]{1,0:T(8,128)S(1)}, u32[]{:S(2)}, u32[]{:S(2)}) collective-permute-start(f32[32,128]{1,0:T(8,128)S(1)} %get-tuple-element.75), channel_id=1, source_target_pairs={{8,16},{16,8},{24,0},{0,24},{9,17},{17,9},{25,1},{1,25},{10,18},{1... | collective-permute-start | bytes 49160 | tf_op jit(solution)/shard_map/ppermute | solution.py:44
  19.1 1.6 %collective-permute-start.8 = (f32[16,128]{1,0:T(8,128)S(1)}, f32[16,128]{1,0:T(8,128)S(1)}, u32[]{:S(2)}, u32[]{:S(2)}) collective-permute-start(f32[16,128]{1,0:T(8,128)S(1)} %get-tuple-element.74), channel_id=1, source_target_pairs={{0,8},{8,0},{16,24},{24,16},{1,9},{9,1},{17,25},{25,17},{2,10},{10... | collective-permute-start | bytes 24584 | tf_op jit(solution)/shard_map/ppermute | solution.py:44
  21.4 7.6 %collective-permute-start.10 = (bf16[2,48,512]{2,1,0:T(8,128)(2,1)S(1)}, bf16[2,48,512]{2,1,0:T(8,128)(2,1)S(1)}, u32[]{:S(2)}, u32[]{:S(2)}) collective-permute-start(bf16[2,48,512]{2,1,0:T(8,128)(2,1)S(1)} %get-tuple-element.82), channel_id=1, source_target_pairs={{0,1},{1,2},{2,3},{3,4},{4,5},{5,6},{6,7},{7,0},{8,9},{9,10},{10,1... | collective-permute-start | bytes 294920 | tf_op jit(solution)/shard_map/ppermute | solution.py:49
  22.2 6.9 %collective-permute-start.11 = (bf16[2,48,512]{2,1,0:T(8,128)(2,1)S(1)}, bf16[2,48,512]{2,1,0:T(8,128)(2,1)S(1)}, u32[]{:S(2)}, u32[]{:S(2)}) collective-permute-start(bf16[2,48,512]{2,1,0:T(8,128)(2,1)S(1)} %get-tuple-element.83), channel_id=1, source_target_pairs={{0,7},{1,0},{2,1},{3,2},{4,3},{5,4},{6,5},{7,6},{8,15},{9,8},{10,9... | collective-permute-start | bytes 294920 | tf_op jit(solution)/shard_map/ppermute | solution.py:49
